TPU v7x, 32 devices: a whole 2x2x4 slice. The times are simulated.
32 devices in a mesh: shard: 8 (over y, x, core), tile: 4 (over z).
Axes of the slice: x: 2, y: 2, z: 4, core: 2. Of those that a mesh axis runs over, the one named last changes fastest.
Arguments:
- embeddings: float32 [32768, 768], P(('shard', 'tile')), may hold values from -12 to 12
- cluster_ids: int32 [32768], P(('shard', 'tile')), may hold values from 0 to 127, as said below
Outputs:
- soft_max_sim: float32 [32768], P(('shard', 'tile'))
Inputs may be any that keep to these rules, and one draw needn't show every extreme that they name: `cluster_ids`: cluster c is owned by group c // 16. Each device holds at most 256 rows of one group's clusters; in every draw, for each tile index, some group gets exactly 256 rows from every device of that tile index.
All inputs are finite; a program needn't handle non-finite values.
Results may differ from a plain program's by a relative error of at most 0.00053.
Values may be sent and summed in bfloat16 or wider, within the bound.
No kernel may reach another device: no remote copies, remote signals or barrier semaphores. Data moves between devices by JAX's collectives and lax.ppermute only.
A program may use at most 64 MiB of HBM per device.

v0:
```python
import jax
import jax.numpy as jnp
from jax import lax
from jax.sharding import PartitionSpec as P

KG = 16


sharpness = 30.0
epsilon = 1e-06


def unit_rows(embeddings):
    energy = jnp.sum(embeddings * embeddings, axis=1, keepdims=True)
    return (embeddings * lax.rsqrt(energy + epsilon)).astype(jnp.bfloat16)


def pair_sums(left, left_labels, left_place, right, right_labels, right_place):
    count = left.shape[0]
    block = min(512, count)
    blocks = count // block

    def step(column_total, items):
        rows_block, labels_block, place_block = items
        scores = lax.dot_general(
            rows_block, right, (((1,), (1,)), ((), ())), preferred_element_type=jnp.float32
        )
        same = (labels_block[:, None] == right_labels[None, :]) & (labels_block[:, None] >= 0)
        same = same & (place_block[:, None] < right_place[None, :])
        terms = jnp.where(same, jnp.exp(sharpness * scores), 0.0)
        return (column_total + jnp.sum(terms, axis=0), jnp.sum(terms, axis=1))

    column_total, row_totals = lax.scan(
        step,
        jnp.zeros((right.shape[0],), jnp.float32),
        (
            left.reshape(blocks, block, left.shape[1]),
            left_labels.reshape(blocks, block),
            left_place.reshape(blocks, block),
        ),
    )
    return (row_totals.reshape(count), column_total)


def add_into(vector, start, values):
    current = lax.dynamic_slice_in_dim(vector, start, values.shape[0])
    return lax.dynamic_update_slice_in_dim(vector, current + values, start, 0)


def body(embeddings, cluster_ids):
    local_rows = embeddings.shape[0]
    shards = lax.axis_size("shard")
    tiles = lax.axis_size("tile")
    capacity = 2 * local_rows // shards
    slot_count = shards * capacity
    unit = unit_rows(embeddings)
    owner = cluster_ids // KG
    onehot = (owner[:, None] == jnp.arange(shards, dtype=jnp.int32)[None, :]).astype(jnp.int32)
    ranks = jnp.sum((jnp.cumsum(onehot, axis=0) - 1) * onehot, axis=1)
    slots = owner * capacity + ranks
    outgoing = jnp.zeros((slot_count, unit.shape[1]), jnp.bfloat16).at[slots].set(unit)
    outgoing_labels = jnp.full((slot_count,), -1, jnp.int32).at[slots].set(cluster_ids)
    arrived, arrived_labels = (
        lax.all_to_all(
            outgoing.reshape(shards, capacity, unit.shape[1]),
            "shard",
            split_axis=0,
            concat_axis=0,
            tiled=True,
        ),
        lax.all_to_all(
            outgoing_labels.reshape(shards, capacity),
            "shard",
            split_axis=0,
            concat_axis=0,
            tiled=True,
        ),
    )
    owned = arrived.reshape(slot_count, unit.shape[1])
    owned_labels = arrived_labels.reshape(slot_count)
    tile_index = lax.axis_index("tile")
    own_start = tile_index * slot_count
    own_place = own_start + jnp.arange(slot_count, dtype=jnp.int32)
    group_size = tiles * slot_count
    initial = (jnp.zeros((slot_count,), jnp.float32), jnp.zeros((group_size,), jnp.float32))
    start = jnp.int32(0)
    piece_rows = lax.all_gather(owned, "tile", axis=0, tiled=True)
    piece_labels = lax.all_gather(owned_labels, "tile", axis=0, tiled=True)
    width = piece_rows.shape[0]
    piece_place = jnp.arange(width, dtype=jnp.int32)

    def work(state):
        row_part, column_part = pair_sums(
            owned, owned_labels, own_place, piece_rows, piece_labels, piece_place
        )
        return (row_part, add_into(state[1], start, column_part))

    def skip(state):
        return state

    row_sum, column_sum = lax.cond(start + width > own_start, work, skip, initial)
    group_total = add_into(column_sum, own_start, row_sum)
    own_totals = lax.psum_scatter(
        group_total.astype(jnp.bfloat16), "tile", scatter_dimension=0, tiled=True
    ).astype(jnp.float32)
    returned = lax.all_to_all(
        own_totals.reshape(shards, capacity), "shard", split_axis=0, concat_axis=0, tiled=True
    )
    totals = returned.reshape(slot_count)[slots]
    return jnp.log(1.0 + totals)


def solution(mesh):
    in_specs = (P(("shard", "tile"), None), P(("shard", "tile")))
    out_specs = P(("shard", "tile"))
    return jax.shard_map(body, mesh=mesh, in_specs=in_specs, out_specs=out_specs, check_vma=False)
```

profile of v0, /device:TPU:0, one launch (start us, length us, event | category | flops | bytes accessed | tf_op | source)
XLA Modules:
  0.0 381.0 jit_solution(687851169894896715)
XLA Ops:
  6.5 0.8 add_select_fusion
  7.4 2.3 reduce-window.6
  10.9 2.2 multiply_reduce_fusion
  13.1 7.7 %scatter_custom_fusion = bf16[2048,768]{1,0:T(8,128)(2,1)} fusion(s32[1024]{0:T(1024)S(1)} %get-tuple-element.139, f32[1024,768]{1,0:T(8,128)S(1)} %copy-done, f32[1024]{0:T(1024)S(1)} %add_rsqrt_fusion, bf16[]{:T(256)} %constant.34.clone.1), kind=kCustom, calls=%fused_computation.14 | custom fusion | flops 1572864 | bytes 6295554 | tf_op jit(solution)/shard_map/scatter | solution.py:61
  20.8 43.1 %all_to_all.28 = bf16[8,256,768]{2,1,0:T(8,128)(2,1)} all-to-all(bf16[8,256,768]{2,1,0:T(8,128)(2,1)} %bitcast.49), channel_id=1, replica_groups=mesh['shard'=8,'tile'=4] {'shard'}, dimensions={0} | all-to-all | bytes 6291456 | tf_op jit(solution)/shard_map/all_to_all | solution.py:64
  64.0 5.0 %scatter_custom_fusion.1 = s32[2048]{0:T(1024)} fusion(s32[1024]{0:T(1024)S(1)} %get-tuple-element.139, s32[1024]{0:T(1024)} %param.7, s32[]{:T(128)} %constant.64.clone.1), kind=kCustom, calls=%fused_computation.34 | custom fusion | bytes 8704 | tf_op jit(solution)/shard_map/scatter | solution.py:62
  69.0 3.3 all-to-all-start.1
  73.6 3.3 all-to-all-done.1
  76.9 21.0 %all_gather.6 = s32[8192]{0:T(1024)S(1)} all-gather(s32[2048]{0:T(1024)S(1)} %bitcast.52), channel_id=1, replica_groups=mesh['shard'=8,'tile'=4] {'tile'}, dimensions={0}, use_global_device_ids=true | all-gather | bytes 40960 | tf_op jit(solution)/shard_map/all_gather | solution.py:88
  97.9 184.9 %all-gather.2.cloned.1.call-done = bf16[8192,768]{1,0:T(8,128)(2,1)} async-done(((bf16[2048,768]{1,0:T(8,128)(2,1)}), bf16[8192,768]{1,0:T(8,128)(2,1)}) %all-gather.2.cloned.1.call-update) | async-done | bytes 12582928 | tf_op jit(solution)/shard_map/all_gather | solution.py:87
  282.8 58.4 %conditional.1 = (f32[2048]{0:T(1024)S(1)}, f32[8192]{0:T(1024)}) conditional(s32[]{:T(128)} %convert_element_type.15, () %tuple.17, (bf16[8,256,768]{2,1,0:T(8,128)(2,1)}, s32[8,1,256]{2,1,0:T(1,128)S(1)}, s32[]{:T(128)}, s32[2048]{0:T(1024)S(1)}, s32[8192]{0:T(1024)S(1)}, /*index=5*/s32[8192]{0:T(1024)S(1)}, bf16[8192,768]{1,0:T(8,128)(2,1)}) %tuple.18), branch_computations={%region_6.7_spmd, %region_7.12_spmd} | conditional | flops 6476015616 | bytes 13670135 | solution.py:101
  282.9 58.3 %while.12 = (s32[]{:T(128)}, f32[8192]{0:T(1024)}, f32[4,512]{1,0:T(4,128)S(1)}, s32[4,512]{1,0:T(4,128)S(1)}, s32[8192]{0:T(1024)S(1)}, /*index=5*/s32[4,512]{1...) while((s32[]{:T(128)}, f32[8192]{0:T(1024)}, ...), condition=%wide.region_11.11_spmd.clone, body=%wide.region_8.10_spmd.clone.sunk | while | flops 6476013568 | bytes 13588095 | solution.py:33
  282.9 13.3 %fusion.19 = (f32[512]{0:T(512)S(1)}, f32[8192]{0:T(1024)S(1)}) fusion(bf16[8192,768]{1,0:T(8,128)(2,1)} %get-tuple-element.237, bf16[4,512,768]{2,1,0:T(8,128)(2,1)} %get-tuple-element.236, s32[]{:T(128)} %get-tuple-element.218, s32[8192]{0:T(1024)S(1)} %get-tuple-element.235, s32[512]{0:T(512)S(1)} %bitcast.53, ...), kind=kOutput, calls=%fused_computation.41.clone.1 | convolution fusion | flops 6475996672 | bytes 13474816 | tf_op jit(solution)/shard_map/cond/branch_1_fun/while/body/eval_jaxpr/dot_general | solution.py:25
  297.0 13.3 %fusion.19 = (f32[512]{0:T(512)S(1)}, f32[8192]{0:T(1024)S(1)}) fusion(bf16[8192,768]{1,0:T(8,128)(2,1)} %get-tuple-element.237, bf16[4,512,768]{2,1,0:T(8,128)(2,1)} %get-tuple-element.236, s32[]{:T(128)} %get-tuple-element.218, s32[8192]{0:T(1024)S(1)} %get-tuple-element.235, s32[512]{0:T(512)S(1)} %bitcast.53, ...), kind=kOutput, calls=%fused_computation.41.clone.1 | convolution fusion | flops 6475996672 | bytes 13474816 | tf_op jit(solution)/shard_map/cond/branch_1_fun/while/body/eval_jaxpr/dot_general | solution.py:25
  310.3 1.4 select_add_fusion.2
  311.7 13.3 %fusion.19 = (f32[512]{0:T(512)S(1)}, f32[8192]{0:T(1024)S(1)}) fusion(bf16[8192,768]{1,0:T(8,128)(2,1)} %get-tuple-element.237, bf16[4,512,768]{2,1,0:T(8,128)(2,1)} %get-tuple-element.236, s32[]{:T(128)} %get-tuple-element.218, s32[8192]{0:T(1024)S(1)} %get-tuple-element.235, s32[512]{0:T(512)S(1)} %bitcast.53, ...), kind=kOutput, calls=%fused_computation.41.clone.1 | convolution fusion | flops 6475996672 | bytes 13474816 | tf_op jit(solution)/shard_map/cond/branch_1_fun/while/body/eval_jaxpr/dot_general | solution.py:25
  325.1 1.4 select_add_fusion.2
  326.5 13.3 %fusion.19 = (f32[512]{0:T(512)S(1)}, f32[8192]{0:T(1024)S(1)}) fusion(bf16[8192,768]{1,0:T(8,128)(2,1)} %get-tuple-element.237, bf16[4,512,768]{2,1,0:T(8,128)(2,1)} %get-tuple-element.236, s32[]{:T(128)} %get-tuple-element.218, s32[8192]{0:T(1024)S(1)} %get-tuple-element.235, s32[512]{0:T(512)S(1)} %bitcast.53, ...), kind=kOutput, calls=%fused_computation.41.clone.1 | convolution fusion | flops 6475996672 | bytes 13474816 | tf_op jit(solution)/shard_map/cond/branch_1_fun/while/body/eval_jaxpr/dot_general | solution.py:25
  339.8 1.4 select_add_fusion.2
  341.3 1.3 add_dynamic-update-slice_fusion
  342.6 0.8 convert_element_type.18
  343.3 15.7 %all-reduce = bf16[8192]{0:T(1024)(128)(2,1)S(1)} all-reduce(bf16[8192]{0:T(1024)(128)(2,1)S(1)} %convert_element_type.18), channel_id=2, replica_groups=mesh['shard'=8,'tile'=4] {'tile'}, use_global_device_ids=true, to_apply=%region_12.13.clone | all-reduce | flops 8192 | bytes 32768
  359.0 8.4 %all_to_all.29 = f32[8,1,256]{2,1,0:T(1,128)S(1)} all-to-all(f32[8,1,256]{2,1,0:T(1,128)S(1)} %bitcast.56), channel_id=1, replica_groups=mesh['shard'=8,'tile'=4] {'shard'}, dimensions={0} | all-to-all | bytes 16384 | tf_op jit(solution)/shard_map/all_to_all | solution.py:106
  367.4 6.1 %gather_fusion = f32[1024]{0:T(1024)S(1)} fusion(f32[2048]{0:T(1024)S(1)} %bitcast.46, s32[1024]{0:T(1024)S(1)} %get-tuple-element.138), kind=kCustom, calls=%fused_computation | custom fusion | bytes 12288 | tf_op jit(solution)/shard_map/gather | solution.py:109
  (38 shorter events, 3.4 us)
Async XLA Ops:
  6.5 6.6 %copy-start = (f32[1024,768]{1,0:T(8,128)S(1)}, f32[1024,768]{1,0:T(8,128)}, u32[]{:S(2)}) copy-start(f32[1024,768]{1,0:T(8,128)} %param.6) | copy-start | bytes 9437188
  6.5 276.3 %all-gather.2.cloned.1.call-start = ((), (), s32[]{:S(2)}) async-start(), calls=%async_computation.3 | async-start | bytes 15728640 | tf_op jit(solution)/shard_map/all_gather | solution.py:87
  63.9 8.4 %copy-start.1 = (u32[32]{0:T(128)S(1)}, u32[32]{0:T(128)}, u32[]{:S(2)}) copy-start(u32[32]{0:T(128)} %constant.71) | copy-start | bytes 388
  69.0 7.9 %all-to-all-start.1 = ((s32[8,1,256]{2,1,0:T(1,128)}), s32[8,1,256]{2,1,0:T(1,128)S(1)}, u32[]{:S(2)}, u32[]{:S(2)}) async-start(s32[8,1,256]{2,1,0:T(1,128)} %bitcast.4), calls=%async_computation.1 | async-start | bytes 16384 | tf_op jit(solution)/shard_map/all_to_all | solution.py:71
Sparse Core Ops, SparseCore 0:
  64.1 218.6 all-gather.1
where the time goes:
time: 382 us; the launch traced here: 381 us
  waiting for transfers between devices  188 us (49%)
  blocking collectives  88.2 us (23%)
  matrix products  53.3 us (14%)
  other arithmetic  21.4 us (6%)
  between operations  14.1 us (4%)
  local copies, waits for them, and re-layouts  12.3 us (3%)
    all_gather x1, waiting for transfers between devices, body(): piece_rows = lax.all_gather(owned, 'tile', axis=0, tiled=True)  185 us
    dot_general x4, matrix products, step(): lax.dot_general(rows_block, right, (((1,), (1,)), ((), ())), preferred_el...  53.3 us
    all_to_all x1, blocking collectives, body(): lax.all_to_all(outgoing.reshape(shards, capacity, unit.shape[1]), 'shard'...  43.1 us
    all_gather x1, blocking collectives, body(): piece_labels = lax.all_gather(owned_labels, 'tile', axis=0, tiled=True)  21 us
    unnamed x1, blocking collectives  15.7 us
    all_to_all x1, blocking collectives, body(): lax.all_to_all(own_totals.reshape(shards, capacity), 'shard', split_axis=...  8.41 us
    scatter x1, other arithmetic, body(): jnp.zeros((slot_count, unit.shape[1]), jnp.bfloat16).at[slots].set(unit)  7.72 us
  transfers between devices with their start and end apart: 2, of which 2 were waited for; matrix products, arithmetic and copies ran while one was open for 1% of the time, Pallas kernels for 0%

commit v1 on v0

v1 whole, which is shorter than its diff:
```python
import functools

import jax
import jax.numpy as jnp
from jax import lax
from jax.experimental import pallas as pl
from jax.experimental.pallas import tpu as pltpu
from jax.sharding import Mesh
from jax.sharding import PartitionSpec as P

KG = 16


sharpness = 30.0
epsilon = 1e-06

VMEM_BYTES = 48 * 1024 * 1024
LANES = 128
FLAG = LANES - 1


def unit_rows(embeddings):
    energy = jnp.sum(embeddings * embeddings, axis=1, keepdims=True)
    return (embeddings * lax.rsqrt(energy + epsilon)).astype(jnp.bfloat16)


def pair_sums(left, left_labels, left_place, right, right_labels, right_place):
    count = left.shape[0]
    block = min(512, count)
    blocks = count // block

    def step(column_total, items):
        rows_block, labels_block, place_block = items
        scores = lax.dot_general(
            rows_block, right, (((1,), (1,)), ((), ())), preferred_element_type=jnp.float32
        )
        same = (labels_block[:, None] == right_labels[None, :]) & (labels_block[:, None] >= 0)
        same = same & (place_block[:, None] < right_place[None, :])
        terms = jnp.where(same, jnp.exp(sharpness * scores), 0.0)
        return (column_total + jnp.sum(terms, axis=0), jnp.sum(terms, axis=1))

    column_total, row_totals = lax.scan(
        step,
        jnp.zeros((right.shape[0],), jnp.float32),
        (
            left.reshape(blocks, block, left.shape[1]),
            left_labels.reshape(blocks, block),
            left_place.reshape(blocks, block),
        ),
    )
    return (row_totals.reshape(count), column_total)


def add_into(vector, start, values):
    current = lax.dynamic_slice_in_dim(vector, start, values.shape[0])
    return lax.dynamic_update_slice_in_dim(vector, current + values, start, 0)


def general_plan(embeddings, cluster_ids):
    shard_axes = ("chip", "core")
    local_rows = embeddings.shape[0]
    shards = lax.axis_size("chip") * lax.axis_size("core")
    tiles = lax.axis_size("tile")
    capacity = 2 * local_rows // shards
    slot_count = shards * capacity
    unit = unit_rows(embeddings)
    owner = cluster_ids // KG
    onehot = (owner[:, None] == jnp.arange(shards, dtype=jnp.int32)[None, :]).astype(jnp.int32)
    ranks = jnp.sum((jnp.cumsum(onehot, axis=0) - 1) * onehot, axis=1)
    slots = owner * capacity + ranks
    outgoing = jnp.zeros((slot_count, unit.shape[1]), jnp.bfloat16).at[slots].set(unit)
    outgoing_labels = jnp.full((slot_count,), -1, jnp.int32).at[slots].set(cluster_ids)
    owned = lax.all_to_all(outgoing, shard_axes, split_axis=0, concat_axis=0, tiled=True)
    owned_labels = lax.all_to_all(
        outgoing_labels, shard_axes, split_axis=0, concat_axis=0, tiled=True
    )
    own_start = lax.axis_index("tile") * slot_count
    own_place = own_start + jnp.arange(slot_count, dtype=jnp.int32)
    group_size = tiles * slot_count
    piece_rows = lax.all_gather(owned, "tile", axis=0, tiled=True)
    piece_labels = lax.all_gather(owned_labels, "tile", axis=0, tiled=True)
    piece_place = jnp.arange(group_size, dtype=jnp.int32)
    row_sum, column_sum = pair_sums(
        owned, owned_labels, own_place, piece_rows, piece_labels, piece_place
    )
    group_total = add_into(column_sum, own_start, row_sum)
    own_totals = lax.psum_scatter(
        group_total.astype(jnp.bfloat16), "tile", scatter_dimension=0, tiled=True
    ).astype(jnp.float32)
    returned = lax.all_to_all(own_totals, shard_axes, split_axis=0, concat_axis=0, tiled=True)
    return jnp.log(1.0 + returned[slots])


def up(value, multiple):
    return -(-value // multiple) * multiple


def exact_dot(left, right):
    return jnp.dot(
        left, right, precision=lax.Precision.HIGHEST, preferred_element_type=jnp.float32
    )


def iota(shape, axis):
    return lax.broadcasted_iota(jnp.int32, shape, axis)


def pack_kernel(chips, labels, cap, emb_ref, ids_ref, out_ref, rank_ref, aug_ref):
    rows, width = emb_ref.shape
    bits = chips.bit_length() - 1
    chunk = 256
    for start in range(0, rows, chunk):
        x = emb_ref[start : start + chunk, :]
        energy = jnp.sum(x * x, axis=1, keepdims=True)
        aug_ref[start : start + chunk, :] = (x * lax.rsqrt(energy + epsilon)).astype(jnp.bfloat16)

    ids = ids_ref[...]
    chip = ids & (chips - 1)
    label = ids >> bits
    key = ((chip * labels + label) * rows + iota((1, rows), 1)).astype(jnp.float32)
    base = (chip * (labels * rows)).astype(jnp.float32)
    key_t = jnp.broadcast_to(key, (LANES, rows)).T
    ranks = []
    for start in range(0, rows, LANES):
        own = key[:, start : start + LANES]
        low = base[:, start : start + LANES]
        before = (key_t < own) & (key_t >= low)
        ranks.append(jnp.sum(jnp.where(before, 1.0, 0.0), axis=0, keepdims=True))
    rank = jnp.concatenate(ranks, axis=1)
    rank_ref[...] = rank
    over = jnp.max(jnp.where(rank >= cap - 1, 1.0, 0.0), axis=1, keepdims=True)
    slot = jnp.where(rank < cap - 1, chip * cap + rank.astype(jnp.int32), -1)

    in_chip = jnp.where(iota((LANES, rows), 0) == chip, 1.0, 0.0).astype(jnp.bfloat16)
    in_label = jnp.where(iota((LANES, rows), 0) == label, 1.0, 0.0).astype(jnp.bfloat16)
    counts = lax.dot_general(
        in_chip, in_label, (((1,), (1,)), ((), ())), preferred_element_type=jnp.float32
    )
    counts = jnp.where(iota((LANES, LANES), 1) == FLAG, over, counts)
    aug_ref[rows:, :] = jnp.zeros((LANES, width), jnp.bfloat16)
    aug_ref[rows:, 0:LANES] = counts.astype(jnp.bfloat16)
    place = iota((1, LANES), 1)
    head = jnp.where(place < chips, place * cap + cap - 1, -1)
    slot = jnp.concatenate([slot, head], axis=1)

    total = chips * cap
    step = 16 * max(d for d in range(1, 17) if (total // 16) % d == 0)
    for start in range(0, total, step):
        pick = jnp.where(iota((step, rows + LANES), 0) + start == slot, 1.0, 0.0)
        out_ref[start : start + step, :] = jnp.dot(
            pick.astype(jnp.bfloat16), aug_ref[...], preferred_element_type=jnp.float32
        ).astype(jnp.bfloat16)


def sort_kernel(chips, labels, cap, rows_ref, out_ref, place_ref, ends_ref):
    total = rows_ref.shape[0]
    space = out_ref.shape[0]
    spot = iota((LANES, total), 1)
    block = iota((LANES, total), 0)
    head = jnp.where(spot == block * cap + cap - 1, 1.0, 0.0).astype(jnp.bfloat16)
    counts = jnp.dot(head, rows_ref[:, 0:LANES], preferred_element_type=jnp.float32)
    flag = jnp.max(counts[:, FLAG:], axis=0, keepdims=True)

    counts_t = counts.T
    lower = jnp.where(iota((LANES, LANES), 0) < iota((LANES, LANES), 1), 1.0, 0.0)
    ahead = exact_dot(counts_t, lower)
    in_block = jnp.zeros((1, LANES), jnp.float32)
    begin = jnp.zeros((1, 1), jnp.float32)
    ends = jnp.zeros((1, LANES), jnp.float32)
    lane = iota((1, LANES), 1)
    table = []
    for label in range(labels):
        own = counts_t[label : label + 1, :]
        table.append(begin + ahead[label : label + 1, :] - in_block)
        in_block = in_block + own
        table.append(in_block)
        begin = begin + jnp.sum(own, axis=1, keepdims=True)
        ends = jnp.where(lane == label, begin, ends)
    table.append((lane * cap).astype(jnp.float32))
    table.extend([jnp.zeros((1, LANES), jnp.float32)] * (up(len(table), 8) - len(table)))
    table = jnp.concatenate(table, axis=0)

    def positions(expand, rank_row):
        where = exact_dot(table, expand)
        rank = rank_row(where)
        place = jnp.full(rank.shape, -1.0, jnp.float32)
        for label in reversed(range(labels)):
            inside = rank < where[2 * label + 1 : 2 * label + 2, :]
            place = jnp.where(inside, where[2 * label : 2 * label + 1, :] + rank, place)
        return place

    spot_block = jnp.where((spot >= block * cap) & (spot < block * cap + cap), 1.0, 0.0)
    spot_row = iota((1, total), 1).astype(jnp.float32)
    place = positions(
        spot_block, lambda where: spot_row - where[2 * labels : 2 * labels + 1, :]
    ).astype(jnp.int32)

    lanes = place_ref.shape[1]
    rank_row = iota((1, lanes), 1).astype(jnp.float32)
    for index in range(chips):
        only = jnp.where(iota((LANES, lanes), 0) == index, 1.0, 0.0)
        place_ref[index : index + 1, :] = positions(only, lambda where: rank_row).astype(jnp.int32)

    flag = jnp.maximum(flag, jnp.where(begin > space, 1.0, 0.0))
    ends = jnp.where(lane == FLAG, flag, ends)
    ends_ref[...] = jnp.broadcast_to(ends, ends_ref.shape).astype(jnp.int32)

    step = 256
    for start in range(0, space, step):
        pick = jnp.where(iota((step, total), 0) + start == place, 1.0, 0.0)
        out_ref[start : start + step, :] = jnp.dot(
            pick.astype(jnp.bfloat16), rows_ref[...], preferred_element_type=jnp.float32
        ).astype(jnp.bfloat16)


def score_kernel(labels, own_ends, other_ends, own_ref, other_ref, place_ref, out_ref, total_ref):
    space = own_ref.shape[0]
    tile = LANES

    def clamp(value):
        return jnp.clip(value, 0, space)

    def label_of(ends, place):
        found = jnp.zeros(place.shape, jnp.int32)
        for label in range(labels):
            found = found + jnp.where(place >= ends[0, label], 1, 0)
        return found

    def first_label(ends, place):
        found = jnp.int32(0)
        for label in range(labels):
            found = found + jnp.where(place >= ends[0, label], 1, 0)
        return found

    def begin_of(ends, label):
        return jnp.where(label > 0, ends[0, jnp.maximum(label - 1, 0)], 0)

    count = clamp(own_ends[0, labels - 1])

    def row_tile(index, carry):
        start = pl.multiple_of(index * tile, tile)
        left = own_ref[pl.ds(start, tile), :]
        left_place = start + iota((tile, tile), 0)
        left_label = label_of(own_ends, left_place)
        low = first_label(own_ends, start)
        high = first_label(own_ends, jnp.minimum(start + tile, count) - 1)
        low = jnp.minimum(low, labels - 1)
        high = jnp.minimum(high, labels - 1)

        def side(ends, right_ref, same_rows, acc):
            begin = clamp(begin_of(ends, low)) // tile
            end = (clamp(ends[0, high]) + tile - 1) // tile

            def column_tile(position, acc):
                offset = pl.multiple_of(position * tile, tile)
                right = right_ref[pl.ds(offset, tile), :]
                scores = lax.dot_general(
                    left, right, (((1,), (1,)), ((), ())), preferred_element_type=jnp.float32
                )
                right_place = offset + iota((1, tile), 1)
                right_label = label_of(ends, right_place)
                right_label = jnp.where(right_label < labels, right_label, -1)
                same = left_label == right_label
                if same_rows:
                    same = same & (left_place != right_place)
                return acc + jnp.where(same, jnp.exp(sharpness * scores), 0.0)

            return lax.fori_loop(begin, end, column_tile, acc)

        acc = jnp.zeros((tile, tile), jnp.float32)
        acc = side(own_ends, own_ref, True, acc)
        acc = side(other_ends, other_ref, False, acc)
        sums = jnp.sum(acc, axis=1, keepdims=True)
        total_ref[pl.ds(start, tile), :] = jnp.broadcast_to(sums, (tile, tile))
        return carry

    total_ref[...] = jnp.zeros(total_ref.shape, jnp.float32)
    lax.fori_loop(0, (count + tile - 1) // tile, row_tile, 0)

    flag = jnp.maximum(own_ends[0, FLAG], other_ends[0, FLAG]).astype(jnp.float32)
    lanes = out_ref.shape[1]
    row = iota((space, LANES), 0)
    for index in range(out_ref.shape[0]):
        for start in range(0, lanes, LANES):
            place = place_ref[index : index + 1, start : start + LANES]
            value = jnp.sum(
                jnp.where(row == place, total_ref[...], 0.0), axis=0, keepdims=True
            )
            if start + LANES == lanes:
                value = jnp.where(iota((1, LANES), 1) == FLAG, flag, value)
            out_ref[index : index + 1, start : start + LANES] = value


def unpack_kernel(chips, ret_ref, ids_ref, rank_ref, out_ref, flag_ref):
    rows = ids_ref.shape[1]
    lanes = ret_ref.shape[1]
    values = ret_ref[...]
    flag = jnp.max(values[:, lanes - 1 :], axis=0, keepdims=True)
    flag_ref[...] = jnp.broadcast_to(flag, flag_ref.shape).astype(jnp.int32)
    chip = ids_ref[...] & (chips - 1)
    rank = rank_ref[...].astype(jnp.int32)
    at_rank = jnp.where(iota((lanes, rows), 0) == rank, 1.0, 0.0)
    found = exact_dot(values, at_rank)
    total = jnp.sum(jnp.where(iota((chips, rows), 0) == chip, found, 0.0), axis=0, keepdims=True)
    out_ref[...] = jnp.log(1.0 + total)


def call(kernel, out_shape, **options):
    return pl.pallas_call(
        kernel,
        out_shape=out_shape,
        compiler_params=pltpu.CompilerParams(vmem_limit_bytes=VMEM_BYTES),
        **options,
    )


def body(embeddings, cluster_ids):
    rows, width = embeddings.shape
    chip_axes = ("chip", "tile")
    chips = lax.axis_size("chip") * lax.axis_size("tile")
    labels = KG * lax.axis_size("chip") * lax.axis_size("core") // chips
    mean = rows // chips
    cap = up(int(mean + 4.75 * mean**0.5) + 1, 8)
    lanes = up(cap + 1, LANES)
    space = rows + 256
    total = chips * cap
    vmem = pl.BlockSpec(memory_space=pltpu.VMEM)
    smem = pl.BlockSpec(memory_space=pltpu.SMEM)
    shape = jax.ShapeDtypeStruct

    ids_row = cluster_ids.reshape(1, rows)
    outgoing, rank = call(
        functools.partial(pack_kernel, chips, labels, cap),
        (shape((total, width), jnp.bfloat16), shape((1, rows), jnp.float32)),
        in_specs=[vmem, vmem],
        out_specs=(vmem, vmem),
        scratch_shapes=[pltpu.VMEM((rows + LANES, width), jnp.bfloat16)],
    )(embeddings, ids_row)
    arrived = lax.all_to_all(outgoing, chip_axes, split_axis=0, concat_axis=0, tiled=True)
    ordered, place, ends = call(
        functools.partial(sort_kernel, chips, labels, cap),
        (
            shape((space, width), jnp.bfloat16),
            shape((chips, lanes), jnp.int32),
            shape((8, LANES), jnp.int32),
        ),
        in_specs=[vmem],
        out_specs=(vmem, vmem, vmem),
    )(arrived)
    swap = [(0, 1), (1, 0)]
    other_ends = lax.ppermute(ends, "core", swap)
    other = lax.ppermute(ordered, "core", swap)
    totals = call(
        functools.partial(score_kernel, labels),
        shape((chips, lanes), jnp.float32),
        in_specs=[smem, smem, vmem, vmem, vmem],
        out_specs=vmem,
        scratch_shapes=[pltpu.VMEM((space, LANES), jnp.float32)],
    )(ends, other_ends, ordered, other, place)
    returned = lax.all_to_all(totals, chip_axes, split_axis=0, concat_axis=0, tiled=True)
    result, flag = call(
        functools.partial(unpack_kernel, chips),
        (shape((1, rows), jnp.float32), shape((8, LANES), jnp.int32)),
        in_specs=[vmem, vmem, vmem],
        out_specs=(vmem, vmem),
    )(returned, ids_row, rank)
    return lax.cond(
        flag[0, 0] > 0,
        lambda: general_plan(embeddings, cluster_ids),
        lambda: result.reshape(rows),
    )


def solution(mesh):
    shards = mesh.shape["shard"]
    tiles = mesh.shape["tile"]
    split = Mesh(mesh.devices.reshape(shards // 2, 2, tiles), ("chip", "core", "tile"))
    rows = ("chip", "core", "tile")
    return jax.shard_map(
        body, mesh=split, in_specs=(P(rows, None), P(rows)), out_specs=P(rows), check_vma=False
    )
```

time: 382 us -> 126 us (0.33)
  waiting for transfers between devices: 188 us -> 10.5 us
  matrix products: 53.3 us -> 0 us
  Pallas kernels: 0 us -> 29.1 us
  other arithmetic: 21.4 us -> 0 us
  blocking collectives: 88.2 us -> 67.8 us
  local copies, waits for them, and re-layouts: 12.3 us -> 1.11 us
    all_gather x1 -> x0, waiting for transfers between devices: 185 us -> none  [body(): piece_rows = lax.all_gather(owned, 'tile', axis=0, tiled=True)]
    dot_general x4 -> x0, matrix products: 53.3 us -> none  [step(): lax.dot_general(rows_block, right, (((1,), (1,)), ((), ())), preferred_el...]
    pallas_call x0 -> x4, Pallas kernels: none -> 29.1 us  [the longest x1 17 us: body(): call(functools.partial(score_kernel, labels), shape((chips, lanes), jnp.f...]
    all_gather x1 -> x0, blocking collectives: 21 us -> none  [body(): piece_labels = lax.all_gather(owned_labels, 'tile', axis=0, tiled=True)]
    all_to_all x2 -> x1, blocking collectives: 51.5 us -> 67.8 us  [body(): lax.all_to_all(outgoing, chip_axes, split_axis=0, concat_axis=0, tiled=True)]
    unnamed x1 -> x0, blocking collectives: 15.7 us -> none
    scatter x1 -> x0, other arithmetic: 7.72 us -> none  [body(): jnp.zeros((slot_count, unit.shape[1]), jnp.bfloat16).at[slots].set(unit)]
    gather x1 -> x0, local copies, waits for them, and re-layouts: 6.15 us -> none  [body(): totals = returned.reshape(slot_count)[slots]]
  transfers between devices with their start and end apart: 2 -> 3, of which waited for: 2 -> 2; matrix products, arithmetic and copies ran while one was open for 1% -> 0% of each run, Pallas kernels for 0% -> 0%
where the time goes in v1:
time: 126 us; the launch traced here: 127 us
  blocking collectives  67.8 us (54%)
  Pallas kernels  29.1 us (23%)
  between operations  14.1 us (11%)
  waiting for transfers between devices  10.5 us (8%)
  starting transfers between devices  4.24 us (3%)
    all_to_all x1, blocking collectives, body(): lax.all_to_all(outgoing, chip_axes, split_axis=0, concat_axis=0, tiled=True)  67.8 us
    pallas_call x1, Pallas kernels, body(): call(functools.partial(score_kernel, labels), shape((chips, lanes), jnp.f...  17 us
    all_to_all x1, waiting for transfers between devices, body(): lax.all_to_all(totals, chip_axes, split_axis=0, concat_axis=0, tiled=True)  7.04 us
    pallas_call x1, Pallas kernels, body(): call(functools.partial(pack_kernel, chips, labels, cap), (shape((total, w...  6.48 us
    pallas_call x1, Pallas kernels, body(): call(functools.partial(sort_kernel, chips, labels, cap), (shape((space, w...  5.27 us
    all_to_all x1, starting transfers between devices, body(): lax.all_to_all(totals, chip_axes, split_axis=0, concat_axis=0, tiled=True)  3.67 us
    ppermute x1, waiting for transfers between devices, body(): other_ends = lax.ppermute(ends, 'core', swap)  3.47 us
  transfers between devices with their start and end apart: 3, of which 2 were waited for; matrix products, arithmetic and copies ran while one was open for 0% of the time, Pallas kernels for 0%

profile of v1, /device:TPU:0, one launch (start us, length us, event | category | flops | bytes accessed | tf_op | source)
XLA Modules:
  0.0 126.9 jit_solution(6217542959529572381)
XLA Ops:
  6.5 6.5 %shard_map.30 = (bf16[1664,768]{1,0:T(8,128)(2,1)S(1)}, f32[1,1024]{1,0:T(1,128)S(1)}) custom-call(f32[1024,768]{1,0:T(8,128)} %emb_ref.1, s32[1,1024]{1,0:T(1,128)} %bitcast.65), custom_call_target="tpu_custom_call" | custom-call | tf_op jit(solution)/shard_map/pallas_call | solution.py:332
  13.0 67.8 %all_to_all.55 = bf16[16,104,768]{2,1,0:T(8,128)(2,1)S(1)} all-to-all(bf16[16,104,768]{2,1,0:T(8,128)(2,1)S(1)} %bitcast.56), channel_id=1, replica_groups=mesh['chip'=4,'core'=2,'tile'=4] {'chip','tile'}, dimensions={0} | all-to-all | bytes 5111808 | tf_op jit(solution)/shard_map/all_to_all | solution.py:339
  80.9 0.0 copy-start.1
  80.9 0.0 copy-start
  80.9 5.3 %shard_map.31 = (bf16[1280,768]{1,0:T(8,128)(2,1)S(1)}, s32[16,128]{1,0:T(8,128)S(1)}, s32[8,128]{1,0:T(8,128)S(1)}) custom-call(bf16[1664,768]{1,0:T(8,128)(2,1)S(1)} %bitcast.55), custom_call_target="tpu_custom_call" | custom-call | tf_op jit(solution)/shard_map/pallas_call | solution.py:340
  86.1 0.1 collective-permute-start.1
  86.2 0.5 collective-permute-start
  86.7 3.5 %collective-permute-done.other_ends = s32[8,128]{1,0:T(8,128)S(1)} collective-permute-done((s32[8,128]{1,0:T(8,128)S(1)}, s32[8,128]{1,0:T(8,128)S(1)}, u32[]{:S(2)}, u32[]{:S(2)}) %collective-permute-start) | collective-permute-done | bytes 4128 | tf_op jit(solution)/shard_map/ppermute | solution.py:351
  90.2 0.0 collective-permute-done.1.other_ref
  90.2 17.0 %shard_map.32 = f32[16,128]{1,0:T(8,128)} custom-call(s32[8,128]{1,0:T(8,128)S(1)} %get-tuple-element.71.own_ends, s32[8,128]{1,0:T(8,128)S(1)} %collective-permute-done.other_ends, bf16[1280,768]{1,0:T(8,128)(2,1)S(1)} %get-tuple-element.72.own_ref, bf16[1280,768]{1,0:T(8,128)(2,1)S(1)} %collective-permute-done.1.other_ref, ...), custom_call_target="tpu_custom_call" | custom-call | tf_op jit(solution)/shard_map/pallas_call | solution.py:353
  107.2 3.7 %all-to-all-start.4 = ((f32[16,1,128]{2,1,0:T(1,128)}), f32[16,1,128]{2,1,0:T(1,128)S(1)}, u32[]{:S(2)}, u32[]{:S(2)}) async-start(f32[16,1,128]{2,1,0:T(1,128)} %bitcast.14), calls=%async_computation.4 | async-start | bytes 16384 | tf_op jit(solution)/shard_map/all_to_all | solution.py:360
  110.8 7.0 %all-to-all-done.4 = f32[16,1,128]{2,1,0:T(1,128)S(1)} async-done(((f32[16,1,128]{2,1,0:T(1,128)}), f32[16,1,128]{2,1,0:T(1,128)S(1)}, u32[]{:S(2)}, u32[]{:S(2)}) %all-to-all-start.4) | async-done | bytes 8224 | tf_op jit(solution)/shard_map/all_to_all | solution.py:360
  117.9 0.0 copy-done.1
  117.9 0.4 shard_map.33
  118.3 0.5 slice.9
  119.5 0.0 copy-done
  119.5 0.0 copy-start.2
  119.5 0.6 copy-done.2
  (1 shorter events, 0.0 us)
Async XLA Ops:
  80.9 37.0 %copy-start.1 = (s32[1024]{0:T(1024)S(1)}, s32[1024]{0:T(1024)}, u32[]{:S(2)}) copy-start(s32[1024]{0:T(1024)} %param.7) | copy-start | bytes 12292
  80.9 38.6 %copy-start = (f32[1024,768]{1,0:T(8,128)S(1)}, f32[1024,768]{1,0:T(8,128)}, u32[]{:S(2)}) copy-start(f32[1024,768]{1,0:T(8,128)} %emb_ref.1) | copy-start | bytes 9437188
  86.1 4.0 %collective-permute-start.1 = (bf16[1280,768]{1,0:T(8,128)(2,1)S(1)}, bf16[1280,768]{1,0:T(8,128)(2,1)S(1)}, u32[]{:S(2)}, u32[]{:S(2)}) collective-permute-start(bf16[1280,768]{1,0:T(8,128)(2,1)S(1)} %get-tuple-element.72.own_ref), channel_id=1, source_target_pairs={{0,4},{4,0},{1,5},{5,1},{2,6},{6,2},{3,7},{7,3},{8,12},{12,8},{9,1... | collective-permute-start | bytes 5898248 | tf_op jit(solution)/shard_map/ppermute | solution.py:352
  86.2 4.0 %collective-permute-start = (s32[8,128]{1,0:T(8,128)S(1)}, s32[8,128]{1,0:T(8,128)S(1)}, u32[]{:S(2)}, u32[]{:S(2)}) collective-permute-start(s32[8,128]{1,0:T(8,128)S(1)} %get-tuple-element.71.own_ends), channel_id=1, source_target_pairs={{0,4},{4,0},{1,5},{5,1},{2,6},{6,2},{3,7},{7,3},{8,12},{12,8},{9,1... | collective-permute-start | bytes 12296 | tf_op jit(solution)/shard_map/ppermute | solution.py:351
  107.2 10.7 %all-to-all-start.4 = ((f32[16,1,128]{2,1,0:T(1,128)}), f32[16,1,128]{2,1,0:T(1,128)S(1)}, u32[]{:S(2)}, u32[]{:S(2)}) async-start(f32[16,1,128]{2,1,0:T(1,128)} %bitcast.14), calls=%async_computation.4 | async-start | bytes 16384 | tf_op jit(solution)/shard_map/all_to_all | solution.py:360
  119.5 0.6 copy-start.2

commit v2 on v1

v2 whole, which is shorter than its diff:
```python
import functools

import jax
import jax.numpy as jnp
from jax import lax
from jax.experimental import pallas as pl
from jax.experimental.pallas import tpu as pltpu
from jax.sharding import Mesh
from jax.sharding import PartitionSpec as P

KG = 16


sharpness = 30.0
epsilon = 1e-06

VMEM_BYTES = 48 * 1024 * 1024
LANES = 128
FLAG = LANES - 1
ALIGN = 16
STEP = 32
LEFT = 192
RIGHT = 384


def unit_rows(embeddings):
    energy = jnp.sum(embeddings * embeddings, axis=1, keepdims=True)
    return (embeddings * lax.rsqrt(energy + epsilon)).astype(jnp.bfloat16)


def row_sums(left, left_labels, right, right_labels, same_rows):
    count = left.shape[0]
    block = min(512, count)
    blocks = count // block

    def step(start, items):
        rows_block, labels_block = items
        scores = lax.dot_general(
            rows_block, right, (((1,), (1,)), ((), ())), preferred_element_type=jnp.float32
        )
        same = (labels_block[:, None] == right_labels[None, :]) & (labels_block[:, None] >= 0)
        itself = (start + jnp.arange(block))[:, None] == jnp.arange(count)[None, :]
        same = same & ~(itself & same_rows)
        terms = jnp.where(same, jnp.exp(sharpness * scores), 0.0)
        return (start + block, jnp.sum(terms, axis=1))

    _, totals = lax.scan(
        step,
        jnp.int32(0),
        (left.reshape(blocks, block, left.shape[1]), left_labels.reshape(blocks, block)),
    )
    return totals.reshape(count)


def general_plan(embeddings, cluster_ids):
    shard_axes = ("chip", "core")
    local_rows = embeddings.shape[0]
    shards = lax.axis_size("chip") * lax.axis_size("core")
    tiles = lax.axis_size("tile")
    capacity = 2 * local_rows // shards
    slot_count = shards * capacity
    unit = unit_rows(embeddings)
    owner = cluster_ids // KG
    onehot = (owner[:, None] == jnp.arange(shards, dtype=jnp.int32)[None, :]).astype(jnp.int32)
    ranks = jnp.sum((jnp.cumsum(onehot, axis=0) - 1) * onehot, axis=1)
    slots = owner * capacity + ranks
    outgoing = jnp.zeros((slot_count, unit.shape[1]), jnp.bfloat16).at[slots].set(unit)
    outgoing_labels = jnp.full((slot_count,), -1, jnp.int32).at[slots].set(cluster_ids)
    owned = lax.all_to_all(outgoing, shard_axes, split_axis=0, concat_axis=0, tiled=True)
    owned_labels = lax.all_to_all(
        outgoing_labels, shard_axes, split_axis=0, concat_axis=0, tiled=True
    )
    around = [(tile, (tile + 1) % tiles) for tile in range(tiles)]

    def visit(step, state):
        totals, rows, labels = state
        totals = totals + row_sums(owned, owned_labels, rows, labels, step == 0)
        return (totals, lax.ppermute(rows, "tile", around), lax.ppermute(labels, "tile", around))

    totals, _, _ = lax.fori_loop(
        0, tiles, visit, (jnp.zeros((slot_count,), jnp.float32), owned, owned_labels)
    )
    returned = lax.all_to_all(totals, shard_axes, split_axis=0, concat_axis=0, tiled=True)
    return jnp.log(1.0 + returned[slots])


def up(value, multiple):
    return -(-value // multiple) * multiple


def room(mean):
    return int(mean + 4.75 * mean**0.5) + 1


def iota(shape, axis):
    return lax.broadcasted_iota(jnp.int32, shape, axis)


def exact_dot(left, right):
    return jnp.dot(
        left, right, precision=lax.Precision.HIGHEST, preferred_element_type=jnp.float32
    )


def pick_rows(places, start, count, rows):
    pick = jnp.where(iota((count, places.shape[1]), 0) + start == places, 1.0, 0.0)
    return jnp.dot(pick.astype(jnp.bfloat16), rows, preferred_element_type=jnp.float32).astype(
        jnp.bfloat16
    )


def pack_kernel(size, emb_ref, ids_ref, *refs):
    *out_refs, rank_ref, aug_ref = refs
    rows, width = emb_ref.shape
    chips, labels, cap = size["chips"], size["labels"], size["cap"]
    across, tiles = size["across"], size["tiles"]
    chunk = 256
    for start in range(0, rows, chunk):
        x = emb_ref[start : start + chunk, :]
        energy = jnp.sum(x * x, axis=1, keepdims=True)
        aug_ref[start : start + chunk, :] = (x * lax.rsqrt(energy + epsilon)).astype(jnp.bfloat16)

    ids = ids_ref[...]
    label = ids >> (chips.bit_length() - 1)
    shift = ((ids & (tiles - 1)) - lax.axis_index("tile")) & (tiles - 1)
    side = ((ids & (chips - 1)) >> (tiles.bit_length() - 1)) ^ lax.axis_index("chip")
    block = shift * across + side
    key = ((block * labels + label) * rows + iota((1, rows), 1)).astype(jnp.float32)
    base = (block * (labels * rows)).astype(jnp.float32)
    key_t = jnp.broadcast_to(key, (LANES, rows)).T
    ranks = []
    for start in range(0, rows, LANES):
        own = key[:, start : start + LANES]
        low = base[:, start : start + LANES]
        before = (key_t < own) & (key_t >= low)
        ranks.append(jnp.sum(jnp.where(before, 1.0, 0.0), axis=0, keepdims=True))
    rank = jnp.concatenate(ranks, axis=1)
    rank_ref[...] = rank
    over = jnp.max(jnp.where(rank >= cap - 1, 1.0, 0.0), axis=1, keepdims=True)
    slot = jnp.where(rank < cap - 1, block * cap + rank.astype(jnp.int32), -1)

    in_block = jnp.where(iota((LANES, rows), 0) == block, 1.0, 0.0).astype(jnp.bfloat16)
    in_label = jnp.where(iota((LANES, rows), 0) == label, 1.0, 0.0).astype(jnp.bfloat16)
    counts = lax.dot_general(
        in_block, in_label, (((1,), (1,)), ((), ())), preferred_element_type=jnp.float32
    )
    counts = jnp.where(iota((LANES, LANES), 1) == FLAG, over, counts)
    aug_ref[rows:, :] = jnp.zeros((LANES, width), jnp.bfloat16)
    aug_ref[rows:, 0:LANES] = counts.astype(jnp.bfloat16)
    place = iota((1, LANES), 1)
    head = jnp.where(place < chips, place * cap + cap - 1, -1)
    slot = jnp.concatenate([slot, head], axis=1)
    aug = aug_ref[...]
    for index, out_ref in enumerate(out_refs):
        out_ref[...] = pick_rows(slot, index * cap, cap, aug)


def sort_kernel(size, *refs):
    across, labels, cap, space = size["across"], size["labels"], size["cap"], size["space"]
    block_refs, (out_ref, place_ref, counts_ref, rows_ref) = refs[:across], refs[across:]
    total = across * cap
    for index, ref in enumerate(block_refs):
        rows_ref[index * cap : (index + 1) * cap, :] = ref[...]
    rows = rows_ref[...]
    spot = iota((LANES, total), 1)
    block = iota((LANES, total), 0)
    head = jnp.where(spot == block * cap + cap - 1, 1.0, 0.0).astype(jnp.bfloat16)
    counts = jnp.dot(head, rows[:, 0:LANES], preferred_element_type=jnp.float32)
    flag = jnp.max(counts[:, FLAG:], axis=0, keepdims=True)

    counts_t = counts.T
    lower = jnp.where(iota((LANES, LANES), 0) < iota((LANES, LANES), 1), 1.0, 0.0)
    ahead = exact_dot(counts_t, lower)
    in_block = jnp.zeros((1, LANES), jnp.float32)
    found = jnp.zeros((1, LANES), jnp.float32)
    begin = jnp.zeros((1, 1), jnp.float32)
    lane = iota((1, LANES), 1)
    table = []
    for label in range(labels):
        own = counts_t[label : label + 1, :]
        table.append(begin + ahead[label : label + 1, :] - in_block)
        in_block = in_block + own
        table.append(in_block)
        count = jnp.sum(own, axis=1, keepdims=True)
        found = jnp.where(lane == label, count, found)
        begin = begin + jnp.floor((count + (ALIGN - 1)) * (1.0 / ALIGN)) * ALIGN
    flag = jnp.maximum(flag, jnp.where(begin > space, 1.0, 0.0))
    found = jnp.where(lane == FLAG, flag, found)
    counts_ref[...] = jnp.broadcast_to(found, counts_ref.shape).astype(jnp.int32)
    table.append((lane * cap).astype(jnp.float32))
    table.extend([jnp.zeros((1, LANES), jnp.float32)] * (up(len(table), 8) - len(table)))
    table = jnp.concatenate(table, axis=0)

    def places(expand, rank_row):
        where = exact_dot(table, expand)
        rank = rank_row(where)
        place = jnp.full(rank.shape, -1.0, jnp.float32)
        for label in reversed(range(labels)):
            inside = rank < where[2 * label + 1 : 2 * label + 2, :]
            place = jnp.where(inside, where[2 * label : 2 * label + 1, :] + rank, place)
        return place.astype(jnp.int32)

    spot_block = jnp.where((spot >= block * cap) & (spot < block * cap + cap), 1.0, 0.0)
    spot_row = iota((1, total), 1).astype(jnp.float32)
    place = places(spot_block, lambda where: spot_row - where[2 * labels : 2 * labels + 1, :])
    lanes = place_ref.shape[1]
    rank_row = iota((1, lanes), 1).astype(jnp.float32)
    for index in range(across):
        only = jnp.where(iota((LANES, lanes), 0) == index, 1.0, 0.0)
        place_ref[index : index + 1, :] = places(only, lambda where: rank_row)

    out_ref[space:, :] = jnp.zeros((STEP, out_ref.shape[1]), jnp.bfloat16)
    for start in range(0, space, ALIGN * 9):
        count = min(ALIGN * 9, space - start)
        out_ref[start : start + count, :] = pick_rows(place, start, count, rows)


def score_kernel(size, *refs):
    across, tiles, labels, space = size["across"], size["tiles"], size["labels"], size["space"]
    pieces = 2 * tiles
    counts_refs, piece_refs, place_refs = (
        refs[:pieces],
        refs[pieces : 2 * pieces],
        refs[2 * pieces : 2 * pieces + tiles],
    )
    out_ref, rows_ref, total_ref, back_ref = refs[2 * pieces + tiles :]
    lane = iota((1, LANES), 1)
    flag = jnp.int32(0)
    for ref in counts_refs:
        flag = jnp.maximum(flag, ref[0, FLAG])

    def aligned(count):
        return (count + (ALIGN - 1)) & -ALIGN

    counts, places, begins = [], [], []
    begin = jnp.int32(0)
    source = [jnp.int32(0)] * pieces
    for label in range(labels):
        begins.append(begin)
        counts.append([])
        places.append([])
        for index in range(pieces):
            free = space - source[index]
            count = jnp.clip(counts_refs[index][0, label], 0, free)
            counts[label].append(count)
            places[label].append((source[index], begin))
            src, dst = source[index], begin

            def move(step, carry, ref=piece_refs[index], src=src, dst=dst):
                rows = pl.ds(pl.multiple_of(src + step * STEP, ALIGN), STEP)
                to = pl.ds(pl.multiple_of(dst + step * STEP, ALIGN), STEP)
                rows_ref[to, :] = ref[rows, :]
                return carry

            move(0, 0)
            lax.fori_loop(1, (count + STEP - 1) // STEP, move, 0)
            source[index] = source[index] + aligned(count)
            begin = begin + aligned(count)

    for label in range(labels):
        first = begins[label]
        own_end = places[label][tiles][1]
        end = begins[label + 1] if label + 1 < labels else begin

        def window(row, column, label=label):
            left = rows_ref[pl.ds(pl.multiple_of(row, ALIGN), LEFT), :]
            right = rows_ref[pl.ds(pl.multiple_of(column, ALIGN), RIGHT), :]
            scores = lax.dot_general(
                left, right, (((1,), (1,)), ((), ())), preferred_element_type=jnp.float32
            )
            at = iota((1, RIGHT), 1) + column
            valid = at < 0
            for index in range(pieces):
                low = places[label][index][1]
                valid = valid | ((at >= low) & (at < low + counts[label][index]))
            at = jnp.where(valid, at, -1)
            itself = iota((LEFT, RIGHT), 0) + row
            counted = (at >= 0) & (at != itself)
            terms = jnp.where(counted, jnp.exp(sharpness * scores), 0.0)
            return jnp.sum(terms, axis=1, keepdims=True)

        def strip(row, first=first, end=end, window=window):
            sums = window(row, first)
            sums = lax.fori_loop(
                1,
                (end - first + RIGHT - 1) // RIGHT,
                lambda step, sums: sums + window(row, first + step * RIGHT),
                sums,
            )
            total_ref[pl.ds(pl.multiple_of(row, ALIGN), LEFT), :] = jnp.broadcast_to(
                sums, (LEFT, LANES)
            )

        def more(step, carry, first=first, strip=strip):
            strip(first + step * LEFT)
            return carry

        strip(first)
        lax.fori_loop(1, (own_end - first + LEFT - 1) // LEFT, more, 0)

    for index in range(tiles):
        for label in range(labels):
            src, dst = places[label][index][1], places[label][index][0]

            def back(step, carry, index=index, src=src, dst=dst):
                rows = pl.ds(pl.multiple_of(src + step * STEP, ALIGN), STEP)
                to = pl.ds(pl.multiple_of(dst + step * STEP, ALIGN), STEP)
                back_ref[index, to, :] = total_ref[rows, :]
                return carry

            back(0, 0)
            lax.fori_loop(1, (counts[label][index] + STEP - 1) // STEP, back, 0)

    lanes = out_ref.shape[1]
    row = iota((space, LANES), 0)
    chip, tile = lax.axis_index("chip"), lax.axis_index("tile")
    for shift in range(tiles):
        for side in range(across):
            home = (chip ^ side) * tiles + ((tile - shift) & (tiles - 1))
            for start in range(0, lanes, LANES):
                place = place_refs[shift][side : side + 1, start : start + LANES]
                value = jnp.sum(
                    jnp.where(row == place, back_ref[shift, 0:space, :], 0.0),
                    axis=0,
                    keepdims=True,
                )
                if start + LANES == lanes:
                    value = jnp.where(lane == FLAG, flag.astype(jnp.float32), value)
                out_ref[pl.ds(home, 1), start : start + LANES] = value


def unpack_kernel(chips, ret_ref, ids_ref, rank_ref, out_ref, flag_ref):
    rows = ids_ref.shape[1]
    lanes = ret_ref.shape[1]
    values = ret_ref[...]
    flag = jnp.max(values[:, lanes - 1 :], axis=0, keepdims=True)
    flag_ref[...] = jnp.broadcast_to(flag, flag_ref.shape).astype(jnp.int32)
    chip = ids_ref[...] & (chips - 1)
    rank = rank_ref[...].astype(jnp.int32)
    at_rank = jnp.where(iota((lanes, rows), 0) == rank, 1.0, 0.0)
    found = exact_dot(values, at_rank)
    total = jnp.sum(jnp.where(iota((chips, rows), 0) == chip, found, 0.0), axis=0, keepdims=True)
    out_ref[...] = jnp.log(1.0 + total)


def call(kernel, name, out_shape, inputs, scalars=0, **options):
    vmem = pl.BlockSpec(memory_space=pltpu.VMEM)
    smem = pl.BlockSpec(memory_space=pltpu.SMEM)
    return pl.pallas_call(
        kernel,
        out_shape=out_shape,
        in_specs=[smem] * scalars + [vmem] * (len(inputs) - scalars),
        out_specs=jax.tree.map(lambda _: vmem, out_shape),
        compiler_params=pltpu.CompilerParams(vmem_limit_bytes=VMEM_BYTES),
        name=name,
        **options,
    )(*inputs)


def body(embeddings, cluster_ids):
    rows, width = embeddings.shape
    across, tiles = lax.axis_size("chip"), lax.axis_size("tile")
    chips = across * tiles
    labels = KG * across * lax.axis_size("core") // chips
    cap = up(room(rows // chips) + 1, ALIGN)
    batch = rows // tiles
    space = up(room(batch) + labels * (ALIGN - 1) - labels * ALIGN // 4, ALIGN)
    size = dict(chips=chips, across=across, tiles=tiles, labels=labels, cap=cap, space=space)
    lanes = up(cap + 1, LANES)
    shape = jax.ShapeDtypeStruct

    ids_row = cluster_ids.reshape(1, rows)
    *blocks, rank = call(
        functools.partial(pack_kernel, size),
        "pack",
        [shape((cap, width), jnp.bfloat16)] * chips + [shape((1, rows), jnp.float32)],
        [embeddings, ids_row],
        scratch_shapes=[pltpu.VMEM((rows + LANES, width), jnp.bfloat16)],
    )
    own, other, own_counts, other_counts, places = [], [], [], [], []
    swap = [(0, 1), (1, 0)]
    for shift in range(tiles):
        arrived = []
        for side in range(across):
            block = blocks[shift * across + side]
            if shift or side:
                route = [
                    (a * tiles + z, (a ^ side) * tiles + (z + shift) % tiles)
                    for a in range(across)
                    for z in range(tiles)
                ]
                block = lax.ppermute(block, ("chip", "tile"), route)
            arrived.append(block)
        ordered, place, counts = call(
            functools.partial(sort_kernel, size),
            "sort",
            [
                shape((space + STEP, width), jnp.bfloat16),
                shape((across, lanes), jnp.int32),
                shape((8, LANES), jnp.int32),
            ],
            arrived,
            scratch_shapes=[pltpu.VMEM((across * cap, width), jnp.bfloat16)],
        )
        own.append(ordered)
        places.append(place)
        own_counts.append(counts)
        other_counts.append(lax.ppermute(counts, "core", swap))
        other.append(lax.ppermute(ordered, "core", swap))
    room_all = 2 * tiles * space + RIGHT
    totals = call(
        functools.partial(score_kernel, size),
        "score",
        shape((chips, lanes), jnp.float32),
        [*own_counts, *other_counts, *own, *other, *places],
        scalars=2 * tiles,
        scratch_shapes=[
            pltpu.VMEM((room_all, width), jnp.bfloat16),
            pltpu.VMEM((room_all, LANES), jnp.float32),
            pltpu.VMEM((tiles, space + STEP, LANES), jnp.float32),
        ],
    )
    returned = lax.all_to_all(totals, ("chip", "tile"), split_axis=0, concat_axis=0, tiled=True)
    result, flag = call(
        functools.partial(unpack_kernel, chips),
        "unpack",
        [shape((1, rows), jnp.float32), shape((8, LANES), jnp.int32)],
        [returned, ids_row, rank],
    )
    return lax.cond(
        flag[0, 0] > 0,
        lambda: general_plan(embeddings, cluster_ids),
        lambda: result.reshape(rows),
    )


def solution(mesh):
    shards = mesh.shape["shard"]
    tiles = mesh.shape["tile"]
    split = Mesh(mesh.devices.reshape(shards // 2, 2, tiles), ("chip", "core", "tile"))
    rows = ("chip", "core", "tile")
    return jax.shard_map(
        body, mesh=split, in_specs=(P(rows, None), P(rows)), out_specs=P(rows), check_vma=False
    )
```

time: 126 us -> 113 us (0.90); the launches traced: 127 us -> 112 us
  blocking collectives: 67.8 us -> 0 us
  starting transfers between devices: 4.24 us -> 55.5 us
  waiting for transfers between devices: 10.5 us -> 34.1 us
  between operations: 14.1 us -> 0.85 us
  Pallas kernels: 29.1 us -> 20.9 us
    all_to_all x1 -> x0, blocking collectives: 67.8 us -> none  [body(): lax.all_to_all(outgoing, chip_axes, split_axis=0, concat_axis=0, tiled=True)]
    ppermute x2 -> x23, starting transfers between devices: 0.57 us -> 48.6 us  [the longest x15 47 us: body(): block = lax.ppermute(block, ('chip', 'tile'), route)]
    ppermute x2 -> x23, waiting for transfers between devices: 3.47 us -> 26.8 us  [the longest x15 22.1 us: body(): block = lax.ppermute(block, ('chip', 'tile'), route)]
    pallas_call x4 -> x7, Pallas kernels: 29.1 us -> 20.9 us  [call(): pl.pallas_call(kernel, out_shape=out_shape, in_specs=[smem] * scalars + [...]
    all_to_all x1, starting transfers between devices: 3.67 us -> 6.9 us  [body(): lax.all_to_all(totals, ('chip', 'tile'), split_axis=0, concat_axis=0, til...]
  transfers between devices with their start and end apart: 3 -> 24, of which waited for: 2 -> 9; matrix products, arithmetic and copies ran while one was open for 0% -> 0% of each run, Pallas kernels for 0% -> 4%
where the time goes in v2:
time: 113 us; the launch traced here: 112 us
  starting transfers between devices  55.5 us (49%)
  waiting for transfers between devices  34.1 us (30%)
  Pallas kernels  20.9 us (18%)
    ppermute x15, starting transfers between devices, body(): block = lax.ppermute(block, ('chip', 'tile'), route)  47 us
    ppermute x15, waiting for transfers between devices, body(): block = lax.ppermute(block, ('chip', 'tile'), route)  22.1 us
    pallas_call x7, Pallas kernels, call(): pl.pallas_call(kernel, out_shape=out_shape, in_specs=[smem] * scalars + [...  20.9 us
    all_to_all x1, waiting for transfers between devices, body(): lax.all_to_all(totals, ('chip', 'tile'), split_axis=0, concat_axis=0, til...  7.3 us
    all_to_all x1, starting transfers between devices, body(): lax.all_to_all(totals, ('chip', 'tile'), split_axis=0, concat_axis=0, til...  6.9 us
    ppermute x4, waiting for transfers between devices, body(): other_counts.append(lax.ppermute(counts, 'core', swap))  4.7 us
  transfers between devices with their start and end apart: 24, of which 9 were waited for; matrix products, arithmetic and copies ran while one was open for 0% of the time, Pallas kernels for 4%

profile of v2, /device:TPU:0, one launch (start us, length us, event | category | flops | bytes accessed | tf_op | source)
XLA Modules:
  0.0 111.9 jit_solution(9890036529342851646)
XLA Ops:
  0.0 7.2 %pack.1 = (bf16[112,768]{1,0:T(8,128)(2,1)S(1)}, bf16[112,768]{1,0:T(8,128)(2,1)S(1)}, bf16[112,768]{1,0:T(8,128)(2,1)S(1)}, bf16[112,768]{1,0:T(8,128)(2,1)S(1)...) custom-call(f32[1024,768]{1,0:T(8,128)} %emb_ref.1, ...), custom_call_target="tpu_custom_call" | custom-call | tf_op jit(solution)/shard_map/pack/pallas_call | solution.py:349
  7.2 3.1 %collective-permute-start.5 = (bf16[112,768]{1,0:T(8,128)(2,1)S(1)}, bf16[112,768]{1,0:T(8,128)(2,1)S(1)}, u32[]{:S(2)}, u32[]{:S(2)}) collective-permute-start(bf16[112,768]{1,0:T(8,128)(2,1)S(1)} %get-tuple-element.302), channel_id=1, source_target_pairs={{0,1},{1,2},{2,3},{3,0},{8,9},{9,10},{10,11},{11,8},{16,17},{17,18... | collective-permute-start | bytes 516104 | tf_op jit(solution)/shard_map/ppermute | solution.py:392
  10.3 2.5 %collective-permute-start.6 = (bf16[112,768]{1,0:T(8,128)(2,1)S(1)}, bf16[112,768]{1,0:T(8,128)(2,1)S(1)}, u32[]{:S(2)}, u32[]{:S(2)}) collective-permute-start(bf16[112,768]{1,0:T(8,128)(2,1)S(1)} %get-tuple-element.303), channel_id=1, source_target_pairs={{0,9},{1,10},{2,11},{3,8},{8,1},{9,2},{10,3},{11,0},{16,25},{17,26... | collective-permute-start | bytes 516104 | tf_op jit(solution)/shard_map/ppermute | solution.py:392
  12.8 1.2 %collective-permute-start.9 = (bf16[112,768]{1,0:T(8,128)(2,1)S(1)}, bf16[112,768]{1,0:T(8,128)(2,1)S(1)}, u32[]{:S(2)}, u32[]{:S(2)}) collective-permute-start(bf16[112,768]{1,0:T(8,128)(2,1)S(1)} %get-tuple-element.307), channel_id=1, source_target_pairs={{0,2},{1,3},{2,0},{3,1},{8,10},{9,11},{10,8},{11,9},{16,18},{17,19... | collective-permute-start | bytes 516104 | tf_op jit(solution)/shard_map/ppermute | solution.py:392
  14.0 1.7 %collective-permute-start.10 = (bf16[112,768]{1,0:T(8,128)(2,1)S(1)}, bf16[112,768]{1,0:T(8,128)(2,1)S(1)}, u32[]{:S(2)}, u32[]{:S(2)}) collective-permute-start(bf16[112,768]{1,0:T(8,128)(2,1)S(1)} %get-tuple-element.308), channel_id=1, source_target_pairs={{0,10},{1,11},{2,8},{3,9},{8,2},{9,3},{10,0},{11,1},{16,26},{17,27... | collective-permute-start | bytes 516104 | tf_op jit(solution)/shard_map/ppermute | solution.py:392
  15.7 2.2 %collective-permute-start.11 = (bf16[112,768]{1,0:T(8,128)(2,1)S(1)}, bf16[112,768]{1,0:T(8,128)(2,1)S(1)}, u32[]{:S(2)}, u32[]{:S(2)}) collective-permute-start(bf16[112,768]{1,0:T(8,128)(2,1)S(1)} %get-tuple-element.309), channel_id=1, source_target_pairs={{0,18},{1,19},{2,16},{3,17},{8,26},{9,27},{10,24},{11,25},{16,2},{... | collective-permute-start | bytes 516104 | tf_op jit(solution)/shard_map/ppermute | solution.py:392
  17.9 2.6 %collective-permute-start.12 = (bf16[112,768]{1,0:T(8,128)(2,1)S(1)}, bf16[112,768]{1,0:T(8,128)(2,1)S(1)}, u32[]{:S(2)}, u32[]{:S(2)}) collective-permute-start(bf16[112,768]{1,0:T(8,128)(2,1)S(1)} %get-tuple-element.310), channel_id=1, source_target_pairs={{0,26},{1,27},{2,24},{3,25},{8,18},{9,19},{10,16},{11,17},{16,10},... | collective-permute-start | bytes 516104 | tf_op jit(solution)/shard_map/ppermute | solution.py:392
  20.4 2.0 %collective-permute-done.6.refs_1_ = bf16[112,768]{1,0:T(8,128)(2,1)S(1)} collective-permute-done((bf16[112,768]{1,0:T(8,128)(2,1)S(1)}, bf16[112,768]{1,0:T(8,128)(2,1)S(1)}, u32[]{:S(2)}, u32[]{:S(2)}) %collective-permute-start.6) | collective-permute-done | bytes 172064 | tf_op jit(solution)/shard_map/ppermute | solution.py:392
  23.4 15.5 %collective-permute-done.9.refs_0_ = bf16[112,768]{1,0:T(8,128)(2,1)S(1)} collective-permute-done((bf16[112,768]{1,0:T(8,128)(2,1)S(1)}, bf16[112,768]{1,0:T(8,128)(2,1)S(1)}, u32[]{:S(2)}, u32[]{:S(2)}) %collective-permute-start.9) | collective-permute-done | bytes 172064 | tf_op jit(solution)/shard_map/ppermute | solution.py:392
  38.9 7.3 %collective-permute-start.14 = (bf16[112,768]{1,0:T(8,128)(2,1)S(1)}, bf16[112,768]{1,0:T(8,128)(2,1)S(1)}, u32[]{:S(2)}, u32[]{:S(2)}) collective-permute-start(bf16[112,768]{1,0:T(8,128)(2,1)S(1)} %get-tuple-element.313), channel_id=1, source_target_pairs={{0,11},{1,8},{2,9},{3,10},{8,3},{9,0},{10,1},{11,2},{16,27},{17,24... | collective-permute-start | bytes 516104 | tf_op jit(solution)/shard_map/ppermute | solution.py:392
  46.2 10.2 %collective-permute-start.15 = (bf16[112,768]{1,0:T(8,128)(2,1)S(1)}, bf16[112,768]{1,0:T(8,128)(2,1)S(1)}, u32[]{:S(2)}, u32[]{:S(2)}) collective-permute-start(bf16[112,768]{1,0:T(8,128)(2,1)S(1)} %get-tuple-element.314), channel_id=1, source_target_pairs={{0,19},{1,16},{2,17},{3,18},{8,27},{9,24},{10,25},{11,26},{16,3},{... | collective-permute-start | bytes 516104 | tf_op jit(solution)/shard_map/ppermute | solution.py:392
  56.4 7.2 %collective-permute-start.16 = (bf16[112,768]{1,0:T(8,128)(2,1)S(1)}, bf16[112,768]{1,0:T(8,128)(2,1)S(1)}, u32[]{:S(2)}, u32[]{:S(2)}) collective-permute-start(bf16[112,768]{1,0:T(8,128)(2,1)S(1)} %get-tuple-element.315), channel_id=1, source_target_pairs={{0,27},{1,24},{2,25},{3,26},{8,19},{9,16},{10,17},{11,18},{16,11},... | collective-permute-start | bytes 516104 | tf_op jit(solution)/shard_map/ppermute | solution.py:392
  63.6 4.7 %collective-permute-start.8 = (bf16[112,768]{1,0:T(8,128)(2,1)S(1)}, bf16[112,768]{1,0:T(8,128)(2,1)S(1)}, u32[]{:S(2)}, u32[]{:S(2)}) collective-permute-start(bf16[112,768]{1,0:T(8,128)(2,1)S(1)} %get-tuple-element.305), channel_id=1, source_target_pairs={{0,25},{1,26},{2,27},{3,24},{8,17},{9,18},{10,19},{11,16},{16,9},{... | collective-permute-start | bytes 516104 | tf_op jit(solution)/shard_map/ppermute | solution.py:392
  68.9 2.9 %collective-permute-start.4 = (bf16[112,768]{1,0:T(8,128)(2,1)S(1)}, bf16[112,768]{1,0:T(8,128)(2,1)S(1)}, u32[]{:S(2)}, u32[]{:S(2)}) collective-permute-start(bf16[112,768]{1,0:T(8,128)(2,1)S(1)} %get-tuple-element.300), channel_id=1, source_target_pairs={{0,24},{1,25},{2,26},{3,27},{8,16},{9,17},{10,18},{11,19},{16,8},{... | collective-permute-start | bytes 516104 | tf_op jit(solution)/shard_map/ppermute | solution.py:392
  71.8 1.2 %sort.6 = (bf16[464,768]{1,0:T(8,128)(2,1)S(1)}, s32[4,128]{1,0:T(4,128)S(1)}, s32[8,128]{1,0:T(8,128)S(1)}) custom-call(bf16[112,768]{1,0:T(8,128)(2,1)S(1)} %collective-permute-done.9.refs_0_, bf16[112,768]{1,0:T(8,128)(2,1)S(1)} %collective-permute-done.10.refs_1_, bf16[112,768]{1,0:T(8,128)(2,1)S(1)} %collective-permute-done.11.refs_2_, ...), custom_call_target="tpu_custom_call" | custom-call | tf_op jit(solution)/shard_map/sort/pallas_call | solution.py:349
  73.0 1.2 %sort.7 = (bf16[464,768]{1,0:T(8,128)(2,1)S(1)}, s32[4,128]{1,0:T(4,128)S(1)}, s32[8,128]{1,0:T(8,128)S(1)}) custom-call(bf16[112,768]{1,0:T(8,128)(2,1)S(1)} %collective-permute-done.13.refs_0_, bf16[112,768]{1,0:T(8,128)(2,1)S(1)} %collective-permute-done.14.refs_1_, bf16[112,768]{1,0:T(8,128)(2,1)S(1)} %collective-permute-done.15.refs_2_, ...), custom_call_target="tpu_custom_call" | custom-call | tf_op jit(solution)/shard_map/sort/pallas_call | solution.py:349
  74.3 1.5 %collective-permute-done.7.refs_2_ = bf16[112,768]{1,0:T(8,128)(2,1)S(1)} collective-permute-done((bf16[112,768]{1,0:T(8,128)(2,1)S(1)}, bf16[112,768]{1,0:T(8,128)(2,1)S(1)}, u32[]{:S(2)}, u32[]{:S(2)}) %collective-permute-start.7) | collective-permute-done | bytes 172064 | tf_op jit(solution)/shard_map/ppermute | solution.py:392
  76.3 1.2 %sort.5 = (bf16[464,768]{1,0:T(8,128)(2,1)S(1)}, s32[4,128]{1,0:T(4,128)S(1)}, s32[8,128]{1,0:T(8,128)S(1)}) custom-call(bf16[112,768]{1,0:T(8,128)(2,1)S(1)} %collective-permute-done.5.refs_0_, bf16[112,768]{1,0:T(8,128)(2,1)S(1)} %collective-permute-done.6.refs_1_, bf16[112,768]{1,0:T(8,128)(2,1)S(1)} %collective-permute-done.7.refs_2_, ...), custom_call_target="tpu_custom_call" | custom-call | tf_op jit(solution)/shard_map/sort/pallas_call | solution.py:349
  77.6 3.0 %collective-permute-done.3.refs_2_ = bf16[112,768]{1,0:T(8,128)(2,1)S(1)} collective-permute-done((bf16[112,768]{1,0:T(8,128)(2,1)S(1)}, bf16[112,768]{1,0:T(8,128)(2,1)S(1)}, u32[]{:S(2)}, u32[]{:S(2)}) %collective-permute-start.3) | collective-permute-done | bytes 172064 | tf_op jit(solution)/shard_map/ppermute | solution.py:392
  80.6 1.2 %sort.4 = (bf16[464,768]{1,0:T(8,128)(2,1)S(1)}, s32[4,128]{1,0:T(4,128)S(1)}, s32[8,128]{1,0:T(8,128)S(1)}) custom-call(bf16[112,768]{1,0:T(8,128)(2,1)S(1)} %get-tuple-element.297.refs_0_, bf16[112,768]{1,0:T(8,128)(2,1)S(1)} %collective-permute-done.2.refs_1_, bf16[112,768]{1,0:T(8,128)(2,1)S(1)} %collective-permute-done.3.refs_2_, ...), custom_call_target="tpu_custom_call" | custom-call | tf_op jit(solution)/shard_map/sort/pallas_call | solution.py:349
  82.5 1.7 %collective-permute-done.17.refs_4_ = s32[8,128]{1,0:T(8,128)S(1)} collective-permute-done((s32[8,128]{1,0:T(8,128)S(1)}, s32[8,128]{1,0:T(8,128)S(1)}, u32[]{:S(2)}, u32[]{:S(2)}) %collective-permute-start.17) | collective-permute-done | bytes 4128 | tf_op jit(solution)/shard_map/ppermute | solution.py:408
  87.7 7.8 %score.1 = f32[16,128]{1,0:T(8,128)} custom-call(s32[8,128]{1,0:T(8,128)S(1)} %get-tuple-element.301.refs_0_, s32[8,128]{1,0:T(8,128)S(1)} %get-tuple-element.306.refs_1_, s32[8,128]{1,0:T(8,128)S(1)} %get-tuple-element.311.refs_2_, s32[8,128]{1,0:T(8,128)S(1)} %get-tuple-element.316.refs_3_, s32[8,128]{1,0:T(8,128)S(1)} %collective-permute-done.17.refs_4_, ...), custom_call_target="tpu_custom_call" | custom-call | tf_op jit(solution)/shard_map/score/pallas_call | solution.py:349
  95.4 6.9 %all-to-all-start.3 = ((f32[16,1,128]{2,1,0:T(1,128)}), f32[16,1,128]{2,1,0:T(1,128)S(1)}, u32[]{:S(2)}, u32[]{:S(2)}) async-start(f32[16,1,128]{2,1,0:T(1,128)} %bitcast.14), calls=%async_computation.3 | async-start | bytes 16384 | tf_op jit(solution)/shard_map/all_to_all | solution.py:423
  102.3 7.3 %all-to-all-done.3 = f32[16,1,128]{2,1,0:T(1,128)S(1)} async-done(((f32[16,1,128]{2,1,0:T(1,128)}), f32[16,1,128]{2,1,0:T(1,128)S(1)}, u32[]{:S(2)}, u32[]{:S(2)}) %all-to-all-start.3) | async-done | bytes 8224 | tf_op jit(solution)/shard_map/all_to_all | solution.py:423
  (37 shorter events, 7.9 us)
Async XLA Ops:
  7.2 10.7 %collective-permute-start.5 = (bf16[112,768]{1,0:T(8,128)(2,1)S(1)}, bf16[112,768]{1,0:T(8,128)(2,1)S(1)}, u32[]{:S(2)}, u32[]{:S(2)}) collective-permute-start(bf16[112,768]{1,0:T(8,128)(2,1)S(1)} %get-tuple-element.302), channel_id=1, source_target_pairs={{0,1},{1,2},{2,3},{3,0},{8,9},{9,10},{10,11},{11,8},{16,17},{17,18... | collective-permute-start | bytes 516104 | tf_op jit(solution)/shard_map/ppermute | solution.py:392
  10.3 12.2 %collective-permute-start.6 = (bf16[112,768]{1,0:T(8,128)(2,1)S(1)}, bf16[112,768]{1,0:T(8,128)(2,1)S(1)}, u32[]{:S(2)}, u32[]{:S(2)}) collective-permute-start(bf16[112,768]{1,0:T(8,128)(2,1)S(1)} %get-tuple-element.303), channel_id=1, source_target_pairs={{0,9},{1,10},{2,11},{3,8},{8,1},{9,2},{10,3},{11,0},{16,25},{17,26... | collective-permute-start | bytes 516104 | tf_op jit(solution)/shard_map/ppermute | solution.py:392
  12.8 26.1 %collective-permute-start.9 = (bf16[112,768]{1,0:T(8,128)(2,1)S(1)}, bf16[112,768]{1,0:T(8,128)(2,1)S(1)}, u32[]{:S(2)}, u32[]{:S(2)}) collective-permute-start(bf16[112,768]{1,0:T(8,128)(2,1)S(1)} %get-tuple-element.307), channel_id=1, source_target_pairs={{0,2},{1,3},{2,0},{3,1},{8,10},{9,11},{10,8},{11,9},{16,18},{17,19... | collective-permute-start | bytes 516104 | tf_op jit(solution)/shard_map/ppermute | solution.py:392
  14.0 32.2 %collective-permute-start.10 = (bf16[112,768]{1,0:T(8,128)(2,1)S(1)}, bf16[112,768]{1,0:T(8,128)(2,1)S(1)}, u32[]{:S(2)}, u32[]{:S(2)}) collective-permute-start(bf16[112,768]{1,0:T(8,128)(2,1)S(1)} %get-tuple-element.308), channel_id=1, source_target_pairs={{0,10},{1,11},{2,8},{3,9},{8,2},{9,3},{10,0},{11,1},{16,26},{17,27... | collective-permute-start | bytes 516104 | tf_op jit(solution)/shard_map/ppermute | solution.py:392
  15.7 40.7 %collective-permute-start.11 = (bf16[112,768]{1,0:T(8,128)(2,1)S(1)}, bf16[112,768]{1,0:T(8,128)(2,1)S(1)}, u32[]{:S(2)}, u32[]{:S(2)}) collective-permute-start(bf16[112,768]{1,0:T(8,128)(2,1)S(1)} %get-tuple-element.309), channel_id=1, source_target_pairs={{0,18},{1,19},{2,16},{3,17},{8,26},{9,27},{10,24},{11,25},{16,2},{... | collective-permute-start | bytes 516104 | tf_op jit(solution)/shard_map/ppermute | solution.py:392
  17.9 45.6 %collective-permute-start.12 = (bf16[112,768]{1,0:T(8,128)(2,1)S(1)}, bf16[112,768]{1,0:T(8,128)(2,1)S(1)}, u32[]{:S(2)}, u32[]{:S(2)}) collective-permute-start(bf16[112,768]{1,0:T(8,128)(2,1)S(1)} %get-tuple-element.310), channel_id=1, source_target_pairs={{0,26},{1,27},{2,24},{3,25},{8,18},{9,19},{10,16},{11,17},{16,10},... | collective-permute-start | bytes 516104 | tf_op jit(solution)/shard_map/ppermute | solution.py:392
  22.5 41.1 %collective-permute-start.13 = (bf16[112,768]{1,0:T(8,128)(2,1)S(1)}, bf16[112,768]{1,0:T(8,128)(2,1)S(1)}, u32[]{:S(2)}, u32[]{:S(2)}) collective-permute-start(bf16[112,768]{1,0:T(8,128)(2,1)S(1)} %get-tuple-element.312), channel_id=1, source_target_pairs={{0,3},{1,0},{2,1},{3,2},{8,11},{9,8},{10,9},{11,10},{16,19},{17,16... | collective-permute-start | bytes 516104 | tf_op jit(solution)/shard_map/ppermute | solution.py:392
  38.9 29.4 %collective-permute-start.14 = (bf16[112,768]{1,0:T(8,128)(2,1)S(1)}, bf16[112,768]{1,0:T(8,128)(2,1)S(1)}, u32[]{:S(2)}, u32[]{:S(2)}) collective-permute-start(bf16[112,768]{1,0:T(8,128)(2,1)S(1)} %get-tuple-element.313), channel_id=1, source_target_pairs={{0,11},{1,8},{2,9},{3,10},{8,3},{9,0},{10,1},{11,2},{16,27},{17,24... | collective-permute-start | bytes 516104 | tf_op jit(solution)/shard_map/ppermute | solution.py:392
  46.2 22.7 %collective-permute-start.15 = (bf16[112,768]{1,0:T(8,128)(2,1)S(1)}, bf16[112,768]{1,0:T(8,128)(2,1)S(1)}, u32[]{:S(2)}, u32[]{:S(2)}) collective-permute-start(bf16[112,768]{1,0:T(8,128)(2,1)S(1)} %get-tuple-element.314), channel_id=1, source_target_pairs={{0,19},{1,16},{2,17},{3,18},{8,27},{9,24},{10,25},{11,26},{16,3},{... | collective-permute-start | bytes 516104 | tf_op jit(solution)/shard_map/ppermute | solution.py:392
  56.4 12.6 %collective-permute-start.16 = (bf16[112,768]{1,0:T(8,128)(2,1)S(1)}, bf16[112,768]{1,0:T(8,128)(2,1)S(1)}, u32[]{:S(2)}, u32[]{:S(2)}) collective-permute-start(bf16[112,768]{1,0:T(8,128)(2,1)S(1)} %get-tuple-element.315), channel_id=1, source_target_pairs={{0,27},{1,24},{2,25},{3,26},{8,19},{9,16},{10,17},{11,18},{16,11},... | collective-permute-start | bytes 516104 | tf_op jit(solution)/shard_map/ppermute | solution.py:392
  63.5 12.2 %collective-permute-start.7 = (bf16[112,768]{1,0:T(8,128)(2,1)S(1)}, bf16[112,768]{1,0:T(8,128)(2,1)S(1)}, u32[]{:S(2)}, u32[]{:S(2)}) collective-permute-start(bf16[112,768]{1,0:T(8,128)(2,1)S(1)} %get-tuple-element.304), channel_id=1, source_target_pairs={{0,17},{1,18},{2,19},{3,16},{8,25},{9,26},{10,27},{11,24},{16,1},{... | collective-permute-start | bytes 516104 | tf_op jit(solution)/shard_map/ppermute | solution.py:392
  63.6 12.2 %collective-permute-start.8 = (bf16[112,768]{1,0:T(8,128)(2,1)S(1)}, bf16[112,768]{1,0:T(8,128)(2,1)S(1)}, u32[]{:S(2)}, u32[]{:S(2)}) collective-permute-start(bf16[112,768]{1,0:T(8,128)(2,1)S(1)} %get-tuple-element.305), channel_id=1, source_target_pairs={{0,25},{1,26},{2,27},{3,24},{8,17},{9,18},{10,19},{11,16},{16,9},{... | collective-permute-start | bytes 516104 | tf_op jit(solution)/shard_map/ppermute | solution.py:392
  68.3 9.3 %collective-permute-start.2 = (bf16[112,768]{1,0:T(8,128)(2,1)S(1)}, bf16[112,768]{1,0:T(8,128)(2,1)S(1)}, u32[]{:S(2)}, u32[]{:S(2)}) collective-permute-start(bf16[112,768]{1,0:T(8,128)(2,1)S(1)} %get-tuple-element.298), channel_id=1, source_target_pairs={{0,8},{1,9},{2,10},{3,11},{8,0},{9,1},{10,2},{11,3},{16,24},{17,25... | collective-permute-start | bytes 516104 | tf_op jit(solution)/shard_map/ppermute | solution.py:392
  68.9 11.7 %collective-permute-start.3 = (bf16[112,768]{1,0:T(8,128)(2,1)S(1)}, bf16[112,768]{1,0:T(8,128)(2,1)S(1)}, u32[]{:S(2)}, u32[]{:S(2)}) collective-permute-start(bf16[112,768]{1,0:T(8,128)(2,1)S(1)} %get-tuple-element.299), channel_id=1, source_target_pairs={{0,16},{1,17},{2,18},{3,19},{8,24},{9,25},{10,26},{11,27},{16,0},{... | collective-permute-start | bytes 516104 | tf_op jit(solution)/shard_map/ppermute | solution.py:392
  68.9 11.7 %collective-permute-start.4 = (bf16[112,768]{1,0:T(8,128)(2,1)S(1)}, bf16[112,768]{1,0:T(8,128)(2,1)S(1)}, u32[]{:S(2)}, u32[]{:S(2)}) collective-permute-start(bf16[112,768]{1,0:T(8,128)(2,1)S(1)} %get-tuple-element.300), channel_id=1, source_target_pairs={{0,24},{1,25},{2,26},{3,27},{8,16},{9,17},{10,18},{11,19},{16,8},{... | collective-permute-start | bytes 516104 | tf_op jit(solution)/shard_map/ppermute | solution.py:392
  75.8 11.9 %collective-permute-start.24 = (bf16[464,768]{1,0:T(8,128)(2,1)S(1)}, bf16[464,768]{1,0:T(8,128)(2,1)S(1)}, u32[]{:S(2)}, u32[]{:S(2)}) collective-permute-start(bf16[464,768]{1,0:T(8,128)(2,1)S(1)} %get-tuple-element.320.refs_11_), channel_id=1, source_target_pairs={{0,4},{4,0},{1,5},{5,1},{2,6},{6,2},{3,7},{7,3},{8,12},{12,8},{9,1... | collective-permute-start | bytes 2138120 | tf_op jit(solution)/shard_map/ppermute | solution.py:409
  75.8 11.9 %collective-permute-start.23 = (bf16[464,768]{1,0:T(8,128)(2,1)S(1)}, bf16[464,768]{1,0:T(8,128)(2,1)S(1)}, u32[]{:S(2)}, u32[]{:S(2)}) collective-permute-start(bf16[464,768]{1,0:T(8,128)(2,1)S(1)} %get-tuple-element.319.refs_10_), channel_id=1, source_target_pairs={{0,4},{4,0},{1,5},{5,1},{2,6},{6,2},{3,7},{7,3},{8,12},{12,8},{9,1... | collective-permute-start | bytes 2138120 | tf_op jit(solution)/shard_map/ppermute | solution.py:409
  77.5 10.1 %collective-permute-start.22 = (bf16[464,768]{1,0:T(8,128)(2,1)S(1)}, bf16[464,768]{1,0:T(8,128)(2,1)S(1)}, u32[]{:S(2)}, u32[]{:S(2)}) collective-permute-start(bf16[464,768]{1,0:T(8,128)(2,1)S(1)} %get-tuple-element.318.refs_9_), channel_id=1, source_target_pairs={{0,4},{4,0},{1,5},{5,1},{2,6},{6,2},{3,7},{7,3},{8,12},{12,8},{9,1... | collective-permute-start | bytes 2138120 | tf_op jit(solution)/shard_map/ppermute | solution.py:409
  81.9 5.8 %collective-permute-start.21 = (bf16[464,768]{1,0:T(8,128)(2,1)S(1)}, bf16[464,768]{1,0:T(8,128)(2,1)S(1)}, u32[]{:S(2)}, u32[]{:S(2)}) collective-permute-start(bf16[464,768]{1,0:T(8,128)(2,1)S(1)} %get-tuple-element.317.refs_8_), channel_id=1, source_target_pairs={{0,4},{4,0},{1,5},{5,1},{2,6},{6,2},{3,7},{7,3},{8,12},{12,8},{9,1... | collective-permute-start | bytes 2138120 | tf_op jit(solution)/shard_map/ppermute | solution.py:409
  82.0 2.2 %collective-permute-start.17 = (s32[8,128]{1,0:T(8,128)S(1)}, s32[8,128]{1,0:T(8,128)S(1)}, u32[]{:S(2)}, u32[]{:S(2)}) collective-permute-start(s32[8,128]{1,0:T(8,128)S(1)} %get-tuple-element.301.refs_0_), channel_id=1, source_target_pairs={{0,4},{4,0},{1,5},{5,1},{2,6},{6,2},{3,7},{7,3},{8,12},{12,8},{9,1... | collective-permute-start | bytes 12296 | tf_op jit(solution)/shard_map/ppermute | solution.py:408
  84.1 1.2 %collective-permute-start.18 = (s32[8,128]{1,0:T(8,128)S(1)}, s32[8,128]{1,0:T(8,128)S(1)}, u32[]{:S(2)}, u32[]{:S(2)}) collective-permute-start(s32[8,128]{1,0:T(8,128)S(1)} %get-tuple-element.306.refs_1_), channel_id=1, source_target_pairs={{0,4},{4,0},{1,5},{5,1},{2,6},{6,2},{3,7},{7,3},{8,12},{12,8},{9,1... | collective-permute-start | bytes 12296 | tf_op jit(solution)/shard_map/ppermute | solution.py:408
  85.3 1.2 %collective-permute-start.19 = (s32[8,128]{1,0:T(8,128)S(1)}, s32[8,128]{1,0:T(8,128)S(1)}, u32[]{:S(2)}, u32[]{:S(2)}) collective-permute-start(s32[8,128]{1,0:T(8,128)S(1)} %get-tuple-element.311.refs_2_), channel_id=1, source_target_pairs={{0,4},{4,0},{1,5},{5,1},{2,6},{6,2},{3,7},{7,3},{8,12},{12,8},{9,1... | collective-permute-start | bytes 12296 | tf_op jit(solution)/shard_map/ppermute | solution.py:408
  86.5 1.2 %collective-permute-start.20 = (s32[8,128]{1,0:T(8,128)S(1)}, s32[8,128]{1,0:T(8,128)S(1)}, u32[]{:S(2)}, u32[]{:S(2)}) collective-permute-start(s32[8,128]{1,0:T(8,128)S(1)} %get-tuple-element.316.refs_3_), channel_id=1, source_target_pairs={{0,4},{4,0},{1,5},{5,1},{2,6},{6,2},{3,7},{7,3},{8,12},{12,8},{9,1... | collective-permute-start | bytes 12296 | tf_op jit(solution)/shard_map/ppermute | solution.py:408
  95.4 14.2 %all-to-all-start.3 = ((f32[16,1,128]{2,1,0:T(1,128)}), f32[16,1,128]{2,1,0:T(1,128)S(1)}, u32[]{:S(2)}, u32[]{:S(2)}) async-start(f32[16,1,128]{2,1,0:T(1,128)} %bitcast.14), calls=%async_computation.3 | async-start | bytes 16384 | tf_op jit(solution)/shard_map/all_to_all | solution.py:423
  (2 other events, 60.1 us)

commit v3 on v2

--- a/solution.py
+++ b/solution.py
@@ -1,4 +1,5 @@
 import functools
+import math
 
 import jax
 import jax.numpy as jnp
@@ -88,8 +89,9 @@
     return -(-value // multiple) * multiple
 
 
-def room(mean):
-    return int(mean + 4.75 * mean**0.5) + 1
+def room(count, parts, sigmas):
+    mean = count / parts
+    return math.ceil(mean + sigmas * (mean * (1 - 1 / parts)) ** 0.5)
 
 
 def iota(shape, axis):
@@ -112,7 +114,7 @@
 def pack_kernel(size, emb_ref, ids_ref, *refs):
     *out_refs, rank_ref, aug_ref = refs
     rows, width = emb_ref.shape
-    chips, labels, cap = size["chips"], size["labels"], size["cap"]
+    chips, labels, cap, pool = size["chips"], size["labels"], size["cap"], size["pool"]
     across, tiles = size["across"], size["tiles"]
     chunk = 256
     for start in range(0, rows, chunk):
@@ -127,17 +129,23 @@
     block = shift * across + side
     key = ((block * labels + label) * rows + iota((1, rows), 1)).astype(jnp.float32)
     base = (block * (labels * rows)).astype(jnp.float32)
+    base_shift = (shift * (across * labels * rows)).astype(jnp.float32)
     key_t = jnp.broadcast_to(key, (LANES, rows)).T
-    ranks = []
+    ranks, pooled = [], []
     for start in range(0, rows, LANES):
-        own = key[:, start : start + LANES]
-        low = base[:, start : start + LANES]
-        before = (key_t < own) & (key_t >= low)
-        ranks.append(jnp.sum(jnp.where(before, 1.0, 0.0), axis=0, keepdims=True))
+        here = slice(start, start + LANES)
+        smaller = key_t < key[:, here]
+        in_block = jnp.where(smaller & (key_t >= base[:, here]), 1.0, 0.0)
+        in_shift = jnp.where(smaller & (key_t >= base_shift[:, here]), 1.0, 0.0)
+        ranks.append(jnp.sum(in_block, axis=0, keepdims=True))
+        pooled.append(jnp.sum(in_shift, axis=0, keepdims=True))
     rank = jnp.concatenate(ranks, axis=1)
     rank_ref[...] = rank
-    over = jnp.max(jnp.where(rank >= cap - 1, 1.0, 0.0), axis=1, keepdims=True)
-    slot = jnp.where(rank < cap - 1, block * cap + rank.astype(jnp.int32), -1)
+    pooled = jnp.concatenate(pooled, axis=1)
+    full = (rank >= cap - 1) | ((shift > 0) & (pooled >= pool - across))
+    over = jnp.max(jnp.where(full, 1.0, 0.0), axis=1, keepdims=True)
+    place = jnp.where(shift > 0, pooled, side * cap + rank).astype(jnp.int32)
+    place = jnp.where(full, -1, place)
 
     in_block = jnp.where(iota((LANES, rows), 0) == block, 1.0, 0.0).astype(jnp.bfloat16)
     in_label = jnp.where(iota((LANES, rows), 0) == label, 1.0, 0.0).astype(jnp.bfloat16)
@@ -147,24 +155,54 @@
     counts = jnp.where(iota((LANES, LANES), 1) == FLAG, over, counts)
     aug_ref[rows:, :] = jnp.zeros((LANES, width), jnp.bfloat16)
     aug_ref[rows:, 0:LANES] = counts.astype(jnp.bfloat16)
-    place = iota((1, LANES), 1)
-    head = jnp.where(place < chips, place * cap + cap - 1, -1)
-    slot = jnp.concatenate([slot, head], axis=1)
+    lane = iota((1, LANES), 1)
+    head_shift = jnp.where(lane < chips, lane >> (across.bit_length() - 1), -1)
+    head_side = lane & (across - 1)
+    head = jnp.where(head_shift > 0, pool - across + head_side, head_side * cap + cap - 1)
+    shift = jnp.concatenate([shift, head_shift], axis=1)
+    place = jnp.concatenate([place, head], axis=1)
     aug = aug_ref[...]
-    for index, out_ref in enumerate(out_refs):
-        out_ref[...] = pick_rows(slot, index * cap, cap, aug)
+    for index in range(1, tiles):
+        out_refs[across + index - 1][...] = pick_rows(
+            jnp.where(shift == index, place, -1), 0, pool, aug
+        )
+    near = jnp.where(shift == 0, place, -1)
+    for index in range(across):
+        out_refs[index][...] = pick_rows(near, index * cap, cap, aug)
+
+
+def regroup_kernel(size, pool_ref, *out_refs):
+    across, cap, pool, labels = size["across"], size["cap"], size["pool"], size["labels"]
+    rows = pool_ref[...]
+    heads = rows[pool - 16 :, 0:LANES].astype(jnp.float32)
+    heads = jnp.where(iota((16, LANES), 1) < labels, heads, 0.0)
+    counts = jnp.sum(heads, axis=1, keepdims=True).astype(jnp.int32)
+    spot = iota((1, pool), 1)
+    place = jnp.full((1, pool), -1, jnp.int32)
+    begin = jnp.zeros((1, 1), jnp.int32)
+    for side in range(across):
+        end = begin + counts[16 - across + side : 17 - across + side, :]
+        place = jnp.where((spot >= begin) & (spot < end), spot - begin + side * cap, place)
+        begin = end
+    place = jnp.where(spot >= pool - across, (spot - (pool - across) + 1) * cap - 1, place)
+    for side, out_ref in enumerate(out_refs):
+        out_ref[...] = pick_rows(place, side * cap, cap, rows)
 
 
 def sort_kernel(size, *refs):
     across, labels, cap, space = size["across"], size["labels"], size["cap"], size["space"]
     block_refs, (out_ref, place_ref, counts_ref, rows_ref) = refs[:across], refs[across:]
-    total = across * cap
+    held = up(cap, ALIGN)
+    total = across * held
     for index, ref in enumerate(block_refs):
-        rows_ref[index * cap : (index + 1) * cap, :] = ref[...]
+        if held > cap:
+            start = (index + 1) * held - ALIGN
+            rows_ref[start : start + ALIGN, :] = jnp.zeros((ALIGN, ref.shape[1]), jnp.bfloat16)
+        rows_ref[index * held : index * held + cap, :] = ref[...]
     rows = rows_ref[...]
     spot = iota((LANES, total), 1)
     block = iota((LANES, total), 0)
-    head = jnp.where(spot == block * cap + cap - 1, 1.0, 0.0).astype(jnp.bfloat16)
+    head = jnp.where(spot == block * held + cap - 1, 1.0, 0.0).astype(jnp.bfloat16)
     counts = jnp.dot(head, rows[:, 0:LANES], preferred_element_type=jnp.float32)
     flag = jnp.max(counts[:, FLAG:], axis=0, keepdims=True)
 
@@ -187,7 +225,7 @@
     flag = jnp.maximum(flag, jnp.where(begin > space, 1.0, 0.0))
     found = jnp.where(lane == FLAG, flag, found)
     counts_ref[...] = jnp.broadcast_to(found, counts_ref.shape).astype(jnp.int32)
-    table.append((lane * cap).astype(jnp.float32))
+    table.append((lane * held).astype(jnp.float32))
     table.extend([jnp.zeros((1, LANES), jnp.float32)] * (up(len(table), 8) - len(table)))
     table = jnp.concatenate(table, axis=0)
 
@@ -200,7 +238,7 @@
             place = jnp.where(inside, where[2 * label : 2 * label + 1, :] + rank, place)
         return place.astype(jnp.int32)
 
-    spot_block = jnp.where((spot >= block * cap) & (spot < block * cap + cap), 1.0, 0.0)
+    spot_block = jnp.where((spot >= block * held) & (spot < block * held + cap), 1.0, 0.0)
     spot_row = iota((1, total), 1).astype(jnp.float32)
     place = places(spot_block, lambda where: spot_row - where[2 * labels : 2 * labels + 1, :])
     lanes = place_ref.shape[1]
@@ -362,35 +400,46 @@
     across, tiles = lax.axis_size("chip"), lax.axis_size("tile")
     chips = across * tiles
     labels = KG * across * lax.axis_size("core") // chips
-    cap = up(room(rows // chips) + 1, ALIGN)
-    batch = rows // tiles
-    space = up(room(batch) + labels * (ALIGN - 1) - labels * ALIGN // 4, ALIGN)
-    size = dict(chips=chips, across=across, tiles=tiles, labels=labels, cap=cap, space=space)
+    cap = up(room(rows, chips, 5.0) + 1, 8)
+    pool = up(room(rows, tiles, 4.25) + across, ALIGN)
+    space = up(room(rows, tiles, 4.75) + labels * (ALIGN - 4), ALIGN)
+    size = dict(
+        chips=chips, across=across, tiles=tiles, labels=labels, cap=cap, pool=pool, space=space
+    )
     lanes = up(cap + 1, LANES)
     shape = jax.ShapeDtypeStruct
 
     ids_row = cluster_ids.reshape(1, rows)
-    *blocks, rank = call(
+    *packed, rank = call(
         functools.partial(pack_kernel, size),
         "pack",
-        [shape((cap, width), jnp.bfloat16)] * chips + [shape((1, rows), jnp.float32)],
+        [shape((cap, width), jnp.bfloat16)] * across
+        + [shape((pool, width), jnp.bfloat16)] * (tiles - 1)
+        + [shape((1, rows), jnp.float32)],
         [embeddings, ids_row],
         scratch_shapes=[pltpu.VMEM((rows + LANES, width), jnp.bfloat16)],
     )
+    pools = {
+        shift: lax.ppermute(
+            packed[across + shift - 1], "tile", [(z, (z + shift) % tiles) for z in range(tiles)]
+        )
+        for shift in sorted(range(1, tiles), key=lambda shift: -min(shift, tiles - shift))
+    }
     own, other, own_counts, other_counts, places = [], [], [], [], []
     swap = [(0, 1), (1, 0)]
     for shift in range(tiles):
-        arrived = []
-        for side in range(across):
-            block = blocks[shift * across + side]
-            if shift or side:
-                route = [
-                    (a * tiles + z, (a ^ side) * tiles + (z + shift) % tiles)
-                    for a in range(across)
-                    for z in range(tiles)
-                ]
-                block = lax.ppermute(block, ("chip", "tile"), route)
-            arrived.append(block)
+        blocks = packed[:across]
+        if shift:
+            blocks = call(
+                functools.partial(regroup_kernel, size),
+                "regroup",
+                [shape((cap, width), jnp.bfloat16)] * across,
+                [pools[shift]],
+            )
+        arrived = [blocks[0]] + [
+            lax.ppermute(blocks[side], "chip", [(a, a ^ side) for a in range(across)])
+            for side in range(1, across)
+        ]
         ordered, place, counts = call(
             functools.partial(sort_kernel, size),
             "sort",
@@ -400,7 +449,7 @@
                 shape((8, LANES), jnp.int32),
             ],
             arrived,
-            scratch_shapes=[pltpu.VMEM((across * cap, width), jnp.bfloat16)],
+            scratch_shapes=[pltpu.VMEM((across * up(cap, ALIGN), width), jnp.bfloat16)],
         )
         own.append(ordered)
         places.append(place)

time: 113 us -> 108 us (0.956)
  starting transfers between devices: 55.5 us -> 50.4 us
  Pallas kernels: 20.9 us -> 23.8 us
  waiting for transfers between devices: 34.1 us -> 32.4 us
    ppermute x15, starting transfers between devices: 47 us -> 33.6 us  [the longest x12 27.5 us: body(): lax.ppermute(blocks[side], 'chip', [(a, a ^ side) for a in range(across)])]
    all_to_all x1, starting transfers between devices: 6.9 us -> 14.4 us  [body(): lax.all_to_all(totals, ('chip', 'tile'), split_axis=0, concat_axis=0, til...]
    pallas_call x7 -> x10, Pallas kernels: 20.9 us -> 23.8 us  [call(): pl.pallas_call(kernel, out_shape=out_shape, in_specs=[smem] * scalars + [...]
    ppermute x15, waiting for transfers between devices: 22.1 us -> 20.9 us  [the longest x3 18.5 us: body(): lax.ppermute(packed[across + shift - 1], 'tile', [(z, (z + shift) % tiles...]
  transfers between devices with their start and end apart: 24 -> 24, of which waited for: 9 -> 8; matrix products, arithmetic and copies ran while one was open for 0% -> 0% of each run, Pallas kernels for 4% -> 7%
where the time goes in v3:
time: 108 us
  starting transfers between devices  50.4 us (47%)
  waiting for transfers between devices  32.4 us (30%)
  Pallas kernels  23.8 us (22%)
    ppermute x12, starting transfers between devices, body(): lax.ppermute(blocks[side], 'chip', [(a, a ^ side) for a in range(across)])  27.5 us
    pallas_call x10, Pallas kernels, call(): pl.pallas_call(kernel, out_shape=out_shape, in_specs=[smem] * scalars + [...  23.8 us
    ppermute x3, waiting for transfers between devices, body(): lax.ppermute(packed[across + shift - 1], 'tile', [(z, (z + shift) % tiles...  18.5 us
    all_to_all x1, starting transfers between devices, body(): lax.all_to_all(totals, ('chip', 'tile'), split_axis=0, concat_axis=0, til...  14.4 us
    all_to_all x1, waiting for transfers between devices, body(): lax.all_to_all(totals, ('chip', 'tile'), split_axis=0, concat_axis=0, til...  7.26 us
    ppermute x3, starting transfers between devices, body(): lax.ppermute(packed[across + shift - 1], 'tile', [(z, (z + shift) % tiles...  6.13 us
    ppermute x4, waiting for transfers between devices, body(): other_counts.append(lax.ppermute(counts, 'core', swap))  4.2 us
    ppermute x12, waiting for transfers between devices, body(): lax.ppermute(blocks[side], 'chip', [(a, a ^ side) for a in range(across)])  2.42 us
  transfers between devices with their start and end apart: 24, of which 8 were waited for; matrix products, arithmetic and copies ran while one was open for 0% of the time, Pallas kernels for 7%

profile of v3, /device:TPU:0, one launch (start us, length us, event | category | flops | bytes accessed | tf_op | source)
XLA Modules:
  0.0 108.0 jit_solution(15594077343919230002)
XLA Ops:
  0.0 6.6 %pack.1 = (bf16[104,768]{1,0:T(8,128)(2,1)S(1)}, bf16[104,768]{1,0:T(8,128)(2,1)S(1)}, bf16[104,768]{1,0:T(8,128)(2,1)S(1)}, bf16[104,768]{1,0:T(8,128)(2,1)S(1)...) custom-call(f32[1024,768]{1,0:T(8,128)} %emb_ref.1, ...), custom_call_target="tpu_custom_call" | custom-call | tf_op jit(solution)/shard_map/pack/pallas_call | solution.py:387
  6.6 4.1 %collective-permute-start.9 = (bf16[320,768]{1,0:T(8,128)(2,1)S(1)}, bf16[320,768]{1,0:T(8,128)(2,1)S(1)}, u32[]{:S(2)}, u32[]{:S(2)}) collective-permute-start(bf16[320,768]{1,0:T(8,128)(2,1)S(1)} %get-tuple-element.311), channel_id=1, source_target_pairs={{0,2},{1,3},{2,0},{3,1},{4,6},{5,7},{6,4},{7,5},{8,10},{9,11},{10,... | collective-permute-start | bytes 1474568 | tf_op jit(solution)/shard_map/ppermute | solution.py:423
  10.7 1.3 %collective-permute-start.13 = (bf16[320,768]{1,0:T(8,128)(2,1)S(1)}, bf16[320,768]{1,0:T(8,128)(2,1)S(1)}, u32[]{:S(2)}, u32[]{:S(2)}) collective-permute-start(bf16[320,768]{1,0:T(8,128)(2,1)S(1)} %get-tuple-element.317), channel_id=1, source_target_pairs={{0,3},{1,0},{2,1},{3,2},{4,7},{5,4},{6,5},{7,6},{8,11},{9,8},{10,9... | collective-permute-start | bytes 1474568 | tf_op jit(solution)/shard_map/ppermute | solution.py:423
  12.7 1.5 %collective-permute-start.2 = (bf16[104,768]{1,0:T(8,128)(2,1)S(1)}, bf16[104,768]{1,0:T(8,128)(2,1)S(1)}, u32[]{:S(2)}, u32[]{:S(2)}) collective-permute-start(bf16[104,768]{1,0:T(8,128)(2,1)S(1)} %get-tuple-element.301), channel_id=1, source_target_pairs={{0,8},{8,0},{16,24},{24,16},{1,9},{9,1},{17,25},{25,17},{2,10},{10... | collective-permute-start | bytes 479240 | tf_op jit(solution)/shard_map/ppermute | solution.py:440
  14.2 1.5 %collective-permute-start.3 = (bf16[104,768]{1,0:T(8,128)(2,1)S(1)}, bf16[104,768]{1,0:T(8,128)(2,1)S(1)}, u32[]{:S(2)}, u32[]{:S(2)}) collective-permute-start(bf16[104,768]{1,0:T(8,128)(2,1)S(1)} %get-tuple-element.302), channel_id=1, source_target_pairs={{0,16},{8,24},{16,0},{24,8},{1,17},{9,25},{17,1},{25,9},{2,18},{10... | collective-permute-start | bytes 479240 | tf_op jit(solution)/shard_map/ppermute | solution.py:440
  15.7 18.5 %collective-permute-done.9.pool_ref = bf16[320,768]{1,0:T(8,128)(2,1)S(1)} collective-permute-done((bf16[320,768]{1,0:T(8,128)(2,1)S(1)}, bf16[320,768]{1,0:T(8,128)(2,1)S(1)}, u32[]{:S(2)}, u32[]{:S(2)}) %collective-permute-start.9) | collective-permute-done | bytes 491552 | tf_op jit(solution)/shard_map/ppermute | solution.py:423
  34.2 12.5 %collective-permute-start.4 = (bf16[104,768]{1,0:T(8,128)(2,1)S(1)}, bf16[104,768]{1,0:T(8,128)(2,1)S(1)}, u32[]{:S(2)}, u32[]{:S(2)}) collective-permute-start(bf16[104,768]{1,0:T(8,128)(2,1)S(1)} %get-tuple-element.303), channel_id=1, source_target_pairs={{0,24},{8,16},{16,8},{24,0},{1,25},{9,17},{17,9},{25,1},{2,26},{10... | collective-permute-start | bytes 479240 | tf_op jit(solution)/shard_map/ppermute | solution.py:440
  48.7 1.6 %collective-permute-start.14 = (bf16[104,768]{1,0:T(8,128)(2,1)S(1)}, bf16[104,768]{1,0:T(8,128)(2,1)S(1)}, u32[]{:S(2)}, u32[]{:S(2)}) collective-permute-start(bf16[104,768]{1,0:T(8,128)(2,1)S(1)} %get-tuple-element.319), channel_id=1, source_target_pairs={{0,8},{8,0},{16,24},{24,16},{1,9},{9,1},{17,25},{25,17},{2,10},{10... | collective-permute-start | bytes 479240 | tf_op jit(solution)/shard_map/ppermute | solution.py:440
  50.7 1.5 %collective-permute-start.16 = (bf16[104,768]{1,0:T(8,128)(2,1)S(1)}, bf16[104,768]{1,0:T(8,128)(2,1)S(1)}, u32[]{:S(2)}, u32[]{:S(2)}) collective-permute-start(bf16[104,768]{1,0:T(8,128)(2,1)S(1)} %get-tuple-element.321), channel_id=1, source_target_pairs={{0,24},{8,16},{16,8},{24,0},{1,25},{9,17},{17,9},{25,1},{2,26},{10... | collective-permute-start | bytes 479240 | tf_op jit(solution)/shard_map/ppermute | solution.py:440
  53.1 1.3 %collective-permute-done.10.refs_1_ = bf16[104,768]{1,0:T(8,128)(2,1)S(1)} collective-permute-done((bf16[104,768]{1,0:T(8,128)(2,1)S(1)}, bf16[104,768]{1,0:T(8,128)(2,1)S(1)}, u32[]{:S(2)}, u32[]{:S(2)}) %collective-permute-start.10) | collective-permute-done | bytes 159776 | tf_op jit(solution)/shard_map/ppermute | solution.py:440
  54.4 2.4 %collective-permute-start.12 = (bf16[104,768]{1,0:T(8,128)(2,1)S(1)}, bf16[104,768]{1,0:T(8,128)(2,1)S(1)}, u32[]{:S(2)}, u32[]{:S(2)}) collective-permute-start(bf16[104,768]{1,0:T(8,128)(2,1)S(1)} %get-tuple-element.315), channel_id=1, source_target_pairs={{0,24},{8,16},{16,8},{24,0},{1,25},{9,17},{17,9},{25,1},{2,26},{10... | collective-permute-start | bytes 479240 | tf_op jit(solution)/shard_map/ppermute | solution.py:440
  56.8 1.0 collective-permute-done.14.refs_1_
  57.8 2.4 %collective-permute-start.6 = (bf16[104,768]{1,0:T(8,128)(2,1)S(1)}, bf16[104,768]{1,0:T(8,128)(2,1)S(1)}, u32[]{:S(2)}, u32[]{:S(2)}) collective-permute-start(bf16[104,768]{1,0:T(8,128)(2,1)S(1)} %get-tuple-element.307), channel_id=1, source_target_pairs={{0,8},{8,0},{16,24},{24,16},{1,9},{9,1},{17,25},{25,17},{2,10},{10... | collective-permute-start | bytes 479240 | tf_op jit(solution)/shard_map/ppermute | solution.py:440
  60.8 2.4 %collective-permute-start.8 = (bf16[104,768]{1,0:T(8,128)(2,1)S(1)}, bf16[104,768]{1,0:T(8,128)(2,1)S(1)}, u32[]{:S(2)}, u32[]{:S(2)}) collective-permute-start(bf16[104,768]{1,0:T(8,128)(2,1)S(1)} %get-tuple-element.309), channel_id=1, source_target_pairs={{0,24},{8,16},{16,8},{24,0},{1,25},{9,17},{17,9},{25,1},{2,26},{10... | collective-permute-start | bytes 479240 | tf_op jit(solution)/shard_map/ppermute | solution.py:440
  63.2 1.2 %sort.4 = (bf16[464,768]{1,0:T(8,128)(2,1)S(1)}, s32[4,128]{1,0:T(4,128)S(1)}, s32[8,128]{1,0:T(8,128)S(1)}) custom-call(bf16[104,768]{1,0:T(8,128)(2,1)S(1)} %get-tuple-element.300.refs_0_, bf16[104,768]{1,0:T(8,128)(2,1)S(1)} %collective-permute-done.2.refs_1_, bf16[104,768]{1,0:T(8,128)(2,1)S(1)} %collective-permute-done.3.refs_2_, ...), custom_call_target="tpu_custom_call" | custom-call | tf_op jit(solution)/shard_map/sort/pallas_call | solution.py:387
  64.4 1.2 %sort.7 = (bf16[464,768]{1,0:T(8,128)(2,1)S(1)}, s32[4,128]{1,0:T(4,128)S(1)}, s32[8,128]{1,0:T(8,128)S(1)}) custom-call(bf16[104,768]{1,0:T(8,128)(2,1)S(1)} %get-tuple-element.318.refs_0_, bf16[104,768]{1,0:T(8,128)(2,1)S(1)} %collective-permute-done.14.refs_1_, bf16[104,768]{1,0:T(8,128)(2,1)S(1)} %collective-permute-done.15.refs_2_, ...), custom_call_target="tpu_custom_call" | custom-call | tf_op jit(solution)/shard_map/sort/pallas_call | solution.py:387
  66.2 1.2 %sort.6 = (bf16[464,768]{1,0:T(8,128)(2,1)S(1)}, s32[4,128]{1,0:T(4,128)S(1)}, s32[8,128]{1,0:T(8,128)S(1)}) custom-call(bf16[104,768]{1,0:T(8,128)(2,1)S(1)} %get-tuple-element.312.refs_0_, bf16[104,768]{1,0:T(8,128)(2,1)S(1)} %collective-permute-done.10.refs_1_, bf16[104,768]{1,0:T(8,128)(2,1)S(1)} %collective-permute-done.11.refs_2_, ...), custom_call_target="tpu_custom_call" | custom-call | tf_op jit(solution)/shard_map/sort/pallas_call | solution.py:387
  67.7 1.2 %sort.5 = (bf16[464,768]{1,0:T(8,128)(2,1)S(1)}, s32[4,128]{1,0:T(4,128)S(1)}, s32[8,128]{1,0:T(8,128)S(1)}) custom-call(bf16[104,768]{1,0:T(8,128)(2,1)S(1)} %get-tuple-element.306.refs_0_, bf16[104,768]{1,0:T(8,128)(2,1)S(1)} %collective-permute-done.6.refs_1_, bf16[104,768]{1,0:T(8,128)(2,1)S(1)} %collective-permute-done.7.refs_2_, ...), custom_call_target="tpu_custom_call" | custom-call | tf_op jit(solution)/shard_map/sort/pallas_call | solution.py:387
  69.5 1.7 %collective-permute-done.17.refs_4_ = s32[8,128]{1,0:T(8,128)S(1)} collective-permute-done((s32[8,128]{1,0:T(8,128)S(1)}, s32[8,128]{1,0:T(8,128)S(1)}, u32[]{:S(2)}, u32[]{:S(2)}) %collective-permute-start.17) | collective-permute-done | bytes 4128 | tf_op jit(solution)/shard_map/ppermute | solution.py:457
  71.6 0.8 collective-permute-done.18.refs_5_
  74.8 9.2 %score.1 = f32[16,128]{1,0:T(8,128)} custom-call(s32[8,128]{1,0:T(8,128)S(1)} %get-tuple-element.304.refs_0_, s32[8,128]{1,0:T(8,128)S(1)} %get-tuple-element.310.refs_1_, s32[8,128]{1,0:T(8,128)S(1)} %get-tuple-element.316.refs_2_, s32[8,128]{1,0:T(8,128)S(1)} %get-tuple-element.322.refs_3_, s32[8,128]{1,0:T(8,128)S(1)} %collective-permute-done.17.refs_4_, ...), custom_call_target="tpu_custom_call" | custom-call | tf_op jit(solution)/shard_map/score/pallas_call | solution.py:387
  83.9 14.4 %all-to-all-start.3 = ((f32[16,1,128]{2,1,0:T(1,128)}), f32[16,1,128]{2,1,0:T(1,128)S(1)}, u32[]{:S(2)}, u32[]{:S(2)}) async-start(f32[16,1,128]{2,1,0:T(1,128)} %bitcast.14), calls=%async_computation.3 | async-start | bytes 16384 | tf_op jit(solution)/shard_map/all_to_all | solution.py:472
  98.4 7.3 %all-to-all-done.3 = f32[16,1,128]{2,1,0:T(1,128)S(1)} async-done(((f32[16,1,128]{2,1,0:T(1,128)}), f32[16,1,128]{2,1,0:T(1,128)S(1)}, u32[]{:S(2)}, u32[]{:S(2)}) %all-to-all-start.3) | async-done | bytes 8224 | tf_op jit(solution)/shard_map/all_to_all | solution.py:472
  105.7 1.0 unpack.1
  (40 shorter events, 9.1 us)
Async XLA Ops:
  6.6 27.6 %collective-permute-start.9 = (bf16[320,768]{1,0:T(8,128)(2,1)S(1)}, bf16[320,768]{1,0:T(8,128)(2,1)S(1)}, u32[]{:S(2)}, u32[]{:S(2)}) collective-permute-start(bf16[320,768]{1,0:T(8,128)(2,1)S(1)} %get-tuple-element.311), channel_id=1, source_target_pairs={{0,2},{1,3},{2,0},{3,1},{4,6},{5,7},{6,4},{7,5},{8,10},{9,11},{10,... | collective-permute-start | bytes 1474568 | tf_op jit(solution)/shard_map/ppermute | solution.py:423
  10.7 36.7 %collective-permute-start.13 = (bf16[320,768]{1,0:T(8,128)(2,1)S(1)}, bf16[320,768]{1,0:T(8,128)(2,1)S(1)}, u32[]{:S(2)}, u32[]{:S(2)}) collective-permute-start(bf16[320,768]{1,0:T(8,128)(2,1)S(1)} %get-tuple-element.317), channel_id=1, source_target_pairs={{0,3},{1,0},{2,1},{3,2},{4,7},{5,4},{6,5},{7,6},{8,11},{9,8},{10,9... | collective-permute-start | bytes 1474568 | tf_op jit(solution)/shard_map/ppermute | solution.py:423
  12.0 38.7 %collective-permute-start.5 = (bf16[320,768]{1,0:T(8,128)(2,1)S(1)}, bf16[320,768]{1,0:T(8,128)(2,1)S(1)}, u32[]{:S(2)}, u32[]{:S(2)}) collective-permute-start(bf16[320,768]{1,0:T(8,128)(2,1)S(1)} %get-tuple-element.305), channel_id=1, source_target_pairs={{0,1},{1,2},{2,3},{3,0},{4,5},{5,6},{6,7},{7,4},{8,9},{9,10},{10,1... | collective-permute-start | bytes 1474568 | tf_op jit(solution)/shard_map/ppermute | solution.py:423
  12.7 35.9 %collective-permute-start.2 = (bf16[104,768]{1,0:T(8,128)(2,1)S(1)}, bf16[104,768]{1,0:T(8,128)(2,1)S(1)}, u32[]{:S(2)}, u32[]{:S(2)}) collective-permute-start(bf16[104,768]{1,0:T(8,128)(2,1)S(1)} %get-tuple-element.301), channel_id=1, source_target_pairs={{0,8},{8,0},{16,24},{24,16},{1,9},{9,1},{17,25},{25,17},{2,10},{10... | collective-permute-start | bytes 479240 | tf_op jit(solution)/shard_map/ppermute | solution.py:440
  14.2 36.0 %collective-permute-start.3 = (bf16[104,768]{1,0:T(8,128)(2,1)S(1)}, bf16[104,768]{1,0:T(8,128)(2,1)S(1)}, u32[]{:S(2)}, u32[]{:S(2)}) collective-permute-start(bf16[104,768]{1,0:T(8,128)(2,1)S(1)} %get-tuple-element.302), channel_id=1, source_target_pairs={{0,16},{8,24},{16,0},{24,8},{1,17},{9,25},{17,1},{25,9},{2,18},{10... | collective-permute-start | bytes 479240 | tf_op jit(solution)/shard_map/ppermute | solution.py:440
  34.2 18.8 %collective-permute-start.4 = (bf16[104,768]{1,0:T(8,128)(2,1)S(1)}, bf16[104,768]{1,0:T(8,128)(2,1)S(1)}, u32[]{:S(2)}, u32[]{:S(2)}) collective-permute-start(bf16[104,768]{1,0:T(8,128)(2,1)S(1)} %get-tuple-element.303), channel_id=1, source_target_pairs={{0,24},{8,16},{16,8},{24,0},{1,25},{9,17},{17,9},{25,1},{2,26},{10... | collective-permute-start | bytes 479240 | tf_op jit(solution)/shard_map/ppermute | solution.py:440
  47.3 7.1 %collective-permute-start.10 = (bf16[104,768]{1,0:T(8,128)(2,1)S(1)}, bf16[104,768]{1,0:T(8,128)(2,1)S(1)}, u32[]{:S(2)}, u32[]{:S(2)}) collective-permute-start(bf16[104,768]{1,0:T(8,128)(2,1)S(1)} %get-tuple-element.313), channel_id=1, source_target_pairs={{0,8},{8,0},{16,24},{24,16},{1,9},{9,1},{17,25},{25,17},{2,10},{10... | collective-permute-start | bytes 479240 | tf_op jit(solution)/shard_map/ppermute | solution.py:440
  48.7 9.2 %collective-permute-start.14 = (bf16[104,768]{1,0:T(8,128)(2,1)S(1)}, bf16[104,768]{1,0:T(8,128)(2,1)S(1)}, u32[]{:S(2)}, u32[]{:S(2)}) collective-permute-start(bf16[104,768]{1,0:T(8,128)(2,1)S(1)} %get-tuple-element.319), channel_id=1, source_target_pairs={{0,8},{8,0},{16,24},{24,16},{1,9},{9,1},{17,25},{25,17},{2,10},{10... | collective-permute-start | bytes 479240 | tf_op jit(solution)/shard_map/ppermute | solution.py:440
  50.2 10.1 %collective-permute-start.15 = (bf16[104,768]{1,0:T(8,128)(2,1)S(1)}, bf16[104,768]{1,0:T(8,128)(2,1)S(1)}, u32[]{:S(2)}, u32[]{:S(2)}) collective-permute-start(bf16[104,768]{1,0:T(8,128)(2,1)S(1)} %get-tuple-element.320), channel_id=1, source_target_pairs={{0,16},{8,24},{16,0},{24,8},{1,17},{9,25},{17,1},{25,9},{2,18},{10... | collective-permute-start | bytes 479240 | tf_op jit(solution)/shard_map/ppermute | solution.py:440
  50.7 10.1 %collective-permute-start.16 = (bf16[104,768]{1,0:T(8,128)(2,1)S(1)}, bf16[104,768]{1,0:T(8,128)(2,1)S(1)}, u32[]{:S(2)}, u32[]{:S(2)}) collective-permute-start(bf16[104,768]{1,0:T(8,128)(2,1)S(1)} %get-tuple-element.321), channel_id=1, source_target_pairs={{0,24},{8,16},{16,8},{24,0},{1,25},{9,17},{17,9},{25,1},{2,26},{10... | collective-permute-start | bytes 479240 | tf_op jit(solution)/shard_map/ppermute | solution.py:440
  52.9 12.7 %collective-permute-start.11 = (bf16[104,768]{1,0:T(8,128)(2,1)S(1)}, bf16[104,768]{1,0:T(8,128)(2,1)S(1)}, u32[]{:S(2)}, u32[]{:S(2)}) collective-permute-start(bf16[104,768]{1,0:T(8,128)(2,1)S(1)} %get-tuple-element.314), channel_id=1, source_target_pairs={{0,16},{8,24},{16,0},{24,8},{1,17},{9,25},{17,1},{25,9},{2,18},{10... | collective-permute-start | bytes 479240 | tf_op jit(solution)/shard_map/ppermute | solution.py:440
  54.4 11.3 %collective-permute-start.12 = (bf16[104,768]{1,0:T(8,128)(2,1)S(1)}, bf16[104,768]{1,0:T(8,128)(2,1)S(1)}, u32[]{:S(2)}, u32[]{:S(2)}) collective-permute-start(bf16[104,768]{1,0:T(8,128)(2,1)S(1)} %get-tuple-element.315), channel_id=1, source_target_pairs={{0,24},{8,16},{16,8},{24,0},{1,25},{9,17},{17,9},{25,1},{2,26},{10... | collective-permute-start | bytes 479240 | tf_op jit(solution)/shard_map/ppermute | solution.py:440
  57.8 9.7 %collective-permute-start.6 = (bf16[104,768]{1,0:T(8,128)(2,1)S(1)}, bf16[104,768]{1,0:T(8,128)(2,1)S(1)}, u32[]{:S(2)}, u32[]{:S(2)}) collective-permute-start(bf16[104,768]{1,0:T(8,128)(2,1)S(1)} %get-tuple-element.307), channel_id=1, source_target_pairs={{0,8},{8,0},{16,24},{24,16},{1,9},{9,1},{17,25},{25,17},{2,10},{10... | collective-permute-start | bytes 479240 | tf_op jit(solution)/shard_map/ppermute | solution.py:440
  60.3 7.4 %collective-permute-start.7 = (bf16[104,768]{1,0:T(8,128)(2,1)S(1)}, bf16[104,768]{1,0:T(8,128)(2,1)S(1)}, u32[]{:S(2)}, u32[]{:S(2)}) collective-permute-start(bf16[104,768]{1,0:T(8,128)(2,1)S(1)} %get-tuple-element.308), channel_id=1, source_target_pairs={{0,16},{8,24},{16,0},{24,8},{1,17},{9,25},{17,1},{25,9},{2,18},{10... | collective-permute-start | bytes 479240 | tf_op jit(solution)/shard_map/ppermute | solution.py:440
  60.8 6.9 %collective-permute-start.8 = (bf16[104,768]{1,0:T(8,128)(2,1)S(1)}, bf16[104,768]{1,0:T(8,128)(2,1)S(1)}, u32[]{:S(2)}, u32[]{:S(2)}) collective-permute-start(bf16[104,768]{1,0:T(8,128)(2,1)S(1)} %get-tuple-element.309), channel_id=1, source_target_pairs={{0,24},{8,16},{16,8},{24,0},{1,25},{9,17},{17,9},{25,1},{2,26},{10... | collective-permute-start | bytes 479240 | tf_op jit(solution)/shard_map/ppermute | solution.py:440
  65.7 9.1 %collective-permute-start.21 = (bf16[464,768]{1,0:T(8,128)(2,1)S(1)}, bf16[464,768]{1,0:T(8,128)(2,1)S(1)}, u32[]{:S(2)}, u32[]{:S(2)}) collective-permute-start(bf16[464,768]{1,0:T(8,128)(2,1)S(1)} %get-tuple-element.323.refs_8_), channel_id=1, source_target_pairs={{0,4},{4,0},{1,5},{5,1},{2,6},{6,2},{3,7},{7,3},{8,12},{12,8},{9,1... | collective-permute-start | bytes 2138120 | tf_op jit(solution)/shard_map/ppermute | solution.py:458
  65.8 9.0 %collective-permute-start.24 = (bf16[464,768]{1,0:T(8,128)(2,1)S(1)}, bf16[464,768]{1,0:T(8,128)(2,1)S(1)}, u32[]{:S(2)}, u32[]{:S(2)}) collective-permute-start(bf16[464,768]{1,0:T(8,128)(2,1)S(1)} %get-tuple-element.326.refs_11_), channel_id=1, source_target_pairs={{0,4},{4,0},{1,5},{5,1},{2,6},{6,2},{3,7},{7,3},{8,12},{12,8},{9,1... | collective-permute-start | bytes 2138120 | tf_op jit(solution)/shard_map/ppermute | solution.py:458
  67.5 7.3 %collective-permute-start.23 = (bf16[464,768]{1,0:T(8,128)(2,1)S(1)}, bf16[464,768]{1,0:T(8,128)(2,1)S(1)}, u32[]{:S(2)}, u32[]{:S(2)}) collective-permute-start(bf16[464,768]{1,0:T(8,128)(2,1)S(1)} %get-tuple-element.325.refs_10_), channel_id=1, source_target_pairs={{0,4},{4,0},{1,5},{5,1},{2,6},{6,2},{3,7},{7,3},{8,12},{12,8},{9,1... | collective-permute-start | bytes 2138120 | tf_op jit(solution)/shard_map/ppermute | solution.py:458
  68.9 5.9 %collective-permute-start.22 = (bf16[464,768]{1,0:T(8,128)(2,1)S(1)}, bf16[464,768]{1,0:T(8,128)(2,1)S(1)}, u32[]{:S(2)}, u32[]{:S(2)}) collective-permute-start(bf16[464,768]{1,0:T(8,128)(2,1)S(1)} %get-tuple-element.324.refs_9_), channel_id=1, source_target_pairs={{0,4},{4,0},{1,5},{5,1},{2,6},{6,2},{3,7},{7,3},{8,12},{12,8},{9,1... | collective-permute-start | bytes 2138120 | tf_op jit(solution)/shard_map/ppermute | solution.py:458
  69.4 1.8 %collective-permute-start.17 = (s32[8,128]{1,0:T(8,128)S(1)}, s32[8,128]{1,0:T(8,128)S(1)}, u32[]{:S(2)}, u32[]{:S(2)}) collective-permute-start(s32[8,128]{1,0:T(8,128)S(1)} %get-tuple-element.304.refs_0_), channel_id=1, source_target_pairs={{0,4},{4,0},{1,5},{5,1},{2,6},{6,2},{3,7},{7,3},{8,12},{12,8},{9,1... | collective-permute-start | bytes 12296 | tf_op jit(solution)/shard_map/ppermute | solution.py:457
  71.2 1.2 %collective-permute-start.18 = (s32[8,128]{1,0:T(8,128)S(1)}, s32[8,128]{1,0:T(8,128)S(1)}, u32[]{:S(2)}, u32[]{:S(2)}) collective-permute-start(s32[8,128]{1,0:T(8,128)S(1)} %get-tuple-element.310.refs_1_), channel_id=1, source_target_pairs={{0,4},{4,0},{1,5},{5,1},{2,6},{6,2},{3,7},{7,3},{8,12},{12,8},{9,1... | collective-permute-start | bytes 12296 | tf_op jit(solution)/shard_map/ppermute | solution.py:457
  72.4 1.2 %collective-permute-start.19 = (s32[8,128]{1,0:T(8,128)S(1)}, s32[8,128]{1,0:T(8,128)S(1)}, u32[]{:S(2)}, u32[]{:S(2)}) collective-permute-start(s32[8,128]{1,0:T(8,128)S(1)} %get-tuple-element.316.refs_2_), channel_id=1, source_target_pairs={{0,4},{4,0},{1,5},{5,1},{2,6},{6,2},{3,7},{7,3},{8,12},{12,8},{9,1... | collective-permute-start | bytes 12296 | tf_op jit(solution)/shard_map/ppermute | solution.py:457
  73.6 1.2 %collective-permute-start.20 = (s32[8,128]{1,0:T(8,128)S(1)}, s32[8,128]{1,0:T(8,128)S(1)}, u32[]{:S(2)}, u32[]{:S(2)}) collective-permute-start(s32[8,128]{1,0:T(8,128)S(1)} %get-tuple-element.322.refs_3_), channel_id=1, source_target_pairs={{0,4},{4,0},{1,5},{5,1},{2,6},{6,2},{3,7},{7,3},{8,12},{12,8},{9,1... | collective-permute-start | bytes 12296 | tf_op jit(solution)/shard_map/ppermute | solution.py:457
  83.9 21.7 %all-to-all-start.3 = ((f32[16,1,128]{2,1,0:T(1,128)}), f32[16,1,128]{2,1,0:T(1,128)S(1)}, u32[]{:S(2)}, u32[]{:S(2)}) async-start(f32[16,1,128]{2,1,0:T(1,128)} %bitcast.14), calls=%async_computation.3 | async-start | bytes 16384 | tf_op jit(solution)/shard_map/all_to_all | solution.py:472
  (2 other events, 78.2 us)

commit v4 on v3

--- a/solution.py
+++ b/solution.py
@@ -22,6 +22,7 @@
 STEP = 32
 LEFT = 192
 RIGHT = 384
+PLACES = 1 << 16
 
 
 def unit_rows(embeddings):
@@ -111,11 +112,10 @@
     )
 
 
-def pack_kernel(size, emb_ref, ids_ref, *refs):
-    *out_refs, rank_ref, aug_ref = refs
+def plan_kernel(size, emb_ref, ids_ref, pool_ref, aug_ref, place_ref, rank_ref):
     rows, width = emb_ref.shape
     chips, labels, cap, pool = size["chips"], size["labels"], size["cap"], size["pool"]
-    across, tiles = size["across"], size["tiles"]
+    across, tiles, direct = size["across"], size["tiles"], size["direct"]
     chunk = 256
     for start in range(0, rows, chunk):
         x = emb_ref[start : start + chunk, :]
@@ -142,9 +142,13 @@
     rank = jnp.concatenate(ranks, axis=1)
     rank_ref[...] = rank
     pooled = jnp.concatenate(pooled, axis=1)
-    full = (rank >= cap - 1) | ((shift > 0) & (pooled >= pool - across))
+
+    def apart(shift):
+        return (shift == 0) | (shift == direct)
+
+    full = (rank >= cap - 1) | (~apart(shift) & (pooled >= pool - across))
     over = jnp.max(jnp.where(full, 1.0, 0.0), axis=1, keepdims=True)
-    place = jnp.where(shift > 0, pooled, side * cap + rank).astype(jnp.int32)
+    place = jnp.where(apart(shift), side * cap + rank.astype(jnp.int32), pooled.astype(jnp.int32))
     place = jnp.where(full, -1, place)
 
     in_block = jnp.where(iota((LANES, rows), 0) == block, 1.0, 0.0).astype(jnp.bfloat16)
@@ -158,17 +162,21 @@
     lane = iota((1, LANES), 1)
     head_shift = jnp.where(lane < chips, lane >> (across.bit_length() - 1), -1)
     head_side = lane & (across - 1)
-    head = jnp.where(head_shift > 0, pool - across + head_side, head_side * cap + cap - 1)
+    head = jnp.where(
+        apart(head_shift), head_side * cap + cap - 1, pool - across + head_side
+    )
     shift = jnp.concatenate([shift, head_shift], axis=1)
     place = jnp.concatenate([place, head], axis=1)
+    place = jnp.where(place >= 0, shift * PLACES + place, -1)
+    place_ref[...] = place
+    pool_ref[...] = pick_rows(place, size["first"] * PLACES, pool, aug_ref[...])
+
+
+def pack_kernel(starts, aug_ref, place_ref, *out_refs):
     aug = aug_ref[...]
-    for index in range(1, tiles):
-        out_refs[across + index - 1][...] = pick_rows(
-            jnp.where(shift == index, place, -1), 0, pool, aug
-        )
-    near = jnp.where(shift == 0, place, -1)
-    for index in range(across):
-        out_refs[index][...] = pick_rows(near, index * cap, cap, aug)
+    place = place_ref[...]
+    for start, out_ref in zip(starts, out_refs):
+        out_ref[...] = pick_rows(place, start, out_ref.shape[0], aug)
 
 
 def regroup_kernel(size, pool_ref, *out_refs):
@@ -403,43 +411,79 @@
     cap = up(room(rows, chips, 5.0) + 1, 8)
     pool = up(room(rows, tiles, 4.25) + across, ALIGN)
     space = up(room(rows, tiles, 4.75) + labels * (ALIGN - 4), ALIGN)
+    order = sorted(range(1, tiles), key=lambda shift: (-min(shift, tiles - shift), shift))
+    direct = order[-1]
     size = dict(
-        chips=chips, across=across, tiles=tiles, labels=labels, cap=cap, pool=pool, space=space
+        chips=chips, across=across, tiles=tiles, labels=labels, cap=cap, pool=pool, space=space,
+        first=order[0], direct=direct,
     )
     lanes = up(cap + 1, LANES)
     shape = jax.ShapeDtypeStruct
 
     ids_row = cluster_ids.reshape(1, rows)
-    *packed, rank = call(
-        functools.partial(pack_kernel, size),
-        "pack",
-        [shape((cap, width), jnp.bfloat16)] * across
-        + [shape((pool, width), jnp.bfloat16)] * (tiles - 1)
-        + [shape((1, rows), jnp.float32)],
+    first, aug, slots, rank = call(
+        functools.partial(plan_kernel, size),
+        "plan",
+        [
+            shape((pool, width), jnp.bfloat16),
+            shape((rows + LANES, width), jnp.bfloat16),
+            shape((1, rows + LANES), jnp.int32),
+            shape((1, rows), jnp.float32),
+        ],
         [embeddings, ids_row],
-        scratch_shapes=[pltpu.VMEM((rows + LANES, width), jnp.bfloat16)],
-    )
-    pools = {
-        shift: lax.ppermute(
-            packed[across + shift - 1], "tile", [(z, (z + shift) % tiles) for z in range(tiles)]
+    )
+
+    def pack(shift, count, step):
+        return call(
+            functools.partial(
+                pack_kernel, [shift * PLACES + index * step for index in range(count)]
+            ),
+            "pack",
+            [shape((step, width), jnp.bfloat16)] * count,
+            [aug, slots],
         )
-        for shift in sorted(range(1, tiles), key=lambda shift: -min(shift, tiles - shift))
-    }
+
+    def along(shift):
+        return [(z, (z + shift) % tiles) for z in range(tiles)]
+
+    def over(side):
+        return [(a, a ^ side) for a in range(across)]
+
+    near = pack(0, across, cap)
+    pools, last = {}, None
+    for shift in order[:-1]:
+        pool_rows = first if shift == order[0] else pack(shift, 1, pool)[0]
+        if last is not None:
+            pool_rows, _ = lax.optimization_barrier((pool_rows, last))
+        last = pools[shift] = lax.ppermute(pool_rows, "tile", along(shift))
+    far = pack(direct, across, cap)
+    if last is not None:
+        *far, _ = lax.optimization_barrier((*far, last))
+
     own, other, own_counts, other_counts, places = [], [], [], [], []
     swap = [(0, 1), (1, 0)]
     for shift in range(tiles):
-        blocks = packed[:across]
-        if shift:
-            blocks = call(
-                functools.partial(regroup_kernel, size),
-                "regroup",
-                [shape((cap, width), jnp.bfloat16)] * across,
-                [pools[shift]],
-            )
-        arrived = [blocks[0]] + [
-            lax.ppermute(blocks[side], "chip", [(a, a ^ side) for a in range(across)])
-            for side in range(1, across)
-        ]
+        if shift == direct:
+            arrived = [
+                lax.ppermute(
+                    far[side],
+                    ("chip", "tile"),
+                    [(a * tiles + z, b * tiles + y) for a, b in over(side) for z, y in along(shift)],
+                )
+                for side in range(across)
+            ]
+        else:
+            blocks = near
+            if shift:
+                blocks = call(
+                    functools.partial(regroup_kernel, size),
+                    "regroup",
+                    [shape((cap, width), jnp.bfloat16)] * across,
+                    [pools[shift]],
+                )
+            arrived = [blocks[0]] + [
+                lax.ppermute(blocks[side], "chip", over(side)) for side in range(1, across)
+            ]
         ordered, place, counts = call(
             functools.partial(sort_kernel, size),
             "sort",

time: 108 us -> 99.1 us (0.918)
  starting transfers between devices: 50.4 us -> 28.8 us
  waiting for transfers between devices: 32.4 us -> 45.3 us
    ppermute x15, waiting for transfers between devices: 20.9 us -> 34.5 us  [the longest x2 27 us: body(): last = pools[shift] = lax.ppermute(pool_rows, 'tile', along(shift))]
    ppermute x15, starting transfers between devices: 33.6 us -> 23 us  [the longest x9 11.8 us: body(): lax.ppermute(blocks[side], 'chip', over(side))]
    all_to_all x1, starting transfers between devices: 14.4 us -> 4.09 us  [body(): lax.all_to_all(totals, ('chip', 'tile'), split_axis=0, concat_axis=0, til...]
    pallas_call x10 -> x12, Pallas kernels: 23.8 us -> 22.8 us  [call(): pl.pallas_call(kernel, out_shape=out_shape, in_specs=[smem] * scalars + [...]
  transfers between devices with their start and end apart: 24 -> 24, of which waited for: 8 -> 11; matrix products, arithmetic and copies ran while one was open for 0% -> 0% of each run, Pallas kernels for 7% -> 10%
where the time goes in v4:
time: 99.1 us; the launch traced here: 98.4 us
  waiting for transfers between devices  45.3 us (46%)
  starting transfers between devices  28.8 us (29%)
  Pallas kernels  22.8 us (23%)
    ppermute x2, waiting for transfers between devices, body(): last = pools[shift] = lax.ppermute(pool_rows, 'tile', along(shift))  27 us
    pallas_call x12, Pallas kernels, call(): pl.pallas_call(kernel, out_shape=out_shape, in_specs=[smem] * scalars + [...  22.8 us
    ppermute x9, starting transfers between devices, body(): lax.ppermute(blocks[side], 'chip', over(side))  11.8 us
    all_to_all x1, waiting for transfers between devices, body(): lax.all_to_all(totals, ('chip', 'tile'), split_axis=0, concat_axis=0, til...  7.25 us
    ppermute x4, starting transfers between devices, body(): lax.ppermute(far[side], ('chip', 'tile'), [(a * tiles + z, b * tiles + y)...  6.37 us
    ppermute x9, waiting for transfers between devices, body(): lax.ppermute(blocks[side], 'chip', over(side))  5.74 us
    ppermute x2, starting transfers between devices, body(): last = pools[shift] = lax.ppermute(pool_rows, 'tile', along(shift))  4.82 us
    all_to_all x1, starting transfers between devices, body(): lax.all_to_all(totals, ('chip', 'tile'), split_axis=0, concat_axis=0, til...  4.09 us
  transfers between devices with their start and end apart: 24, of which 11 were waited for; matrix products, arithmetic and copies ran while one was open for 0% of the time, Pallas kernels for 10%

profile of v4, /device:TPU:0, one launch (start us, length us, event | category | flops | bytes accessed | tf_op | source)
XLA Modules:
  0.0 98.4 jit_solution(5415369363997686773)
XLA Ops:
  0.0 4.4 %plan.1 = (bf16[320,768]{1,0:T(8,128)(2,1)S(1)}, bf16[1152,768]{1,0:T(8,128)(2,1)S(1)}, s32[1,1152]{1,0:T(1,128)S(1)}, f32[1,1024]{1,0:T(1,128)S(1)}) custom-call(f32[1024,768]{1,0:T(8,128)} %emb_ref.1, s32[1,1024]{1,0:T(1,128)} %bitcast.74), custom_call_target="tpu_custom_call" | custom-call | tf_op jit(solution)/shard_map/plan/pallas_call | solution.py:395
  4.4 4.1 %collective-permute-start.5 = (bf16[320,768]{1,0:T(8,128)(2,1)S(1)}, bf16[320,768]{1,0:T(8,128)(2,1)S(1)}, u32[]{:S(2)}, u32[]{:S(2)}) collective-permute-start(bf16[320,768]{1,0:T(8,128)(2,1)S(1)} %get-tuple-element.312), channel_id=1, source_target_pairs={{0,2},{1,3},{2,0},{3,1},{4,6},{5,7},{6,4},{7,5},{8,10},{9,11},{10,... | collective-permute-start | bytes 1474568 | tf_op jit(solution)/shard_map/ppermute | solution.py:458
  9.4 20.9 %collective-permute-done.5.pool_ref = bf16[320,768]{1,0:T(8,128)(2,1)S(1)} collective-permute-done((bf16[320,768]{1,0:T(8,128)(2,1)S(1)}, bf16[320,768]{1,0:T(8,128)(2,1)S(1)}, u32[]{:S(2)}, u32[]{:S(2)}) %collective-permute-start.5) | collective-permute-done | bytes 491552 | tf_op jit(solution)/shard_map/ppermute | solution.py:458
  31.0 1.2 %pack.3 = (bf16[104,768]{1,0:T(8,128)(2,1)S(1)}, bf16[104,768]{1,0:T(8,128)(2,1)S(1)}, bf16[104,768]{1,0:T(8,128)(2,1)S(1)}, bf16[104,768]{1,0:T(8,128)(2,1)S(1)}) custom-call(bf16[1152,768]{1,0:T(8,128)(2,1)S(1)} %get-tuple-element.305.aug_ref, s32[1,1152]{1,0:T(1,128)S(1)} %get-tuple-element.306.place_ref), custom_call_target="tpu_custom_call" | custom-call | tf_op jit(solution)/shard_map/pack/pallas_call | solution.py:395
  32.2 1.6 %collective-permute-start.2 = (bf16[104,768]{1,0:T(8,128)(2,1)S(1)}, bf16[104,768]{1,0:T(8,128)(2,1)S(1)}, u32[]{:S(2)}, u32[]{:S(2)}) collective-permute-start(bf16[104,768]{1,0:T(8,128)(2,1)S(1)} %get-tuple-element.308), channel_id=1, source_target_pairs={{0,8},{8,0},{16,24},{24,16},{1,9},{9,1},{17,25},{25,17},{2,10},{10... | collective-permute-start | bytes 479240 | tf_op jit(solution)/shard_map/ppermute | solution.py:485
  33.7 1.5 %collective-permute-start.3 = (bf16[104,768]{1,0:T(8,128)(2,1)S(1)}, bf16[104,768]{1,0:T(8,128)(2,1)S(1)}, u32[]{:S(2)}, u32[]{:S(2)}) collective-permute-start(bf16[104,768]{1,0:T(8,128)(2,1)S(1)} %get-tuple-element.309), channel_id=1, source_target_pairs={{0,16},{8,24},{16,0},{24,8},{1,17},{9,25},{17,1},{25,9},{2,18},{10... | collective-permute-start | bytes 479240 | tf_op jit(solution)/shard_map/ppermute | solution.py:485
  36.4 1.6 %collective-permute-start.10 = (bf16[104,768]{1,0:T(8,128)(2,1)S(1)}, bf16[104,768]{1,0:T(8,128)(2,1)S(1)}, u32[]{:S(2)}, u32[]{:S(2)}) collective-permute-start(bf16[104,768]{1,0:T(8,128)(2,1)S(1)} %get-tuple-element.320), channel_id=1, source_target_pairs={{0,8},{8,0},{16,24},{24,16},{1,9},{9,1},{17,25},{25,17},{2,10},{10... | collective-permute-start | bytes 479240 | tf_op jit(solution)/shard_map/ppermute | solution.py:485
  38.0 1.2 %pack.5 = (bf16[104,768]{1,0:T(8,128)(2,1)S(1)}, bf16[104,768]{1,0:T(8,128)(2,1)S(1)}, bf16[104,768]{1,0:T(8,128)(2,1)S(1)}, bf16[104,768]{1,0:T(8,128)(2,1)S(1)}) custom-call(bf16[1152,768]{1,0:T(8,128)(2,1)S(1)} %get-tuple-element.305.aug_ref, s32[1,1152]{1,0:T(1,128)S(1)} %get-tuple-element.306.place_ref), custom_call_target="tpu_custom_call" | custom-call | tf_op jit(solution)/shard_map/pack/pallas_call | solution.py:395
  39.2 6.0 %collective-permute-done.6.pool_ref = bf16[320,768]{1,0:T(8,128)(2,1)S(1)} collective-permute-done((bf16[320,768]{1,0:T(8,128)(2,1)S(1)}, bf16[320,768]{1,0:T(8,128)(2,1)S(1)}, u32[]{:S(2)}, u32[]{:S(2)}) %collective-permute-start.6) | collective-permute-done | bytes 491552 | tf_op jit(solution)/shard_map/ppermute | solution.py:458
  45.2 1.5 %collective-permute-start.11 = (bf16[104,768]{1,0:T(8,128)(2,1)S(1)}, bf16[104,768]{1,0:T(8,128)(2,1)S(1)}, u32[]{:S(2)}, u32[]{:S(2)}) collective-permute-start(bf16[104,768]{1,0:T(8,128)(2,1)S(1)} %get-tuple-element.321), channel_id=1, source_target_pairs={{0,16},{8,24},{16,0},{24,8},{1,17},{9,25},{17,1},{25,9},{2,18},{10... | collective-permute-start | bytes 479240 | tf_op jit(solution)/shard_map/ppermute | solution.py:485
  46.8 1.4 %collective-permute-start.12 = (bf16[104,768]{1,0:T(8,128)(2,1)S(1)}, bf16[104,768]{1,0:T(8,128)(2,1)S(1)}, u32[]{:S(2)}, u32[]{:S(2)}) collective-permute-start(bf16[104,768]{1,0:T(8,128)(2,1)S(1)} %get-tuple-element.322), channel_id=1, source_target_pairs={{0,24},{8,16},{16,8},{24,0},{1,25},{9,17},{17,9},{25,1},{2,26},{10... | collective-permute-start | bytes 479240 | tf_op jit(solution)/shard_map/ppermute | solution.py:485
  48.2 1.7 %collective-permute-start.13 = (bf16[104,768]{1,0:T(8,128)(2,1)S(1)}, bf16[104,768]{1,0:T(8,128)(2,1)S(1)}, u32[]{:S(2)}, u32[]{:S(2)}) collective-permute-start(bf16[104,768]{1,0:T(8,128)(2,1)S(1)} %get-tuple-element.328), channel_id=1, source_target_pairs={{0,3},{1,0},{2,1},{3,2},{8,11},{9,8},{10,9},{11,10},{16,19},{17,16... | collective-permute-start | bytes 479240 | tf_op jit(solution)/shard_map/ppermute | solution.py:468
  51.7 2.2 %collective-permute-done.11.refs_2_ = bf16[104,768]{1,0:T(8,128)(2,1)S(1)} collective-permute-done((bf16[104,768]{1,0:T(8,128)(2,1)S(1)}, bf16[104,768]{1,0:T(8,128)(2,1)S(1)}, u32[]{:S(2)}, u32[]{:S(2)}) %collective-permute-start.11) | collective-permute-done | bytes 159776 | tf_op jit(solution)/shard_map/ppermute | solution.py:485
  53.9 3.5 %collective-permute-start.16 = (bf16[104,768]{1,0:T(8,128)(2,1)S(1)}, bf16[104,768]{1,0:T(8,128)(2,1)S(1)}, u32[]{:S(2)}, u32[]{:S(2)}) collective-permute-start(bf16[104,768]{1,0:T(8,128)(2,1)S(1)} %get-tuple-element.331), channel_id=1, source_target_pairs={{0,27},{1,24},{2,25},{3,26},{8,19},{9,16},{10,17},{11,18},{16,11},... | collective-permute-start | bytes 479240 | tf_op jit(solution)/shard_map/ppermute | solution.py:468
  58.6 2.6 %collective-permute-start.9 = (bf16[104,768]{1,0:T(8,128)(2,1)S(1)}, bf16[104,768]{1,0:T(8,128)(2,1)S(1)}, u32[]{:S(2)}, u32[]{:S(2)}) collective-permute-start(bf16[104,768]{1,0:T(8,128)(2,1)S(1)} %get-tuple-element.317), channel_id=1, source_target_pairs={{0,24},{8,16},{16,8},{24,0},{1,25},{9,17},{17,9},{25,1},{2,26},{10... | collective-permute-start | bytes 479240 | tf_op jit(solution)/shard_map/ppermute | solution.py:485
  61.2 1.2 %sort.4 = (bf16[464,768]{1,0:T(8,128)(2,1)S(1)}, s32[4,128]{1,0:T(4,128)S(1)}, s32[8,128]{1,0:T(8,128)S(1)}) custom-call(bf16[104,768]{1,0:T(8,128)(2,1)S(1)} %get-tuple-element.307.refs_0_, bf16[104,768]{1,0:T(8,128)(2,1)S(1)} %collective-permute-done.2.refs_1_, bf16[104,768]{1,0:T(8,128)(2,1)S(1)} %collective-permute-done.3.refs_2_, ...), custom_call_target="tpu_custom_call" | custom-call | tf_op jit(solution)/shard_map/sort/pallas_call | solution.py:395
  63.3 1.2 %sort.6 = (bf16[464,768]{1,0:T(8,128)(2,1)S(1)}, s32[4,128]{1,0:T(4,128)S(1)}, s32[8,128]{1,0:T(8,128)S(1)}) custom-call(bf16[104,768]{1,0:T(8,128)(2,1)S(1)} %get-tuple-element.319.refs_0_, bf16[104,768]{1,0:T(8,128)(2,1)S(1)} %collective-permute-done.10.refs_1_, bf16[104,768]{1,0:T(8,128)(2,1)S(1)} %collective-permute-done.11.refs_2_, ...), custom_call_target="tpu_custom_call" | custom-call | tf_op jit(solution)/shard_map/sort/pallas_call | solution.py:395
  65.5 1.2 %sort.7 = (bf16[464,768]{1,0:T(8,128)(2,1)S(1)}, s32[4,128]{1,0:T(4,128)S(1)}, s32[8,128]{1,0:T(8,128)S(1)}) custom-call(bf16[104,768]{1,0:T(8,128)(2,1)S(1)} %collective-permute-done.13.refs_0_, bf16[104,768]{1,0:T(8,128)(2,1)S(1)} %collective-permute-done.14.refs_1_, bf16[104,768]{1,0:T(8,128)(2,1)S(1)} %collective-permute-done.15.refs_2_, ...), custom_call_target="tpu_custom_call" | custom-call | tf_op jit(solution)/shard_map/sort/pallas_call | solution.py:395
  67.3 3.5 %collective-permute-done.8.refs_2_ = bf16[104,768]{1,0:T(8,128)(2,1)S(1)} collective-permute-done((bf16[104,768]{1,0:T(8,128)(2,1)S(1)}, bf16[104,768]{1,0:T(8,128)(2,1)S(1)}, u32[]{:S(2)}, u32[]{:S(2)}) %collective-permute-start.8) | collective-permute-done | bytes 159776 | tf_op jit(solution)/shard_map/ppermute | solution.py:485
  70.9 1.2 %sort.5 = (bf16[464,768]{1,0:T(8,128)(2,1)S(1)}, s32[4,128]{1,0:T(4,128)S(1)}, s32[8,128]{1,0:T(8,128)S(1)}) custom-call(bf16[104,768]{1,0:T(8,128)(2,1)S(1)} %get-tuple-element.314.refs_0_, bf16[104,768]{1,0:T(8,128)(2,1)S(1)} %collective-permute-done.7.refs_1_, bf16[104,768]{1,0:T(8,128)(2,1)S(1)} %collective-permute-done.8.refs_2_, ...), custom_call_target="tpu_custom_call" | custom-call | tf_op jit(solution)/shard_map/sort/pallas_call | solution.py:395
  72.7 1.7 %collective-permute-done.17.refs_4_ = s32[8,128]{1,0:T(8,128)S(1)} collective-permute-done((s32[8,128]{1,0:T(8,128)S(1)}, s32[8,128]{1,0:T(8,128)S(1)}, u32[]{:S(2)}, u32[]{:S(2)}) %collective-permute-start.17) | collective-permute-done | bytes 4128 | tf_op jit(solution)/shard_map/ppermute | solution.py:501
  76.9 7.8 %score.1 = f32[16,128]{1,0:T(8,128)} custom-call(s32[8,128]{1,0:T(8,128)S(1)} %get-tuple-element.311.refs_0_, s32[8,128]{1,0:T(8,128)S(1)} %get-tuple-element.318.refs_1_, s32[8,128]{1,0:T(8,128)S(1)} %get-tuple-element.323.refs_2_, s32[8,128]{1,0:T(8,128)S(1)} %get-tuple-element.332.refs_3_, s32[8,128]{1,0:T(8,128)S(1)} %collective-permute-done.17.refs_4_, ...), custom_call_target="tpu_custom_call" | custom-call | tf_op jit(solution)/shard_map/score/pallas_call | solution.py:395
  84.7 4.1 %all-to-all-start.3 = ((f32[16,1,128]{2,1,0:T(1,128)}), f32[16,1,128]{2,1,0:T(1,128)S(1)}, u32[]{:S(2)}, u32[]{:S(2)}) async-start(f32[16,1,128]{2,1,0:T(1,128)} %bitcast.14), calls=%async_computation.3 | async-start | bytes 16384 | tf_op jit(solution)/shard_map/all_to_all | solution.py:516
  88.8 7.3 %all-to-all-done.3 = f32[16,1,128]{2,1,0:T(1,128)S(1)} async-done(((f32[16,1,128]{2,1,0:T(1,128)}), f32[16,1,128]{2,1,0:T(1,128)S(1)}, u32[]{:S(2)}, u32[]{:S(2)}) %all-to-all-start.3) | async-done | bytes 8224 | tf_op jit(solution)/shard_map/all_to_all | solution.py:516
  (42 shorter events, 12.7 us)
Async XLA Ops:
  4.4 25.9 %collective-permute-start.5 = (bf16[320,768]{1,0:T(8,128)(2,1)S(1)}, bf16[320,768]{1,0:T(8,128)(2,1)S(1)}, u32[]{:S(2)}, u32[]{:S(2)}) collective-permute-start(bf16[320,768]{1,0:T(8,128)(2,1)S(1)} %get-tuple-element.312), channel_id=1, source_target_pairs={{0,2},{1,3},{2,0},{3,1},{4,6},{5,7},{6,4},{7,5},{8,10},{9,11},{10,... | collective-permute-start | bytes 1474568 | tf_op jit(solution)/shard_map/ppermute | solution.py:458
  30.3 14.9 %collective-permute-start.6 = (bf16[320,768]{1,0:T(8,128)(2,1)S(1)}, bf16[320,768]{1,0:T(8,128)(2,1)S(1)}, u32[]{:S(2)}, u32[]{:S(2)}) collective-permute-start(bf16[320,768]{1,0:T(8,128)(2,1)S(1)} %pack.4), channel_id=1, source_target_pairs={{0,1},{1,2},{2,3},{3,0},{4,5},{5,6},{6,7},{7,4},{8,9},{9,10},{10,1... | collective-permute-start | bytes 1474568 | tf_op jit(solution)/shard_map/ppermute | solution.py:458
  32.2 14.6 %collective-permute-start.2 = (bf16[104,768]{1,0:T(8,128)(2,1)S(1)}, bf16[104,768]{1,0:T(8,128)(2,1)S(1)}, u32[]{:S(2)}, u32[]{:S(2)}) collective-permute-start(bf16[104,768]{1,0:T(8,128)(2,1)S(1)} %get-tuple-element.308), channel_id=1, source_target_pairs={{0,8},{8,0},{16,24},{24,16},{1,9},{9,1},{17,25},{25,17},{2,10},{10... | collective-permute-start | bytes 479240 | tf_op jit(solution)/shard_map/ppermute | solution.py:485
  33.7 14.4 %collective-permute-start.3 = (bf16[104,768]{1,0:T(8,128)(2,1)S(1)}, bf16[104,768]{1,0:T(8,128)(2,1)S(1)}, u32[]{:S(2)}, u32[]{:S(2)}) collective-permute-start(bf16[104,768]{1,0:T(8,128)(2,1)S(1)} %get-tuple-element.309), channel_id=1, source_target_pairs={{0,16},{8,24},{16,0},{24,8},{1,17},{9,25},{17,1},{25,9},{2,18},{10... | collective-permute-start | bytes 479240 | tf_op jit(solution)/shard_map/ppermute | solution.py:485
  35.3 14.7 %collective-permute-start.4 = (bf16[104,768]{1,0:T(8,128)(2,1)S(1)}, bf16[104,768]{1,0:T(8,128)(2,1)S(1)}, u32[]{:S(2)}, u32[]{:S(2)}) collective-permute-start(bf16[104,768]{1,0:T(8,128)(2,1)S(1)} %get-tuple-element.310), channel_id=1, source_target_pairs={{0,24},{8,16},{16,8},{24,0},{1,25},{9,17},{17,9},{25,1},{2,26},{10... | collective-permute-start | bytes 479240 | tf_op jit(solution)/shard_map/ppermute | solution.py:485
  36.4 13.5 %collective-permute-start.10 = (bf16[104,768]{1,0:T(8,128)(2,1)S(1)}, bf16[104,768]{1,0:T(8,128)(2,1)S(1)}, u32[]{:S(2)}, u32[]{:S(2)}) collective-permute-start(bf16[104,768]{1,0:T(8,128)(2,1)S(1)} %get-tuple-element.320), channel_id=1, source_target_pairs={{0,8},{8,0},{16,24},{24,16},{1,9},{9,1},{17,25},{25,17},{2,10},{10... | collective-permute-start | bytes 479240 | tf_op jit(solution)/shard_map/ppermute | solution.py:485
  45.2 8.7 %collective-permute-start.11 = (bf16[104,768]{1,0:T(8,128)(2,1)S(1)}, bf16[104,768]{1,0:T(8,128)(2,1)S(1)}, u32[]{:S(2)}, u32[]{:S(2)}) collective-permute-start(bf16[104,768]{1,0:T(8,128)(2,1)S(1)} %get-tuple-element.321), channel_id=1, source_target_pairs={{0,16},{8,24},{16,0},{24,8},{1,17},{9,25},{17,1},{25,9},{2,18},{10... | collective-permute-start | bytes 479240 | tf_op jit(solution)/shard_map/ppermute | solution.py:485
  46.8 10.7 %collective-permute-start.12 = (bf16[104,768]{1,0:T(8,128)(2,1)S(1)}, bf16[104,768]{1,0:T(8,128)(2,1)S(1)}, u32[]{:S(2)}, u32[]{:S(2)}) collective-permute-start(bf16[104,768]{1,0:T(8,128)(2,1)S(1)} %get-tuple-element.322), channel_id=1, source_target_pairs={{0,24},{8,16},{16,8},{24,0},{1,25},{9,17},{17,9},{25,1},{2,26},{10... | collective-permute-start | bytes 479240 | tf_op jit(solution)/shard_map/ppermute | solution.py:485
  48.2 9.8 %collective-permute-start.13 = (bf16[104,768]{1,0:T(8,128)(2,1)S(1)}, bf16[104,768]{1,0:T(8,128)(2,1)S(1)}, u32[]{:S(2)}, u32[]{:S(2)}) collective-permute-start(bf16[104,768]{1,0:T(8,128)(2,1)S(1)} %get-tuple-element.328), channel_id=1, source_target_pairs={{0,3},{1,0},{2,1},{3,2},{8,11},{9,8},{10,9},{11,10},{16,19},{17,16... | collective-permute-start | bytes 479240 | tf_op jit(solution)/shard_map/ppermute | solution.py:468
  49.9 8.7 %collective-permute-start.14 = (bf16[104,768]{1,0:T(8,128)(2,1)S(1)}, bf16[104,768]{1,0:T(8,128)(2,1)S(1)}, u32[]{:S(2)}, u32[]{:S(2)}) collective-permute-start(bf16[104,768]{1,0:T(8,128)(2,1)S(1)} %get-tuple-element.329), channel_id=1, source_target_pairs={{0,11},{1,8},{2,9},{3,10},{8,3},{9,0},{10,1},{11,2},{16,27},{17,24... | collective-permute-start | bytes 479240 | tf_op jit(solution)/shard_map/ppermute | solution.py:468
  50.0 13.4 %collective-permute-start.15 = (bf16[104,768]{1,0:T(8,128)(2,1)S(1)}, bf16[104,768]{1,0:T(8,128)(2,1)S(1)}, u32[]{:S(2)}, u32[]{:S(2)}) collective-permute-start(bf16[104,768]{1,0:T(8,128)(2,1)S(1)} %get-tuple-element.330), channel_id=1, source_target_pairs={{0,19},{1,16},{2,17},{3,18},{8,27},{9,24},{10,25},{11,26},{16,3},{... | collective-permute-start | bytes 479240 | tf_op jit(solution)/shard_map/ppermute | solution.py:468
  53.9 11.6 %collective-permute-start.16 = (bf16[104,768]{1,0:T(8,128)(2,1)S(1)}, bf16[104,768]{1,0:T(8,128)(2,1)S(1)}, u32[]{:S(2)}, u32[]{:S(2)}) collective-permute-start(bf16[104,768]{1,0:T(8,128)(2,1)S(1)} %get-tuple-element.331), channel_id=1, source_target_pairs={{0,27},{1,24},{2,25},{3,26},{8,19},{9,16},{10,17},{11,18},{16,11},... | collective-permute-start | bytes 479240 | tf_op jit(solution)/shard_map/ppermute | solution.py:468
  57.5 9.3 %collective-permute-start.7 = (bf16[104,768]{1,0:T(8,128)(2,1)S(1)}, bf16[104,768]{1,0:T(8,128)(2,1)S(1)}, u32[]{:S(2)}, u32[]{:S(2)}) collective-permute-start(bf16[104,768]{1,0:T(8,128)(2,1)S(1)} %get-tuple-element.315), channel_id=1, source_target_pairs={{0,8},{8,0},{16,24},{24,16},{1,9},{9,1},{17,25},{25,17},{2,10},{10... | collective-permute-start | bytes 479240 | tf_op jit(solution)/shard_map/ppermute | solution.py:485
  58.0 12.8 %collective-permute-start.8 = (bf16[104,768]{1,0:T(8,128)(2,1)S(1)}, bf16[104,768]{1,0:T(8,128)(2,1)S(1)}, u32[]{:S(2)}, u32[]{:S(2)}) collective-permute-start(bf16[104,768]{1,0:T(8,128)(2,1)S(1)} %get-tuple-element.316), channel_id=1, source_target_pairs={{0,16},{8,24},{16,0},{24,8},{1,17},{9,25},{17,1},{25,9},{2,18},{10... | collective-permute-start | bytes 479240 | tf_op jit(solution)/shard_map/ppermute | solution.py:485
  58.6 12.2 %collective-permute-start.9 = (bf16[104,768]{1,0:T(8,128)(2,1)S(1)}, bf16[104,768]{1,0:T(8,128)(2,1)S(1)}, u32[]{:S(2)}, u32[]{:S(2)}) collective-permute-start(bf16[104,768]{1,0:T(8,128)(2,1)S(1)} %get-tuple-element.317), channel_id=1, source_target_pairs={{0,24},{8,16},{16,8},{24,0},{1,25},{9,17},{17,9},{25,1},{2,26},{10... | collective-permute-start | bytes 479240 | tf_op jit(solution)/shard_map/ppermute | solution.py:485
  63.3 12.4 %collective-permute-start.21 = (bf16[464,768]{1,0:T(8,128)(2,1)S(1)}, bf16[464,768]{1,0:T(8,128)(2,1)S(1)}, u32[]{:S(2)}, u32[]{:S(2)}) collective-permute-start(bf16[464,768]{1,0:T(8,128)(2,1)S(1)} %get-tuple-element.333.refs_8_), channel_id=1, source_target_pairs={{0,4},{4,0},{1,5},{5,1},{2,6},{6,2},{3,7},{7,3},{8,12},{12,8},{9,1... | collective-permute-start | bytes 2138120 | tf_op jit(solution)/shard_map/ppermute | solution.py:502
  65.5 11.4 %collective-permute-start.23 = (bf16[464,768]{1,0:T(8,128)(2,1)S(1)}, bf16[464,768]{1,0:T(8,128)(2,1)S(1)}, u32[]{:S(2)}, u32[]{:S(2)}) collective-permute-start(bf16[464,768]{1,0:T(8,128)(2,1)S(1)} %get-tuple-element.335.refs_10_), channel_id=1, source_target_pairs={{0,4},{4,0},{1,5},{5,1},{2,6},{6,2},{3,7},{7,3},{8,12},{12,8},{9,1... | collective-permute-start | bytes 2138120 | tf_op jit(solution)/shard_map/ppermute | solution.py:502
  66.8 10.1 %collective-permute-start.24 = (bf16[464,768]{1,0:T(8,128)(2,1)S(1)}, bf16[464,768]{1,0:T(8,128)(2,1)S(1)}, u32[]{:S(2)}, u32[]{:S(2)}) collective-permute-start(bf16[464,768]{1,0:T(8,128)(2,1)S(1)} %get-tuple-element.336.refs_11_), channel_id=1, source_target_pairs={{0,4},{4,0},{1,5},{5,1},{2,6},{6,2},{3,7},{7,3},{8,12},{12,8},{9,1... | collective-permute-start | bytes 2138120 | tf_op jit(solution)/shard_map/ppermute | solution.py:502
  72.1 4.8 %collective-permute-start.22 = (bf16[464,768]{1,0:T(8,128)(2,1)S(1)}, bf16[464,768]{1,0:T(8,128)(2,1)S(1)}, u32[]{:S(2)}, u32[]{:S(2)}) collective-permute-start(bf16[464,768]{1,0:T(8,128)(2,1)S(1)} %get-tuple-element.334.refs_9_), channel_id=1, source_target_pairs={{0,4},{4,0},{1,5},{5,1},{2,6},{6,2},{3,7},{7,3},{8,12},{12,8},{9,1... | collective-permute-start | bytes 2138120 | tf_op jit(solution)/shard_map/ppermute | solution.py:502
  72.2 2.2 %collective-permute-start.17 = (s32[8,128]{1,0:T(8,128)S(1)}, s32[8,128]{1,0:T(8,128)S(1)}, u32[]{:S(2)}, u32[]{:S(2)}) collective-permute-start(s32[8,128]{1,0:T(8,128)S(1)} %get-tuple-element.311.refs_0_), channel_id=1, source_target_pairs={{0,4},{4,0},{1,5},{5,1},{2,6},{6,2},{3,7},{7,3},{8,12},{12,8},{9,1... | collective-permute-start | bytes 12296 | tf_op jit(solution)/shard_map/ppermute | solution.py:501
  74.4 1.2 %collective-permute-start.19 = (s32[8,128]{1,0:T(8,128)S(1)}, s32[8,128]{1,0:T(8,128)S(1)}, u32[]{:S(2)}, u32[]{:S(2)}) collective-permute-start(s32[8,128]{1,0:T(8,128)S(1)} %get-tuple-element.323.refs_2_), channel_id=1, source_target_pairs={{0,4},{4,0},{1,5},{5,1},{2,6},{6,2},{3,7},{7,3},{8,12},{12,8},{9,1... | collective-permute-start | bytes 12296 | tf_op jit(solution)/shard_map/ppermute | solution.py:501
  75.5 1.2 %collective-permute-start.18 = (s32[8,128]{1,0:T(8,128)S(1)}, s32[8,128]{1,0:T(8,128)S(1)}, u32[]{:S(2)}, u32[]{:S(2)}) collective-permute-start(s32[8,128]{1,0:T(8,128)S(1)} %get-tuple-element.318.refs_1_), channel_id=1, source_target_pairs={{0,4},{4,0},{1,5},{5,1},{2,6},{6,2},{3,7},{7,3},{8,12},{12,8},{9,1... | collective-permute-start | bytes 12296 | tf_op jit(solution)/shard_map/ppermute | solution.py:501
  75.7 1.2 %collective-permute-start.20 = (s32[8,128]{1,0:T(8,128)S(1)}, s32[8,128]{1,0:T(8,128)S(1)}, u32[]{:S(2)}, u32[]{:S(2)}) collective-permute-start(s32[8,128]{1,0:T(8,128)S(1)} %get-tuple-element.332.refs_3_), channel_id=1, source_target_pairs={{0,4},{4,0},{1,5},{5,1},{2,6},{6,2},{3,7},{7,3},{8,12},{12,8},{9,1... | collective-permute-start | bytes 12296 | tf_op jit(solution)/shard_map/ppermute | solution.py:501
  84.7 11.4 %all-to-all-start.3 = ((f32[16,1,128]{2,1,0:T(1,128)}), f32[16,1,128]{2,1,0:T(1,128)S(1)}, u32[]{:S(2)}, u32[]{:S(2)}) async-start(f32[16,1,128]{2,1,0:T(1,128)} %bitcast.14), calls=%async_computation.3 | async-start | bytes 16384 | tf_op jit(solution)/shard_map/all_to_all | solution.py:516
  (2 other events, 52.6 us)

commit v5 on v4

--- a/solution.py
+++ b/solution.py
@@ -18,6 +18,7 @@
 VMEM_BYTES = 48 * 1024 * 1024
 LANES = 128
 FLAG = LANES - 1
+LOW = LANES // 2
 ALIGN = 16
 STEP = 32
 LEFT = 192
@@ -115,7 +116,7 @@
 def plan_kernel(size, emb_ref, ids_ref, pool_ref, aug_ref, place_ref, rank_ref):
     rows, width = emb_ref.shape
     chips, labels, cap, pool = size["chips"], size["labels"], size["cap"], size["pool"]
-    across, tiles, direct = size["across"], size["tiles"], size["direct"]
+    across, tiles = size["across"], size["tiles"]
     chunk = 256
     for start in range(0, rows, chunk):
         x = emb_ref[start : start + chunk, :]
@@ -144,7 +145,7 @@
     pooled = jnp.concatenate(pooled, axis=1)
 
     def apart(shift):
-        return (shift == 0) | (shift == direct)
+        return shift != size["first"]
 
     full = (rank >= cap - 1) | (~apart(shift) & (pooled >= pool - across))
     over = jnp.max(jnp.where(full, 1.0, 0.0), axis=1, keepdims=True)
@@ -199,7 +200,7 @@
 
 def sort_kernel(size, *refs):
     across, labels, cap, space = size["across"], size["labels"], size["cap"], size["space"]
-    block_refs, (out_ref, place_ref, counts_ref, rows_ref) = refs[:across], refs[across:]
+    block_refs, (out_ref, place_ref, rows_ref) = refs[:across], refs[across:]
     held = up(cap, ALIGN)
     total = across * held
     for index, ref in enumerate(block_refs):
@@ -228,11 +229,12 @@
         in_block = in_block + own
         table.append(in_block)
         count = jnp.sum(own, axis=1, keepdims=True)
-        found = jnp.where(lane == label, count, found)
+        high = jnp.floor(count * (1.0 / LANES))
+        found = jnp.where(lane == label, high, found)
+        found = jnp.where(lane == LOW + label, count - high * LANES, found)
         begin = begin + jnp.floor((count + (ALIGN - 1)) * (1.0 / ALIGN)) * ALIGN
     flag = jnp.maximum(flag, jnp.where(begin > space, 1.0, 0.0))
     found = jnp.where(lane == FLAG, flag, found)
-    counts_ref[...] = jnp.broadcast_to(found, counts_ref.shape).astype(jnp.int32)
     table.append((lane * held).astype(jnp.float32))
     table.extend([jnp.zeros((1, LANES), jnp.float32)] * (up(len(table), 8) - len(table)))
     table = jnp.concatenate(table, axis=0)
@@ -256,6 +258,9 @@
         place_ref[index : index + 1, :] = places(only, lambda where: rank_row)
 
     out_ref[space:, :] = jnp.zeros((STEP, out_ref.shape[1]), jnp.bfloat16)
+    out_ref[space : space + ALIGN, 0:LANES] = jnp.broadcast_to(found, (ALIGN, LANES)).astype(
+        jnp.bfloat16
+    )
     for start in range(0, space, ALIGN * 9):
         count = min(ALIGN * 9, space - start)
         out_ref[start : start + count, :] = pick_rows(place, start, count, rows)
@@ -264,16 +269,17 @@
 def score_kernel(size, *refs):
     across, tiles, labels, space = size["across"], size["tiles"], size["labels"], size["space"]
     pieces = 2 * tiles
-    counts_refs, piece_refs, place_refs = (
-        refs[:pieces],
-        refs[pieces : 2 * pieces],
-        refs[2 * pieces : 2 * pieces + tiles],
-    )
-    out_ref, rows_ref, total_ref, back_ref = refs[2 * pieces + tiles :]
+    piece_refs, place_refs = refs[:pieces], refs[pieces : pieces + tiles]
+    out_ref, rows_ref, total_ref, back_ref, heads_ref, counts_ref, sem = refs[pieces + tiles :]
     lane = iota((1, LANES), 1)
+    heads = [ref[space : space + ALIGN, 0:LANES].astype(jnp.float32)[0:1, :] for ref in piece_refs]
+    heads_ref[...] = jnp.concatenate(heads, axis=0).astype(jnp.int32)
+    copy = pltpu.make_async_copy(heads_ref, counts_ref, sem)
+    copy.start()
+    copy.wait()
     flag = jnp.int32(0)
-    for ref in counts_refs:
-        flag = jnp.maximum(flag, ref[0, FLAG])
+    for index in range(pieces):
+        flag = jnp.maximum(flag, counts_ref[index, FLAG])
 
     def aligned(count):
         return (count + (ALIGN - 1)) & -ALIGN
@@ -287,7 +293,8 @@
         places.append([])
         for index in range(pieces):
             free = space - source[index]
-            count = jnp.clip(counts_refs[index][0, label], 0, free)
+            count = counts_ref[index, label] * LANES + counts_ref[index, LOW + label]
+            count = jnp.clip(count, 0, free)
             counts[label].append(count)
             places[label].append((source[index], begin))
             src, dst = source[index], begin
@@ -389,13 +396,12 @@
     out_ref[...] = jnp.log(1.0 + total)
 
 
-def call(kernel, name, out_shape, inputs, scalars=0, **options):
+def call(kernel, name, out_shape, inputs, **options):
     vmem = pl.BlockSpec(memory_space=pltpu.VMEM)
-    smem = pl.BlockSpec(memory_space=pltpu.SMEM)
     return pl.pallas_call(
         kernel,
         out_shape=out_shape,
-        in_specs=[smem] * scalars + [vmem] * (len(inputs) - scalars),
+        in_specs=[vmem] * len(inputs),
         out_specs=jax.tree.map(lambda _: vmem, out_shape),
         compiler_params=pltpu.CompilerParams(vmem_limit_bytes=VMEM_BYTES),
         name=name,
@@ -412,10 +418,9 @@
     pool = up(room(rows, tiles, 4.25) + across, ALIGN)
     space = up(room(rows, tiles, 4.75) + labels * (ALIGN - 4), ALIGN)
     order = sorted(range(1, tiles), key=lambda shift: (-min(shift, tiles - shift), shift))
-    direct = order[-1]
     size = dict(
         chips=chips, across=across, tiles=tiles, labels=labels, cap=cap, pool=pool, space=space,
-        first=order[0], direct=direct,
+        first=order[0],
     )
     lanes = up(cap + 1, LANES)
     shape = jax.ShapeDtypeStruct
@@ -449,68 +454,75 @@
     def over(side):
         return [(a, a ^ side) for a in range(across)]
 
-    near = pack(0, across, cap)
-    pools, last = {}, None
-    for shift in order[:-1]:
-        pool_rows = first if shift == order[0] else pack(shift, 1, pool)[0]
-        if last is not None:
-            pool_rows, _ = lax.optimization_barrier((pool_rows, last))
-        last = pools[shift] = lax.ppermute(pool_rows, "tile", along(shift))
-    far = pack(direct, across, cap)
-    if last is not None:
-        *far, _ = lax.optimization_barrier((*far, last))
-
-    own, other, own_counts, other_counts, places = [], [], [], [], []
+    def after(value, *others):
+        return lax.optimization_barrier((value, others))[0]
+
+    def send_across(blocks):
+        return [blocks[0]] + [
+            lax.ppermute(blocks[side], "chip", over(side)) for side in range(1, across)
+        ]
+
+    def send_far(blocks, shift, side):
+        route = [(a * tiles + z, b * tiles + y) for a, b in over(side) for z, y in along(shift)]
+        return lax.ppermute(blocks[side], ("chip", "tile"), route)
+
     swap = [(0, 1), (1, 0)]
-    for shift in range(tiles):
-        if shift == direct:
-            arrived = [
-                lax.ppermute(
-                    far[side],
-                    ("chip", "tile"),
-                    [(a * tiles + z, b * tiles + y) for a, b in over(side) for z, y in along(shift)],
-                )
-                for side in range(across)
-            ]
-        else:
-            blocks = near
-            if shift:
-                blocks = call(
-                    functools.partial(regroup_kernel, size),
-                    "regroup",
-                    [shape((cap, width), jnp.bfloat16)] * across,
-                    [pools[shift]],
-                )
-            arrived = [blocks[0]] + [
-                lax.ppermute(blocks[side], "chip", over(side)) for side in range(1, across)
-            ]
-        ordered, place, counts = call(
+    own, other, places = {}, {}, {}
+
+    def finish(shift, arrived):
+        own[shift], places[shift] = call(
             functools.partial(sort_kernel, size),
             "sort",
             [
                 shape((space + STEP, width), jnp.bfloat16),
                 shape((across, lanes), jnp.int32),
-                shape((8, LANES), jnp.int32),
             ],
             arrived,
             scratch_shapes=[pltpu.VMEM((across * up(cap, ALIGN), width), jnp.bfloat16)],
         )
-        own.append(ordered)
-        places.append(place)
-        own_counts.append(counts)
-        other_counts.append(lax.ppermute(counts, "core", swap))
-        other.append(lax.ppermute(ordered, "core", swap))
+        other[shift] = lax.ppermute(own[shift], "core", swap)
+
+    pooled = lax.ppermute(first, "tile", along(order[0]))
+    before = []
+    for shift in order[1:-1]:
+        blocks = pack(shift, across, cap)
+        arrived = [send_far(blocks, shift, side) for side in range(across)]
+        finish(shift, arrived)
+        before += arrived
+    near = send_across(pack(0, across, cap))
+    finish(0, near)
+    before += near
+    arrived = []
+    if len(order) > 1:
+        blocks = after(pack(order[-1], across, cap), *near)
+        arrived = [send_far(blocks, order[-1], 0)]
+        blocks = after(blocks, pooled, *arrived)
+    regrouped = call(
+        functools.partial(regroup_kernel, size),
+        "regroup",
+        [shape((cap, width), jnp.bfloat16)] * across,
+        [after(pooled, *before, *arrived)],
+    )
+    finish(order[0], send_across(regrouped))
+    if len(order) > 1:
+        arrived += [send_far(blocks, order[-1], side) for side in range(1, across)]
+        finish(order[-1], arrived)
+    own, other, places = (
+        [found[shift] for shift in range(tiles)] for found in (own, other, places)
+    )
     room_all = 2 * tiles * space + RIGHT
     totals = call(
         functools.partial(score_kernel, size),
         "score",
         shape((chips, lanes), jnp.float32),
-        [*own_counts, *other_counts, *own, *other, *places],
-        scalars=2 * tiles,
+        [*own, *other, *places],
         scratch_shapes=[
             pltpu.VMEM((room_all, width), jnp.bfloat16),
             pltpu.VMEM((room_all, LANES), jnp.float32),
             pltpu.VMEM((tiles, space + STEP, LANES), jnp.float32),
+            pltpu.VMEM((2 * tiles, LANES), jnp.int32),
+            pltpu.SMEM((2 * tiles, LANES), jnp.int32),
+            pltpu.SemaphoreType.DMA,
         ],
     )
     returned = lax.all_to_all(totals, ("chip", "tile"), split_axis=0, concat_axis=0, tiled=True)

time: 99.1 us -> 96 us (0.969)
  starting transfers between devices: 28.8 us -> 26.1 us
    ppermute x23 -> x19, starting transfers between devices: 24.7 us -> 21.7 us  [the longest x8 9.81 us: send_far(): return lax.ppermute(blocks[side], ('chip', 'tile'), route)]
    pallas_call x12 -> x11, Pallas kernels: 22.8 us -> 21.9 us  [call(): pl.pallas_call(kernel, out_shape=out_shape, in_specs=[vmem] * len(inputs)...]
    ppermute x23 -> x19, waiting for transfers between devices: 38.1 us -> 38.2 us  [the longest x8 27.3 us: send_far(): return lax.ppermute(blocks[side], ('chip', 'tile'), route)]
  transfers between devices with their start and end apart: 24 -> 20, of which waited for: 11 -> 9; matrix products, arithmetic and copies ran while one was open for 0% -> 0% of each run, Pallas kernels for 10% -> 10%
where the time goes in v5:
time: 96 us; the launch traced here: 94.9 us
  waiting for transfers between devices  45.4 us (47%)
  starting transfers between devices  26.1 us (27%)
  Pallas kernels  21.9 us (23%)
    ppermute x8, waiting for transfers between devices, send_far(): return lax.ppermute(blocks[side], ('chip', 'tile'), route)  27.3 us
    pallas_call x11, Pallas kernels, call(): pl.pallas_call(kernel, out_shape=out_shape, in_specs=[vmem] * len(inputs)...  21.9 us
    ppermute x8, starting transfers between devices, send_far(): return lax.ppermute(blocks[side], ('chip', 'tile'), route)  9.81 us
    ppermute x6, waiting for transfers between devices, send_across(): lax.ppermute(blocks[side], 'chip', over(side))  8.71 us
    all_to_all x1, waiting for transfers between devices, body(): lax.all_to_all(totals, ('chip', 'tile'), split_axis=0, concat_axis=0, til...  7.26 us
    ppermute x6, starting transfers between devices, send_across(): lax.ppermute(blocks[side], 'chip', over(side))  7.11 us
    all_to_all x1, starting transfers between devices, body(): lax.all_to_all(totals, ('chip', 'tile'), split_axis=0, concat_axis=0, til...  4.47 us
    ppermute x1, starting transfers between devices, body(): pooled = lax.ppermute(first, 'tile', along(order[0]))  4.1 us
  transfers between devices with their start and end apart: 20, of which 9 were waited for; matrix products, arithmetic and copies ran while one was open for 0% of the time, Pallas kernels for 10%

profile of v5, /device:TPU:0, one launch (start us, length us, event | category | flops | bytes accessed | tf_op | source)
XLA Modules:
  0.0 94.9 jit_solution(9260577934371319551)
XLA Ops:
  0.0 4.4 %plan.1 = (bf16[320,768]{1,0:T(8,128)(2,1)S(1)}, bf16[1152,768]{1,0:T(8,128)(2,1)S(1)}, s32[1,1152]{1,0:T(1,128)S(1)}, f32[1,1024]{1,0:T(1,128)S(1)}) custom-call(f32[1024,768]{1,0:T(8,128)} %emb_ref.1, s32[1,1024]{1,0:T(1,128)} %bitcast.74), custom_call_target="tpu_custom_call" | custom-call | tf_op jit(solution)/shard_map/plan/pallas_call | solution.py:401
  4.4 4.1 %collective-permute-start.9 = (bf16[320,768]{1,0:T(8,128)(2,1)S(1)}, bf16[320,768]{1,0:T(8,128)(2,1)S(1)}, u32[]{:S(2)}, u32[]{:S(2)}) collective-permute-start(bf16[320,768]{1,0:T(8,128)(2,1)S(1)} %get-tuple-element.316), channel_id=1, source_target_pairs={{0,2},{1,3},{2,0},{3,1},{4,6},{5,7},{6,4},{7,5},{8,10},{9,11},{10,... | collective-permute-start | bytes 1474568 | tf_op jit(solution)/shard_map/ppermute | solution.py:485
  9.7 1.6 %collective-permute-start.2 = (bf16[104,768]{1,0:T(8,128)(2,1)S(1)}, bf16[104,768]{1,0:T(8,128)(2,1)S(1)}, u32[]{:S(2)}, u32[]{:S(2)}) collective-permute-start(bf16[104,768]{1,0:T(8,128)(2,1)S(1)} %get-tuple-element.307), channel_id=1, source_target_pairs={{0,8},{8,0},{16,24},{24,16},{1,9},{9,1},{17,25},{25,17},{2,10},{10... | collective-permute-start | bytes 479240 | tf_op jit(solution)/shard_map/ppermute | solution.py:462
  11.3 1.5 %collective-permute-start.3 = (bf16[104,768]{1,0:T(8,128)(2,1)S(1)}, bf16[104,768]{1,0:T(8,128)(2,1)S(1)}, u32[]{:S(2)}, u32[]{:S(2)}) collective-permute-start(bf16[104,768]{1,0:T(8,128)(2,1)S(1)} %get-tuple-element.308), channel_id=1, source_target_pairs={{0,16},{8,24},{16,0},{24,8},{1,17},{9,25},{17,1},{25,9},{2,18},{10... | collective-permute-start | bytes 479240 | tf_op jit(solution)/shard_map/ppermute | solution.py:462
  14.4 1.9 %collective-permute-done.2.refs_1_ = bf16[104,768]{1,0:T(8,128)(2,1)S(1)} collective-permute-done((bf16[104,768]{1,0:T(8,128)(2,1)S(1)}, bf16[104,768]{1,0:T(8,128)(2,1)S(1)}, u32[]{:S(2)}, u32[]{:S(2)}) %collective-permute-start.2) | collective-permute-done | bytes 159776 | tf_op jit(solution)/shard_map/ppermute | solution.py:462
  16.4 3.6 %collective-permute-done.3.refs_2_ = bf16[104,768]{1,0:T(8,128)(2,1)S(1)} collective-permute-done((bf16[104,768]{1,0:T(8,128)(2,1)S(1)}, bf16[104,768]{1,0:T(8,128)(2,1)S(1)}, u32[]{:S(2)}, u32[]{:S(2)}) %collective-permute-start.3) | collective-permute-done | bytes 159776 | tf_op jit(solution)/shard_map/ppermute | solution.py:462
  20.0 1.4 %collective-permute-start.10 = (bf16[104,768]{1,0:T(8,128)(2,1)S(1)}, bf16[104,768]{1,0:T(8,128)(2,1)S(1)}, u32[]{:S(2)}, u32[]{:S(2)}) collective-permute-start(bf16[104,768]{1,0:T(8,128)(2,1)S(1)} %get-tuple-element.321), channel_id=1, source_target_pairs={{0,3},{1,0},{2,1},{3,2},{8,11},{9,8},{10,9},{11,10},{16,19},{17,16... | collective-permute-start | bytes 479240 | tf_op jit(solution)/shard_map/ppermute | solution.py:467
  23.2 2.2 %collective-permute-start.6 = (bf16[104,768]{1,0:T(8,128)(2,1)S(1)}, bf16[104,768]{1,0:T(8,128)(2,1)S(1)}, u32[]{:S(2)}, u32[]{:S(2)}) collective-permute-start(bf16[104,768]{1,0:T(8,128)(2,1)S(1)} %get-tuple-element.312), channel_id=1, source_target_pairs={{0,9},{1,10},{2,11},{3,8},{8,1},{9,2},{10,3},{11,0},{16,25},{17,26... | collective-permute-start | bytes 479240 | tf_op jit(solution)/shard_map/ppermute | solution.py:467
  25.8 18.2 %collective-permute-done.10.refs_0_ = bf16[104,768]{1,0:T(8,128)(2,1)S(1)} collective-permute-done((bf16[104,768]{1,0:T(8,128)(2,1)S(1)}, bf16[104,768]{1,0:T(8,128)(2,1)S(1)}, u32[]{:S(2)}, u32[]{:S(2)}) %collective-permute-start.10) | collective-permute-done | bytes 159776 | tf_op jit(solution)/shard_map/ppermute | solution.py:467
  44.0 2.5 %collective-permute-start.8 = (bf16[104,768]{1,0:T(8,128)(2,1)S(1)}, bf16[104,768]{1,0:T(8,128)(2,1)S(1)}, u32[]{:S(2)}, u32[]{:S(2)}) collective-permute-start(bf16[104,768]{1,0:T(8,128)(2,1)S(1)} %get-tuple-element.314), channel_id=1, source_target_pairs={{0,25},{1,26},{2,27},{3,24},{8,17},{9,18},{10,19},{11,16},{16,9},{... | collective-permute-start | bytes 479240 | tf_op jit(solution)/shard_map/ppermute | solution.py:467
  46.5 2.6 %collective-permute-start.14 = (bf16[104,768]{1,0:T(8,128)(2,1)S(1)}, bf16[104,768]{1,0:T(8,128)(2,1)S(1)}, u32[]{:S(2)}, u32[]{:S(2)}) collective-permute-start(bf16[104,768]{1,0:T(8,128)(2,1)S(1)} %get-tuple-element.331), channel_id=1, source_target_pairs={{0,11},{1,8},{2,9},{3,10},{8,3},{9,0},{10,1},{11,2},{16,27},{17,24... | collective-permute-start | bytes 479240 | tf_op jit(solution)/shard_map/ppermute | solution.py:467
  49.2 5.4 %collective-permute-done.8.refs_3_ = bf16[104,768]{1,0:T(8,128)(2,1)S(1)} collective-permute-done((bf16[104,768]{1,0:T(8,128)(2,1)S(1)}, bf16[104,768]{1,0:T(8,128)(2,1)S(1)}, u32[]{:S(2)}, u32[]{:S(2)}) %collective-permute-start.8) | collective-permute-done | bytes 159776 | tf_op jit(solution)/shard_map/ppermute | solution.py:467
  55.3 1.6 %collective-permute-start.11 = (bf16[104,768]{1,0:T(8,128)(2,1)S(1)}, bf16[104,768]{1,0:T(8,128)(2,1)S(1)}, u32[]{:S(2)}, u32[]{:S(2)}) collective-permute-start(bf16[104,768]{1,0:T(8,128)(2,1)S(1)} %get-tuple-element.324), channel_id=1, source_target_pairs={{0,8},{8,0},{16,24},{24,16},{1,9},{9,1},{17,25},{25,17},{2,10},{10... | collective-permute-start | bytes 479240 | tf_op jit(solution)/shard_map/ppermute | solution.py:462
  57.1 1.7 %collective-permute-start.13 = (bf16[104,768]{1,0:T(8,128)(2,1)S(1)}, bf16[104,768]{1,0:T(8,128)(2,1)S(1)}, u32[]{:S(2)}, u32[]{:S(2)}) collective-permute-start(bf16[104,768]{1,0:T(8,128)(2,1)S(1)} %get-tuple-element.326), channel_id=1, source_target_pairs={{0,24},{8,16},{16,8},{24,0},{1,25},{9,17},{17,9},{25,1},{2,26},{10... | collective-permute-start | bytes 479240 | tf_op jit(solution)/shard_map/ppermute | solution.py:462
  60.1 1.2 %sort.5 = (bf16[464,768]{1,0:T(8,128)(2,1)S(1)}, s32[4,128]{1,0:T(4,128)S(1)}) custom-call(bf16[104,768]{1,0:T(8,128)(2,1)S(1)} %collective-permute-done.5.refs_0_, bf16[104,768]{1,0:T(8,128)(2,1)S(1)} %collective-permute-done.6.refs_1_, bf16[104,768]{1,0:T(8,128)(2,1)S(1)} %collective-permute-done.7.refs_2_, bf16[104,768]{1,0:T(8,128)(2,1)S(1)} %collective-permute-done.8.refs_3_), custom_call_target="tpu_custom_call" | custom-call | tf_op jit(solution)/shard_map/sort/pallas_call | solution.py:401
  61.4 1.7 %collective-permute-done.15.refs_2_ = bf16[104,768]{1,0:T(8,128)(2,1)S(1)} collective-permute-done((bf16[104,768]{1,0:T(8,128)(2,1)S(1)}, bf16[104,768]{1,0:T(8,128)(2,1)S(1)}, u32[]{:S(2)}, u32[]{:S(2)}) %collective-permute-start.15) | collective-permute-done | bytes 159776 | tf_op jit(solution)/shard_map/ppermute | solution.py:467
  63.1 1.9 %collective-permute-done.16.refs_3_ = bf16[104,768]{1,0:T(8,128)(2,1)S(1)} collective-permute-done((bf16[104,768]{1,0:T(8,128)(2,1)S(1)}, bf16[104,768]{1,0:T(8,128)(2,1)S(1)}, u32[]{:S(2)}, u32[]{:S(2)}) %collective-permute-start.16) | collective-permute-done | bytes 159776 | tf_op jit(solution)/shard_map/ppermute | solution.py:467
  65.0 1.2 %sort.7 = (bf16[464,768]{1,0:T(8,128)(2,1)S(1)}, s32[4,128]{1,0:T(4,128)S(1)}) custom-call(bf16[104,768]{1,0:T(8,128)(2,1)S(1)} %collective-permute-done.10.refs_0_, bf16[104,768]{1,0:T(8,128)(2,1)S(1)} %collective-permute-done.14.refs_1_, bf16[104,768]{1,0:T(8,128)(2,1)S(1)} %collective-permute-done.15.refs_2_, ...), custom_call_target="tpu_custom_call" | custom-call | tf_op jit(solution)/shard_map/sort/pallas_call | solution.py:401
  66.9 3.2 %collective-permute-done.12.refs_2_ = bf16[104,768]{1,0:T(8,128)(2,1)S(1)} collective-permute-done((bf16[104,768]{1,0:T(8,128)(2,1)S(1)}, bf16[104,768]{1,0:T(8,128)(2,1)S(1)}, u32[]{:S(2)}, u32[]{:S(2)}) %collective-permute-start.12) | collective-permute-done | bytes 159776 | tf_op jit(solution)/shard_map/ppermute | solution.py:462
  70.0 1.2 %sort.6 = (bf16[464,768]{1,0:T(8,128)(2,1)S(1)}, s32[4,128]{1,0:T(4,128)S(1)}) custom-call(bf16[104,768]{1,0:T(8,128)(2,1)S(1)} %get-tuple-element.323.refs_0_, bf16[104,768]{1,0:T(8,128)(2,1)S(1)} %collective-permute-done.11.refs_1_, bf16[104,768]{1,0:T(8,128)(2,1)S(1)} %collective-permute-done.12.refs_2_, bf16[104,768]{1,0:T(8,128)(2,1)S(1)} %collective-permute-done.13.refs_3_), custom_call_target="tpu_custom_call" | custom-call | tf_op jit(solution)/shard_map/sort/pallas_call | solution.py:401
  71.4 2.1 %collective-permute-done.19.refs_6_ = bf16[464,768]{1,0:T(8,128)(2,1)S(1)} collective-permute-done((bf16[464,768]{1,0:T(8,128)(2,1)S(1)}, bf16[464,768]{1,0:T(8,128)(2,1)S(1)}, u32[]{:S(2)}, u32[]{:S(2)}) %collective-permute-start.19) | collective-permute-done | bytes 712736 | tf_op jit(solution)/shard_map/ppermute | solution.py:483
  73.5 7.3 %score.1 = f32[16,128]{1,0:T(8,128)} custom-call(bf16[464,768]{1,0:T(8,128)(2,1)S(1)} %get-tuple-element.310.refs_0_, bf16[464,768]{1,0:T(8,128)(2,1)S(1)} %get-tuple-element.315.refs_1_, bf16[464,768]{1,0:T(8,128)(2,1)S(1)} %get-tuple-element.327.refs_2_, bf16[464,768]{1,0:T(8,128)(2,1)S(1)} %get-tuple-element.334.refs_3_, ...), custom_call_target="tpu_custom_call" | custom-call | tf_op jit(solution)/shard_map/score/pallas_call | solution.py:401
  80.8 4.5 %all-to-all-start.3 = ((f32[16,1,128]{2,1,0:T(1,128)}), f32[16,1,128]{2,1,0:T(1,128)S(1)}, u32[]{:S(2)}, u32[]{:S(2)}) async-start(f32[16,1,128]{2,1,0:T(1,128)} %bitcast.14), calls=%async_computation.3 | async-start | bytes 16384 | tf_op jit(solution)/shard_map/all_to_all | solution.py:528
  85.3 7.3 %all-to-all-done.3 = f32[16,1,128]{2,1,0:T(1,128)S(1)} async-done(((f32[16,1,128]{2,1,0:T(1,128)}), f32[16,1,128]{2,1,0:T(1,128)S(1)}, u32[]{:S(2)}, u32[]{:S(2)}) %all-to-all-start.3) | async-done | bytes 8224 | tf_op jit(solution)/shard_map/all_to_all | solution.py:528
  (33 shorter events, 9.4 us)
Async XLA Ops:
  4.4 42.1 %collective-permute-start.9 = (bf16[320,768]{1,0:T(8,128)(2,1)S(1)}, bf16[320,768]{1,0:T(8,128)(2,1)S(1)}, u32[]{:S(2)}, u32[]{:S(2)}) collective-permute-start(bf16[320,768]{1,0:T(8,128)(2,1)S(1)} %get-tuple-element.316), channel_id=1, source_target_pairs={{0,2},{1,3},{2,0},{3,1},{4,6},{5,7},{6,4},{7,5},{8,10},{9,11},{10,... | collective-permute-start | bytes 1474568 | tf_op jit(solution)/shard_map/ppermute | solution.py:485
  9.7 6.7 %collective-permute-start.2 = (bf16[104,768]{1,0:T(8,128)(2,1)S(1)}, bf16[104,768]{1,0:T(8,128)(2,1)S(1)}, u32[]{:S(2)}, u32[]{:S(2)}) collective-permute-start(bf16[104,768]{1,0:T(8,128)(2,1)S(1)} %get-tuple-element.307), channel_id=1, source_target_pairs={{0,8},{8,0},{16,24},{24,16},{1,9},{9,1},{17,25},{25,17},{2,10},{10... | collective-permute-start | bytes 479240 | tf_op jit(solution)/shard_map/ppermute | solution.py:462
  11.3 8.7 %collective-permute-start.3 = (bf16[104,768]{1,0:T(8,128)(2,1)S(1)}, bf16[104,768]{1,0:T(8,128)(2,1)S(1)}, u32[]{:S(2)}, u32[]{:S(2)}) collective-permute-start(bf16[104,768]{1,0:T(8,128)(2,1)S(1)} %get-tuple-element.308), channel_id=1, source_target_pairs={{0,16},{8,24},{16,0},{24,8},{1,17},{9,25},{17,1},{25,9},{2,18},{10... | collective-permute-start | bytes 479240 | tf_op jit(solution)/shard_map/ppermute | solution.py:462
  12.8 7.2 %collective-permute-start.4 = (bf16[104,768]{1,0:T(8,128)(2,1)S(1)}, bf16[104,768]{1,0:T(8,128)(2,1)S(1)}, u32[]{:S(2)}, u32[]{:S(2)}) collective-permute-start(bf16[104,768]{1,0:T(8,128)(2,1)S(1)} %get-tuple-element.309), channel_id=1, source_target_pairs={{0,24},{8,16},{16,8},{24,0},{1,25},{9,17},{17,9},{25,1},{2,26},{10... | collective-permute-start | bytes 479240 | tf_op jit(solution)/shard_map/ppermute | solution.py:462
  20.0 24.0 %collective-permute-start.10 = (bf16[104,768]{1,0:T(8,128)(2,1)S(1)}, bf16[104,768]{1,0:T(8,128)(2,1)S(1)}, u32[]{:S(2)}, u32[]{:S(2)}) collective-permute-start(bf16[104,768]{1,0:T(8,128)(2,1)S(1)} %get-tuple-element.321), channel_id=1, source_target_pairs={{0,3},{1,0},{2,1},{3,2},{8,11},{9,8},{10,9},{11,10},{16,19},{17,16... | collective-permute-start | bytes 479240 | tf_op jit(solution)/shard_map/ppermute | solution.py:467
  22.5 26.6 %collective-permute-start.5 = (bf16[104,768]{1,0:T(8,128)(2,1)S(1)}, bf16[104,768]{1,0:T(8,128)(2,1)S(1)}, u32[]{:S(2)}, u32[]{:S(2)}) collective-permute-start(bf16[104,768]{1,0:T(8,128)(2,1)S(1)} %get-tuple-element.311), channel_id=1, source_target_pairs={{0,1},{1,2},{2,3},{3,0},{8,9},{9,10},{10,11},{11,8},{16,17},{17,18... | collective-permute-start | bytes 479240 | tf_op jit(solution)/shard_map/ppermute | solution.py:467
  23.2 25.9 %collective-permute-start.6 = (bf16[104,768]{1,0:T(8,128)(2,1)S(1)}, bf16[104,768]{1,0:T(8,128)(2,1)S(1)}, u32[]{:S(2)}, u32[]{:S(2)}) collective-permute-start(bf16[104,768]{1,0:T(8,128)(2,1)S(1)} %get-tuple-element.312), channel_id=1, source_target_pairs={{0,9},{1,10},{2,11},{3,8},{8,1},{9,2},{10,3},{11,0},{16,25},{17,26... | collective-permute-start | bytes 479240 | tf_op jit(solution)/shard_map/ppermute | solution.py:467
  25.5 23.7 %collective-permute-start.7 = (bf16[104,768]{1,0:T(8,128)(2,1)S(1)}, bf16[104,768]{1,0:T(8,128)(2,1)S(1)}, u32[]{:S(2)}, u32[]{:S(2)}) collective-permute-start(bf16[104,768]{1,0:T(8,128)(2,1)S(1)} %get-tuple-element.313), channel_id=1, source_target_pairs={{0,17},{1,18},{2,19},{3,16},{8,25},{9,26},{10,27},{11,24},{16,1},{... | collective-permute-start | bytes 479240 | tf_op jit(solution)/shard_map/ppermute | solution.py:467
  44.0 10.6 %collective-permute-start.8 = (bf16[104,768]{1,0:T(8,128)(2,1)S(1)}, bf16[104,768]{1,0:T(8,128)(2,1)S(1)}, u32[]{:S(2)}, u32[]{:S(2)}) collective-permute-start(bf16[104,768]{1,0:T(8,128)(2,1)S(1)} %get-tuple-element.314), channel_id=1, source_target_pairs={{0,25},{1,26},{2,27},{3,24},{8,17},{9,18},{10,19},{11,16},{16,9},{... | collective-permute-start | bytes 479240 | tf_op jit(solution)/shard_map/ppermute | solution.py:467
  46.5 10.6 %collective-permute-start.14 = (bf16[104,768]{1,0:T(8,128)(2,1)S(1)}, bf16[104,768]{1,0:T(8,128)(2,1)S(1)}, u32[]{:S(2)}, u32[]{:S(2)}) collective-permute-start(bf16[104,768]{1,0:T(8,128)(2,1)S(1)} %get-tuple-element.331), channel_id=1, source_target_pairs={{0,11},{1,8},{2,9},{3,10},{8,3},{9,0},{10,1},{11,2},{16,27},{17,24... | collective-permute-start | bytes 479240 | tf_op jit(solution)/shard_map/ppermute | solution.py:467
  54.6 8.5 %collective-permute-start.15 = (bf16[104,768]{1,0:T(8,128)(2,1)S(1)}, bf16[104,768]{1,0:T(8,128)(2,1)S(1)}, u32[]{:S(2)}, u32[]{:S(2)}) collective-permute-start(bf16[104,768]{1,0:T(8,128)(2,1)S(1)} %get-tuple-element.332), channel_id=1, source_target_pairs={{0,19},{1,16},{2,17},{3,18},{8,27},{9,24},{10,25},{11,26},{16,3},{... | collective-permute-start | bytes 479240 | tf_op jit(solution)/shard_map/ppermute | solution.py:467
  54.6 10.4 %collective-permute-start.16 = (bf16[104,768]{1,0:T(8,128)(2,1)S(1)}, bf16[104,768]{1,0:T(8,128)(2,1)S(1)}, u32[]{:S(2)}, u32[]{:S(2)}) collective-permute-start(bf16[104,768]{1,0:T(8,128)(2,1)S(1)} %get-tuple-element.333), channel_id=1, source_target_pairs={{0,27},{1,24},{2,25},{3,26},{8,19},{9,16},{10,17},{11,18},{16,11},... | collective-permute-start | bytes 479240 | tf_op jit(solution)/shard_map/ppermute | solution.py:467
  55.3 11.0 %collective-permute-start.11 = (bf16[104,768]{1,0:T(8,128)(2,1)S(1)}, bf16[104,768]{1,0:T(8,128)(2,1)S(1)}, u32[]{:S(2)}, u32[]{:S(2)}) collective-permute-start(bf16[104,768]{1,0:T(8,128)(2,1)S(1)} %get-tuple-element.324), channel_id=1, source_target_pairs={{0,8},{8,0},{16,24},{24,16},{1,9},{9,1},{17,25},{25,17},{2,10},{10... | collective-permute-start | bytes 479240 | tf_op jit(solution)/shard_map/ppermute | solution.py:462
  56.9 13.1 %collective-permute-start.12 = (bf16[104,768]{1,0:T(8,128)(2,1)S(1)}, bf16[104,768]{1,0:T(8,128)(2,1)S(1)}, u32[]{:S(2)}, u32[]{:S(2)}) collective-permute-start(bf16[104,768]{1,0:T(8,128)(2,1)S(1)} %get-tuple-element.325), channel_id=1, source_target_pairs={{0,16},{8,24},{16,0},{24,8},{1,17},{9,25},{17,1},{25,9},{2,18},{10... | collective-permute-start | bytes 479240 | tf_op jit(solution)/shard_map/ppermute | solution.py:462
  57.1 12.9 %collective-permute-start.13 = (bf16[104,768]{1,0:T(8,128)(2,1)S(1)}, bf16[104,768]{1,0:T(8,128)(2,1)S(1)}, u32[]{:S(2)}, u32[]{:S(2)}) collective-permute-start(bf16[104,768]{1,0:T(8,128)(2,1)S(1)} %get-tuple-element.326), channel_id=1, source_target_pairs={{0,24},{8,16},{16,8},{24,0},{1,25},{9,17},{17,9},{25,1},{2,26},{10... | collective-permute-start | bytes 479240 | tf_op jit(solution)/shard_map/ppermute | solution.py:462
  63.1 8.3 %collective-permute-start.18 = (bf16[464,768]{1,0:T(8,128)(2,1)S(1)}, bf16[464,768]{1,0:T(8,128)(2,1)S(1)}, u32[]{:S(2)}, u32[]{:S(2)}) collective-permute-start(bf16[464,768]{1,0:T(8,128)(2,1)S(1)} %get-tuple-element.315.refs_1_), channel_id=1, source_target_pairs={{0,4},{4,0},{1,5},{5,1},{2,6},{6,2},{3,7},{7,3},{8,12},{12,8},{9,1... | collective-permute-start | bytes 2138120 | tf_op jit(solution)/shard_map/ppermute | solution.py:483
  65.0 6.3 %collective-permute-start.17 = (bf16[464,768]{1,0:T(8,128)(2,1)S(1)}, bf16[464,768]{1,0:T(8,128)(2,1)S(1)}, u32[]{:S(2)}, u32[]{:S(2)}) collective-permute-start(bf16[464,768]{1,0:T(8,128)(2,1)S(1)} %get-tuple-element.310.refs_0_), channel_id=1, source_target_pairs={{0,4},{4,0},{1,5},{5,1},{2,6},{6,2},{3,7},{7,3},{8,12},{12,8},{9,1... | collective-permute-start | bytes 2138120 | tf_op jit(solution)/shard_map/ppermute | solution.py:483
  66.3 5.1 %collective-permute-start.20 = (bf16[464,768]{1,0:T(8,128)(2,1)S(1)}, bf16[464,768]{1,0:T(8,128)(2,1)S(1)}, u32[]{:S(2)}, u32[]{:S(2)}) collective-permute-start(bf16[464,768]{1,0:T(8,128)(2,1)S(1)} %get-tuple-element.334.refs_3_), channel_id=1, source_target_pairs={{0,4},{4,0},{1,5},{5,1},{2,6},{6,2},{3,7},{7,3},{8,12},{12,8},{9,1... | collective-permute-start | bytes 2138120 | tf_op jit(solution)/shard_map/ppermute | solution.py:483
  70.0 22.6 %copy-start.3 = (s32[1024]{0:T(1024)S(1)}, s32[1024]{0:T(1024)}, u32[]{:S(2)}) copy-start(s32[1024]{0:T(1024)} %param.9) | copy-start | bytes 12292
  70.0 24.7 %copy-start = (f32[1024,768]{1,0:T(8,128)S(1)}, f32[1024,768]{1,0:T(8,128)}, u32[]{:S(2)}) copy-start(f32[1024,768]{1,0:T(8,128)} %emb_ref.1) | copy-start | bytes 9437188
  71.3 2.2 %collective-permute-start.19 = (bf16[464,768]{1,0:T(8,128)(2,1)S(1)}, bf16[464,768]{1,0:T(8,128)(2,1)S(1)}, u32[]{:S(2)}, u32[]{:S(2)}) collective-permute-start(bf16[464,768]{1,0:T(8,128)(2,1)S(1)} %get-tuple-element.327.refs_2_), channel_id=1, source_target_pairs={{0,4},{4,0},{1,5},{5,1},{2,6},{6,2},{3,7},{7,3},{8,12},{12,8},{9,1... | collective-permute-start | bytes 2138120 | tf_op jit(solution)/shard_map/ppermute | solution.py:483
  80.8 11.7 %all-to-all-start.3 = ((f32[16,1,128]{2,1,0:T(1,128)}), f32[16,1,128]{2,1,0:T(1,128)S(1)}, u32[]{:S(2)}, u32[]{:S(2)}) async-start(f32[16,1,128]{2,1,0:T(1,128)} %bitcast.14), calls=%async_computation.3 | async-start | bytes 16384 | tf_op jit(solution)/shard_map/all_to_all | solution.py:528

commit v6 on v5

--- a/solution.py
+++ b/solution.py
@@ -20,9 +20,9 @@
 FLAG = LANES - 1
 LOW = LANES // 2
 ALIGN = 16
-STEP = 32
-LEFT = 192
-RIGHT = 384
+STEP = 96
+LEFT = 256
+RIGHT = 512
 PLACES = 1 << 16
 
 
@@ -284,85 +284,103 @@
     def aligned(count):
         return (count + (ALIGN - 1)) & -ALIGN
 
-    counts, places, begins = [], [], []
+    runs, ends = [], []
     begin = jnp.int32(0)
     source = [jnp.int32(0)] * pieces
+    many = jnp.bool_(False)
     for label in range(labels):
-        begins.append(begin)
-        counts.append([])
-        places.append([])
+        runs.append([])
         for index in range(pieces):
-            free = space - source[index]
             count = counts_ref[index, label] * LANES + counts_ref[index, LOW + label]
-            count = jnp.clip(count, 0, free)
-            counts[label].append(count)
-            places[label].append((source[index], begin))
-            src, dst = source[index], begin
-
-            def move(step, carry, ref=piece_refs[index], src=src, dst=dst):
-                rows = pl.ds(pl.multiple_of(src + step * STEP, ALIGN), STEP)
-                to = pl.ds(pl.multiple_of(dst + step * STEP, ALIGN), STEP)
-                rows_ref[to, :] = ref[rows, :]
-                return carry
-
-            move(0, 0)
-            lax.fori_loop(1, (count + STEP - 1) // STEP, move, 0)
+            count = jnp.clip(count, 0, space - source[index])
+            runs[label].append((source[index], begin, count))
+            many = many | (count > STEP)
             source[index] = source[index] + aligned(count)
             begin = begin + aligned(count)
+        ends.append(begin)
+
+    def span(start, step, size):
+        return pl.ds(pl.multiple_of(start + step * size, ALIGN), size)
+
+    def gather(index, src, dst, step):
+        rows_ref[span(dst, step, STEP), :] = piece_refs[index][span(src, step, STEP), :]
+
+    def repeat(first, end, act):
+        def once(step, carry):
+            act(step)
+            return carry
+
+        lax.fori_loop(first, end, once, 0)
+
+    def cover(count, size):
+        return (count + size - 1) // size
 
     for label in range(labels):
-        first = begins[label]
-        own_end = places[label][tiles][1]
-        end = begins[label + 1] if label + 1 < labels else begin
-
-        def window(row, column, label=label):
-            left = rows_ref[pl.ds(pl.multiple_of(row, ALIGN), LEFT), :]
-            right = rows_ref[pl.ds(pl.multiple_of(column, ALIGN), RIGHT), :]
-            scores = lax.dot_general(
-                left, right, (((1,), (1,)), ((), ())), preferred_element_type=jnp.float32
-            )
-            at = iota((1, RIGHT), 1) + column
-            valid = at < 0
-            for index in range(pieces):
-                low = places[label][index][1]
-                valid = valid | ((at >= low) & (at < low + counts[label][index]))
-            at = jnp.where(valid, at, -1)
-            itself = iota((LEFT, RIGHT), 0) + row
-            counted = (at >= 0) & (at != itself)
-            terms = jnp.where(counted, jnp.exp(sharpness * scores), 0.0)
-            return jnp.sum(terms, axis=1, keepdims=True)
-
-        def strip(row, first=first, end=end, window=window):
-            sums = window(row, first)
-            sums = lax.fori_loop(
-                1,
-                (end - first + RIGHT - 1) // RIGHT,
-                lambda step, sums: sums + window(row, first + step * RIGHT),
-                sums,
-            )
-            total_ref[pl.ds(pl.multiple_of(row, ALIGN), LEFT), :] = jnp.broadcast_to(
-                sums, (LEFT, LANES)
-            )
-
-        def more(step, carry, first=first, strip=strip):
-            strip(first + step * LEFT)
-            return carry
-
-        strip(first)
-        lax.fori_loop(1, (own_end - first + LEFT - 1) // LEFT, more, 0)
+        for index, (src, dst, count) in enumerate(runs[label]):
+            gather(index, src, dst, 0)
+
+    @pl.when(many)
+    def _():
+        for label in range(labels):
+            for index, (src, dst, count) in enumerate(runs[label]):
+                repeat(0, cover(count, STEP), functools.partial(gather, index, src, dst))
+
+    def window(label, row, column):
+        left = rows_ref[span(row, 0, LEFT), :]
+        right = rows_ref[span(column, 0, RIGHT), :]
+        scores = lax.dot_general(
+            left, right, (((1,), (1,)), ((), ())), preferred_element_type=jnp.float32
+        )
+        at = iota((1, RIGHT), 1) + column
+        valid = at < 0
+        for _, low, count in runs[label]:
+            valid = valid | ((at >= low) & (at < low + count))
+        at = jnp.where(valid, at, -1)
+        itself = iota((LEFT, RIGHT), 0) + row
+        counted = (at >= 0) & (at != itself)
+        terms = jnp.where(counted, jnp.exp(sharpness * scores), 0.0)
+        sums = jnp.sum(terms, axis=1, keepdims=True)
+        return jnp.broadcast_to(sums, (LEFT, LANES))
+
+    wide = jnp.bool_(False)
+    for label in range(labels):
+        first, own_end = runs[label][0][1], runs[label][tiles][1]
+        total_ref[label, 0:LEFT, :] = window(label, first, first)
+        wide = wide | (own_end - first > LEFT) | (ends[label] - first > RIGHT)
+
+    @pl.when(wide)
+    def _():
+        for label in range(labels):
+            first, own_end = runs[label][0][1], runs[label][tiles][1]
+            across_steps = cover(ends[label] - first, RIGHT)
+
+            def add(strip, step, label=label, first=first):
+                row, column = first + strip * LEFT, first + step * RIGHT
+                total_ref[label, span(0, strip, LEFT), :] += window(label, row, column)
+
+            def strips(strip, label=label, add=add, across_steps=across_steps):
+                total_ref[label, span(0, strip, LEFT), :] = jnp.zeros((LEFT, LANES), jnp.float32)
+                repeat(0, across_steps, functools.partial(add, strip))
+
+            repeat(1, across_steps, functools.partial(add, 0))
+            repeat(1, cover(own_end - first, LEFT), strips)
+
+    def scatter(label, index, step):
+        src, dst, _ = runs[label][index]
+        back_ref[index, span(src, step, STEP), :] = total_ref[
+            label, span(dst - runs[label][0][1], step, STEP), :
+        ]
 
     for index in range(tiles):
         for label in range(labels):
-            src, dst = places[label][index][1], places[label][index][0]
-
-            def back(step, carry, index=index, src=src, dst=dst):
-                rows = pl.ds(pl.multiple_of(src + step * STEP, ALIGN), STEP)
-                to = pl.ds(pl.multiple_of(dst + step * STEP, ALIGN), STEP)
-                back_ref[index, to, :] = total_ref[rows, :]
-                return carry
-
-            back(0, 0)
-            lax.fori_loop(1, (counts[label][index] + STEP - 1) // STEP, back, 0)
+            scatter(label, index, 0)
+
+    @pl.when(many)
+    def _():
+        for index in range(tiles):
+            for label in range(labels):
+                count = runs[label][index][2]
+                repeat(0, cover(count, STEP), functools.partial(scatter, label, index))
 
     lanes = out_ref.shape[1]
     row = iota((space, LANES), 0)
@@ -426,7 +444,7 @@
     shape = jax.ShapeDtypeStruct
 
     ids_row = cluster_ids.reshape(1, rows)
-    first, aug, slots, rank = call(
+    pool_rows, aug, slots, rank = call(
         functools.partial(plan_kernel, size),
         "plan",
         [
@@ -482,43 +500,34 @@
         )
         other[shift] = lax.ppermute(own[shift], "core", swap)
 
-    pooled = lax.ppermute(first, "tile", along(order[0]))
-    before = []
-    for shift in order[1:-1]:
-        blocks = pack(shift, across, cap)
-        arrived = [send_far(blocks, shift, side) for side in range(across)]
-        finish(shift, arrived)
-        before += arrived
+    pooled = lax.ppermute(pool_rows, "tile", along(order[0]))
     near = send_across(pack(0, across, cap))
     finish(0, near)
-    before += near
-    arrived = []
-    if len(order) > 1:
-        blocks = after(pack(order[-1], across, cap), *near)
-        arrived = [send_far(blocks, order[-1], 0)]
-        blocks = after(blocks, pooled, *arrived)
+    packed = {shift: pack(shift, across, cap) for shift in order[1:]}
+    ready = [block for shift in order[1:] for block in packed[shift]]
     regrouped = call(
         functools.partial(regroup_kernel, size),
         "regroup",
         [shape((cap, width), jnp.bfloat16)] * across,
-        [after(pooled, *before, *arrived)],
-    )
-    finish(order[0], send_across(regrouped))
-    if len(order) > 1:
-        arrived += [send_far(blocks, order[-1], side) for side in range(1, across)]
-        finish(order[-1], arrived)
+        [after(pooled, *near, *ready)],
+    )
+    passed = send_across(regrouped)
+    finish(order[0], passed)
+    for shift in order[1:]:
+        blocks = after(packed[shift], pooled)
+        finish(shift, [send_far(blocks, shift, side) for side in range(across)])
     own, other, places = (
         [found[shift] for shift in range(tiles)] for found in (own, other, places)
     )
-    room_all = 2 * tiles * space + RIGHT
+    room_own = tiles * space + LEFT + STEP
     totals = call(
         functools.partial(score_kernel, size),
         "score",
         shape((chips, lanes), jnp.float32),
         [*own, *other, *places],
         scratch_shapes=[
-            pltpu.VMEM((room_all, width), jnp.bfloat16),
-            pltpu.VMEM((room_all, LANES), jnp.float32),
+            pltpu.VMEM((2 * tiles * space + LEFT + RIGHT, width), jnp.bfloat16),
+            pltpu.VMEM((labels, room_own, LANES), jnp.float32),
             pltpu.VMEM((tiles, space + STEP, LANES), jnp.float32),
             pltpu.VMEM((2 * tiles, LANES), jnp.int32),
             pltpu.SMEM((2 * tiles, LANES), jnp.int32),

time: 96 us -> 91.1 us (0.949)
  waiting for transfers between devices: 45.4 us -> 35.6 us
  starting transfers between devices: 26.1 us -> 31.9 us
  Pallas kernels: 21.9 us -> 20.9 us
  local copies, waits for them, and re-layouts: 0.52 us -> 1.48 us
    ppermute x8, waiting for transfers between devices: 27.3 us -> 6.02 us  [send_far(): return lax.ppermute(blocks[side], ('chip', 'tile'), route)]
    ppermute x1, waiting for transfers between devices: 0.01 us -> 15.8 us  [body(): pooled = lax.ppermute(pool_rows, 'tile', along(order[0]))]
    ppermute x8, starting transfers between devices: 9.81 us -> 14.5 us  [send_far(): return lax.ppermute(blocks[side], ('chip', 'tile'), route)]
    ppermute x6, waiting for transfers between devices: 8.71 us -> 4.19 us  [send_across(): lax.ppermute(blocks[side], 'chip', over(side))]
    pallas_call x11, Pallas kernels: 21.9 us -> 20.9 us  [call(): pl.pallas_call(kernel, out_shape=out_shape, in_specs=[vmem] * len(inputs)...]
  transfers between devices with their start and end apart: 20 -> 20, of which waited for: 9 -> 7; matrix products, arithmetic and copies ran while one was open for 0% -> 0% of each run, Pallas kernels for 10% -> 10%
where the time goes in v6:
time: 91.1 us; the launch traced here: 90.9 us
  waiting for transfers between devices  35.6 us (39%)
  starting transfers between devices  31.9 us (35%)
  Pallas kernels  20.9 us (23%)
  local copies, waits for them, and re-layouts  1.48 us (2%)
  between operations  1.02 us (1%)
    pallas_call x11, Pallas kernels, call(): pl.pallas_call(kernel, out_shape=out_shape, in_specs=[vmem] * len(inputs)...  20.9 us
    ppermute x1, waiting for transfers between devices, body(): pooled = lax.ppermute(pool_rows, 'tile', along(order[0]))  15.8 us
    ppermute x8, starting transfers between devices, send_far(): return lax.ppermute(blocks[side], ('chip', 'tile'), route)  14.5 us
    all_to_all x1, waiting for transfers between devices, body(): lax.all_to_all(totals, ('chip', 'tile'), split_axis=0, concat_axis=0, til...  7.26 us
    ppermute x6, starting transfers between devices, send_across(): lax.ppermute(blocks[side], 'chip', over(side))  7.11 us
    ppermute x8, waiting for transfers between devices, send_far(): return lax.ppermute(blocks[side], ('chip', 'tile'), route)  6.02 us
    all_to_all x1, starting transfers between devices, body(): lax.all_to_all(totals, ('chip', 'tile'), split_axis=0, concat_axis=0, til...  5.36 us
    ppermute x6, waiting for transfers between devices, send_across(): lax.ppermute(blocks[side], 'chip', over(side))  4.19 us
  transfers between devices with their start and end apart: 20, of which 7 were waited for; matrix products, arithmetic and copies ran while one was open for 0% of the time, Pallas kernels for 10%

profile of v6, /device:TPU:0, one launch (start us, length us, event | category | flops | bytes accessed | tf_op | source)
XLA Modules:
  0.0 90.9 jit_solution(12952091166275682658)
XLA Ops:
  0.0 4.4 %plan.1 = (bf16[320,768]{1,0:T(8,128)(2,1)S(1)}, bf16[1152,768]{1,0:T(8,128)(2,1)S(1)}, s32[1,1152]{1,0:T(1,128)S(1)}, f32[1,1024]{1,0:T(1,128)S(1)}) custom-call(f32[1024,768]{1,0:T(8,128)} %emb_ref.1, s32[1,1024]{1,0:T(1,128)} %bitcast.74), custom_call_target="tpu_custom_call" | custom-call | tf_op jit(solution)/shard_map/plan/pallas_call | solution.py:419
  4.4 4.1 %collective-permute-start.5 = (bf16[320,768]{1,0:T(8,128)(2,1)S(1)}, bf16[320,768]{1,0:T(8,128)(2,1)S(1)}, u32[]{:S(2)}, u32[]{:S(2)}) collective-permute-start(bf16[320,768]{1,0:T(8,128)(2,1)S(1)} %get-tuple-element.316), channel_id=1, source_target_pairs={{0,2},{1,3},{2,0},{3,1},{4,6},{5,7},{6,4},{7,5},{8,10},{9,11},{10,... | collective-permute-start | bytes 1474568 | tf_op jit(solution)/shard_map/ppermute | solution.py:503
  8.5 1.2 %pack.3 = (bf16[104,768]{1,0:T(8,128)(2,1)S(1)}, bf16[104,768]{1,0:T(8,128)(2,1)S(1)}, bf16[104,768]{1,0:T(8,128)(2,1)S(1)}, bf16[104,768]{1,0:T(8,128)(2,1)S(1)}) custom-call(bf16[1152,768]{1,0:T(8,128)(2,1)S(1)} %get-tuple-element.305.aug_ref, s32[1,1152]{1,0:T(1,128)S(1)} %get-tuple-element.306.place_ref), custom_call_target="tpu_custom_call" | custom-call | tf_op jit(solution)/shard_map/pack/pallas_call | solution.py:419
  9.7 1.6 %collective-permute-start.2 = (bf16[104,768]{1,0:T(8,128)(2,1)S(1)}, bf16[104,768]{1,0:T(8,128)(2,1)S(1)}, u32[]{:S(2)}, u32[]{:S(2)}) collective-permute-start(bf16[104,768]{1,0:T(8,128)(2,1)S(1)} %get-tuple-element.308), channel_id=1, source_target_pairs={{0,8},{8,0},{16,24},{24,16},{1,9},{9,1},{17,25},{25,17},{2,10},{10... | collective-permute-start | bytes 479240 | tf_op jit(solution)/shard_map/ppermute | solution.py:480
  11.3 1.5 %collective-permute-start.3 = (bf16[104,768]{1,0:T(8,128)(2,1)S(1)}, bf16[104,768]{1,0:T(8,128)(2,1)S(1)}, u32[]{:S(2)}, u32[]{:S(2)}) collective-permute-start(bf16[104,768]{1,0:T(8,128)(2,1)S(1)} %get-tuple-element.309), channel_id=1, source_target_pairs={{0,16},{8,24},{16,0},{24,8},{1,17},{9,25},{17,1},{25,9},{2,18},{10... | collective-permute-start | bytes 479240 | tf_op jit(solution)/shard_map/ppermute | solution.py:480
  13.3 1.2 %pack.4 = (bf16[104,768]{1,0:T(8,128)(2,1)S(1)}, bf16[104,768]{1,0:T(8,128)(2,1)S(1)}, bf16[104,768]{1,0:T(8,128)(2,1)S(1)}, bf16[104,768]{1,0:T(8,128)(2,1)S(1)}) custom-call(bf16[1152,768]{1,0:T(8,128)(2,1)S(1)} %get-tuple-element.305.aug_ref, s32[1,1152]{1,0:T(1,128)S(1)} %get-tuple-element.306.place_ref), custom_call_target="tpu_custom_call" | custom-call | tf_op jit(solution)/shard_map/pack/pallas_call | solution.py:419
  14.4 15.8 %collective-permute-done.5.pool_ref = bf16[320,768]{1,0:T(8,128)(2,1)S(1)} collective-permute-done((bf16[320,768]{1,0:T(8,128)(2,1)S(1)}, bf16[320,768]{1,0:T(8,128)(2,1)S(1)}, u32[]{:S(2)}, u32[]{:S(2)}) %collective-permute-start.5) | collective-permute-done | bytes 491552 | tf_op jit(solution)/shard_map/ppermute | solution.py:503
  31.0 1.2 %pack.5 = (bf16[104,768]{1,0:T(8,128)(2,1)S(1)}, bf16[104,768]{1,0:T(8,128)(2,1)S(1)}, bf16[104,768]{1,0:T(8,128)(2,1)S(1)}, bf16[104,768]{1,0:T(8,128)(2,1)S(1)}) custom-call(bf16[1152,768]{1,0:T(8,128)(2,1)S(1)} %get-tuple-element.305.aug_ref, s32[1,1152]{1,0:T(1,128)S(1)} %get-tuple-element.306.place_ref), custom_call_target="tpu_custom_call" | custom-call | tf_op jit(solution)/shard_map/pack/pallas_call | solution.py:419
  33.2 4.9 %collective-permute-start.8 = (bf16[104,768]{1,0:T(8,128)(2,1)S(1)}, bf16[104,768]{1,0:T(8,128)(2,1)S(1)}, u32[]{:S(2)}, u32[]{:S(2)}) collective-permute-start(bf16[104,768]{1,0:T(8,128)(2,1)S(1)} %get-tuple-element.319), channel_id=1, source_target_pairs={{0,17},{1,18},{2,19},{3,16},{8,25},{9,26},{10,27},{11,24},{16,1},{... | collective-permute-start | bytes 479240 | tf_op jit(solution)/shard_map/ppermute | solution.py:485
  39.9 2.5 %collective-permute-start.12 = (bf16[104,768]{1,0:T(8,128)(2,1)S(1)}, bf16[104,768]{1,0:T(8,128)(2,1)S(1)}, u32[]{:S(2)}, u32[]{:S(2)}) collective-permute-start(bf16[104,768]{1,0:T(8,128)(2,1)S(1)} %get-tuple-element.330), channel_id=1, source_target_pairs={{0,24},{8,16},{16,8},{24,0},{1,25},{9,17},{17,9},{25,1},{2,26},{10... | collective-permute-start | bytes 479240 | tf_op jit(solution)/shard_map/ppermute | solution.py:480
  43.5 2.6 %collective-permute-done.8.refs_2_ = bf16[104,768]{1,0:T(8,128)(2,1)S(1)} collective-permute-done((bf16[104,768]{1,0:T(8,128)(2,1)S(1)}, bf16[104,768]{1,0:T(8,128)(2,1)S(1)}, u32[]{:S(2)}, u32[]{:S(2)}) %collective-permute-start.8) | collective-permute-done | bytes 159776 | tf_op jit(solution)/shard_map/ppermute | solution.py:485
  46.1 2.8 %collective-permute-start.13 = (bf16[104,768]{1,0:T(8,128)(2,1)S(1)}, bf16[104,768]{1,0:T(8,128)(2,1)S(1)}, u32[]{:S(2)}, u32[]{:S(2)}) collective-permute-start(bf16[104,768]{1,0:T(8,128)(2,1)S(1)} %get-tuple-element.332), channel_id=1, source_target_pairs={{0,3},{1,0},{2,1},{3,2},{8,11},{9,8},{10,9},{11,10},{16,19},{17,16... | collective-permute-start | bytes 479240 | tf_op jit(solution)/shard_map/ppermute | solution.py:485
  48.8 1.6 %collective-permute-start.14 = (bf16[104,768]{1,0:T(8,128)(2,1)S(1)}, bf16[104,768]{1,0:T(8,128)(2,1)S(1)}, u32[]{:S(2)}, u32[]{:S(2)}) collective-permute-start(bf16[104,768]{1,0:T(8,128)(2,1)S(1)} %get-tuple-element.333), channel_id=1, source_target_pairs={{0,11},{1,8},{2,9},{3,10},{8,3},{9,0},{10,1},{11,2},{16,27},{17,24... | collective-permute-start | bytes 479240 | tf_op jit(solution)/shard_map/ppermute | solution.py:485
  50.4 4.2 %collective-permute-done.11.refs_2_ = bf16[104,768]{1,0:T(8,128)(2,1)S(1)} collective-permute-done((bf16[104,768]{1,0:T(8,128)(2,1)S(1)}, bf16[104,768]{1,0:T(8,128)(2,1)S(1)}, u32[]{:S(2)}, u32[]{:S(2)}) %collective-permute-start.11) | collective-permute-done | bytes 159776 | tf_op jit(solution)/shard_map/ppermute | solution.py:480
  54.6 3.6 %collective-permute-start.16 = (bf16[104,768]{1,0:T(8,128)(2,1)S(1)}, bf16[104,768]{1,0:T(8,128)(2,1)S(1)}, u32[]{:S(2)}, u32[]{:S(2)}) collective-permute-start(bf16[104,768]{1,0:T(8,128)(2,1)S(1)} %get-tuple-element.335), channel_id=1, source_target_pairs={{0,27},{1,24},{2,25},{3,26},{8,19},{9,16},{10,17},{11,18},{16,11},... | collective-permute-start | bytes 479240 | tf_op jit(solution)/shard_map/ppermute | solution.py:485
  58.2 1.2 %sort.4 = (bf16[528,768]{1,0:T(8,128)(2,1)S(1)}, s32[4,128]{1,0:T(4,128)S(1)}) custom-call(bf16[104,768]{1,0:T(8,128)(2,1)S(1)} %get-tuple-element.307.refs_0_, bf16[104,768]{1,0:T(8,128)(2,1)S(1)} %collective-permute-done.2.refs_1_, bf16[104,768]{1,0:T(8,128)(2,1)S(1)} %collective-permute-done.3.refs_2_, bf16[104,768]{1,0:T(8,128)(2,1)S(1)} %collective-permute-done.4.refs_3_), custom_call_target="tpu_custom_call" | custom-call | tf_op jit(solution)/shard_map/sort/pallas_call | solution.py:419
  59.4 1.2 %sort.6 = (bf16[528,768]{1,0:T(8,128)(2,1)S(1)}, s32[4,128]{1,0:T(4,128)S(1)}) custom-call(bf16[104,768]{1,0:T(8,128)(2,1)S(1)} %get-tuple-element.327.refs_0_, bf16[104,768]{1,0:T(8,128)(2,1)S(1)} %collective-permute-done.10.refs_1_, bf16[104,768]{1,0:T(8,128)(2,1)S(1)} %collective-permute-done.11.refs_2_, bf16[104,768]{1,0:T(8,128)(2,1)S(1)} %collective-permute-done.12.refs_3_), custom_call_target="tpu_custom_call" | custom-call | tf_op jit(solution)/shard_map/sort/pallas_call | solution.py:419
  60.8 1.2 %sort.5 = (bf16[528,768]{1,0:T(8,128)(2,1)S(1)}, s32[4,128]{1,0:T(4,128)S(1)}) custom-call(bf16[104,768]{1,0:T(8,128)(2,1)S(1)} %collective-permute-done.6.refs_0_, bf16[104,768]{1,0:T(8,128)(2,1)S(1)} %collective-permute-done.7.refs_1_, bf16[104,768]{1,0:T(8,128)(2,1)S(1)} %collective-permute-done.8.refs_2_, bf16[104,768]{1,0:T(8,128)(2,1)S(1)} %collective-permute-done.9.refs_3_), custom_call_target="tpu_custom_call" | custom-call | tf_op jit(solution)/shard_map/sort/pallas_call | solution.py:419
  62.7 2.3 %collective-permute-done.16.refs_3_ = bf16[104,768]{1,0:T(8,128)(2,1)S(1)} collective-permute-done((bf16[104,768]{1,0:T(8,128)(2,1)S(1)}, bf16[104,768]{1,0:T(8,128)(2,1)S(1)}, u32[]{:S(2)}, u32[]{:S(2)}) %collective-permute-start.16) | collective-permute-done | bytes 159776 | tf_op jit(solution)/shard_map/ppermute | solution.py:485
  65.0 1.2 %sort.7 = (bf16[528,768]{1,0:T(8,128)(2,1)S(1)}, s32[4,128]{1,0:T(4,128)S(1)}) custom-call(bf16[104,768]{1,0:T(8,128)(2,1)S(1)} %collective-permute-done.13.refs_0_, bf16[104,768]{1,0:T(8,128)(2,1)S(1)} %collective-permute-done.14.refs_1_, bf16[104,768]{1,0:T(8,128)(2,1)S(1)} %collective-permute-done.15.refs_2_, ...), custom_call_target="tpu_custom_call" | custom-call | tf_op jit(solution)/shard_map/sort/pallas_call | solution.py:419
  66.3 2.3 %collective-permute-done.20.refs_7_ = bf16[528,768]{1,0:T(8,128)(2,1)S(1)} collective-permute-done((bf16[528,768]{1,0:T(8,128)(2,1)S(1)}, bf16[528,768]{1,0:T(8,128)(2,1)S(1)}, u32[]{:S(2)}, u32[]{:S(2)}) %collective-permute-start.20) | collective-permute-done | bytes 811040 | tf_op jit(solution)/shard_map/ppermute | solution.py:501
  69.5 6.3 %score.1 = f32[16,128]{1,0:T(8,128)} custom-call(bf16[528,768]{1,0:T(8,128)(2,1)S(1)} %get-tuple-element.311.refs_0_, bf16[528,768]{1,0:T(8,128)(2,1)S(1)} %get-tuple-element.321.refs_1_, bf16[528,768]{1,0:T(8,128)(2,1)S(1)} %get-tuple-element.331.refs_2_, bf16[528,768]{1,0:T(8,128)(2,1)S(1)} %get-tuple-element.336.refs_3_, ...), custom_call_target="tpu_custom_call" | custom-call | tf_op jit(solution)/shard_map/score/pallas_call | solution.py:419
  75.8 5.4 %all-to-all-start.3 = ((f32[16,1,128]{2,1,0:T(1,128)}), f32[16,1,128]{2,1,0:T(1,128)S(1)}, u32[]{:S(2)}, u32[]{:S(2)}) async-start(f32[16,1,128]{2,1,0:T(1,128)} %bitcast.14), calls=%async_computation.3 | async-start | bytes 16384 | tf_op jit(solution)/shard_map/all_to_all | solution.py:537
  81.2 7.3 %all-to-all-done.3 = f32[16,1,128]{2,1,0:T(1,128)S(1)} async-done(((f32[16,1,128]{2,1,0:T(1,128)}), f32[16,1,128]{2,1,0:T(1,128)S(1)}, u32[]{:S(2)}, u32[]{:S(2)}) %all-to-all-start.3) | async-done | bytes 8224 | tf_op jit(solution)/shard_map/all_to_all | solution.py:537
  (35 shorter events, 8.4 us)
Async XLA Ops:
  4.4 25.9 %collective-permute-start.5 = (bf16[320,768]{1,0:T(8,128)(2,1)S(1)}, bf16[320,768]{1,0:T(8,128)(2,1)S(1)}, u32[]{:S(2)}, u32[]{:S(2)}) collective-permute-start(bf16[320,768]{1,0:T(8,128)(2,1)S(1)} %get-tuple-element.316), channel_id=1, source_target_pairs={{0,2},{1,3},{2,0},{3,1},{4,6},{5,7},{6,4},{7,5},{8,10},{9,11},{10,... | collective-permute-start | bytes 1474568 | tf_op jit(solution)/shard_map/ppermute | solution.py:503
  9.7 23.5 %collective-permute-start.2 = (bf16[104,768]{1,0:T(8,128)(2,1)S(1)}, bf16[104,768]{1,0:T(8,128)(2,1)S(1)}, u32[]{:S(2)}, u32[]{:S(2)}) collective-permute-start(bf16[104,768]{1,0:T(8,128)(2,1)S(1)} %get-tuple-element.308), channel_id=1, source_target_pairs={{0,8},{8,0},{16,24},{24,16},{1,9},{9,1},{17,25},{25,17},{2,10},{10... | collective-permute-start | bytes 479240 | tf_op jit(solution)/shard_map/ppermute | solution.py:480
  11.3 26.8 %collective-permute-start.3 = (bf16[104,768]{1,0:T(8,128)(2,1)S(1)}, bf16[104,768]{1,0:T(8,128)(2,1)S(1)}, u32[]{:S(2)}, u32[]{:S(2)}) collective-permute-start(bf16[104,768]{1,0:T(8,128)(2,1)S(1)} %get-tuple-element.309), channel_id=1, source_target_pairs={{0,16},{8,24},{16,0},{24,8},{1,17},{9,25},{17,1},{25,9},{2,18},{10... | collective-permute-start | bytes 479240 | tf_op jit(solution)/shard_map/ppermute | solution.py:480
  12.8 25.3 %collective-permute-start.4 = (bf16[104,768]{1,0:T(8,128)(2,1)S(1)}, bf16[104,768]{1,0:T(8,128)(2,1)S(1)}, u32[]{:S(2)}, u32[]{:S(2)}) collective-permute-start(bf16[104,768]{1,0:T(8,128)(2,1)S(1)} %get-tuple-element.310), channel_id=1, source_target_pairs={{0,24},{8,16},{16,8},{24,0},{1,25},{9,17},{17,9},{25,1},{2,26},{10... | collective-permute-start | bytes 479240 | tf_op jit(solution)/shard_map/ppermute | solution.py:480
  30.3 9.6 %collective-permute-start.6 = (bf16[104,768]{1,0:T(8,128)(2,1)S(1)}, bf16[104,768]{1,0:T(8,128)(2,1)S(1)}, u32[]{:S(2)}, u32[]{:S(2)}) collective-permute-start(bf16[104,768]{1,0:T(8,128)(2,1)S(1)} %get-tuple-element.317), channel_id=1, source_target_pairs={{0,1},{1,2},{2,3},{3,0},{8,9},{9,10},{10,11},{11,8},{16,17},{17,18... | collective-permute-start | bytes 479240 | tf_op jit(solution)/shard_map/ppermute | solution.py:485
  32.2 11.3 %collective-permute-start.7 = (bf16[104,768]{1,0:T(8,128)(2,1)S(1)}, bf16[104,768]{1,0:T(8,128)(2,1)S(1)}, u32[]{:S(2)}, u32[]{:S(2)}) collective-permute-start(bf16[104,768]{1,0:T(8,128)(2,1)S(1)} %get-tuple-element.318), channel_id=1, source_target_pairs={{0,9},{1,10},{2,11},{3,8},{8,1},{9,2},{10,3},{11,0},{16,25},{17,26... | collective-permute-start | bytes 479240 | tf_op jit(solution)/shard_map/ppermute | solution.py:485
  33.2 12.9 %collective-permute-start.8 = (bf16[104,768]{1,0:T(8,128)(2,1)S(1)}, bf16[104,768]{1,0:T(8,128)(2,1)S(1)}, u32[]{:S(2)}, u32[]{:S(2)}) collective-permute-start(bf16[104,768]{1,0:T(8,128)(2,1)S(1)} %get-tuple-element.319), channel_id=1, source_target_pairs={{0,17},{1,18},{2,19},{3,16},{8,25},{9,26},{10,27},{11,24},{16,1},{... | collective-permute-start | bytes 479240 | tf_op jit(solution)/shard_map/ppermute | solution.py:485
  38.8 10.0 %collective-permute-start.10 = (bf16[104,768]{1,0:T(8,128)(2,1)S(1)}, bf16[104,768]{1,0:T(8,128)(2,1)S(1)}, u32[]{:S(2)}, u32[]{:S(2)}) collective-permute-start(bf16[104,768]{1,0:T(8,128)(2,1)S(1)} %get-tuple-element.328), channel_id=1, source_target_pairs={{0,8},{8,0},{16,24},{24,16},{1,9},{9,1},{17,25},{25,17},{2,10},{10... | collective-permute-start | bytes 479240 | tf_op jit(solution)/shard_map/ppermute | solution.py:480
  39.4 15.2 %collective-permute-start.11 = (bf16[104,768]{1,0:T(8,128)(2,1)S(1)}, bf16[104,768]{1,0:T(8,128)(2,1)S(1)}, u32[]{:S(2)}, u32[]{:S(2)}) collective-permute-start(bf16[104,768]{1,0:T(8,128)(2,1)S(1)} %get-tuple-element.329), channel_id=1, source_target_pairs={{0,16},{8,24},{16,0},{24,8},{1,17},{9,25},{17,1},{25,9},{2,18},{10... | collective-permute-start | bytes 479240 | tf_op jit(solution)/shard_map/ppermute | solution.py:480
  39.9 14.7 %collective-permute-start.12 = (bf16[104,768]{1,0:T(8,128)(2,1)S(1)}, bf16[104,768]{1,0:T(8,128)(2,1)S(1)}, u32[]{:S(2)}, u32[]{:S(2)}) collective-permute-start(bf16[104,768]{1,0:T(8,128)(2,1)S(1)} %get-tuple-element.330), channel_id=1, source_target_pairs={{0,24},{8,16},{16,8},{24,0},{1,25},{9,17},{17,9},{25,1},{2,26},{10... | collective-permute-start | bytes 479240 | tf_op jit(solution)/shard_map/ppermute | solution.py:480
  43.5 17.2 %collective-permute-start.9 = (bf16[104,768]{1,0:T(8,128)(2,1)S(1)}, bf16[104,768]{1,0:T(8,128)(2,1)S(1)}, u32[]{:S(2)}, u32[]{:S(2)}) collective-permute-start(bf16[104,768]{1,0:T(8,128)(2,1)S(1)} %get-tuple-element.320), channel_id=1, source_target_pairs={{0,25},{1,26},{2,27},{3,24},{8,17},{9,18},{10,19},{11,16},{16,9},{... | collective-permute-start | bytes 479240 | tf_op jit(solution)/shard_map/ppermute | solution.py:485
  46.1 15.9 %collective-permute-start.13 = (bf16[104,768]{1,0:T(8,128)(2,1)S(1)}, bf16[104,768]{1,0:T(8,128)(2,1)S(1)}, u32[]{:S(2)}, u32[]{:S(2)}) collective-permute-start(bf16[104,768]{1,0:T(8,128)(2,1)S(1)} %get-tuple-element.332), channel_id=1, source_target_pairs={{0,3},{1,0},{2,1},{3,2},{8,11},{9,8},{10,9},{11,10},{16,19},{17,16... | collective-permute-start | bytes 479240 | tf_op jit(solution)/shard_map/ppermute | solution.py:485
  48.8 13.8 %collective-permute-start.14 = (bf16[104,768]{1,0:T(8,128)(2,1)S(1)}, bf16[104,768]{1,0:T(8,128)(2,1)S(1)}, u32[]{:S(2)}, u32[]{:S(2)}) collective-permute-start(bf16[104,768]{1,0:T(8,128)(2,1)S(1)} %get-tuple-element.333), channel_id=1, source_target_pairs={{0,11},{1,8},{2,9},{3,10},{8,3},{9,0},{10,1},{11,2},{16,27},{17,24... | collective-permute-start | bytes 479240 | tf_op jit(solution)/shard_map/ppermute | solution.py:485
  54.6 8.1 %collective-permute-start.15 = (bf16[104,768]{1,0:T(8,128)(2,1)S(1)}, bf16[104,768]{1,0:T(8,128)(2,1)S(1)}, u32[]{:S(2)}, u32[]{:S(2)}) collective-permute-start(bf16[104,768]{1,0:T(8,128)(2,1)S(1)} %get-tuple-element.334), channel_id=1, source_target_pairs={{0,19},{1,16},{2,17},{3,18},{8,27},{9,24},{10,25},{11,26},{16,3},{... | collective-permute-start | bytes 479240 | tf_op jit(solution)/shard_map/ppermute | solution.py:485
  54.6 10.4 %collective-permute-start.16 = (bf16[104,768]{1,0:T(8,128)(2,1)S(1)}, bf16[104,768]{1,0:T(8,128)(2,1)S(1)}, u32[]{:S(2)}, u32[]{:S(2)}) collective-permute-start(bf16[104,768]{1,0:T(8,128)(2,1)S(1)} %get-tuple-element.335), channel_id=1, source_target_pairs={{0,27},{1,24},{2,25},{3,26},{8,19},{9,16},{10,17},{11,18},{16,11},... | collective-permute-start | bytes 479240 | tf_op jit(solution)/shard_map/ppermute | solution.py:485
  60.7 5.6 %collective-permute-start.17 = (bf16[528,768]{1,0:T(8,128)(2,1)S(1)}, bf16[528,768]{1,0:T(8,128)(2,1)S(1)}, u32[]{:S(2)}, u32[]{:S(2)}) collective-permute-start(bf16[528,768]{1,0:T(8,128)(2,1)S(1)} %get-tuple-element.311.refs_0_), channel_id=1, source_target_pairs={{0,4},{4,0},{1,5},{5,1},{2,6},{6,2},{3,7},{7,3},{8,12},{12,8},{9,1... | collective-permute-start | bytes 2433032 | tf_op jit(solution)/shard_map/ppermute | solution.py:501
  62.0 4.3 %collective-permute-start.18 = (bf16[528,768]{1,0:T(8,128)(2,1)S(1)}, bf16[528,768]{1,0:T(8,128)(2,1)S(1)}, u32[]{:S(2)}, u32[]{:S(2)}) collective-permute-start(bf16[528,768]{1,0:T(8,128)(2,1)S(1)} %get-tuple-element.321.refs_1_), channel_id=1, source_target_pairs={{0,4},{4,0},{1,5},{5,1},{2,6},{6,2},{3,7},{7,3},{8,12},{12,8},{9,1... | collective-permute-start | bytes 2433032 | tf_op jit(solution)/shard_map/ppermute | solution.py:501
  62.6 3.7 %collective-permute-start.19 = (bf16[528,768]{1,0:T(8,128)(2,1)S(1)}, bf16[528,768]{1,0:T(8,128)(2,1)S(1)}, u32[]{:S(2)}, u32[]{:S(2)}) collective-permute-start(bf16[528,768]{1,0:T(8,128)(2,1)S(1)} %get-tuple-element.331.refs_2_), channel_id=1, source_target_pairs={{0,4},{4,0},{1,5},{5,1},{2,6},{6,2},{3,7},{7,3},{8,12},{12,8},{9,1... | collective-permute-start | bytes 2433032 | tf_op jit(solution)/shard_map/ppermute | solution.py:501
  66.2 2.4 %collective-permute-start.20 = (bf16[528,768]{1,0:T(8,128)(2,1)S(1)}, bf16[528,768]{1,0:T(8,128)(2,1)S(1)}, u32[]{:S(2)}, u32[]{:S(2)}) collective-permute-start(bf16[528,768]{1,0:T(8,128)(2,1)S(1)} %get-tuple-element.336.refs_3_), channel_id=1, source_target_pairs={{0,4},{4,0},{1,5},{5,1},{2,6},{6,2},{3,7},{7,3},{8,12},{12,8},{9,1... | collective-permute-start | bytes 2433032 | tf_op jit(solution)/shard_map/ppermute | solution.py:501
  68.6 0.9 copy-start.2
  69.5 18.9 %copy-start.4 = (s32[1024]{0:T(1024)S(1)}, s32[1024]{0:T(1024)}, u32[]{:S(2)}) copy-start(s32[1024]{0:T(1024)} %param.9) | copy-start | bytes 12292
  69.5 21.2 %copy-start = (f32[1024,768]{1,0:T(8,128)S(1)}, f32[1024,768]{1,0:T(8,128)}, u32[]{:S(2)}) copy-start(f32[1024,768]{1,0:T(8,128)} %emb_ref.1) | copy-start | bytes 9437188
  75.8 12.6 %all-to-all-start.3 = ((f32[16,1,128]{2,1,0:T(1,128)}), f32[16,1,128]{2,1,0:T(1,128)S(1)}, u32[]{:S(2)}, u32[]{:S(2)}) async-start(f32[16,1,128]{2,1,0:T(1,128)} %bitcast.14), calls=%async_computation.3 | async-start | bytes 16384 | tf_op jit(solution)/shard_map/all_to_all | solution.py:537

commit v7 on v6

--- a/solution.py
+++ b/solution.py
@@ -15,7 +15,7 @@
 sharpness = 30.0
 epsilon = 1e-06
 
-VMEM_BYTES = 48 * 1024 * 1024
+MIB = 1024 * 1024
 LANES = 128
 FLAG = LANES - 1
 LOW = LANES // 2
@@ -405,7 +405,7 @@
     lanes = ret_ref.shape[1]
     values = ret_ref[...]
     flag = jnp.max(values[:, lanes - 1 :], axis=0, keepdims=True)
-    flag_ref[...] = jnp.broadcast_to(flag, flag_ref.shape).astype(jnp.int32)
+    flag_ref[0, 0] = jnp.sum(flag).astype(jnp.int32)
     chip = ids_ref[...] & (chips - 1)
     rank = rank_ref[...].astype(jnp.int32)
     at_rank = jnp.where(iota((lanes, rows), 0) == rank, 1.0, 0.0)
@@ -414,14 +414,14 @@
     out_ref[...] = jnp.log(1.0 + total)
 
 
-def call(kernel, name, out_shape, inputs, **options):
+def call(kernel, name, out_shape, inputs, vmem_mib=12, **options):
     vmem = pl.BlockSpec(memory_space=pltpu.VMEM)
     return pl.pallas_call(
         kernel,
         out_shape=out_shape,
         in_specs=[vmem] * len(inputs),
-        out_specs=jax.tree.map(lambda _: vmem, out_shape),
-        compiler_params=pltpu.CompilerParams(vmem_limit_bytes=VMEM_BYTES),
+        out_specs=options.pop("out_specs", jax.tree.map(lambda _: vmem, out_shape)),
+        compiler_params=pltpu.CompilerParams(vmem_limit_bytes=vmem_mib * MIB),
         name=name,
         **options,
     )(*inputs)
@@ -456,15 +456,20 @@
         [embeddings, ids_row],
     )
 
-    def pack(shift, count, step):
-        return call(
-            functools.partial(
-                pack_kernel, [shift * PLACES + index * step for index in range(count)]
-            ),
-            "pack",
-            [shape((step, width), jnp.bfloat16)] * count,
-            [aug, slots],
-        )
+    near_and_far = [0, *order[1:]]
+    blocks = call(
+        functools.partial(
+            pack_kernel,
+            [shift * PLACES + side * cap for shift in near_and_far for side in range(across)],
+        ),
+        "pack",
+        [shape((cap, width), jnp.bfloat16)] * (across * len(near_and_far)),
+        [aug, slots],
+    )
+    packed = {
+        shift: blocks[place * across : (place + 1) * across]
+        for place, shift in enumerate(near_and_far)
+    }
 
     def along(shift):
         return [(z, (z + shift) % tiles) for z in range(tiles)]
@@ -501,15 +506,13 @@
         other[shift] = lax.ppermute(own[shift], "core", swap)
 
     pooled = lax.ppermute(pool_rows, "tile", along(order[0]))
-    near = send_across(pack(0, across, cap))
+    near = send_across(packed[0])
     finish(0, near)
-    packed = {shift: pack(shift, across, cap) for shift in order[1:]}
-    ready = [block for shift in order[1:] for block in packed[shift]]
     regrouped = call(
         functools.partial(regroup_kernel, size),
         "regroup",
         [shape((cap, width), jnp.bfloat16)] * across,
-        [after(pooled, *near, *ready)],
+        [after(pooled, *near)],
     )
     passed = send_across(regrouped)
     finish(order[0], passed)
@@ -525,6 +528,7 @@
         "score",
         shape((chips, lanes), jnp.float32),
         [*own, *other, *places],
+        vmem_mib=26,
         scratch_shapes=[
             pltpu.VMEM((2 * tiles * space + LEFT + RIGHT, width), jnp.bfloat16),
             pltpu.VMEM((labels, room_own, LANES), jnp.float32),
@@ -538,11 +542,15 @@
     result, flag = call(
         functools.partial(unpack_kernel, chips),
         "unpack",
-        [shape((1, rows), jnp.float32), shape((8, LANES), jnp.int32)],
+        [shape((1, rows), jnp.float32), shape((1, 1), jnp.int32)],
         [returned, ids_row, rank],
+        out_specs=[
+            pl.BlockSpec(memory_space=pltpu.VMEM),
+            pl.BlockSpec(memory_space=pltpu.SMEM),
+        ],
     )
     return lax.cond(
-        flag[0, 0] > 0,
+        flag.reshape(()) > 0,
         lambda: general_plan(embeddings, cluster_ids),
         lambda: result.reshape(rows),
     )

time: 91.1 us -> 87.9 us (0.965)
  starting transfers between devices: 31.9 us -> 34.1 us
  waiting for transfers between devices: 35.6 us -> 33.4 us
  Pallas kernels: 20.9 us -> 19.3 us
  local copies, waits for them, and re-layouts: 1.48 us -> 0.01 us
    ppermute x6, waiting for transfers between devices: 4.19 us -> 0.02 us  [send_across(): lax.ppermute(blocks[side], 'chip', over(side))]
    ppermute x8, waiting for transfers between devices: 6.02 us -> 8.76 us  [send_far(): return lax.ppermute(blocks[side], ('chip', 'tile'), route)]
    pallas_call x11 -> x9, Pallas kernels: 20.9 us -> 19.3 us  [call(): pl.pallas_call(kernel, out_shape=out_shape, in_specs=[vmem] * len(inputs)...]
    ppermute x6, starting transfers between devices: 7.11 us -> 8.13 us  [send_across(): lax.ppermute(blocks[side], 'chip', over(side))]
  transfers between devices with their start and end apart: 20 -> 20, of which waited for: 7 -> 8; matrix products, arithmetic and copies ran while one was open for 0% -> 0% of each run, Pallas kernels for 10% -> 10%
where the time goes in v7:
time: 87.9 us; the launch traced here: 87.7 us
  starting transfers between devices  34.1 us (39%)
  waiting for transfers between devices  33.4 us (38%)
  Pallas kernels  19.3 us (22%)
  between operations  0.96 us (1%)
    pallas_call x9, Pallas kernels, call(): pl.pallas_call(kernel, out_shape=out_shape, in_specs=[vmem] * len(inputs)...  19.3 us
    ppermute x8, starting transfers between devices, send_far(): return lax.ppermute(blocks[side], ('chip', 'tile'), route)  15.4 us
    ppermute x1, waiting for transfers between devices, body(): pooled = lax.ppermute(pool_rows, 'tile', along(order[0]))  15 us
    ppermute x8, waiting for transfers between devices, send_far(): return lax.ppermute(blocks[side], ('chip', 'tile'), route)  8.76 us
    ppermute x6, starting transfers between devices, send_across(): lax.ppermute(blocks[side], 'chip', over(side))  8.13 us
    all_to_all x1, waiting for transfers between devices, body(): lax.all_to_all(totals, ('chip', 'tile'), split_axis=0, concat_axis=0, til...  7.26 us
    all_to_all x1, starting transfers between devices, body(): lax.all_to_all(totals, ('chip', 'tile'), split_axis=0, concat_axis=0, til...  5.74 us
    ppermute x1, starting transfers between devices, body(): pooled = lax.ppermute(pool_rows, 'tile', along(order[0]))  4.1 us
  transfers between devices with their start and end apart: 20, of which 8 were waited for; matrix products, arithmetic and copies ran while one was open for 0% of the time, Pallas kernels for 10%

profile of v7, /device:TPU:0, one launch (start us, length us, event | category | flops | bytes accessed | tf_op | source)
XLA Modules:
  0.0 87.7 jit_solution(12289218366101977884)
XLA Ops:
  0.0 4.4 %plan.1 = (bf16[320,768]{1,0:T(8,128)(2,1)S(1)}, bf16[1152,768]{1,0:T(8,128)(2,1)S(1)}, s32[1,1152]{1,0:T(1,128)S(1)}, f32[1,1024]{1,0:T(1,128)S(1)}) custom-call(f32[1024,768]{1,0:T(8,128)} %emb_ref.1, s32[1,1024]{1,0:T(1,128)} %bitcast.74), custom_call_target="tpu_custom_call" | custom-call | tf_op jit(solution)/shard_map/plan/pallas_call | solution.py:419
  4.4 4.1 %collective-permute-start.5 = (bf16[320,768]{1,0:T(8,128)(2,1)S(1)}, bf16[320,768]{1,0:T(8,128)(2,1)S(1)}, u32[]{:S(2)}, u32[]{:S(2)}) collective-permute-start(bf16[320,768]{1,0:T(8,128)(2,1)S(1)} %get-tuple-element.316), channel_id=1, source_target_pairs={{0,2},{1,3},{2,0},{3,1},{4,6},{5,7},{6,4},{7,5},{8,10},{9,11},{10,... | collective-permute-start | bytes 1474568 | tf_op jit(solution)/shard_map/ppermute | solution.py:508
  8.5 3.2 %pack.1 = (bf16[104,768]{1,0:T(8,128)(2,1)S(1)}, bf16[104,768]{1,0:T(8,128)(2,1)S(1)}, bf16[104,768]{1,0:T(8,128)(2,1)S(1)}, bf16[104,768]{1,0:T(8,128)(2,1)S(1)...) custom-call(bf16[1152,768]{1,0:T(8,128)(2,1)S(1)} %get-tuple-element, ...), custom_call_target="tpu_custom_call" | custom-call | tf_op jit(solution)/shard_map/pack/pallas_call | solution.py:419
  11.7 1.6 %collective-permute-start.2 = (bf16[104,768]{1,0:T(8,128)(2,1)S(1)}, bf16[104,768]{1,0:T(8,128)(2,1)S(1)}, u32[]{:S(2)}, u32[]{:S(2)}) collective-permute-start(bf16[104,768]{1,0:T(8,128)(2,1)S(1)} %get-tuple-element.308), channel_id=1, source_target_pairs={{0,8},{8,0},{16,24},{24,16},{1,9},{9,1},{17,25},{25,17},{2,10},{10... | collective-permute-start | bytes 479240 | tf_op jit(solution)/shard_map/ppermute | solution.py:485
  13.3 1.5 %collective-permute-start.3 = (bf16[104,768]{1,0:T(8,128)(2,1)S(1)}, bf16[104,768]{1,0:T(8,128)(2,1)S(1)}, u32[]{:S(2)}, u32[]{:S(2)}) collective-permute-start(bf16[104,768]{1,0:T(8,128)(2,1)S(1)} %get-tuple-element.309), channel_id=1, source_target_pairs={{0,16},{8,24},{16,0},{24,8},{1,17},{9,25},{17,1},{25,9},{2,18},{10... | collective-permute-start | bytes 479240 | tf_op jit(solution)/shard_map/ppermute | solution.py:485
  15.3 15.0 %collective-permute-done.5.pool_ref = bf16[320,768]{1,0:T(8,128)(2,1)S(1)} collective-permute-done((bf16[320,768]{1,0:T(8,128)(2,1)S(1)}, bf16[320,768]{1,0:T(8,128)(2,1)S(1)}, u32[]{:S(2)}, u32[]{:S(2)}) %collective-permute-start.5) | collective-permute-done | bytes 491552 | tf_op jit(solution)/shard_map/ppermute | solution.py:508
  32.0 5.0 %collective-permute-start.8 = (bf16[104,768]{1,0:T(8,128)(2,1)S(1)}, bf16[104,768]{1,0:T(8,128)(2,1)S(1)}, u32[]{:S(2)}, u32[]{:S(2)}) collective-permute-start(bf16[104,768]{1,0:T(8,128)(2,1)S(1)} %get-tuple-element.319), channel_id=1, source_target_pairs={{0,17},{1,18},{2,19},{3,16},{8,25},{9,26},{10,27},{11,24},{16,1},{... | collective-permute-start | bytes 479240 | tf_op jit(solution)/shard_map/ppermute | solution.py:490
  37.8 1.6 %collective-permute-start.10 = (bf16[104,768]{1,0:T(8,128)(2,1)S(1)}, bf16[104,768]{1,0:T(8,128)(2,1)S(1)}, u32[]{:S(2)}, u32[]{:S(2)}) collective-permute-start(bf16[104,768]{1,0:T(8,128)(2,1)S(1)} %get-tuple-element.324), channel_id=1, source_target_pairs={{0,8},{8,0},{16,24},{24,16},{1,9},{9,1},{17,25},{25,17},{2,10},{10... | collective-permute-start | bytes 479240 | tf_op jit(solution)/shard_map/ppermute | solution.py:485
  39.4 1.5 %collective-permute-start.11 = (bf16[104,768]{1,0:T(8,128)(2,1)S(1)}, bf16[104,768]{1,0:T(8,128)(2,1)S(1)}, u32[]{:S(2)}, u32[]{:S(2)}) collective-permute-start(bf16[104,768]{1,0:T(8,128)(2,1)S(1)} %get-tuple-element.325), channel_id=1, source_target_pairs={{0,16},{8,24},{16,0},{24,8},{1,17},{9,25},{17,1},{25,9},{2,18},{10... | collective-permute-start | bytes 479240 | tf_op jit(solution)/shard_map/ppermute | solution.py:485
  40.9 2.6 %collective-permute-done.7.refs_1_ = bf16[104,768]{1,0:T(8,128)(2,1)S(1)} collective-permute-done((bf16[104,768]{1,0:T(8,128)(2,1)S(1)}, bf16[104,768]{1,0:T(8,128)(2,1)S(1)}, u32[]{:S(2)}, u32[]{:S(2)}) %collective-permute-start.7) | collective-permute-done | bytes 159776 | tf_op jit(solution)/shard_map/ppermute | solution.py:490
  43.5 1.4 %collective-permute-start.12 = (bf16[104,768]{1,0:T(8,128)(2,1)S(1)}, bf16[104,768]{1,0:T(8,128)(2,1)S(1)}, u32[]{:S(2)}, u32[]{:S(2)}) collective-permute-start(bf16[104,768]{1,0:T(8,128)(2,1)S(1)} %get-tuple-element.326), channel_id=1, source_target_pairs={{0,24},{8,16},{16,8},{24,0},{1,25},{9,17},{17,9},{25,1},{2,26},{10... | collective-permute-start | bytes 479240 | tf_op jit(solution)/shard_map/ppermute | solution.py:485
  45.0 2.3 %collective-permute-done.8.refs_2_ = bf16[104,768]{1,0:T(8,128)(2,1)S(1)} collective-permute-done((bf16[104,768]{1,0:T(8,128)(2,1)S(1)}, bf16[104,768]{1,0:T(8,128)(2,1)S(1)}, u32[]{:S(2)}, u32[]{:S(2)}) %collective-permute-start.8) | collective-permute-done | bytes 159776 | tf_op jit(solution)/shard_map/ppermute | solution.py:490
  47.2 1.7 %collective-permute-start.13 = (bf16[104,768]{1,0:T(8,128)(2,1)S(1)}, bf16[104,768]{1,0:T(8,128)(2,1)S(1)}, u32[]{:S(2)}, u32[]{:S(2)}) collective-permute-start(bf16[104,768]{1,0:T(8,128)(2,1)S(1)} %get-tuple-element.332), channel_id=1, source_target_pairs={{0,3},{1,0},{2,1},{3,2},{8,11},{9,8},{10,9},{11,10},{16,19},{17,16... | collective-permute-start | bytes 479240 | tf_op jit(solution)/shard_map/ppermute | solution.py:490
  48.9 2.5 %collective-permute-done.9.refs_3_ = bf16[104,768]{1,0:T(8,128)(2,1)S(1)} collective-permute-done((bf16[104,768]{1,0:T(8,128)(2,1)S(1)}, bf16[104,768]{1,0:T(8,128)(2,1)S(1)}, u32[]{:S(2)}, u32[]{:S(2)}) %collective-permute-start.9) | collective-permute-done | bytes 159776 | tf_op jit(solution)/shard_map/ppermute | solution.py:490
  51.4 3.1 %collective-permute-start.14 = (bf16[104,768]{1,0:T(8,128)(2,1)S(1)}, bf16[104,768]{1,0:T(8,128)(2,1)S(1)}, u32[]{:S(2)}, u32[]{:S(2)}) collective-permute-start(bf16[104,768]{1,0:T(8,128)(2,1)S(1)} %get-tuple-element.333), channel_id=1, source_target_pairs={{0,11},{1,8},{2,9},{3,10},{8,3},{9,0},{10,1},{11,2},{16,27},{17,24... | collective-permute-start | bytes 479240 | tf_op jit(solution)/shard_map/ppermute | solution.py:490
  54.5 3.7 %collective-permute-start.16 = (bf16[104,768]{1,0:T(8,128)(2,1)S(1)}, bf16[104,768]{1,0:T(8,128)(2,1)S(1)}, u32[]{:S(2)}, u32[]{:S(2)}) collective-permute-start(bf16[104,768]{1,0:T(8,128)(2,1)S(1)} %get-tuple-element.335), channel_id=1, source_target_pairs={{0,27},{1,24},{2,25},{3,26},{8,19},{9,16},{10,17},{11,18},{16,11},... | collective-permute-start | bytes 479240 | tf_op jit(solution)/shard_map/ppermute | solution.py:490
  58.3 1.2 %sort.4 = (bf16[528,768]{1,0:T(8,128)(2,1)S(1)}, s32[4,128]{1,0:T(4,128)S(1)}) custom-call(bf16[104,768]{1,0:T(8,128)(2,1)S(1)} %get-tuple-element.307.refs_0_, bf16[104,768]{1,0:T(8,128)(2,1)S(1)} %collective-permute-done.2.refs_1_, bf16[104,768]{1,0:T(8,128)(2,1)S(1)} %collective-permute-done.3.refs_2_, bf16[104,768]{1,0:T(8,128)(2,1)S(1)} %collective-permute-done.4.refs_3_), custom_call_target="tpu_custom_call" | custom-call | tf_op jit(solution)/shard_map/sort/pallas_call | solution.py:419
  59.6 1.2 %sort.5 = (bf16[528,768]{1,0:T(8,128)(2,1)S(1)}, s32[4,128]{1,0:T(4,128)S(1)}) custom-call(bf16[104,768]{1,0:T(8,128)(2,1)S(1)} %collective-permute-done.6.refs_0_, bf16[104,768]{1,0:T(8,128)(2,1)S(1)} %collective-permute-done.7.refs_1_, bf16[104,768]{1,0:T(8,128)(2,1)S(1)} %collective-permute-done.8.refs_2_, bf16[104,768]{1,0:T(8,128)(2,1)S(1)} %collective-permute-done.9.refs_3_), custom_call_target="tpu_custom_call" | custom-call | tf_op jit(solution)/shard_map/sort/pallas_call | solution.py:419
  60.9 1.2 %sort.6 = (bf16[528,768]{1,0:T(8,128)(2,1)S(1)}, s32[4,128]{1,0:T(4,128)S(1)}) custom-call(bf16[104,768]{1,0:T(8,128)(2,1)S(1)} %get-tuple-element.323.refs_0_, bf16[104,768]{1,0:T(8,128)(2,1)S(1)} %collective-permute-done.10.refs_1_, bf16[104,768]{1,0:T(8,128)(2,1)S(1)} %collective-permute-done.11.refs_2_, bf16[104,768]{1,0:T(8,128)(2,1)S(1)} %collective-permute-done.12.refs_3_), custom_call_target="tpu_custom_call" | custom-call | tf_op jit(solution)/shard_map/sort/pallas_call | solution.py:419
  62.8 1.4 %collective-permute-done.16.refs_3_ = bf16[104,768]{1,0:T(8,128)(2,1)S(1)} collective-permute-done((bf16[104,768]{1,0:T(8,128)(2,1)S(1)}, bf16[104,768]{1,0:T(8,128)(2,1)S(1)}, u32[]{:S(2)}, u32[]{:S(2)}) %collective-permute-start.16) | collective-permute-done | bytes 159776 | tf_op jit(solution)/shard_map/ppermute | solution.py:490
  65.8 2.0 %collective-permute-done.20.refs_7_ = bf16[528,768]{1,0:T(8,128)(2,1)S(1)} collective-permute-done((bf16[528,768]{1,0:T(8,128)(2,1)S(1)}, bf16[528,768]{1,0:T(8,128)(2,1)S(1)}, u32[]{:S(2)}, u32[]{:S(2)}) %collective-permute-start.20) | collective-permute-done | bytes 811040 | tf_op jit(solution)/shard_map/ppermute | solution.py:506
  67.9 5.0 %score.1 = f32[16,128]{1,0:T(8,128)} custom-call(bf16[528,768]{1,0:T(8,128)(2,1)S(1)} %get-tuple-element.311.refs_0_, bf16[528,768]{1,0:T(8,128)(2,1)S(1)} %get-tuple-element.321.refs_1_, bf16[528,768]{1,0:T(8,128)(2,1)S(1)} %get-tuple-element.327.refs_2_, bf16[528,768]{1,0:T(8,128)(2,1)S(1)} %get-tuple-element.336.refs_3_, ...), custom_call_target="tpu_custom_call" | custom-call | tf_op jit(solution)/shard_map/score/pallas_call | solution.py:419
  72.9 5.7 %all-to-all-start.3 = ((f32[16,1,128]{2,1,0:T(1,128)}), f32[16,1,128]{2,1,0:T(1,128)S(1)}, u32[]{:S(2)}, u32[]{:S(2)}) async-start(f32[16,1,128]{2,1,0:T(1,128)} %bitcast.14), calls=%async_computation.3 | async-start | bytes 16384 | tf_op jit(solution)/shard_map/all_to_all | solution.py:541
  78.6 7.3 %all-to-all-done.3 = f32[16,1,128]{2,1,0:T(1,128)S(1)} async-done(((f32[16,1,128]{2,1,0:T(1,128)}), f32[16,1,128]{2,1,0:T(1,128)S(1)}, u32[]{:S(2)}, u32[]{:S(2)}) %all-to-all-start.3) | async-done | bytes 8224 | tf_op jit(solution)/shard_map/all_to_all | solution.py:541
  (30 shorter events, 6.4 us)
Async XLA Ops:
  4.4 25.9 %collective-permute-start.5 = (bf16[320,768]{1,0:T(8,128)(2,1)S(1)}, bf16[320,768]{1,0:T(8,128)(2,1)S(1)}, u32[]{:S(2)}, u32[]{:S(2)}) collective-permute-start(bf16[320,768]{1,0:T(8,128)(2,1)S(1)} %get-tuple-element.316), channel_id=1, source_target_pairs={{0,2},{1,3},{2,0},{3,1},{4,6},{5,7},{6,4},{7,5},{8,10},{9,11},{10,... | collective-permute-start | bytes 1474568 | tf_op jit(solution)/shard_map/ppermute | solution.py:508
  11.7 20.2 %collective-permute-start.2 = (bf16[104,768]{1,0:T(8,128)(2,1)S(1)}, bf16[104,768]{1,0:T(8,128)(2,1)S(1)}, u32[]{:S(2)}, u32[]{:S(2)}) collective-permute-start(bf16[104,768]{1,0:T(8,128)(2,1)S(1)} %get-tuple-element.308), channel_id=1, source_target_pairs={{0,8},{8,0},{16,24},{24,16},{1,9},{9,1},{17,25},{25,17},{2,10},{10... | collective-permute-start | bytes 479240 | tf_op jit(solution)/shard_map/ppermute | solution.py:485
  13.3 18.7 %collective-permute-start.3 = (bf16[104,768]{1,0:T(8,128)(2,1)S(1)}, bf16[104,768]{1,0:T(8,128)(2,1)S(1)}, u32[]{:S(2)}, u32[]{:S(2)}) collective-permute-start(bf16[104,768]{1,0:T(8,128)(2,1)S(1)} %get-tuple-element.309), channel_id=1, source_target_pairs={{0,16},{8,24},{16,0},{24,8},{1,17},{9,25},{17,1},{25,9},{2,18},{10... | collective-permute-start | bytes 479240 | tf_op jit(solution)/shard_map/ppermute | solution.py:485
  14.8 17.2 %collective-permute-start.4 = (bf16[104,768]{1,0:T(8,128)(2,1)S(1)}, bf16[104,768]{1,0:T(8,128)(2,1)S(1)}, u32[]{:S(2)}, u32[]{:S(2)}) collective-permute-start(bf16[104,768]{1,0:T(8,128)(2,1)S(1)} %get-tuple-element.310), channel_id=1, source_target_pairs={{0,24},{8,16},{16,8},{24,0},{1,25},{9,17},{17,9},{25,1},{2,26},{10... | collective-permute-start | bytes 479240 | tf_op jit(solution)/shard_map/ppermute | solution.py:485
  30.3 9.1 %collective-permute-start.6 = (bf16[104,768]{1,0:T(8,128)(2,1)S(1)}, bf16[104,768]{1,0:T(8,128)(2,1)S(1)}, u32[]{:S(2)}, u32[]{:S(2)}) collective-permute-start(bf16[104,768]{1,0:T(8,128)(2,1)S(1)} %get-tuple-element.317), channel_id=1, source_target_pairs={{0,1},{1,2},{2,3},{3,0},{8,9},{9,10},{10,11},{11,8},{16,17},{17,18... | collective-permute-start | bytes 479240 | tf_op jit(solution)/shard_map/ppermute | solution.py:490
  31.0 12.5 %collective-permute-start.7 = (bf16[104,768]{1,0:T(8,128)(2,1)S(1)}, bf16[104,768]{1,0:T(8,128)(2,1)S(1)}, u32[]{:S(2)}, u32[]{:S(2)}) collective-permute-start(bf16[104,768]{1,0:T(8,128)(2,1)S(1)} %get-tuple-element.318), channel_id=1, source_target_pairs={{0,9},{1,10},{2,11},{3,8},{8,1},{9,2},{10,3},{11,0},{16,25},{17,26... | collective-permute-start | bytes 479240 | tf_op jit(solution)/shard_map/ppermute | solution.py:490
  32.0 15.3 %collective-permute-start.8 = (bf16[104,768]{1,0:T(8,128)(2,1)S(1)}, bf16[104,768]{1,0:T(8,128)(2,1)S(1)}, u32[]{:S(2)}, u32[]{:S(2)}) collective-permute-start(bf16[104,768]{1,0:T(8,128)(2,1)S(1)} %get-tuple-element.319), channel_id=1, source_target_pairs={{0,17},{1,18},{2,19},{3,16},{8,25},{9,26},{10,27},{11,24},{16,1},{... | collective-permute-start | bytes 479240 | tf_op jit(solution)/shard_map/ppermute | solution.py:490
  36.9 14.5 %collective-permute-start.9 = (bf16[104,768]{1,0:T(8,128)(2,1)S(1)}, bf16[104,768]{1,0:T(8,128)(2,1)S(1)}, u32[]{:S(2)}, u32[]{:S(2)}) collective-permute-start(bf16[104,768]{1,0:T(8,128)(2,1)S(1)} %get-tuple-element.320), channel_id=1, source_target_pairs={{0,25},{1,26},{2,27},{3,24},{8,17},{9,18},{10,19},{11,16},{16,9},{... | collective-permute-start | bytes 479240 | tf_op jit(solution)/shard_map/ppermute | solution.py:490
  37.8 16.7 %collective-permute-start.10 = (bf16[104,768]{1,0:T(8,128)(2,1)S(1)}, bf16[104,768]{1,0:T(8,128)(2,1)S(1)}, u32[]{:S(2)}, u32[]{:S(2)}) collective-permute-start(bf16[104,768]{1,0:T(8,128)(2,1)S(1)} %get-tuple-element.324), channel_id=1, source_target_pairs={{0,8},{8,0},{16,24},{24,16},{1,9},{9,1},{17,25},{25,17},{2,10},{10... | collective-permute-start | bytes 479240 | tf_op jit(solution)/shard_map/ppermute | solution.py:485
  39.4 15.1 %collective-permute-start.11 = (bf16[104,768]{1,0:T(8,128)(2,1)S(1)}, bf16[104,768]{1,0:T(8,128)(2,1)S(1)}, u32[]{:S(2)}, u32[]{:S(2)}) collective-permute-start(bf16[104,768]{1,0:T(8,128)(2,1)S(1)} %get-tuple-element.325), channel_id=1, source_target_pairs={{0,16},{8,24},{16,0},{24,8},{1,17},{9,25},{17,1},{25,9},{2,18},{10... | collective-permute-start | bytes 479240 | tf_op jit(solution)/shard_map/ppermute | solution.py:485
  43.5 17.3 %collective-permute-start.12 = (bf16[104,768]{1,0:T(8,128)(2,1)S(1)}, bf16[104,768]{1,0:T(8,128)(2,1)S(1)}, u32[]{:S(2)}, u32[]{:S(2)}) collective-permute-start(bf16[104,768]{1,0:T(8,128)(2,1)S(1)} %get-tuple-element.326), channel_id=1, source_target_pairs={{0,24},{8,16},{16,8},{24,0},{1,25},{9,17},{17,9},{25,1},{2,26},{10... | collective-permute-start | bytes 479240 | tf_op jit(solution)/shard_map/ppermute | solution.py:485
  47.2 14.9 %collective-permute-start.13 = (bf16[104,768]{1,0:T(8,128)(2,1)S(1)}, bf16[104,768]{1,0:T(8,128)(2,1)S(1)}, u32[]{:S(2)}, u32[]{:S(2)}) collective-permute-start(bf16[104,768]{1,0:T(8,128)(2,1)S(1)} %get-tuple-element.332), channel_id=1, source_target_pairs={{0,3},{1,0},{2,1},{3,2},{8,11},{9,8},{10,9},{11,10},{16,19},{17,16... | collective-permute-start | bytes 479240 | tf_op jit(solution)/shard_map/ppermute | solution.py:490
  51.4 11.3 %collective-permute-start.14 = (bf16[104,768]{1,0:T(8,128)(2,1)S(1)}, bf16[104,768]{1,0:T(8,128)(2,1)S(1)}, u32[]{:S(2)}, u32[]{:S(2)}) collective-permute-start(bf16[104,768]{1,0:T(8,128)(2,1)S(1)} %get-tuple-element.333), channel_id=1, source_target_pairs={{0,11},{1,8},{2,9},{3,10},{8,3},{9,0},{10,1},{11,2},{16,27},{17,24... | collective-permute-start | bytes 479240 | tf_op jit(solution)/shard_map/ppermute | solution.py:490
  54.5 8.3 %collective-permute-start.15 = (bf16[104,768]{1,0:T(8,128)(2,1)S(1)}, bf16[104,768]{1,0:T(8,128)(2,1)S(1)}, u32[]{:S(2)}, u32[]{:S(2)}) collective-permute-start(bf16[104,768]{1,0:T(8,128)(2,1)S(1)} %get-tuple-element.334), channel_id=1, source_target_pairs={{0,19},{1,16},{2,17},{3,18},{8,27},{9,24},{10,25},{11,26},{16,3},{... | collective-permute-start | bytes 479240 | tf_op jit(solution)/shard_map/ppermute | solution.py:490
  54.5 9.7 %collective-permute-start.16 = (bf16[104,768]{1,0:T(8,128)(2,1)S(1)}, bf16[104,768]{1,0:T(8,128)(2,1)S(1)}, u32[]{:S(2)}, u32[]{:S(2)}) collective-permute-start(bf16[104,768]{1,0:T(8,128)(2,1)S(1)} %get-tuple-element.335), channel_id=1, source_target_pairs={{0,27},{1,24},{2,25},{3,26},{8,19},{9,16},{10,17},{11,18},{16,11},... | collective-permute-start | bytes 479240 | tf_op jit(solution)/shard_map/ppermute | solution.py:490
  60.8 4.7 %collective-permute-start.17 = (bf16[528,768]{1,0:T(8,128)(2,1)S(1)}, bf16[528,768]{1,0:T(8,128)(2,1)S(1)}, u32[]{:S(2)}, u32[]{:S(2)}) collective-permute-start(bf16[528,768]{1,0:T(8,128)(2,1)S(1)} %get-tuple-element.311.refs_0_), channel_id=1, source_target_pairs={{0,4},{4,0},{1,5},{5,1},{2,6},{6,2},{3,7},{7,3},{8,12},{12,8},{9,1... | collective-permute-start | bytes 2433032 | tf_op jit(solution)/shard_map/ppermute | solution.py:506
  62.2 3.4 %collective-permute-start.19 = (bf16[528,768]{1,0:T(8,128)(2,1)S(1)}, bf16[528,768]{1,0:T(8,128)(2,1)S(1)}, u32[]{:S(2)}, u32[]{:S(2)}) collective-permute-start(bf16[528,768]{1,0:T(8,128)(2,1)S(1)} %get-tuple-element.327.refs_2_), channel_id=1, source_target_pairs={{0,4},{4,0},{1,5},{5,1},{2,6},{6,2},{3,7},{7,3},{8,12},{12,8},{9,1... | collective-permute-start | bytes 2433032 | tf_op jit(solution)/shard_map/ppermute | solution.py:506
  62.7 3.1 %collective-permute-start.18 = (bf16[528,768]{1,0:T(8,128)(2,1)S(1)}, bf16[528,768]{1,0:T(8,128)(2,1)S(1)}, u32[]{:S(2)}, u32[]{:S(2)}) collective-permute-start(bf16[528,768]{1,0:T(8,128)(2,1)S(1)} %get-tuple-element.321.refs_1_), channel_id=1, source_target_pairs={{0,4},{4,0},{1,5},{5,1},{2,6},{6,2},{3,7},{7,3},{8,12},{12,8},{9,1... | collective-permute-start | bytes 2433032 | tf_op jit(solution)/shard_map/ppermute | solution.py:506
  65.5 2.4 %collective-permute-start.20 = (bf16[528,768]{1,0:T(8,128)(2,1)S(1)}, bf16[528,768]{1,0:T(8,128)(2,1)S(1)}, u32[]{:S(2)}, u32[]{:S(2)}) collective-permute-start(bf16[528,768]{1,0:T(8,128)(2,1)S(1)} %get-tuple-element.336.refs_3_), channel_id=1, source_target_pairs={{0,4},{4,0},{1,5},{5,1},{2,6},{6,2},{3,7},{7,3},{8,12},{12,8},{9,1... | collective-permute-start | bytes 2433032 | tf_op jit(solution)/shard_map/ppermute | solution.py:506
  67.8 18.0 %copy-start.3 = (s32[1024]{0:T(1024)S(1)}, s32[1024]{0:T(1024)}, u32[]{:S(2)}) copy-start(s32[1024]{0:T(1024)} %param.9) | copy-start | bytes 12292
  67.8 19.7 %copy-start = (f32[1024,768]{1,0:T(8,128)S(1)}, f32[1024,768]{1,0:T(8,128)}, u32[]{:S(2)}) copy-start(f32[1024,768]{1,0:T(8,128)} %emb_ref.1) | copy-start | bytes 9437188
  72.9 13.0 %all-to-all-start.3 = ((f32[16,1,128]{2,1,0:T(1,128)}), f32[16,1,128]{2,1,0:T(1,128)S(1)}, u32[]{:S(2)}, u32[]{:S(2)}) async-start(f32[16,1,128]{2,1,0:T(1,128)} %bitcast.14), calls=%async_computation.3 | async-start | bytes 16384 | tf_op jit(solution)/shard_map/all_to_all | solution.py:541

commit v8 on v7

--- a/solution.py
+++ b/solution.py
@@ -508,17 +508,23 @@
     pooled = lax.ppermute(pool_rows, "tile", along(order[0]))
     near = send_across(packed[0])
     finish(0, near)
+    blocks = [(shift, side) for shift in order[1:] for side in range(across)]
+    beside = blocks[:1]
+    arrived = {
+        (shift, side): send_far(after(packed[shift], *near), shift, side) for shift, side in beside
+    }
     regrouped = call(
         functools.partial(regroup_kernel, size),
         "regroup",
         [shape((cap, width), jnp.bfloat16)] * across,
-        [after(pooled, *near)],
+        [after(pooled, *near, *arrived.values())],
     )
     passed = send_across(regrouped)
     finish(order[0], passed)
+    for shift, side in blocks[len(beside) :]:
+        arrived[shift, side] = send_far(after(packed[shift], pooled), shift, side)
     for shift in order[1:]:
-        blocks = after(packed[shift], pooled)
-        finish(shift, [send_far(blocks, shift, side) for side in range(across)])
+        finish(shift, [arrived[shift, side] for side in range(across)])
     own, other, places = (
         [found[shift] for shift in range(tiles)] for found in (own, other, places)
     )

time: 87.9 us -> 85.9 us (0.977)
  starting transfers between devices: 34.1 us -> 28.8 us
  waiting for transfers between devices: 33.4 us -> 36.7 us
    ppermute x6, waiting for transfers between devices: 0.02 us -> 7.44 us  [send_across(): lax.ppermute(blocks[side], 'chip', over(side))]
    ppermute x1, waiting for transfers between devices: 15 us -> 10.1 us  [body(): pooled = lax.ppermute(pool_rows, 'tile', along(order[0]))]
    ppermute x8, starting transfers between devices: 15.4 us -> 11 us  [send_far(): return lax.ppermute(blocks[side], ('chip', 'tile'), route)]
    all_to_all x1, starting transfers between devices: 5.74 us -> 4.7 us  [body(): lax.all_to_all(totals, ('chip', 'tile'), split_axis=0, concat_axis=0, til...]
  transfers between devices with their start and end apart: 20 -> 20, of which waited for: 8 -> 11; matrix products, arithmetic and copies ran while one was open for 0% -> 0% of each run, Pallas kernels for 10% -> 10%
where the time goes in v8:
time: 85.9 us; the launch traced here: 85.7 us
  waiting for transfers between devices  36.7 us (43%)
  starting transfers between devices  28.8 us (34%)
  Pallas kernels  19.3 us (22%)
  between operations  0.96 us (1%)
    pallas_call x9, Pallas kernels, call(): pl.pallas_call(kernel, out_shape=out_shape, in_specs=[vmem] * len(inputs)...  19.3 us
    ppermute x8, starting transfers between devices, send_far(): return lax.ppermute(blocks[side], ('chip', 'tile'), route)  11 us
    ppermute x1, waiting for transfers between devices, body(): pooled = lax.ppermute(pool_rows, 'tile', along(order[0]))  10.1 us
    ppermute x8, waiting for transfers between devices, send_far(): return lax.ppermute(blocks[side], ('chip', 'tile'), route)  9.57 us
    ppermute x6, starting transfers between devices, send_across(): lax.ppermute(blocks[side], 'chip', over(side))  8.17 us
    ppermute x6, waiting for transfers between devices, send_across(): lax.ppermute(blocks[side], 'chip', over(side))  7.44 us
    all_to_all x1, waiting for transfers between devices, body(): lax.all_to_all(totals, ('chip', 'tile'), split_axis=0, concat_axis=0, til...  7.26 us
    all_to_all x1, starting transfers between devices, body(): lax.all_to_all(totals, ('chip', 'tile'), split_axis=0, concat_axis=0, til...  4.7 us
  transfers between devices with their start and end apart: 20, of which 11 were waited for; matrix products, arithmetic and copies ran while one was open for 0% of the time, Pallas kernels for 10%

profile of v8, /device:TPU:0, one launch (start us, length us, event | category | flops | bytes accessed | tf_op | source)
XLA Modules:
  0.0 85.7 jit_solution(10993199070838377846)
XLA Ops:
  0.0 4.4 %plan.1 = (bf16[320,768]{1,0:T(8,128)(2,1)S(1)}, bf16[1152,768]{1,0:T(8,128)(2,1)S(1)}, s32[1,1152]{1,0:T(1,128)S(1)}, f32[1,1024]{1,0:T(1,128)S(1)}) custom-call(f32[1024,768]{1,0:T(8,128)} %emb_ref.1, s32[1,1024]{1,0:T(1,128)} %bitcast.74), custom_call_target="tpu_custom_call" | custom-call | tf_op jit(solution)/shard_map/plan/pallas_call | solution.py:419
  4.4 4.1 %collective-permute-start.6 = (bf16[320,768]{1,0:T(8,128)(2,1)S(1)}, bf16[320,768]{1,0:T(8,128)(2,1)S(1)}, u32[]{:S(2)}, u32[]{:S(2)}) collective-permute-start(bf16[320,768]{1,0:T(8,128)(2,1)S(1)} %get-tuple-element.317), channel_id=1, source_target_pairs={{0,2},{1,3},{2,0},{3,1},{4,6},{5,7},{6,4},{7,5},{8,10},{9,11},{10,... | collective-permute-start | bytes 1474568 | tf_op jit(solution)/shard_map/ppermute | solution.py:508
  8.5 3.2 %pack.1 = (bf16[104,768]{1,0:T(8,128)(2,1)S(1)}, bf16[104,768]{1,0:T(8,128)(2,1)S(1)}, bf16[104,768]{1,0:T(8,128)(2,1)S(1)}, bf16[104,768]{1,0:T(8,128)(2,1)S(1)...) custom-call(bf16[1152,768]{1,0:T(8,128)(2,1)S(1)} %get-tuple-element, ...), custom_call_target="tpu_custom_call" | custom-call | tf_op jit(solution)/shard_map/pack/pallas_call | solution.py:419
  11.7 1.6 %collective-permute-start.2 = (bf16[104,768]{1,0:T(8,128)(2,1)S(1)}, bf16[104,768]{1,0:T(8,128)(2,1)S(1)}, u32[]{:S(2)}, u32[]{:S(2)}) collective-permute-start(bf16[104,768]{1,0:T(8,128)(2,1)S(1)} %get-tuple-element.308), channel_id=1, source_target_pairs={{0,8},{8,0},{16,24},{24,16},{1,9},{9,1},{17,25},{25,17},{2,10},{10... | collective-permute-start | bytes 479240 | tf_op jit(solution)/shard_map/ppermute | solution.py:485
  13.3 1.5 %collective-permute-start.3 = (bf16[104,768]{1,0:T(8,128)(2,1)S(1)}, bf16[104,768]{1,0:T(8,128)(2,1)S(1)}, u32[]{:S(2)}, u32[]{:S(2)}) collective-permute-start(bf16[104,768]{1,0:T(8,128)(2,1)S(1)} %get-tuple-element.309), channel_id=1, source_target_pairs={{0,16},{8,24},{16,0},{24,8},{1,17},{9,25},{17,1},{25,9},{2,18},{10... | collective-permute-start | bytes 479240 | tf_op jit(solution)/shard_map/ppermute | solution.py:485
  15.3 3.1 %collective-permute-done.2.refs_1_ = bf16[104,768]{1,0:T(8,128)(2,1)S(1)} collective-permute-done((bf16[104,768]{1,0:T(8,128)(2,1)S(1)}, bf16[104,768]{1,0:T(8,128)(2,1)S(1)}, u32[]{:S(2)}, u32[]{:S(2)}) %collective-permute-start.2) | collective-permute-done | bytes 159776 | tf_op jit(solution)/shard_map/ppermute | solution.py:485
  18.4 3.6 %collective-permute-done.3.refs_2_ = bf16[104,768]{1,0:T(8,128)(2,1)S(1)} collective-permute-done((bf16[104,768]{1,0:T(8,128)(2,1)S(1)}, bf16[104,768]{1,0:T(8,128)(2,1)S(1)}, u32[]{:S(2)}, u32[]{:S(2)}) %collective-permute-start.3) | collective-permute-done | bytes 159776 | tf_op jit(solution)/shard_map/ppermute | solution.py:485
  22.0 1.6 %collective-permute-start.5 = (bf16[104,768]{1,0:T(8,128)(2,1)S(1)}, bf16[104,768]{1,0:T(8,128)(2,1)S(1)}, u32[]{:S(2)}, u32[]{:S(2)}) collective-permute-start(bf16[104,768]{1,0:T(8,128)(2,1)S(1)} %get-tuple-element.316), channel_id=1, source_target_pairs={{0,1},{1,2},{2,3},{3,0},{8,9},{9,10},{10,11},{11,8},{16,17},{17,18... | collective-permute-start | bytes 479240 | tf_op jit(solution)/shard_map/ppermute | solution.py:490
  23.6 10.1 %collective-permute-done.6.pool_ref = bf16[320,768]{1,0:T(8,128)(2,1)S(1)} collective-permute-done((bf16[320,768]{1,0:T(8,128)(2,1)S(1)}, bf16[320,768]{1,0:T(8,128)(2,1)S(1)}, u32[]{:S(2)}, u32[]{:S(2)}) %collective-permute-start.6) | collective-permute-done | bytes 491552 | tf_op jit(solution)/shard_map/ppermute | solution.py:508
  33.7 2.0 %collective-permute-start.8 = (bf16[104,768]{1,0:T(8,128)(2,1)S(1)}, bf16[104,768]{1,0:T(8,128)(2,1)S(1)}, u32[]{:S(2)}, u32[]{:S(2)}) collective-permute-start(bf16[104,768]{1,0:T(8,128)(2,1)S(1)} %get-tuple-element.319), channel_id=1, source_target_pairs={{0,17},{1,18},{2,19},{3,16},{8,25},{9,26},{10,27},{11,24},{16,1},{... | collective-permute-start | bytes 479240 | tf_op jit(solution)/shard_map/ppermute | solution.py:490
  35.8 3.1 %collective-permute-start.9 = (bf16[104,768]{1,0:T(8,128)(2,1)S(1)}, bf16[104,768]{1,0:T(8,128)(2,1)S(1)}, u32[]{:S(2)}, u32[]{:S(2)}) collective-permute-start(bf16[104,768]{1,0:T(8,128)(2,1)S(1)} %get-tuple-element.320), channel_id=1, source_target_pairs={{0,25},{1,26},{2,27},{3,24},{8,17},{9,18},{10,19},{11,16},{16,9},{... | collective-permute-start | bytes 479240 | tf_op jit(solution)/shard_map/ppermute | solution.py:490
  40.2 1.5 %collective-permute-start.11 = (bf16[104,768]{1,0:T(8,128)(2,1)S(1)}, bf16[104,768]{1,0:T(8,128)(2,1)S(1)}, u32[]{:S(2)}, u32[]{:S(2)}) collective-permute-start(bf16[104,768]{1,0:T(8,128)(2,1)S(1)} %get-tuple-element.325), channel_id=1, source_target_pairs={{0,16},{8,24},{16,0},{24,8},{1,17},{9,25},{17,1},{25,9},{2,18},{10... | collective-permute-start | bytes 479240 | tf_op jit(solution)/shard_map/ppermute | solution.py:485
  41.7 1.9 %collective-permute-done.7.refs_1_ = bf16[104,768]{1,0:T(8,128)(2,1)S(1)} collective-permute-done((bf16[104,768]{1,0:T(8,128)(2,1)S(1)}, bf16[104,768]{1,0:T(8,128)(2,1)S(1)}, u32[]{:S(2)}, u32[]{:S(2)}) %collective-permute-start.7) | collective-permute-done | bytes 159776 | tf_op jit(solution)/shard_map/ppermute | solution.py:490
  43.6 2.5 %collective-permute-start.12 = (bf16[104,768]{1,0:T(8,128)(2,1)S(1)}, bf16[104,768]{1,0:T(8,128)(2,1)S(1)}, u32[]{:S(2)}, u32[]{:S(2)}) collective-permute-start(bf16[104,768]{1,0:T(8,128)(2,1)S(1)} %get-tuple-element.326), channel_id=1, source_target_pairs={{0,24},{8,16},{16,8},{24,0},{1,25},{9,17},{17,9},{25,1},{2,26},{10... | collective-permute-start | bytes 479240 | tf_op jit(solution)/shard_map/ppermute | solution.py:485
  46.1 1.9 %collective-permute-done.8.refs_2_ = bf16[104,768]{1,0:T(8,128)(2,1)S(1)} collective-permute-done((bf16[104,768]{1,0:T(8,128)(2,1)S(1)}, bf16[104,768]{1,0:T(8,128)(2,1)S(1)}, u32[]{:S(2)}, u32[]{:S(2)}) %collective-permute-start.8) | collective-permute-done | bytes 159776 | tf_op jit(solution)/shard_map/ppermute | solution.py:490
  47.9 3.3 %collective-permute-done.9.refs_3_ = bf16[104,768]{1,0:T(8,128)(2,1)S(1)} collective-permute-done((bf16[104,768]{1,0:T(8,128)(2,1)S(1)}, bf16[104,768]{1,0:T(8,128)(2,1)S(1)}, u32[]{:S(2)}, u32[]{:S(2)}) %collective-permute-start.9) | collective-permute-done | bytes 159776 | tf_op jit(solution)/shard_map/ppermute | solution.py:490
  53.1 3.1 %collective-permute-start.16 = (bf16[104,768]{1,0:T(8,128)(2,1)S(1)}, bf16[104,768]{1,0:T(8,128)(2,1)S(1)}, u32[]{:S(2)}, u32[]{:S(2)}) collective-permute-start(bf16[104,768]{1,0:T(8,128)(2,1)S(1)} %get-tuple-element.335), channel_id=1, source_target_pairs={{0,27},{1,24},{2,25},{3,26},{8,19},{9,16},{10,17},{11,18},{16,11},... | collective-permute-start | bytes 479240 | tf_op jit(solution)/shard_map/ppermute | solution.py:490
  56.2 1.3 %sort.4 = (bf16[528,768]{1,0:T(8,128)(2,1)S(1)}, s32[4,128]{1,0:T(4,128)S(1)}) custom-call(bf16[104,768]{1,0:T(8,128)(2,1)S(1)} %get-tuple-element.307.refs_0_, bf16[104,768]{1,0:T(8,128)(2,1)S(1)} %collective-permute-done.2.refs_1_, bf16[104,768]{1,0:T(8,128)(2,1)S(1)} %collective-permute-done.3.refs_2_, bf16[104,768]{1,0:T(8,128)(2,1)S(1)} %collective-permute-done.4.refs_3_), custom_call_target="tpu_custom_call" | custom-call | tf_op jit(solution)/shard_map/sort/pallas_call | solution.py:419
  57.4 1.2 %sort.5 = (bf16[528,768]{1,0:T(8,128)(2,1)S(1)}, s32[4,128]{1,0:T(4,128)S(1)}) custom-call(bf16[104,768]{1,0:T(8,128)(2,1)S(1)} %collective-permute-done.5.refs_0_, bf16[104,768]{1,0:T(8,128)(2,1)S(1)} %collective-permute-done.7.refs_1_, bf16[104,768]{1,0:T(8,128)(2,1)S(1)} %collective-permute-done.8.refs_2_, bf16[104,768]{1,0:T(8,128)(2,1)S(1)} %collective-permute-done.9.refs_3_), custom_call_target="tpu_custom_call" | custom-call | tf_op jit(solution)/shard_map/sort/pallas_call | solution.py:419
  61.5 1.7 %collective-permute-done.16.refs_3_ = bf16[104,768]{1,0:T(8,128)(2,1)S(1)} collective-permute-done((bf16[104,768]{1,0:T(8,128)(2,1)S(1)}, bf16[104,768]{1,0:T(8,128)(2,1)S(1)}, u32[]{:S(2)}, u32[]{:S(2)}) %collective-permute-start.16) | collective-permute-done | bytes 159776 | tf_op jit(solution)/shard_map/ppermute | solution.py:490
  64.6 2.3 %collective-permute-done.20.refs_7_ = bf16[528,768]{1,0:T(8,128)(2,1)S(1)} collective-permute-done((bf16[528,768]{1,0:T(8,128)(2,1)S(1)}, bf16[528,768]{1,0:T(8,128)(2,1)S(1)}, u32[]{:S(2)}, u32[]{:S(2)}) %collective-permute-start.20) | collective-permute-done | bytes 811040 | tf_op jit(solution)/shard_map/ppermute | solution.py:506
  66.9 5.0 %score.1 = f32[16,128]{1,0:T(8,128)} custom-call(bf16[528,768]{1,0:T(8,128)(2,1)S(1)} %get-tuple-element.311.refs_0_, bf16[528,768]{1,0:T(8,128)(2,1)S(1)} %get-tuple-element.321.refs_1_, bf16[528,768]{1,0:T(8,128)(2,1)S(1)} %get-tuple-element.327.refs_2_, bf16[528,768]{1,0:T(8,128)(2,1)S(1)} %get-tuple-element.336.refs_3_, ...), custom_call_target="tpu_custom_call" | custom-call | tf_op jit(solution)/shard_map/score/pallas_call | solution.py:419
  71.9 4.7 %all-to-all-start.3 = ((f32[16,1,128]{2,1,0:T(1,128)}), f32[16,1,128]{2,1,0:T(1,128)S(1)}, u32[]{:S(2)}, u32[]{:S(2)}) async-start(f32[16,1,128]{2,1,0:T(1,128)} %bitcast.14), calls=%async_computation.3 | async-start | bytes 16384 | tf_op jit(solution)/shard_map/all_to_all | solution.py:547
  76.6 7.3 %all-to-all-done.3 = f32[16,1,128]{2,1,0:T(1,128)S(1)} async-done(((f32[16,1,128]{2,1,0:T(1,128)}), f32[16,1,128]{2,1,0:T(1,128)S(1)}, u32[]{:S(2)}, u32[]{:S(2)}) %all-to-all-start.3) | async-done | bytes 8224 | tf_op jit(solution)/shard_map/all_to_all | solution.py:547
  (30 shorter events, 8.8 us)
Async XLA Ops:
  4.4 29.3 %collective-permute-start.6 = (bf16[320,768]{1,0:T(8,128)(2,1)S(1)}, bf16[320,768]{1,0:T(8,128)(2,1)S(1)}, u32[]{:S(2)}, u32[]{:S(2)}) collective-permute-start(bf16[320,768]{1,0:T(8,128)(2,1)S(1)} %get-tuple-element.317), channel_id=1, source_target_pairs={{0,2},{1,3},{2,0},{3,1},{4,6},{5,7},{6,4},{7,5},{8,10},{9,11},{10,... | collective-permute-start | bytes 1474568 | tf_op jit(solution)/shard_map/ppermute | solution.py:508
  11.7 6.7 %collective-permute-start.2 = (bf16[104,768]{1,0:T(8,128)(2,1)S(1)}, bf16[104,768]{1,0:T(8,128)(2,1)S(1)}, u32[]{:S(2)}, u32[]{:S(2)}) collective-permute-start(bf16[104,768]{1,0:T(8,128)(2,1)S(1)} %get-tuple-element.308), channel_id=1, source_target_pairs={{0,8},{8,0},{16,24},{24,16},{1,9},{9,1},{17,25},{25,17},{2,10},{10... | collective-permute-start | bytes 479240 | tf_op jit(solution)/shard_map/ppermute | solution.py:485
  13.3 8.7 %collective-permute-start.3 = (bf16[104,768]{1,0:T(8,128)(2,1)S(1)}, bf16[104,768]{1,0:T(8,128)(2,1)S(1)}, u32[]{:S(2)}, u32[]{:S(2)}) collective-permute-start(bf16[104,768]{1,0:T(8,128)(2,1)S(1)} %get-tuple-element.309), channel_id=1, source_target_pairs={{0,16},{8,24},{16,0},{24,8},{1,17},{9,25},{17,1},{25,9},{2,18},{10... | collective-permute-start | bytes 479240 | tf_op jit(solution)/shard_map/ppermute | solution.py:485
  14.8 7.2 %collective-permute-start.4 = (bf16[104,768]{1,0:T(8,128)(2,1)S(1)}, bf16[104,768]{1,0:T(8,128)(2,1)S(1)}, u32[]{:S(2)}, u32[]{:S(2)}) collective-permute-start(bf16[104,768]{1,0:T(8,128)(2,1)S(1)} %get-tuple-element.310), channel_id=1, source_target_pairs={{0,24},{8,16},{16,8},{24,0},{1,25},{9,17},{17,9},{25,1},{2,26},{10... | collective-permute-start | bytes 479240 | tf_op jit(solution)/shard_map/ppermute | solution.py:485
  22.0 11.7 %collective-permute-start.5 = (bf16[104,768]{1,0:T(8,128)(2,1)S(1)}, bf16[104,768]{1,0:T(8,128)(2,1)S(1)}, u32[]{:S(2)}, u32[]{:S(2)}) collective-permute-start(bf16[104,768]{1,0:T(8,128)(2,1)S(1)} %get-tuple-element.316), channel_id=1, source_target_pairs={{0,1},{1,2},{2,3},{3,0},{8,9},{9,10},{10,11},{11,8},{16,17},{17,18... | collective-permute-start | bytes 479240 | tf_op jit(solution)/shard_map/ppermute | solution.py:490
  33.7 9.8 %collective-permute-start.7 = (bf16[104,768]{1,0:T(8,128)(2,1)S(1)}, bf16[104,768]{1,0:T(8,128)(2,1)S(1)}, u32[]{:S(2)}, u32[]{:S(2)}) collective-permute-start(bf16[104,768]{1,0:T(8,128)(2,1)S(1)} %get-tuple-element.318), channel_id=1, source_target_pairs={{0,9},{1,10},{2,11},{3,8},{8,1},{9,2},{10,3},{11,0},{16,25},{17,26... | collective-permute-start | bytes 479240 | tf_op jit(solution)/shard_map/ppermute | solution.py:490
  33.7 14.2 %collective-permute-start.8 = (bf16[104,768]{1,0:T(8,128)(2,1)S(1)}, bf16[104,768]{1,0:T(8,128)(2,1)S(1)}, u32[]{:S(2)}, u32[]{:S(2)}) collective-permute-start(bf16[104,768]{1,0:T(8,128)(2,1)S(1)} %get-tuple-element.319), channel_id=1, source_target_pairs={{0,17},{1,18},{2,19},{3,16},{8,25},{9,26},{10,27},{11,24},{16,1},{... | collective-permute-start | bytes 479240 | tf_op jit(solution)/shard_map/ppermute | solution.py:490
  35.8 15.5 %collective-permute-start.9 = (bf16[104,768]{1,0:T(8,128)(2,1)S(1)}, bf16[104,768]{1,0:T(8,128)(2,1)S(1)}, u32[]{:S(2)}, u32[]{:S(2)}) collective-permute-start(bf16[104,768]{1,0:T(8,128)(2,1)S(1)} %get-tuple-element.320), channel_id=1, source_target_pairs={{0,25},{1,26},{2,27},{3,24},{8,17},{9,18},{10,19},{11,16},{16,9},{... | collective-permute-start | bytes 479240 | tf_op jit(solution)/shard_map/ppermute | solution.py:490
  39.6 11.6 %collective-permute-start.10 = (bf16[104,768]{1,0:T(8,128)(2,1)S(1)}, bf16[104,768]{1,0:T(8,128)(2,1)S(1)}, u32[]{:S(2)}, u32[]{:S(2)}) collective-permute-start(bf16[104,768]{1,0:T(8,128)(2,1)S(1)} %get-tuple-element.324), channel_id=1, source_target_pairs={{0,8},{8,0},{16,24},{24,16},{1,9},{9,1},{17,25},{25,17},{2,10},{10... | collective-permute-start | bytes 479240 | tf_op jit(solution)/shard_map/ppermute | solution.py:485
  40.2 13.0 %collective-permute-start.11 = (bf16[104,768]{1,0:T(8,128)(2,1)S(1)}, bf16[104,768]{1,0:T(8,128)(2,1)S(1)}, u32[]{:S(2)}, u32[]{:S(2)}) collective-permute-start(bf16[104,768]{1,0:T(8,128)(2,1)S(1)} %get-tuple-element.325), channel_id=1, source_target_pairs={{0,16},{8,24},{16,0},{24,8},{1,17},{9,25},{17,1},{25,9},{2,18},{10... | collective-permute-start | bytes 479240 | tf_op jit(solution)/shard_map/ppermute | solution.py:485
  43.6 15.2 %collective-permute-start.12 = (bf16[104,768]{1,0:T(8,128)(2,1)S(1)}, bf16[104,768]{1,0:T(8,128)(2,1)S(1)}, u32[]{:S(2)}, u32[]{:S(2)}) collective-permute-start(bf16[104,768]{1,0:T(8,128)(2,1)S(1)} %get-tuple-element.326), channel_id=1, source_target_pairs={{0,24},{8,16},{16,8},{24,0},{1,25},{9,17},{17,9},{25,1},{2,26},{10... | collective-permute-start | bytes 479240 | tf_op jit(solution)/shard_map/ppermute | solution.py:485
  47.9 12.1 %collective-permute-start.13 = (bf16[104,768]{1,0:T(8,128)(2,1)S(1)}, bf16[104,768]{1,0:T(8,128)(2,1)S(1)}, u32[]{:S(2)}, u32[]{:S(2)}) collective-permute-start(bf16[104,768]{1,0:T(8,128)(2,1)S(1)} %get-tuple-element.332), channel_id=1, source_target_pairs={{0,3},{1,0},{2,1},{3,2},{8,11},{9,8},{10,9},{11,10},{16,19},{17,16... | collective-permute-start | bytes 479240 | tf_op jit(solution)/shard_map/ppermute | solution.py:490
  51.2 9.4 %collective-permute-start.14 = (bf16[104,768]{1,0:T(8,128)(2,1)S(1)}, bf16[104,768]{1,0:T(8,128)(2,1)S(1)}, u32[]{:S(2)}, u32[]{:S(2)}) collective-permute-start(bf16[104,768]{1,0:T(8,128)(2,1)S(1)} %get-tuple-element.333), channel_id=1, source_target_pairs={{0,11},{1,8},{2,9},{3,10},{8,3},{9,0},{10,1},{11,2},{16,27},{17,24... | collective-permute-start | bytes 479240 | tf_op jit(solution)/shard_map/ppermute | solution.py:490
  51.2 10.3 %collective-permute-start.15 = (bf16[104,768]{1,0:T(8,128)(2,1)S(1)}, bf16[104,768]{1,0:T(8,128)(2,1)S(1)}, u32[]{:S(2)}, u32[]{:S(2)}) collective-permute-start(bf16[104,768]{1,0:T(8,128)(2,1)S(1)} %get-tuple-element.334), channel_id=1, source_target_pairs={{0,19},{1,16},{2,17},{3,18},{8,27},{9,24},{10,25},{11,26},{16,3},{... | collective-permute-start | bytes 479240 | tf_op jit(solution)/shard_map/ppermute | solution.py:490
  53.1 10.1 %collective-permute-start.16 = (bf16[104,768]{1,0:T(8,128)(2,1)S(1)}, bf16[104,768]{1,0:T(8,128)(2,1)S(1)}, u32[]{:S(2)}, u32[]{:S(2)}) collective-permute-start(bf16[104,768]{1,0:T(8,128)(2,1)S(1)} %get-tuple-element.335), channel_id=1, source_target_pairs={{0,27},{1,24},{2,25},{3,26},{8,19},{9,16},{10,17},{11,18},{16,11},... | collective-permute-start | bytes 479240 | tf_op jit(solution)/shard_map/ppermute | solution.py:490
  58.7 5.9 %collective-permute-start.17 = (bf16[528,768]{1,0:T(8,128)(2,1)S(1)}, bf16[528,768]{1,0:T(8,128)(2,1)S(1)}, u32[]{:S(2)}, u32[]{:S(2)}) collective-permute-start(bf16[528,768]{1,0:T(8,128)(2,1)S(1)} %get-tuple-element.311.refs_0_), channel_id=1, source_target_pairs={{0,4},{4,0},{1,5},{5,1},{2,6},{6,2},{3,7},{7,3},{8,12},{12,8},{9,1... | collective-permute-start | bytes 2433032 | tf_op jit(solution)/shard_map/ppermute | solution.py:506
  60.1 4.5 %collective-permute-start.19 = (bf16[528,768]{1,0:T(8,128)(2,1)S(1)}, bf16[528,768]{1,0:T(8,128)(2,1)S(1)}, u32[]{:S(2)}, u32[]{:S(2)}) collective-permute-start(bf16[528,768]{1,0:T(8,128)(2,1)S(1)} %get-tuple-element.327.refs_2_), channel_id=1, source_target_pairs={{0,4},{4,0},{1,5},{5,1},{2,6},{6,2},{3,7},{7,3},{8,12},{12,8},{9,1... | collective-permute-start | bytes 2433032 | tf_op jit(solution)/shard_map/ppermute | solution.py:506
  60.6 4.0 %collective-permute-start.18 = (bf16[528,768]{1,0:T(8,128)(2,1)S(1)}, bf16[528,768]{1,0:T(8,128)(2,1)S(1)}, u32[]{:S(2)}, u32[]{:S(2)}) collective-permute-start(bf16[528,768]{1,0:T(8,128)(2,1)S(1)} %get-tuple-element.321.refs_1_), channel_id=1, source_target_pairs={{0,4},{4,0},{1,5},{5,1},{2,6},{6,2},{3,7},{7,3},{8,12},{12,8},{9,1... | collective-permute-start | bytes 2433032 | tf_op jit(solution)/shard_map/ppermute | solution.py:506
  64.5 2.4 %collective-permute-start.20 = (bf16[528,768]{1,0:T(8,128)(2,1)S(1)}, bf16[528,768]{1,0:T(8,128)(2,1)S(1)}, u32[]{:S(2)}, u32[]{:S(2)}) collective-permute-start(bf16[528,768]{1,0:T(8,128)(2,1)S(1)} %get-tuple-element.336.refs_3_), channel_id=1, source_target_pairs={{0,4},{4,0},{1,5},{5,1},{2,6},{6,2},{3,7},{7,3},{8,12},{12,8},{9,1... | collective-permute-start | bytes 2433032 | tf_op jit(solution)/shard_map/ppermute | solution.py:506
  66.9 17.0 %copy-start.3 = (s32[1024]{0:T(1024)S(1)}, s32[1024]{0:T(1024)}, u32[]{:S(2)}) copy-start(s32[1024]{0:T(1024)} %param.9) | copy-start | bytes 12292
  66.9 18.6 %copy-start = (f32[1024,768]{1,0:T(8,128)S(1)}, f32[1024,768]{1,0:T(8,128)}, u32[]{:S(2)}) copy-start(f32[1024,768]{1,0:T(8,128)} %emb_ref.1) | copy-start | bytes 9437188
  71.9 12.0 %all-to-all-start.3 = ((f32[16,1,128]{2,1,0:T(1,128)}), f32[16,1,128]{2,1,0:T(1,128)S(1)}, u32[]{:S(2)}, u32[]{:S(2)}) async-start(f32[16,1,128]{2,1,0:T(1,128)} %bitcast.14), calls=%async_computation.3 | async-start | bytes 16384 | tf_op jit(solution)/shard_map/all_to_all | solution.py:547

commit v9 on v8

--- a/solution.py
+++ b/solution.py
@@ -128,21 +128,29 @@
     shift = ((ids & (tiles - 1)) - lax.axis_index("tile")) & (tiles - 1)
     side = ((ids & (chips - 1)) >> (tiles.bit_length() - 1)) ^ lax.axis_index("chip")
     block = shift * across + side
+    in_block = jnp.where(iota((LANES, rows), 0) == block, 1.0, 0.0).astype(jnp.bfloat16)
+    in_label = jnp.where(iota((LANES, rows), 0) == label, 1.0, 0.0).astype(jnp.bfloat16)
+    counts = lax.dot_general(
+        in_block, in_label, (((1,), (1,)), ((), ())), preferred_element_type=jnp.float32
+    )
+    of_block = jnp.broadcast_to(jnp.sum(counts, axis=1, keepdims=True), (LANES, LANES))
+    lower = jnp.where(iota((LANES, LANES), 1) < iota((LANES, LANES), 0), 1.0, 0.0)
+    starts = exact_dot(lower, of_block)[0:chips, 0:1]
+
+    def start_of(block):
+        mine = iota((chips, rows), 0) == block
+        return jnp.sum(jnp.where(mine, starts, 0.0), axis=0, keepdims=True)
+
     key = ((block * labels + label) * rows + iota((1, rows), 1)).astype(jnp.float32)
-    base = (block * (labels * rows)).astype(jnp.float32)
-    base_shift = (shift * (across * labels * rows)).astype(jnp.float32)
     key_t = jnp.broadcast_to(key, (LANES, rows)).T
-    ranks, pooled = [], []
+    order = []
     for start in range(0, rows, LANES):
-        here = slice(start, start + LANES)
-        smaller = key_t < key[:, here]
-        in_block = jnp.where(smaller & (key_t >= base[:, here]), 1.0, 0.0)
-        in_shift = jnp.where(smaller & (key_t >= base_shift[:, here]), 1.0, 0.0)
-        ranks.append(jnp.sum(in_block, axis=0, keepdims=True))
-        pooled.append(jnp.sum(in_shift, axis=0, keepdims=True))
-    rank = jnp.concatenate(ranks, axis=1)
+        smaller = jnp.where(key_t < key[:, start : start + LANES], 1.0, 0.0)
+        order.append(jnp.sum(smaller, axis=0, keepdims=True))
+    order = jnp.concatenate(order, axis=1)
+    rank = order - start_of(block)
+    pooled = order - start_of(shift * across)
     rank_ref[...] = rank
-    pooled = jnp.concatenate(pooled, axis=1)
 
     def apart(shift):
         return shift != size["first"]
@@ -152,11 +160,6 @@
     place = jnp.where(apart(shift), side * cap + rank.astype(jnp.int32), pooled.astype(jnp.int32))
     place = jnp.where(full, -1, place)
 
-    in_block = jnp.where(iota((LANES, rows), 0) == block, 1.0, 0.0).astype(jnp.bfloat16)
-    in_label = jnp.where(iota((LANES, rows), 0) == label, 1.0, 0.0).astype(jnp.bfloat16)
-    counts = lax.dot_general(
-        in_block, in_label, (((1,), (1,)), ((), ())), preferred_element_type=jnp.float32
-    )
     counts = jnp.where(iota((LANES, LANES), 1) == FLAG, over, counts)
     aug_ref[rows:, :] = jnp.zeros((LANES, width), jnp.bfloat16)
     aug_ref[rows:, 0:LANES] = counts.astype(jnp.bfloat16)
@@ -509,7 +512,7 @@
     near = send_across(packed[0])
     finish(0, near)
     blocks = [(shift, side) for shift in order[1:] for side in range(across)]
-    beside = blocks[:1]
+    beside = [(shift, across - 1) for shift in order[1:2]]
     arrived = {
         (shift, side): send_far(after(packed[shift], *near), shift, side) for shift, side in beside
     }
@@ -521,8 +524,9 @@
     )
     passed = send_across(regrouped)
     finish(order[0], passed)
-    for shift, side in blocks[len(beside) :]:
-        arrived[shift, side] = send_far(after(packed[shift], pooled), shift, side)
+    for shift, side in sorted(set(blocks) - set(beside), key=lambda block: (block[1] > 0, block)):
+        ready = after(packed[shift], pooled if side == 0 else pooled)
+        arrived[shift, side] = send_far(ready, shift, side)
     for shift in order[1:]:
         finish(shift, [arrived[shift, side] for side in range(across)])
     own, other, places = (

time: 85.9 us -> 85.5 us (level)
  starting transfers between devices: 28.8 us -> 27.6 us
  waiting for transfers between devices: 36.7 us -> 37.7 us
    ppermute x8, starting transfers between devices: 11 us -> 9.56 us  [send_far(): return lax.ppermute(blocks[side], ('chip', 'tile'), route)]
    ppermute x6, waiting for transfers between devices: 7.44 us -> 8.73 us  [send_across(): lax.ppermute(blocks[side], 'chip', over(side))]
    ppermute x1, waiting for transfers between devices: 10.1 us -> 9.22 us  [body(): pooled = lax.ppermute(pool_rows, 'tile', along(order[0]))]
    ppermute x6, starting transfers between devices: 8.17 us -> 9.05 us  [send_across(): lax.ppermute(blocks[side], 'chip', over(side))]
  transfers between devices with their start and end apart: 20 -> 20, of which waited for: 11 -> 10; matrix products, arithmetic and copies ran while one was open for 0% -> 0% of each run, Pallas kernels for 10% -> 10%
where the time goes in v9:
time: 85.5 us; the launch traced here: 85.3 us
  waiting for transfers between devices  37.7 us (44%)
  starting transfers between devices  27.6 us (32%)
  Pallas kernels  18.7 us (22%)
  between operations  0.98 us (1%)
    pallas_call x9, Pallas kernels, call(): pl.pallas_call(kernel, out_shape=out_shape, in_specs=[vmem] * len(inputs)...  18.7 us
    ppermute x8, waiting for transfers between devices, send_far(): return lax.ppermute(blocks[side], ('chip', 'tile'), route)  10.2 us
    ppermute x8, starting transfers between devices, send_far(): return lax.ppermute(blocks[side], ('chip', 'tile'), route)  9.56 us
    ppermute x1, waiting for transfers between devices, body(): pooled = lax.ppermute(pool_rows, 'tile', along(order[0]))  9.22 us
    ppermute x6, starting transfers between devices, send_across(): lax.ppermute(blocks[side], 'chip', over(side))  9.05 us
    ppermute x6, waiting for transfers between devices, send_across(): lax.ppermute(blocks[side], 'chip', over(side))  8.73 us
    all_to_all x1, waiting for transfers between devices, body(): lax.all_to_all(totals, ('chip', 'tile'), split_axis=0, concat_axis=0, til...  7.26 us
    all_to_all x1, starting transfers between devices, body(): lax.all_to_all(totals, ('chip', 'tile'), split_axis=0, concat_axis=0, til...  4.11 us
  transfers between devices with their start and end apart: 20, of which 10 were waited for; matrix products, arithmetic and copies ran while one was open for 0% of the time, Pallas kernels for 10%

profile of v9, /device:TPU:0, one launch (start us, length us, event | category | flops | bytes accessed | tf_op | source)
XLA Modules:
  0.0 85.3 jit_solution(14886165884417478404)
XLA Ops:
  0.0 3.9 %plan.1 = (bf16[320,768]{1,0:T(8,128)(2,1)S(1)}, bf16[1152,768]{1,0:T(8,128)(2,1)S(1)}, s32[1,1152]{1,0:T(1,128)S(1)}, f32[1,1024]{1,0:T(1,128)S(1)}) custom-call(f32[1024,768]{1,0:T(8,128)} %emb_ref.1, s32[1,1024]{1,0:T(1,128)} %bitcast.74), custom_call_target="tpu_custom_call" | custom-call | tf_op jit(solution)/shard_map/plan/pallas_call | solution.py:422
  3.9 4.1 %collective-permute-start.5 = (bf16[320,768]{1,0:T(8,128)(2,1)S(1)}, bf16[320,768]{1,0:T(8,128)(2,1)S(1)}, u32[]{:S(2)}, u32[]{:S(2)}) collective-permute-start(bf16[320,768]{1,0:T(8,128)(2,1)S(1)} %get-tuple-element.316), channel_id=1, source_target_pairs={{0,2},{1,3},{2,0},{3,1},{4,6},{5,7},{6,4},{7,5},{8,10},{9,11},{10,... | collective-permute-start | bytes 1474568 | tf_op jit(solution)/shard_map/ppermute | solution.py:511
  8.0 3.2 %pack.1 = (bf16[104,768]{1,0:T(8,128)(2,1)S(1)}, bf16[104,768]{1,0:T(8,128)(2,1)S(1)}, bf16[104,768]{1,0:T(8,128)(2,1)S(1)}, bf16[104,768]{1,0:T(8,128)(2,1)S(1)...) custom-call(bf16[1152,768]{1,0:T(8,128)(2,1)S(1)} %get-tuple-element, ...), custom_call_target="tpu_custom_call" | custom-call | tf_op jit(solution)/shard_map/pack/pallas_call | solution.py:422
  11.2 1.6 %collective-permute-start.2 = (bf16[104,768]{1,0:T(8,128)(2,1)S(1)}, bf16[104,768]{1,0:T(8,128)(2,1)S(1)}, u32[]{:S(2)}, u32[]{:S(2)}) collective-permute-start(bf16[104,768]{1,0:T(8,128)(2,1)S(1)} %get-tuple-element.308), channel_id=1, source_target_pairs={{0,8},{8,0},{16,24},{24,16},{1,9},{9,1},{17,25},{25,17},{2,10},{10... | collective-permute-start | bytes 479240 | tf_op jit(solution)/shard_map/ppermute | solution.py:488
  12.7 1.5 %collective-permute-start.3 = (bf16[104,768]{1,0:T(8,128)(2,1)S(1)}, bf16[104,768]{1,0:T(8,128)(2,1)S(1)}, u32[]{:S(2)}, u32[]{:S(2)}) collective-permute-start(bf16[104,768]{1,0:T(8,128)(2,1)S(1)} %get-tuple-element.309), channel_id=1, source_target_pairs={{0,16},{8,24},{16,0},{24,8},{1,17},{9,25},{17,1},{25,9},{2,18},{10... | collective-permute-start | bytes 479240 | tf_op jit(solution)/shard_map/ppermute | solution.py:488
  14.7 3.1 %collective-permute-done.2.refs_1_ = bf16[104,768]{1,0:T(8,128)(2,1)S(1)} collective-permute-done((bf16[104,768]{1,0:T(8,128)(2,1)S(1)}, bf16[104,768]{1,0:T(8,128)(2,1)S(1)}, u32[]{:S(2)}, u32[]{:S(2)}) %collective-permute-start.2) | collective-permute-done | bytes 159776 | tf_op jit(solution)/shard_map/ppermute | solution.py:488
  17.8 3.6 %collective-permute-done.3.refs_2_ = bf16[104,768]{1,0:T(8,128)(2,1)S(1)} collective-permute-done((bf16[104,768]{1,0:T(8,128)(2,1)S(1)}, bf16[104,768]{1,0:T(8,128)(2,1)S(1)}, u32[]{:S(2)}, u32[]{:S(2)}) %collective-permute-start.3) | collective-permute-done | bytes 159776 | tf_op jit(solution)/shard_map/ppermute | solution.py:488
  21.4 2.5 %collective-permute-start.9 = (bf16[104,768]{1,0:T(8,128)(2,1)S(1)}, bf16[104,768]{1,0:T(8,128)(2,1)S(1)}, u32[]{:S(2)}, u32[]{:S(2)}) collective-permute-start(bf16[104,768]{1,0:T(8,128)(2,1)S(1)} %get-tuple-element.320), channel_id=1, source_target_pairs={{0,25},{1,26},{2,27},{3,24},{8,17},{9,18},{10,19},{11,16},{16,9},{... | collective-permute-start | bytes 479240 | tf_op jit(solution)/shard_map/ppermute | solution.py:493
  23.9 9.2 %collective-permute-done.5.pool_ref = bf16[320,768]{1,0:T(8,128)(2,1)S(1)} collective-permute-done((bf16[320,768]{1,0:T(8,128)(2,1)S(1)}, bf16[320,768]{1,0:T(8,128)(2,1)S(1)}, u32[]{:S(2)}, u32[]{:S(2)}) %collective-permute-start.5) | collective-permute-done | bytes 491552 | tf_op jit(solution)/shard_map/ppermute | solution.py:511
  33.2 1.8 %collective-permute-start.7 = (bf16[104,768]{1,0:T(8,128)(2,1)S(1)}, bf16[104,768]{1,0:T(8,128)(2,1)S(1)}, u32[]{:S(2)}, u32[]{:S(2)}) collective-permute-start(bf16[104,768]{1,0:T(8,128)(2,1)S(1)} %get-tuple-element.318), channel_id=1, source_target_pairs={{0,9},{1,10},{2,11},{3,8},{8,1},{9,2},{10,3},{11,0},{16,25},{17,26... | collective-permute-start | bytes 479240 | tf_op jit(solution)/shard_map/ppermute | solution.py:493
  34.9 3.4 %collective-permute-start.8 = (bf16[104,768]{1,0:T(8,128)(2,1)S(1)}, bf16[104,768]{1,0:T(8,128)(2,1)S(1)}, u32[]{:S(2)}, u32[]{:S(2)}) collective-permute-start(bf16[104,768]{1,0:T(8,128)(2,1)S(1)} %get-tuple-element.319), channel_id=1, source_target_pairs={{0,17},{1,18},{2,19},{3,16},{8,25},{9,26},{10,27},{11,24},{16,1},{... | collective-permute-start | bytes 479240 | tf_op jit(solution)/shard_map/ppermute | solution.py:493
  39.0 1.6 %collective-permute-start.10 = (bf16[104,768]{1,0:T(8,128)(2,1)S(1)}, bf16[104,768]{1,0:T(8,128)(2,1)S(1)}, u32[]{:S(2)}, u32[]{:S(2)}) collective-permute-start(bf16[104,768]{1,0:T(8,128)(2,1)S(1)} %get-tuple-element.324), channel_id=1, source_target_pairs={{0,8},{8,0},{16,24},{24,16},{1,9},{9,1},{17,25},{25,17},{2,10},{10... | collective-permute-start | bytes 479240 | tf_op jit(solution)/shard_map/ppermute | solution.py:488
  40.5 1.5 %collective-permute-start.11 = (bf16[104,768]{1,0:T(8,128)(2,1)S(1)}, bf16[104,768]{1,0:T(8,128)(2,1)S(1)}, u32[]{:S(2)}, u32[]{:S(2)}) collective-permute-start(bf16[104,768]{1,0:T(8,128)(2,1)S(1)} %get-tuple-element.325), channel_id=1, source_target_pairs={{0,16},{8,24},{16,0},{24,8},{1,17},{9,25},{17,1},{25,9},{2,18},{10... | collective-permute-start | bytes 479240 | tf_op jit(solution)/shard_map/ppermute | solution.py:488
  42.1 2.4 %collective-permute-start.12 = (bf16[104,768]{1,0:T(8,128)(2,1)S(1)}, bf16[104,768]{1,0:T(8,128)(2,1)S(1)}, u32[]{:S(2)}, u32[]{:S(2)}) collective-permute-start(bf16[104,768]{1,0:T(8,128)(2,1)S(1)} %get-tuple-element.326), channel_id=1, source_target_pairs={{0,24},{8,16},{16,8},{24,0},{1,25},{9,17},{17,9},{25,1},{2,26},{10... | collective-permute-start | bytes 479240 | tf_op jit(solution)/shard_map/ppermute | solution.py:488
  44.5 1.9 %collective-permute-done.7.refs_1_ = bf16[104,768]{1,0:T(8,128)(2,1)S(1)} collective-permute-done((bf16[104,768]{1,0:T(8,128)(2,1)S(1)}, bf16[104,768]{1,0:T(8,128)(2,1)S(1)}, u32[]{:S(2)}, u32[]{:S(2)}) %collective-permute-start.7) | collective-permute-done | bytes 159776 | tf_op jit(solution)/shard_map/ppermute | solution.py:493
  46.6 3.6 %collective-permute-done.8.refs_2_ = bf16[104,768]{1,0:T(8,128)(2,1)S(1)} collective-permute-done((bf16[104,768]{1,0:T(8,128)(2,1)S(1)}, bf16[104,768]{1,0:T(8,128)(2,1)S(1)}, u32[]{:S(2)}, u32[]{:S(2)}) %collective-permute-start.8) | collective-permute-done | bytes 159776 | tf_op jit(solution)/shard_map/ppermute | solution.py:493
  50.8 2.0 %collective-permute-done.11.refs_2_ = bf16[104,768]{1,0:T(8,128)(2,1)S(1)} collective-permute-done((bf16[104,768]{1,0:T(8,128)(2,1)S(1)}, bf16[104,768]{1,0:T(8,128)(2,1)S(1)}, u32[]{:S(2)}, u32[]{:S(2)}) %collective-permute-start.11) | collective-permute-done | bytes 159776 | tf_op jit(solution)/shard_map/ppermute | solution.py:488
  54.0 1.3 %sort.4 = (bf16[528,768]{1,0:T(8,128)(2,1)S(1)}, s32[4,128]{1,0:T(4,128)S(1)}) custom-call(bf16[104,768]{1,0:T(8,128)(2,1)S(1)} %get-tuple-element.307.refs_0_, bf16[104,768]{1,0:T(8,128)(2,1)S(1)} %collective-permute-done.2.refs_1_, bf16[104,768]{1,0:T(8,128)(2,1)S(1)} %collective-permute-done.3.refs_2_, bf16[104,768]{1,0:T(8,128)(2,1)S(1)} %collective-permute-done.4.refs_3_), custom_call_target="tpu_custom_call" | custom-call | tf_op jit(solution)/shard_map/sort/pallas_call | solution.py:422
  58.5 2.6 %collective-permute-done.15.refs_2_ = bf16[104,768]{1,0:T(8,128)(2,1)S(1)} collective-permute-done((bf16[104,768]{1,0:T(8,128)(2,1)S(1)}, bf16[104,768]{1,0:T(8,128)(2,1)S(1)}, u32[]{:S(2)}, u32[]{:S(2)}) %collective-permute-start.15) | collective-permute-done | bytes 159776 | tf_op jit(solution)/shard_map/ppermute | solution.py:493
  61.1 2.1 %collective-permute-done.16.refs_3_ = bf16[104,768]{1,0:T(8,128)(2,1)S(1)} collective-permute-done((bf16[104,768]{1,0:T(8,128)(2,1)S(1)}, bf16[104,768]{1,0:T(8,128)(2,1)S(1)}, u32[]{:S(2)}, u32[]{:S(2)}) %collective-permute-start.16) | collective-permute-done | bytes 159776 | tf_op jit(solution)/shard_map/ppermute | solution.py:493
  64.5 2.3 %collective-permute-done.20.refs_7_ = bf16[528,768]{1,0:T(8,128)(2,1)S(1)} collective-permute-done((bf16[528,768]{1,0:T(8,128)(2,1)S(1)}, bf16[528,768]{1,0:T(8,128)(2,1)S(1)}, u32[]{:S(2)}, u32[]{:S(2)}) %collective-permute-start.20) | collective-permute-done | bytes 811040 | tf_op jit(solution)/shard_map/ppermute | solution.py:509
  66.8 5.0 %score.1 = f32[16,128]{1,0:T(8,128)} custom-call(bf16[528,768]{1,0:T(8,128)(2,1)S(1)} %get-tuple-element.311.refs_0_, bf16[528,768]{1,0:T(8,128)(2,1)S(1)} %get-tuple-element.321.refs_1_, bf16[528,768]{1,0:T(8,128)(2,1)S(1)} %get-tuple-element.327.refs_2_, bf16[528,768]{1,0:T(8,128)(2,1)S(1)} %get-tuple-element.336.refs_3_, ...), custom_call_target="tpu_custom_call" | custom-call | tf_op jit(solution)/shard_map/score/pallas_call | solution.py:422
  71.8 4.1 %all-to-all-start.3 = ((f32[16,1,128]{2,1,0:T(1,128)}), f32[16,1,128]{2,1,0:T(1,128)S(1)}, u32[]{:S(2)}, u32[]{:S(2)}) async-start(f32[16,1,128]{2,1,0:T(1,128)} %bitcast.14), calls=%async_computation.3 | async-start | bytes 16384 | tf_op jit(solution)/shard_map/all_to_all | solution.py:551
  75.9 7.3 %all-to-all-done.3 = f32[16,1,128]{2,1,0:T(1,128)S(1)} async-done(((f32[16,1,128]{2,1,0:T(1,128)}), f32[16,1,128]{2,1,0:T(1,128)S(1)}, u32[]{:S(2)}, u32[]{:S(2)}) %all-to-all-start.3) | async-done | bytes 8224 | tf_op jit(solution)/shard_map/all_to_all | solution.py:551
  (30 shorter events, 9.0 us)
Async XLA Ops:
  3.9 29.3 %collective-permute-start.5 = (bf16[320,768]{1,0:T(8,128)(2,1)S(1)}, bf16[320,768]{1,0:T(8,128)(2,1)S(1)}, u32[]{:S(2)}, u32[]{:S(2)}) collective-permute-start(bf16[320,768]{1,0:T(8,128)(2,1)S(1)} %get-tuple-element.316), channel_id=1, source_target_pairs={{0,2},{1,3},{2,0},{3,1},{4,6},{5,7},{6,4},{7,5},{8,10},{9,11},{10,... | collective-permute-start | bytes 1474568 | tf_op jit(solution)/shard_map/ppermute | solution.py:511
  11.2 6.7 %collective-permute-start.2 = (bf16[104,768]{1,0:T(8,128)(2,1)S(1)}, bf16[104,768]{1,0:T(8,128)(2,1)S(1)}, u32[]{:S(2)}, u32[]{:S(2)}) collective-permute-start(bf16[104,768]{1,0:T(8,128)(2,1)S(1)} %get-tuple-element.308), channel_id=1, source_target_pairs={{0,8},{8,0},{16,24},{24,16},{1,9},{9,1},{17,25},{25,17},{2,10},{10... | collective-permute-start | bytes 479240 | tf_op jit(solution)/shard_map/ppermute | solution.py:488
  12.7 8.7 %collective-permute-start.3 = (bf16[104,768]{1,0:T(8,128)(2,1)S(1)}, bf16[104,768]{1,0:T(8,128)(2,1)S(1)}, u32[]{:S(2)}, u32[]{:S(2)}) collective-permute-start(bf16[104,768]{1,0:T(8,128)(2,1)S(1)} %get-tuple-element.309), channel_id=1, source_target_pairs={{0,16},{8,24},{16,0},{24,8},{1,17},{9,25},{17,1},{25,9},{2,18},{10... | collective-permute-start | bytes 479240 | tf_op jit(solution)/shard_map/ppermute | solution.py:488
  14.2 7.2 %collective-permute-start.4 = (bf16[104,768]{1,0:T(8,128)(2,1)S(1)}, bf16[104,768]{1,0:T(8,128)(2,1)S(1)}, u32[]{:S(2)}, u32[]{:S(2)}) collective-permute-start(bf16[104,768]{1,0:T(8,128)(2,1)S(1)} %get-tuple-element.310), channel_id=1, source_target_pairs={{0,24},{8,16},{16,8},{24,0},{1,25},{9,17},{17,9},{25,1},{2,26},{10... | collective-permute-start | bytes 479240 | tf_op jit(solution)/shard_map/ppermute | solution.py:488
  21.4 11.7 %collective-permute-start.9 = (bf16[104,768]{1,0:T(8,128)(2,1)S(1)}, bf16[104,768]{1,0:T(8,128)(2,1)S(1)}, u32[]{:S(2)}, u32[]{:S(2)}) collective-permute-start(bf16[104,768]{1,0:T(8,128)(2,1)S(1)} %get-tuple-element.320), channel_id=1, source_target_pairs={{0,25},{1,26},{2,27},{3,24},{8,17},{9,18},{10,19},{11,16},{16,9},{... | collective-permute-start | bytes 479240 | tf_op jit(solution)/shard_map/ppermute | solution.py:493
  33.2 8.9 %collective-permute-start.6 = (bf16[104,768]{1,0:T(8,128)(2,1)S(1)}, bf16[104,768]{1,0:T(8,128)(2,1)S(1)}, u32[]{:S(2)}, u32[]{:S(2)}) collective-permute-start(bf16[104,768]{1,0:T(8,128)(2,1)S(1)} %get-tuple-element.317), channel_id=1, source_target_pairs={{0,1},{1,2},{2,3},{3,0},{8,9},{9,10},{10,11},{11,8},{16,17},{17,18... | collective-permute-start | bytes 479240 | tf_op jit(solution)/shard_map/ppermute | solution.py:493
  33.2 13.3 %collective-permute-start.7 = (bf16[104,768]{1,0:T(8,128)(2,1)S(1)}, bf16[104,768]{1,0:T(8,128)(2,1)S(1)}, u32[]{:S(2)}, u32[]{:S(2)}) collective-permute-start(bf16[104,768]{1,0:T(8,128)(2,1)S(1)} %get-tuple-element.318), channel_id=1, source_target_pairs={{0,9},{1,10},{2,11},{3,8},{8,1},{9,2},{10,3},{11,0},{16,25},{17,26... | collective-permute-start | bytes 479240 | tf_op jit(solution)/shard_map/ppermute | solution.py:493
  34.9 15.3 %collective-permute-start.8 = (bf16[104,768]{1,0:T(8,128)(2,1)S(1)}, bf16[104,768]{1,0:T(8,128)(2,1)S(1)}, u32[]{:S(2)}, u32[]{:S(2)}) collective-permute-start(bf16[104,768]{1,0:T(8,128)(2,1)S(1)} %get-tuple-element.319), channel_id=1, source_target_pairs={{0,17},{1,18},{2,19},{3,16},{8,25},{9,26},{10,27},{11,24},{16,1},{... | collective-permute-start | bytes 479240 | tf_op jit(solution)/shard_map/ppermute | solution.py:493
  39.0 11.2 %collective-permute-start.10 = (bf16[104,768]{1,0:T(8,128)(2,1)S(1)}, bf16[104,768]{1,0:T(8,128)(2,1)S(1)}, u32[]{:S(2)}, u32[]{:S(2)}) collective-permute-start(bf16[104,768]{1,0:T(8,128)(2,1)S(1)} %get-tuple-element.324), channel_id=1, source_target_pairs={{0,8},{8,0},{16,24},{24,16},{1,9},{9,1},{17,25},{25,17},{2,10},{10... | collective-permute-start | bytes 479240 | tf_op jit(solution)/shard_map/ppermute | solution.py:488
  40.5 12.3 %collective-permute-start.11 = (bf16[104,768]{1,0:T(8,128)(2,1)S(1)}, bf16[104,768]{1,0:T(8,128)(2,1)S(1)}, u32[]{:S(2)}, u32[]{:S(2)}) collective-permute-start(bf16[104,768]{1,0:T(8,128)(2,1)S(1)} %get-tuple-element.325), channel_id=1, source_target_pairs={{0,16},{8,24},{16,0},{24,8},{1,17},{9,25},{17,1},{25,9},{2,18},{10... | collective-permute-start | bytes 479240 | tf_op jit(solution)/shard_map/ppermute | solution.py:488
  42.1 14.4 %collective-permute-start.12 = (bf16[104,768]{1,0:T(8,128)(2,1)S(1)}, bf16[104,768]{1,0:T(8,128)(2,1)S(1)}, u32[]{:S(2)}, u32[]{:S(2)}) collective-permute-start(bf16[104,768]{1,0:T(8,128)(2,1)S(1)} %get-tuple-element.326), channel_id=1, source_target_pairs={{0,24},{8,16},{16,8},{24,0},{1,25},{9,17},{17,9},{25,1},{2,26},{10... | collective-permute-start | bytes 479240 | tf_op jit(solution)/shard_map/ppermute | solution.py:488
  46.4 11.4 %collective-permute-start.13 = (bf16[104,768]{1,0:T(8,128)(2,1)S(1)}, bf16[104,768]{1,0:T(8,128)(2,1)S(1)}, u32[]{:S(2)}, u32[]{:S(2)}) collective-permute-start(bf16[104,768]{1,0:T(8,128)(2,1)S(1)} %get-tuple-element.332), channel_id=1, source_target_pairs={{0,3},{1,0},{2,1},{3,2},{8,11},{9,8},{10,9},{11,10},{16,19},{17,16... | collective-permute-start | bytes 479240 | tf_op jit(solution)/shard_map/ppermute | solution.py:493
  50.2 8.2 %collective-permute-start.14 = (bf16[104,768]{1,0:T(8,128)(2,1)S(1)}, bf16[104,768]{1,0:T(8,128)(2,1)S(1)}, u32[]{:S(2)}, u32[]{:S(2)}) collective-permute-start(bf16[104,768]{1,0:T(8,128)(2,1)S(1)} %get-tuple-element.333), channel_id=1, source_target_pairs={{0,11},{1,8},{2,9},{3,10},{8,3},{9,0},{10,1},{11,2},{16,27},{17,24... | collective-permute-start | bytes 479240 | tf_op jit(solution)/shard_map/ppermute | solution.py:493
  50.2 10.9 %collective-permute-start.15 = (bf16[104,768]{1,0:T(8,128)(2,1)S(1)}, bf16[104,768]{1,0:T(8,128)(2,1)S(1)}, u32[]{:S(2)}, u32[]{:S(2)}) collective-permute-start(bf16[104,768]{1,0:T(8,128)(2,1)S(1)} %get-tuple-element.334), channel_id=1, source_target_pairs={{0,19},{1,16},{2,17},{3,18},{8,27},{9,24},{10,25},{11,26},{16,3},{... | collective-permute-start | bytes 479240 | tf_op jit(solution)/shard_map/ppermute | solution.py:493
  52.8 10.3 %collective-permute-start.16 = (bf16[104,768]{1,0:T(8,128)(2,1)S(1)}, bf16[104,768]{1,0:T(8,128)(2,1)S(1)}, u32[]{:S(2)}, u32[]{:S(2)}) collective-permute-start(bf16[104,768]{1,0:T(8,128)(2,1)S(1)} %get-tuple-element.335), channel_id=1, source_target_pairs={{0,27},{1,24},{2,25},{3,26},{8,19},{9,16},{10,17},{11,18},{16,11},... | collective-permute-start | bytes 479240 | tf_op jit(solution)/shard_map/ppermute | solution.py:493
  56.5 8.0 %collective-permute-start.17 = (bf16[528,768]{1,0:T(8,128)(2,1)S(1)}, bf16[528,768]{1,0:T(8,128)(2,1)S(1)}, u32[]{:S(2)}, u32[]{:S(2)}) collective-permute-start(bf16[528,768]{1,0:T(8,128)(2,1)S(1)} %get-tuple-element.311.refs_0_), channel_id=1, source_target_pairs={{0,4},{4,0},{1,5},{5,1},{2,6},{6,2},{3,7},{7,3},{8,12},{12,8},{9,1... | collective-permute-start | bytes 2433032 | tf_op jit(solution)/shard_map/ppermute | solution.py:509
  57.9 6.6 %collective-permute-start.19 = (bf16[528,768]{1,0:T(8,128)(2,1)S(1)}, bf16[528,768]{1,0:T(8,128)(2,1)S(1)}, u32[]{:S(2)}, u32[]{:S(2)}) collective-permute-start(bf16[528,768]{1,0:T(8,128)(2,1)S(1)} %get-tuple-element.327.refs_2_), channel_id=1, source_target_pairs={{0,4},{4,0},{1,5},{5,1},{2,6},{6,2},{3,7},{7,3},{8,12},{12,8},{9,1... | collective-permute-start | bytes 2433032 | tf_op jit(solution)/shard_map/ppermute | solution.py:509
  58.4 6.1 %collective-permute-start.18 = (bf16[528,768]{1,0:T(8,128)(2,1)S(1)}, bf16[528,768]{1,0:T(8,128)(2,1)S(1)}, u32[]{:S(2)}, u32[]{:S(2)}) collective-permute-start(bf16[528,768]{1,0:T(8,128)(2,1)S(1)} %get-tuple-element.321.refs_1_), channel_id=1, source_target_pairs={{0,4},{4,0},{1,5},{5,1},{2,6},{6,2},{3,7},{7,3},{8,12},{12,8},{9,1... | collective-permute-start | bytes 2433032 | tf_op jit(solution)/shard_map/ppermute | solution.py:509
  64.4 2.4 %collective-permute-start.20 = (bf16[528,768]{1,0:T(8,128)(2,1)S(1)}, bf16[528,768]{1,0:T(8,128)(2,1)S(1)}, u32[]{:S(2)}, u32[]{:S(2)}) collective-permute-start(bf16[528,768]{1,0:T(8,128)(2,1)S(1)} %get-tuple-element.336.refs_3_), channel_id=1, source_target_pairs={{0,4},{4,0},{1,5},{5,1},{2,6},{6,2},{3,7},{7,3},{8,12},{12,8},{9,1... | collective-permute-start | bytes 2433032 | tf_op jit(solution)/shard_map/ppermute | solution.py:509
  66.8 16.4 %copy-start.3 = (s32[1024]{0:T(1024)S(1)}, s32[1024]{0:T(1024)}, u32[]{:S(2)}) copy-start(s32[1024]{0:T(1024)} %param.9) | copy-start | bytes 12292
  66.8 18.0 %copy-start = (f32[1024,768]{1,0:T(8,128)S(1)}, f32[1024,768]{1,0:T(8,128)}, u32[]{:S(2)}) copy-start(f32[1024,768]{1,0:T(8,128)} %emb_ref.1) | copy-start | bytes 9437188
  71.8 11.4 %all-to-all-start.3 = ((f32[16,1,128]{2,1,0:T(1,128)}), f32[16,1,128]{2,1,0:T(1,128)S(1)}, u32[]{:S(2)}, u32[]{:S(2)}) async-start(f32[16,1,128]{2,1,0:T(1,128)} %bitcast.14), calls=%async_computation.3 | async-start | bytes 16384 | tf_op jit(solution)/shard_map/all_to_all | solution.py:551

commit v10 on v9

--- a/solution.py
+++ b/solution.py
@@ -514,7 +514,7 @@
     blocks = [(shift, side) for shift in order[1:] for side in range(across)]
     beside = [(shift, across - 1) for shift in order[1:2]]
     arrived = {
-        (shift, side): send_far(after(packed[shift], *near), shift, side) for shift, side in beside
+        (shift, side): send_far(packed[shift], shift, side) for shift, side in beside
     }
     regrouped = call(
         functools.partial(regroup_kernel, size),

time: 85.5 us -> 84.5 us (0.988)
  waiting for transfers between devices: 37.7 us -> 35 us
  starting transfers between devices: 27.6 us -> 29.4 us
    ppermute x6, waiting for transfers between devices: 8.73 us -> 0.23 us  [send_across(): lax.ppermute(blocks[side], 'chip', over(side))]
    ppermute x1, waiting for transfers between devices: 9.22 us -> 15 us  [body(): pooled = lax.ppermute(pool_rows, 'tile', along(order[0]))]
    ppermute x8, starting transfers between devices: 9.56 us -> 11.8 us  [send_far(): return lax.ppermute(blocks[side], ('chip', 'tile'), route)]
  transfers between devices with their start and end apart: 20 -> 20, of which waited for: 10 -> 8; matrix products, arithmetic and copies ran while one was open for 0% -> 0% of each run, Pallas kernels for 10% -> 10%
where the time goes in v10:
time: 84.5 us; the launch traced here: 84.3 us
  waiting for transfers between devices  35 us (41%)
  starting transfers between devices  29.4 us (35%)
  Pallas kernels  18.7 us (22%)
  between operations  1 us (1%)
    pallas_call x9, Pallas kernels, call(): pl.pallas_call(kernel, out_shape=out_shape, in_specs=[vmem] * len(inputs)...  18.7 us
    ppermute x1, waiting for transfers between devices, body(): pooled = lax.ppermute(pool_rows, 'tile', along(order[0]))  15 us
    ppermute x8, starting transfers between devices, send_far(): return lax.ppermute(blocks[side], ('chip', 'tile'), route)  11.8 us
    ppermute x8, waiting for transfers between devices, send_far(): return lax.ppermute(blocks[side], ('chip', 'tile'), route)  10.2 us
    ppermute x6, starting transfers between devices, send_across(): lax.ppermute(blocks[side], 'chip', over(side))  9.05 us
    all_to_all x1, waiting for transfers between devices, body(): lax.all_to_all(totals, ('chip', 'tile'), split_axis=0, concat_axis=0, til...  7.26 us
    ppermute x1, starting transfers between devices, body(): pooled = lax.ppermute(pool_rows, 'tile', along(order[0]))  4.1 us
    all_to_all x1, starting transfers between devices, body(): lax.all_to_all(totals, ('chip', 'tile'), split_axis=0, concat_axis=0, til...  3.59 us
  transfers between devices with their start and end apart: 20, of which 8 were waited for; matrix products, arithmetic and copies ran while one was open for 0% of the time, Pallas kernels for 10%

profile of v10, /device:TPU:0, one launch (start us, length us, event | category | flops | bytes accessed | tf_op | source)
XLA Modules:
  0.0 84.3 jit_solution(10708778334966152702)
XLA Ops:
  0.0 3.9 %plan.1 = (bf16[320,768]{1,0:T(8,128)(2,1)S(1)}, bf16[1152,768]{1,0:T(8,128)(2,1)S(1)}, s32[1,1152]{1,0:T(1,128)S(1)}, f32[1,1024]{1,0:T(1,128)S(1)}) custom-call(f32[1024,768]{1,0:T(8,128)} %emb_ref.1, s32[1,1024]{1,0:T(1,128)} %bitcast.74), custom_call_target="tpu_custom_call" | custom-call | tf_op jit(solution)/shard_map/plan/pallas_call | solution.py:422
  3.9 4.1 %collective-permute-start.5 = (bf16[320,768]{1,0:T(8,128)(2,1)S(1)}, bf16[320,768]{1,0:T(8,128)(2,1)S(1)}, u32[]{:S(2)}, u32[]{:S(2)}) collective-permute-start(bf16[320,768]{1,0:T(8,128)(2,1)S(1)} %get-tuple-element.315), channel_id=1, source_target_pairs={{0,2},{1,3},{2,0},{3,1},{4,6},{5,7},{6,4},{7,5},{8,10},{9,11},{10,... | collective-permute-start | bytes 1474568 | tf_op jit(solution)/shard_map/ppermute | solution.py:511
  8.0 3.2 %pack.1 = (bf16[104,768]{1,0:T(8,128)(2,1)S(1)}, bf16[104,768]{1,0:T(8,128)(2,1)S(1)}, bf16[104,768]{1,0:T(8,128)(2,1)S(1)}, bf16[104,768]{1,0:T(8,128)(2,1)S(1)...) custom-call(bf16[1152,768]{1,0:T(8,128)(2,1)S(1)} %get-tuple-element, ...), custom_call_target="tpu_custom_call" | custom-call | tf_op jit(solution)/shard_map/pack/pallas_call | solution.py:422
  11.1 1.6 %collective-permute-start.2 = (bf16[104,768]{1,0:T(8,128)(2,1)S(1)}, bf16[104,768]{1,0:T(8,128)(2,1)S(1)}, u32[]{:S(2)}, u32[]{:S(2)}) collective-permute-start(bf16[104,768]{1,0:T(8,128)(2,1)S(1)} %get-tuple-element.307), channel_id=1, source_target_pairs={{0,8},{8,0},{16,24},{24,16},{1,9},{9,1},{17,25},{25,17},{2,10},{10... | collective-permute-start | bytes 479240 | tf_op jit(solution)/shard_map/ppermute | solution.py:488
  12.7 1.5 %collective-permute-start.3 = (bf16[104,768]{1,0:T(8,128)(2,1)S(1)}, bf16[104,768]{1,0:T(8,128)(2,1)S(1)}, u32[]{:S(2)}, u32[]{:S(2)}) collective-permute-start(bf16[104,768]{1,0:T(8,128)(2,1)S(1)} %get-tuple-element.308), channel_id=1, source_target_pairs={{0,16},{8,24},{16,0},{24,8},{1,17},{9,25},{17,1},{25,9},{2,18},{10... | collective-permute-start | bytes 479240 | tf_op jit(solution)/shard_map/ppermute | solution.py:488
  14.7 3.5 %collective-permute-start.9 = (bf16[104,768]{1,0:T(8,128)(2,1)S(1)}, bf16[104,768]{1,0:T(8,128)(2,1)S(1)}, u32[]{:S(2)}, u32[]{:S(2)}) collective-permute-start(bf16[104,768]{1,0:T(8,128)(2,1)S(1)} %get-tuple-element.314), channel_id=1, source_target_pairs={{0,25},{1,26},{2,27},{3,24},{8,17},{9,18},{10,19},{11,16},{16,9},{... | collective-permute-start | bytes 479240 | tf_op jit(solution)/shard_map/ppermute | solution.py:493
  18.2 15.0 %collective-permute-done.5.pool_ref = bf16[320,768]{1,0:T(8,128)(2,1)S(1)} collective-permute-done((bf16[320,768]{1,0:T(8,128)(2,1)S(1)}, bf16[320,768]{1,0:T(8,128)(2,1)S(1)}, u32[]{:S(2)}, u32[]{:S(2)}) %collective-permute-start.5) | collective-permute-done | bytes 491552 | tf_op jit(solution)/shard_map/ppermute | solution.py:511
  33.2 1.7 %collective-permute-start.7 = (bf16[104,768]{1,0:T(8,128)(2,1)S(1)}, bf16[104,768]{1,0:T(8,128)(2,1)S(1)}, u32[]{:S(2)}, u32[]{:S(2)}) collective-permute-start(bf16[104,768]{1,0:T(8,128)(2,1)S(1)} %get-tuple-element.317), channel_id=1, source_target_pairs={{0,9},{1,10},{2,11},{3,8},{8,1},{9,2},{10,3},{11,0},{16,25},{17,26... | collective-permute-start | bytes 479240 | tf_op jit(solution)/shard_map/ppermute | solution.py:493
  34.9 3.4 %collective-permute-start.8 = (bf16[104,768]{1,0:T(8,128)(2,1)S(1)}, bf16[104,768]{1,0:T(8,128)(2,1)S(1)}, u32[]{:S(2)}, u32[]{:S(2)}) collective-permute-start(bf16[104,768]{1,0:T(8,128)(2,1)S(1)} %get-tuple-element.318), channel_id=1, source_target_pairs={{0,17},{1,18},{2,19},{3,16},{8,25},{9,26},{10,27},{11,24},{16,1},{... | collective-permute-start | bytes 479240 | tf_op jit(solution)/shard_map/ppermute | solution.py:493
  39.0 1.5 %collective-permute-start.10 = (bf16[104,768]{1,0:T(8,128)(2,1)S(1)}, bf16[104,768]{1,0:T(8,128)(2,1)S(1)}, u32[]{:S(2)}, u32[]{:S(2)}) collective-permute-start(bf16[104,768]{1,0:T(8,128)(2,1)S(1)} %get-tuple-element.322), channel_id=1, source_target_pairs={{0,8},{8,0},{16,24},{24,16},{1,9},{9,1},{17,25},{25,17},{2,10},{10... | collective-permute-start | bytes 479240 | tf_op jit(solution)/shard_map/ppermute | solution.py:488
  40.5 1.5 %collective-permute-start.11 = (bf16[104,768]{1,0:T(8,128)(2,1)S(1)}, bf16[104,768]{1,0:T(8,128)(2,1)S(1)}, u32[]{:S(2)}, u32[]{:S(2)}) collective-permute-start(bf16[104,768]{1,0:T(8,128)(2,1)S(1)} %get-tuple-element.323), channel_id=1, source_target_pairs={{0,16},{8,24},{16,0},{24,8},{1,17},{9,25},{17,1},{25,9},{2,18},{10... | collective-permute-start | bytes 479240 | tf_op jit(solution)/shard_map/ppermute | solution.py:488
  42.0 2.5 %collective-permute-start.12 = (bf16[104,768]{1,0:T(8,128)(2,1)S(1)}, bf16[104,768]{1,0:T(8,128)(2,1)S(1)}, u32[]{:S(2)}, u32[]{:S(2)}) collective-permute-start(bf16[104,768]{1,0:T(8,128)(2,1)S(1)} %get-tuple-element.324), channel_id=1, source_target_pairs={{0,24},{8,16},{16,8},{24,0},{1,25},{9,17},{17,9},{25,1},{2,26},{10... | collective-permute-start | bytes 479240 | tf_op jit(solution)/shard_map/ppermute | solution.py:488
  44.5 1.9 %collective-permute-done.7.refs_1_ = bf16[104,768]{1,0:T(8,128)(2,1)S(1)} collective-permute-done((bf16[104,768]{1,0:T(8,128)(2,1)S(1)}, bf16[104,768]{1,0:T(8,128)(2,1)S(1)}, u32[]{:S(2)}, u32[]{:S(2)}) %collective-permute-start.7) | collective-permute-done | bytes 159776 | tf_op jit(solution)/shard_map/ppermute | solution.py:493
  46.4 3.7 %collective-permute-done.8.refs_2_ = bf16[104,768]{1,0:T(8,128)(2,1)S(1)} collective-permute-done((bf16[104,768]{1,0:T(8,128)(2,1)S(1)}, bf16[104,768]{1,0:T(8,128)(2,1)S(1)}, u32[]{:S(2)}, u32[]{:S(2)}) %collective-permute-start.8) | collective-permute-done | bytes 159776 | tf_op jit(solution)/shard_map/ppermute | solution.py:493
  50.1 2.8 %collective-permute-start.15 = (bf16[104,768]{1,0:T(8,128)(2,1)S(1)}, bf16[104,768]{1,0:T(8,128)(2,1)S(1)}, u32[]{:S(2)}, u32[]{:S(2)}) collective-permute-start(bf16[104,768]{1,0:T(8,128)(2,1)S(1)} %get-tuple-element.332), channel_id=1, source_target_pairs={{0,19},{1,16},{2,17},{3,18},{8,27},{9,24},{10,25},{11,26},{16,3},{... | collective-permute-start | bytes 479240 | tf_op jit(solution)/shard_map/ppermute | solution.py:493
  53.6 1.2 %sort.4 = (bf16[528,768]{1,0:T(8,128)(2,1)S(1)}, s32[4,128]{1,0:T(4,128)S(1)}) custom-call(bf16[104,768]{1,0:T(8,128)(2,1)S(1)} %get-tuple-element.306.refs_0_, bf16[104,768]{1,0:T(8,128)(2,1)S(1)} %collective-permute-done.2.refs_1_, bf16[104,768]{1,0:T(8,128)(2,1)S(1)} %collective-permute-done.3.refs_2_, bf16[104,768]{1,0:T(8,128)(2,1)S(1)} %collective-permute-done.4.refs_3_), custom_call_target="tpu_custom_call" | custom-call | tf_op jit(solution)/shard_map/sort/pallas_call | solution.py:422
  54.9 1.2 %sort.5 = (bf16[528,768]{1,0:T(8,128)(2,1)S(1)}, s32[4,128]{1,0:T(4,128)S(1)}) custom-call(bf16[104,768]{1,0:T(8,128)(2,1)S(1)} %collective-permute-done.6.refs_0_, bf16[104,768]{1,0:T(8,128)(2,1)S(1)} %collective-permute-done.7.refs_1_, bf16[104,768]{1,0:T(8,128)(2,1)S(1)} %collective-permute-done.8.refs_2_, bf16[104,768]{1,0:T(8,128)(2,1)S(1)} %collective-permute-done.9.refs_3_), custom_call_target="tpu_custom_call" | custom-call | tf_op jit(solution)/shard_map/sort/pallas_call | solution.py:422
  56.2 1.3 %sort.6 = (bf16[528,768]{1,0:T(8,128)(2,1)S(1)}, s32[4,128]{1,0:T(4,128)S(1)}) custom-call(bf16[104,768]{1,0:T(8,128)(2,1)S(1)} %get-tuple-element.321.refs_0_, bf16[104,768]{1,0:T(8,128)(2,1)S(1)} %collective-permute-done.10.refs_1_, bf16[104,768]{1,0:T(8,128)(2,1)S(1)} %collective-permute-done.11.refs_2_, bf16[104,768]{1,0:T(8,128)(2,1)S(1)} %collective-permute-done.12.refs_3_), custom_call_target="tpu_custom_call" | custom-call | tf_op jit(solution)/shard_map/sort/pallas_call | solution.py:422
  58.1 2.8 %collective-permute-done.15.refs_2_ = bf16[104,768]{1,0:T(8,128)(2,1)S(1)} collective-permute-done((bf16[104,768]{1,0:T(8,128)(2,1)S(1)}, bf16[104,768]{1,0:T(8,128)(2,1)S(1)}, u32[]{:S(2)}, u32[]{:S(2)}) %collective-permute-start.15) | collective-permute-done | bytes 159776 | tf_op jit(solution)/shard_map/ppermute | solution.py:493
  60.9 1.8 %collective-permute-done.16.refs_3_ = bf16[104,768]{1,0:T(8,128)(2,1)S(1)} collective-permute-done((bf16[104,768]{1,0:T(8,128)(2,1)S(1)}, bf16[104,768]{1,0:T(8,128)(2,1)S(1)}, u32[]{:S(2)}, u32[]{:S(2)}) %collective-permute-start.16) | collective-permute-done | bytes 159776 | tf_op jit(solution)/shard_map/ppermute | solution.py:493
  64.1 2.3 %collective-permute-done.20.refs_7_ = bf16[528,768]{1,0:T(8,128)(2,1)S(1)} collective-permute-done((bf16[528,768]{1,0:T(8,128)(2,1)S(1)}, bf16[528,768]{1,0:T(8,128)(2,1)S(1)}, u32[]{:S(2)}, u32[]{:S(2)}) %collective-permute-start.20) | collective-permute-done | bytes 811040 | tf_op jit(solution)/shard_map/ppermute | solution.py:509
  66.4 5.0 %score.1 = f32[16,128]{1,0:T(8,128)} custom-call(bf16[528,768]{1,0:T(8,128)(2,1)S(1)} %get-tuple-element.310.refs_0_, bf16[528,768]{1,0:T(8,128)(2,1)S(1)} %get-tuple-element.319.refs_1_, bf16[528,768]{1,0:T(8,128)(2,1)S(1)} %get-tuple-element.325.refs_2_, bf16[528,768]{1,0:T(8,128)(2,1)S(1)} %get-tuple-element.334.refs_3_, ...), custom_call_target="tpu_custom_call" | custom-call | tf_op jit(solution)/shard_map/score/pallas_call | solution.py:422
  71.3 3.6 %all-to-all-start.3 = ((f32[16,1,128]{2,1,0:T(1,128)}), f32[16,1,128]{2,1,0:T(1,128)S(1)}, u32[]{:S(2)}, u32[]{:S(2)}) async-start(f32[16,1,128]{2,1,0:T(1,128)} %bitcast.14), calls=%async_computation.3 | async-start | bytes 16384 | tf_op jit(solution)/shard_map/all_to_all | solution.py:551
  74.9 7.3 %all-to-all-done.3 = f32[16,1,128]{2,1,0:T(1,128)S(1)} async-done(((f32[16,1,128]{2,1,0:T(1,128)}), f32[16,1,128]{2,1,0:T(1,128)S(1)}, u32[]{:S(2)}, u32[]{:S(2)}) %all-to-all-start.3) | async-done | bytes 8224 | tf_op jit(solution)/shard_map/all_to_all | solution.py:551
  (30 shorter events, 5.2 us)
Async XLA Ops:
  3.9 29.3 %collective-permute-start.5 = (bf16[320,768]{1,0:T(8,128)(2,1)S(1)}, bf16[320,768]{1,0:T(8,128)(2,1)S(1)}, u32[]{:S(2)}, u32[]{:S(2)}) collective-permute-start(bf16[320,768]{1,0:T(8,128)(2,1)S(1)} %get-tuple-element.315), channel_id=1, source_target_pairs={{0,2},{1,3},{2,0},{3,1},{4,6},{5,7},{6,4},{7,5},{8,10},{9,11},{10,... | collective-permute-start | bytes 1474568 | tf_op jit(solution)/shard_map/ppermute | solution.py:511
  11.1 22.0 %collective-permute-start.2 = (bf16[104,768]{1,0:T(8,128)(2,1)S(1)}, bf16[104,768]{1,0:T(8,128)(2,1)S(1)}, u32[]{:S(2)}, u32[]{:S(2)}) collective-permute-start(bf16[104,768]{1,0:T(8,128)(2,1)S(1)} %get-tuple-element.307), channel_id=1, source_target_pairs={{0,8},{8,0},{16,24},{24,16},{1,9},{9,1},{17,25},{25,17},{2,10},{10... | collective-permute-start | bytes 479240 | tf_op jit(solution)/shard_map/ppermute | solution.py:488
  12.7 20.5 %collective-permute-start.3 = (bf16[104,768]{1,0:T(8,128)(2,1)S(1)}, bf16[104,768]{1,0:T(8,128)(2,1)S(1)}, u32[]{:S(2)}, u32[]{:S(2)}) collective-permute-start(bf16[104,768]{1,0:T(8,128)(2,1)S(1)} %get-tuple-element.308), channel_id=1, source_target_pairs={{0,16},{8,24},{16,0},{24,8},{1,17},{9,25},{17,1},{25,9},{2,18},{10... | collective-permute-start | bytes 479240 | tf_op jit(solution)/shard_map/ppermute | solution.py:488
  14.2 18.9 %collective-permute-start.4 = (bf16[104,768]{1,0:T(8,128)(2,1)S(1)}, bf16[104,768]{1,0:T(8,128)(2,1)S(1)}, u32[]{:S(2)}, u32[]{:S(2)}) collective-permute-start(bf16[104,768]{1,0:T(8,128)(2,1)S(1)} %get-tuple-element.309), channel_id=1, source_target_pairs={{0,24},{8,16},{16,8},{24,0},{1,25},{9,17},{17,9},{25,1},{2,26},{10... | collective-permute-start | bytes 479240 | tf_op jit(solution)/shard_map/ppermute | solution.py:488
  14.7 18.5 %collective-permute-start.9 = (bf16[104,768]{1,0:T(8,128)(2,1)S(1)}, bf16[104,768]{1,0:T(8,128)(2,1)S(1)}, u32[]{:S(2)}, u32[]{:S(2)}) collective-permute-start(bf16[104,768]{1,0:T(8,128)(2,1)S(1)} %get-tuple-element.314), channel_id=1, source_target_pairs={{0,25},{1,26},{2,27},{3,24},{8,17},{9,18},{10,19},{11,16},{16,9},{... | collective-permute-start | bytes 479240 | tf_op jit(solution)/shard_map/ppermute | solution.py:493
  33.1 8.9 %collective-permute-start.6 = (bf16[104,768]{1,0:T(8,128)(2,1)S(1)}, bf16[104,768]{1,0:T(8,128)(2,1)S(1)}, u32[]{:S(2)}, u32[]{:S(2)}) collective-permute-start(bf16[104,768]{1,0:T(8,128)(2,1)S(1)} %get-tuple-element.316), channel_id=1, source_target_pairs={{0,1},{1,2},{2,3},{3,0},{8,9},{9,10},{10,11},{11,8},{16,17},{17,18... | collective-permute-start | bytes 479240 | tf_op jit(solution)/shard_map/ppermute | solution.py:493
  33.2 13.2 %collective-permute-start.7 = (bf16[104,768]{1,0:T(8,128)(2,1)S(1)}, bf16[104,768]{1,0:T(8,128)(2,1)S(1)}, u32[]{:S(2)}, u32[]{:S(2)}) collective-permute-start(bf16[104,768]{1,0:T(8,128)(2,1)S(1)} %get-tuple-element.317), channel_id=1, source_target_pairs={{0,9},{1,10},{2,11},{3,8},{8,1},{9,2},{10,3},{11,0},{16,25},{17,26... | collective-permute-start | bytes 479240 | tf_op jit(solution)/shard_map/ppermute | solution.py:493
  34.9 15.2 %collective-permute-start.8 = (bf16[104,768]{1,0:T(8,128)(2,1)S(1)}, bf16[104,768]{1,0:T(8,128)(2,1)S(1)}, u32[]{:S(2)}, u32[]{:S(2)}) collective-permute-start(bf16[104,768]{1,0:T(8,128)(2,1)S(1)} %get-tuple-element.318), channel_id=1, source_target_pairs={{0,17},{1,18},{2,19},{3,16},{8,25},{9,26},{10,27},{11,24},{16,1},{... | collective-permute-start | bytes 479240 | tf_op jit(solution)/shard_map/ppermute | solution.py:493
  39.0 11.2 %collective-permute-start.10 = (bf16[104,768]{1,0:T(8,128)(2,1)S(1)}, bf16[104,768]{1,0:T(8,128)(2,1)S(1)}, u32[]{:S(2)}, u32[]{:S(2)}) collective-permute-start(bf16[104,768]{1,0:T(8,128)(2,1)S(1)} %get-tuple-element.322), channel_id=1, source_target_pairs={{0,8},{8,0},{16,24},{24,16},{1,9},{9,1},{17,25},{25,17},{2,10},{10... | collective-permute-start | bytes 479240 | tf_op jit(solution)/shard_map/ppermute | solution.py:488
  40.5 12.7 %collective-permute-start.11 = (bf16[104,768]{1,0:T(8,128)(2,1)S(1)}, bf16[104,768]{1,0:T(8,128)(2,1)S(1)}, u32[]{:S(2)}, u32[]{:S(2)}) collective-permute-start(bf16[104,768]{1,0:T(8,128)(2,1)S(1)} %get-tuple-element.323), channel_id=1, source_target_pairs={{0,16},{8,24},{16,0},{24,8},{1,17},{9,25},{17,1},{25,9},{2,18},{10... | collective-permute-start | bytes 479240 | tf_op jit(solution)/shard_map/ppermute | solution.py:488
  42.0 14.1 %collective-permute-start.12 = (bf16[104,768]{1,0:T(8,128)(2,1)S(1)}, bf16[104,768]{1,0:T(8,128)(2,1)S(1)}, u32[]{:S(2)}, u32[]{:S(2)}) collective-permute-start(bf16[104,768]{1,0:T(8,128)(2,1)S(1)} %get-tuple-element.324), channel_id=1, source_target_pairs={{0,24},{8,16},{16,8},{24,0},{1,25},{9,17},{17,9},{25,1},{2,26},{10... | collective-permute-start | bytes 479240 | tf_op jit(solution)/shard_map/ppermute | solution.py:488
  46.4 11.1 %collective-permute-start.13 = (bf16[104,768]{1,0:T(8,128)(2,1)S(1)}, bf16[104,768]{1,0:T(8,128)(2,1)S(1)}, u32[]{:S(2)}, u32[]{:S(2)}) collective-permute-start(bf16[104,768]{1,0:T(8,128)(2,1)S(1)} %get-tuple-element.330), channel_id=1, source_target_pairs={{0,3},{1,0},{2,1},{3,2},{8,11},{9,8},{10,9},{11,10},{16,19},{17,16... | collective-permute-start | bytes 479240 | tf_op jit(solution)/shard_map/ppermute | solution.py:493
  50.1 7.9 %collective-permute-start.14 = (bf16[104,768]{1,0:T(8,128)(2,1)S(1)}, bf16[104,768]{1,0:T(8,128)(2,1)S(1)}, u32[]{:S(2)}, u32[]{:S(2)}) collective-permute-start(bf16[104,768]{1,0:T(8,128)(2,1)S(1)} %get-tuple-element.331), channel_id=1, source_target_pairs={{0,11},{1,8},{2,9},{3,10},{8,3},{9,0},{10,1},{11,2},{16,27},{17,24... | collective-permute-start | bytes 479240 | tf_op jit(solution)/shard_map/ppermute | solution.py:493
  50.1 10.8 %collective-permute-start.15 = (bf16[104,768]{1,0:T(8,128)(2,1)S(1)}, bf16[104,768]{1,0:T(8,128)(2,1)S(1)}, u32[]{:S(2)}, u32[]{:S(2)}) collective-permute-start(bf16[104,768]{1,0:T(8,128)(2,1)S(1)} %get-tuple-element.332), channel_id=1, source_target_pairs={{0,19},{1,16},{2,17},{3,18},{8,27},{9,24},{10,25},{11,26},{16,3},{... | collective-permute-start | bytes 479240 | tf_op jit(solution)/shard_map/ppermute | solution.py:493
  53.2 9.5 %collective-permute-start.16 = (bf16[104,768]{1,0:T(8,128)(2,1)S(1)}, bf16[104,768]{1,0:T(8,128)(2,1)S(1)}, u32[]{:S(2)}, u32[]{:S(2)}) collective-permute-start(bf16[104,768]{1,0:T(8,128)(2,1)S(1)} %get-tuple-element.333), channel_id=1, source_target_pairs={{0,27},{1,24},{2,25},{3,26},{8,19},{9,16},{10,17},{11,18},{16,11},... | collective-permute-start | bytes 479240 | tf_op jit(solution)/shard_map/ppermute | solution.py:493
  56.1 7.9 %collective-permute-start.17 = (bf16[528,768]{1,0:T(8,128)(2,1)S(1)}, bf16[528,768]{1,0:T(8,128)(2,1)S(1)}, u32[]{:S(2)}, u32[]{:S(2)}) collective-permute-start(bf16[528,768]{1,0:T(8,128)(2,1)S(1)} %get-tuple-element.310.refs_0_), channel_id=1, source_target_pairs={{0,4},{4,0},{1,5},{5,1},{2,6},{6,2},{3,7},{7,3},{8,12},{12,8},{9,1... | collective-permute-start | bytes 2433032 | tf_op jit(solution)/shard_map/ppermute | solution.py:509
  57.5 6.6 %collective-permute-start.19 = (bf16[528,768]{1,0:T(8,128)(2,1)S(1)}, bf16[528,768]{1,0:T(8,128)(2,1)S(1)}, u32[]{:S(2)}, u32[]{:S(2)}) collective-permute-start(bf16[528,768]{1,0:T(8,128)(2,1)S(1)} %get-tuple-element.325.refs_2_), channel_id=1, source_target_pairs={{0,4},{4,0},{1,5},{5,1},{2,6},{6,2},{3,7},{7,3},{8,12},{12,8},{9,1... | collective-permute-start | bytes 2433032 | tf_op jit(solution)/shard_map/ppermute | solution.py:509
  58.1 6.0 %collective-permute-start.18 = (bf16[528,768]{1,0:T(8,128)(2,1)S(1)}, bf16[528,768]{1,0:T(8,128)(2,1)S(1)}, u32[]{:S(2)}, u32[]{:S(2)}) collective-permute-start(bf16[528,768]{1,0:T(8,128)(2,1)S(1)} %get-tuple-element.319.refs_1_), channel_id=1, source_target_pairs={{0,4},{4,0},{1,5},{5,1},{2,6},{6,2},{3,7},{7,3},{8,12},{12,8},{9,1... | collective-permute-start | bytes 2433032 | tf_op jit(solution)/shard_map/ppermute | solution.py:509
  64.0 2.4 %collective-permute-start.20 = (bf16[528,768]{1,0:T(8,128)(2,1)S(1)}, bf16[528,768]{1,0:T(8,128)(2,1)S(1)}, u32[]{:S(2)}, u32[]{:S(2)}) collective-permute-start(bf16[528,768]{1,0:T(8,128)(2,1)S(1)} %get-tuple-element.334.refs_3_), channel_id=1, source_target_pairs={{0,4},{4,0},{1,5},{5,1},{2,6},{6,2},{3,7},{7,3},{8,12},{12,8},{9,1... | collective-permute-start | bytes 2433032 | tf_op jit(solution)/shard_map/ppermute | solution.py:509
  66.3 15.8 %copy-start.3 = (s32[1024]{0:T(1024)S(1)}, s32[1024]{0:T(1024)}, u32[]{:S(2)}) copy-start(s32[1024]{0:T(1024)} %param.9) | copy-start | bytes 12292
  66.4 17.5 %copy-start = (f32[1024,768]{1,0:T(8,128)S(1)}, f32[1024,768]{1,0:T(8,128)}, u32[]{:S(2)}) copy-start(f32[1024,768]{1,0:T(8,128)} %emb_ref.1) | copy-start | bytes 9437188
  71.3 10.9 %all-to-all-start.3 = ((f32[16,1,128]{2,1,0:T(1,128)}), f32[16,1,128]{2,1,0:T(1,128)S(1)}, u32[]{:S(2)}, u32[]{:S(2)}) async-start(f32[16,1,128]{2,1,0:T(1,128)} %bitcast.14), calls=%async_computation.3 | async-start | bytes 16384 | tf_op jit(solution)/shard_map/all_to_all | solution.py:551

commit v11 on v10

--- a/solution.py
+++ b/solution.py
@@ -242,9 +242,7 @@
     table.extend([jnp.zeros((1, LANES), jnp.float32)] * (up(len(table), 8) - len(table)))
     table = jnp.concatenate(table, axis=0)
 
-    def places(expand, rank_row):
-        where = exact_dot(table, expand)
-        rank = rank_row(where)
+    def places(where, rank):
         place = jnp.full(rank.shape, -1.0, jnp.float32)
         for label in reversed(range(labels)):
             inside = rank < where[2 * label + 1 : 2 * label + 2, :]
@@ -253,12 +251,12 @@
 
     spot_block = jnp.where((spot >= block * held) & (spot < block * held + cap), 1.0, 0.0)
     spot_row = iota((1, total), 1).astype(jnp.float32)
-    place = places(spot_block, lambda where: spot_row - where[2 * labels : 2 * labels + 1, :])
+    where = exact_dot(table, spot_block)
+    place = places(where, spot_row - where[2 * labels : 2 * labels + 1, :])
     lanes = place_ref.shape[1]
     rank_row = iota((1, lanes), 1).astype(jnp.float32)
     for index in range(across):
-        only = jnp.where(iota((LANES, lanes), 0) == index, 1.0, 0.0)
-        place_ref[index : index + 1, :] = places(only, lambda where: rank_row)
+        place_ref[index : index + 1, :] = places(table[:, index : index + 1], rank_row)
 
     out_ref[space:, :] = jnp.zeros((STEP, out_ref.shape[1]), jnp.bfloat16)
     out_ref[space : space + ALIGN, 0:LANES] = jnp.broadcast_to(found, (ALIGN, LANES)).astype(

time: 84.5 us -> 84.5 us (level)
  no operation moved by 1% of the time
where the time goes in v11:
time: 84.5 us; the launch traced here: 84.3 us
  waiting for transfers between devices  35 us (41%)
  starting transfers between devices  29.4 us (35%)
  Pallas kernels  18.7 us (22%)
  between operations  1 us (1%)
    pallas_call x9, Pallas kernels, call(): pl.pallas_call(kernel, out_shape=out_shape, in_specs=[vmem] * len(inputs)...  18.7 us
    ppermute x1, waiting for transfers between devices, body(): pooled = lax.ppermute(pool_rows, 'tile', along(order[0]))  15 us
    ppermute x8, starting transfers between devices, send_far(): return lax.ppermute(blocks[side], ('chip', 'tile'), route)  11.8 us
    ppermute x8, waiting for transfers between devices, send_far(): return lax.ppermute(blocks[side], ('chip', 'tile'), route)  10.2 us
    ppermute x6, starting transfers between devices, send_across(): lax.ppermute(blocks[side], 'chip', over(side))  9.05 us
    all_to_all x1, waiting for transfers between devices, body(): lax.all_to_all(totals, ('chip', 'tile'), split_axis=0, concat_axis=0, til...  7.26 us
    ppermute x1, starting transfers between devices, body(): pooled = lax.ppermute(pool_rows, 'tile', along(order[0]))  4.1 us
    all_to_all x1, starting transfers between devices, body(): lax.all_to_all(totals, ('chip', 'tile'), split_axis=0, concat_axis=0, til...  3.61 us
  transfers between devices with their start and end apart: 20, of which 8 were waited for; matrix products, arithmetic and copies ran while one was open for 0% of the time, Pallas kernels for 10%

profile of v11, /device:TPU:0, one launch (start us, length us, event | category | flops | bytes accessed | tf_op | source)
XLA Modules:
  0.0 84.3 jit_solution(15701105687461547897)
XLA Ops:
  0.0 3.9 %plan.1 = (bf16[320,768]{1,0:T(8,128)(2,1)S(1)}, bf16[1152,768]{1,0:T(8,128)(2,1)S(1)}, s32[1,1152]{1,0:T(1,128)S(1)}, f32[1,1024]{1,0:T(1,128)S(1)}) custom-call(f32[1024,768]{1,0:T(8,128)} %emb_ref.1, s32[1,1024]{1,0:T(1,128)} %bitcast.74), custom_call_target="tpu_custom_call" | custom-call | tf_op jit(solution)/shard_map/plan/pallas_call | solution.py:420
  3.9 4.1 %collective-permute-start.5 = (bf16[320,768]{1,0:T(8,128)(2,1)S(1)}, bf16[320,768]{1,0:T(8,128)(2,1)S(1)}, u32[]{:S(2)}, u32[]{:S(2)}) collective-permute-start(bf16[320,768]{1,0:T(8,128)(2,1)S(1)} %get-tuple-element.315), channel_id=1, source_target_pairs={{0,2},{1,3},{2,0},{3,1},{4,6},{5,7},{6,4},{7,5},{8,10},{9,11},{10,... | collective-permute-start | bytes 1474568 | tf_op jit(solution)/shard_map/ppermute | solution.py:509
  8.0 3.2 %pack.1 = (bf16[104,768]{1,0:T(8,128)(2,1)S(1)}, bf16[104,768]{1,0:T(8,128)(2,1)S(1)}, bf16[104,768]{1,0:T(8,128)(2,1)S(1)}, bf16[104,768]{1,0:T(8,128)(2,1)S(1)...) custom-call(bf16[1152,768]{1,0:T(8,128)(2,1)S(1)} %get-tuple-element, ...), custom_call_target="tpu_custom_call" | custom-call | tf_op jit(solution)/shard_map/pack/pallas_call | solution.py:420
  11.1 1.6 %collective-permute-start.2 = (bf16[104,768]{1,0:T(8,128)(2,1)S(1)}, bf16[104,768]{1,0:T(8,128)(2,1)S(1)}, u32[]{:S(2)}, u32[]{:S(2)}) collective-permute-start(bf16[104,768]{1,0:T(8,128)(2,1)S(1)} %get-tuple-element.307), channel_id=1, source_target_pairs={{0,8},{8,0},{16,24},{24,16},{1,9},{9,1},{17,25},{25,17},{2,10},{10... | collective-permute-start | bytes 479240 | tf_op jit(solution)/shard_map/ppermute | solution.py:486
  12.7 1.5 %collective-permute-start.3 = (bf16[104,768]{1,0:T(8,128)(2,1)S(1)}, bf16[104,768]{1,0:T(8,128)(2,1)S(1)}, u32[]{:S(2)}, u32[]{:S(2)}) collective-permute-start(bf16[104,768]{1,0:T(8,128)(2,1)S(1)} %get-tuple-element.308), channel_id=1, source_target_pairs={{0,16},{8,24},{16,0},{24,8},{1,17},{9,25},{17,1},{25,9},{2,18},{10... | collective-permute-start | bytes 479240 | tf_op jit(solution)/shard_map/ppermute | solution.py:486
  14.7 3.5 %collective-permute-start.9 = (bf16[104,768]{1,0:T(8,128)(2,1)S(1)}, bf16[104,768]{1,0:T(8,128)(2,1)S(1)}, u32[]{:S(2)}, u32[]{:S(2)}) collective-permute-start(bf16[104,768]{1,0:T(8,128)(2,1)S(1)} %get-tuple-element.314), channel_id=1, source_target_pairs={{0,25},{1,26},{2,27},{3,24},{8,17},{9,18},{10,19},{11,16},{16,9},{... | collective-permute-start | bytes 479240 | tf_op jit(solution)/shard_map/ppermute | solution.py:491
  18.2 15.0 %collective-permute-done.5.pool_ref = bf16[320,768]{1,0:T(8,128)(2,1)S(1)} collective-permute-done((bf16[320,768]{1,0:T(8,128)(2,1)S(1)}, bf16[320,768]{1,0:T(8,128)(2,1)S(1)}, u32[]{:S(2)}, u32[]{:S(2)}) %collective-permute-start.5) | collective-permute-done | bytes 491552 | tf_op jit(solution)/shard_map/ppermute | solution.py:509
  33.2 1.7 %collective-permute-start.7 = (bf16[104,768]{1,0:T(8,128)(2,1)S(1)}, bf16[104,768]{1,0:T(8,128)(2,1)S(1)}, u32[]{:S(2)}, u32[]{:S(2)}) collective-permute-start(bf16[104,768]{1,0:T(8,128)(2,1)S(1)} %get-tuple-element.317), channel_id=1, source_target_pairs={{0,9},{1,10},{2,11},{3,8},{8,1},{9,2},{10,3},{11,0},{16,25},{17,26... | collective-permute-start | bytes 479240 | tf_op jit(solution)/shard_map/ppermute | solution.py:491
  34.9 3.4 %collective-permute-start.8 = (bf16[104,768]{1,0:T(8,128)(2,1)S(1)}, bf16[104,768]{1,0:T(8,128)(2,1)S(1)}, u32[]{:S(2)}, u32[]{:S(2)}) collective-permute-start(bf16[104,768]{1,0:T(8,128)(2,1)S(1)} %get-tuple-element.318), channel_id=1, source_target_pairs={{0,17},{1,18},{2,19},{3,16},{8,25},{9,26},{10,27},{11,24},{16,1},{... | collective-permute-start | bytes 479240 | tf_op jit(solution)/shard_map/ppermute | solution.py:491
  39.0 1.5 %collective-permute-start.10 = (bf16[104,768]{1,0:T(8,128)(2,1)S(1)}, bf16[104,768]{1,0:T(8,128)(2,1)S(1)}, u32[]{:S(2)}, u32[]{:S(2)}) collective-permute-start(bf16[104,768]{1,0:T(8,128)(2,1)S(1)} %get-tuple-element.322), channel_id=1, source_target_pairs={{0,8},{8,0},{16,24},{24,16},{1,9},{9,1},{17,25},{25,17},{2,10},{10... | collective-permute-start | bytes 479240 | tf_op jit(solution)/shard_map/ppermute | solution.py:486
  40.5 1.5 %collective-permute-start.11 = (bf16[104,768]{1,0:T(8,128)(2,1)S(1)}, bf16[104,768]{1,0:T(8,128)(2,1)S(1)}, u32[]{:S(2)}, u32[]{:S(2)}) collective-permute-start(bf16[104,768]{1,0:T(8,128)(2,1)S(1)} %get-tuple-element.323), channel_id=1, source_target_pairs={{0,16},{8,24},{16,0},{24,8},{1,17},{9,25},{17,1},{25,9},{2,18},{10... | collective-permute-start | bytes 479240 | tf_op jit(solution)/shard_map/ppermute | solution.py:486
  42.0 2.5 %collective-permute-start.12 = (bf16[104,768]{1,0:T(8,128)(2,1)S(1)}, bf16[104,768]{1,0:T(8,128)(2,1)S(1)}, u32[]{:S(2)}, u32[]{:S(2)}) collective-permute-start(bf16[104,768]{1,0:T(8,128)(2,1)S(1)} %get-tuple-element.324), channel_id=1, source_target_pairs={{0,24},{8,16},{16,8},{24,0},{1,25},{9,17},{17,9},{25,1},{2,26},{10... | collective-permute-start | bytes 479240 | tf_op jit(solution)/shard_map/ppermute | solution.py:486
  44.5 1.9 %collective-permute-done.7.refs_1_ = bf16[104,768]{1,0:T(8,128)(2,1)S(1)} collective-permute-done((bf16[104,768]{1,0:T(8,128)(2,1)S(1)}, bf16[104,768]{1,0:T(8,128)(2,1)S(1)}, u32[]{:S(2)}, u32[]{:S(2)}) %collective-permute-start.7) | collective-permute-done | bytes 159776 | tf_op jit(solution)/shard_map/ppermute | solution.py:491
  46.4 3.7 %collective-permute-done.8.refs_2_ = bf16[104,768]{1,0:T(8,128)(2,1)S(1)} collective-permute-done((bf16[104,768]{1,0:T(8,128)(2,1)S(1)}, bf16[104,768]{1,0:T(8,128)(2,1)S(1)}, u32[]{:S(2)}, u32[]{:S(2)}) %collective-permute-start.8) | collective-permute-done | bytes 159776 | tf_op jit(solution)/shard_map/ppermute | solution.py:491
  50.1 2.8 %collective-permute-start.15 = (bf16[104,768]{1,0:T(8,128)(2,1)S(1)}, bf16[104,768]{1,0:T(8,128)(2,1)S(1)}, u32[]{:S(2)}, u32[]{:S(2)}) collective-permute-start(bf16[104,768]{1,0:T(8,128)(2,1)S(1)} %get-tuple-element.332), channel_id=1, source_target_pairs={{0,19},{1,16},{2,17},{3,18},{8,27},{9,24},{10,25},{11,26},{16,3},{... | collective-permute-start | bytes 479240 | tf_op jit(solution)/shard_map/ppermute | solution.py:491
  53.6 1.2 %sort.4 = (bf16[528,768]{1,0:T(8,128)(2,1)S(1)}, s32[4,128]{1,0:T(4,128)S(1)}) custom-call(bf16[104,768]{1,0:T(8,128)(2,1)S(1)} %get-tuple-element.306.refs_0_, bf16[104,768]{1,0:T(8,128)(2,1)S(1)} %collective-permute-done.2.refs_1_, bf16[104,768]{1,0:T(8,128)(2,1)S(1)} %collective-permute-done.3.refs_2_, bf16[104,768]{1,0:T(8,128)(2,1)S(1)} %collective-permute-done.4.refs_3_), custom_call_target="tpu_custom_call" | custom-call | tf_op jit(solution)/shard_map/sort/pallas_call | solution.py:420
  54.9 1.3 %sort.5 = (bf16[528,768]{1,0:T(8,128)(2,1)S(1)}, s32[4,128]{1,0:T(4,128)S(1)}) custom-call(bf16[104,768]{1,0:T(8,128)(2,1)S(1)} %collective-permute-done.6.refs_0_, bf16[104,768]{1,0:T(8,128)(2,1)S(1)} %collective-permute-done.7.refs_1_, bf16[104,768]{1,0:T(8,128)(2,1)S(1)} %collective-permute-done.8.refs_2_, bf16[104,768]{1,0:T(8,128)(2,1)S(1)} %collective-permute-done.9.refs_3_), custom_call_target="tpu_custom_call" | custom-call | tf_op jit(solution)/shard_map/sort/pallas_call | solution.py:420
  56.2 1.2 %sort.6 = (bf16[528,768]{1,0:T(8,128)(2,1)S(1)}, s32[4,128]{1,0:T(4,128)S(1)}) custom-call(bf16[104,768]{1,0:T(8,128)(2,1)S(1)} %get-tuple-element.321.refs_0_, bf16[104,768]{1,0:T(8,128)(2,1)S(1)} %collective-permute-done.10.refs_1_, bf16[104,768]{1,0:T(8,128)(2,1)S(1)} %collective-permute-done.11.refs_2_, bf16[104,768]{1,0:T(8,128)(2,1)S(1)} %collective-permute-done.12.refs_3_), custom_call_target="tpu_custom_call" | custom-call | tf_op jit(solution)/shard_map/sort/pallas_call | solution.py:420
  58.1 2.8 %collective-permute-done.15.refs_2_ = bf16[104,768]{1,0:T(8,128)(2,1)S(1)} collective-permute-done((bf16[104,768]{1,0:T(8,128)(2,1)S(1)}, bf16[104,768]{1,0:T(8,128)(2,1)S(1)}, u32[]{:S(2)}, u32[]{:S(2)}) %collective-permute-start.15) | collective-permute-done | bytes 159776 | tf_op jit(solution)/shard_map/ppermute | solution.py:491
  60.9 1.8 %collective-permute-done.16.refs_3_ = bf16[104,768]{1,0:T(8,128)(2,1)S(1)} collective-permute-done((bf16[104,768]{1,0:T(8,128)(2,1)S(1)}, bf16[104,768]{1,0:T(8,128)(2,1)S(1)}, u32[]{:S(2)}, u32[]{:S(2)}) %collective-permute-start.16) | collective-permute-done | bytes 159776 | tf_op jit(solution)/shard_map/ppermute | solution.py:491
  64.1 2.3 %collective-permute-done.20.refs_7_ = bf16[528,768]{1,0:T(8,128)(2,1)S(1)} collective-permute-done((bf16[528,768]{1,0:T(8,128)(2,1)S(1)}, bf16[528,768]{1,0:T(8,128)(2,1)S(1)}, u32[]{:S(2)}, u32[]{:S(2)}) %collective-permute-start.20) | collective-permute-done | bytes 811040 | tf_op jit(solution)/shard_map/ppermute | solution.py:507
  66.4 5.0 %score.1 = f32[16,128]{1,0:T(8,128)} custom-call(bf16[528,768]{1,0:T(8,128)(2,1)S(1)} %get-tuple-element.310.refs_0_, bf16[528,768]{1,0:T(8,128)(2,1)S(1)} %get-tuple-element.319.refs_1_, bf16[528,768]{1,0:T(8,128)(2,1)S(1)} %get-tuple-element.325.refs_2_, bf16[528,768]{1,0:T(8,128)(2,1)S(1)} %get-tuple-element.334.refs_3_, ...), custom_call_target="tpu_custom_call" | custom-call | tf_op jit(solution)/shard_map/score/pallas_call | solution.py:420
  71.3 3.6 %all-to-all-start.3 = ((f32[16,1,128]{2,1,0:T(1,128)}), f32[16,1,128]{2,1,0:T(1,128)S(1)}, u32[]{:S(2)}, u32[]{:S(2)}) async-start(f32[16,1,128]{2,1,0:T(1,128)} %bitcast.14), calls=%async_computation.3 | async-start | bytes 16384 | tf_op jit(solution)/shard_map/all_to_all | solution.py:549
  74.9 7.3 %all-to-all-done.3 = f32[16,1,128]{2,1,0:T(1,128)S(1)} async-done(((f32[16,1,128]{2,1,0:T(1,128)}), f32[16,1,128]{2,1,0:T(1,128)S(1)}, u32[]{:S(2)}, u32[]{:S(2)}) %all-to-all-start.3) | async-done | bytes 8224 | tf_op jit(solution)/shard_map/all_to_all | solution.py:549
  (30 shorter events, 5.2 us)
Async XLA Ops:
  3.9 29.3 %collective-permute-start.5 = (bf16[320,768]{1,0:T(8,128)(2,1)S(1)}, bf16[320,768]{1,0:T(8,128)(2,1)S(1)}, u32[]{:S(2)}, u32[]{:S(2)}) collective-permute-start(bf16[320,768]{1,0:T(8,128)(2,1)S(1)} %get-tuple-element.315), channel_id=1, source_target_pairs={{0,2},{1,3},{2,0},{3,1},{4,6},{5,7},{6,4},{7,5},{8,10},{9,11},{10,... | collective-permute-start | bytes 1474568 | tf_op jit(solution)/shard_map/ppermute | solution.py:509
  11.1 22.0 %collective-permute-start.2 = (bf16[104,768]{1,0:T(8,128)(2,1)S(1)}, bf16[104,768]{1,0:T(8,128)(2,1)S(1)}, u32[]{:S(2)}, u32[]{:S(2)}) collective-permute-start(bf16[104,768]{1,0:T(8,128)(2,1)S(1)} %get-tuple-element.307), channel_id=1, source_target_pairs={{0,8},{8,0},{16,24},{24,16},{1,9},{9,1},{17,25},{25,17},{2,10},{10... | collective-permute-start | bytes 479240 | tf_op jit(solution)/shard_map/ppermute | solution.py:486
  12.7 20.5 %collective-permute-start.3 = (bf16[104,768]{1,0:T(8,128)(2,1)S(1)}, bf16[104,768]{1,0:T(8,128)(2,1)S(1)}, u32[]{:S(2)}, u32[]{:S(2)}) collective-permute-start(bf16[104,768]{1,0:T(8,128)(2,1)S(1)} %get-tuple-element.308), channel_id=1, source_target_pairs={{0,16},{8,24},{16,0},{24,8},{1,17},{9,25},{17,1},{25,9},{2,18},{10... | collective-permute-start | bytes 479240 | tf_op jit(solution)/shard_map/ppermute | solution.py:486
  14.2 18.9 %collective-permute-start.4 = (bf16[104,768]{1,0:T(8,128)(2,1)S(1)}, bf16[104,768]{1,0:T(8,128)(2,1)S(1)}, u32[]{:S(2)}, u32[]{:S(2)}) collective-permute-start(bf16[104,768]{1,0:T(8,128)(2,1)S(1)} %get-tuple-element.309), channel_id=1, source_target_pairs={{0,24},{8,16},{16,8},{24,0},{1,25},{9,17},{17,9},{25,1},{2,26},{10... | collective-permute-start | bytes 479240 | tf_op jit(solution)/shard_map/ppermute | solution.py:486
  14.7 18.5 %collective-permute-start.9 = (bf16[104,768]{1,0:T(8,128)(2,1)S(1)}, bf16[104,768]{1,0:T(8,128)(2,1)S(1)}, u32[]{:S(2)}, u32[]{:S(2)}) collective-permute-start(bf16[104,768]{1,0:T(8,128)(2,1)S(1)} %get-tuple-element.314), channel_id=1, source_target_pairs={{0,25},{1,26},{2,27},{3,24},{8,17},{9,18},{10,19},{11,16},{16,9},{... | collective-permute-start | bytes 479240 | tf_op jit(solution)/shard_map/ppermute | solution.py:491
  33.1 8.9 %collective-permute-start.6 = (bf16[104,768]{1,0:T(8,128)(2,1)S(1)}, bf16[104,768]{1,0:T(8,128)(2,1)S(1)}, u32[]{:S(2)}, u32[]{:S(2)}) collective-permute-start(bf16[104,768]{1,0:T(8,128)(2,1)S(1)} %get-tuple-element.316), channel_id=1, source_target_pairs={{0,1},{1,2},{2,3},{3,0},{8,9},{9,10},{10,11},{11,8},{16,17},{17,18... | collective-permute-start | bytes 479240 | tf_op jit(solution)/shard_map/ppermute | solution.py:491
  33.2 13.2 %collective-permute-start.7 = (bf16[104,768]{1,0:T(8,128)(2,1)S(1)}, bf16[104,768]{1,0:T(8,128)(2,1)S(1)}, u32[]{:S(2)}, u32[]{:S(2)}) collective-permute-start(bf16[104,768]{1,0:T(8,128)(2,1)S(1)} %get-tuple-element.317), channel_id=1, source_target_pairs={{0,9},{1,10},{2,11},{3,8},{8,1},{9,2},{10,3},{11,0},{16,25},{17,26... | collective-permute-start | bytes 479240 | tf_op jit(solution)/shard_map/ppermute | solution.py:491
  34.9 15.2 %collective-permute-start.8 = (bf16[104,768]{1,0:T(8,128)(2,1)S(1)}, bf16[104,768]{1,0:T(8,128)(2,1)S(1)}, u32[]{:S(2)}, u32[]{:S(2)}) collective-permute-start(bf16[104,768]{1,0:T(8,128)(2,1)S(1)} %get-tuple-element.318), channel_id=1, source_target_pairs={{0,17},{1,18},{2,19},{3,16},{8,25},{9,26},{10,27},{11,24},{16,1},{... | collective-permute-start | bytes 479240 | tf_op jit(solution)/shard_map/ppermute | solution.py:491
  39.0 11.2 %collective-permute-start.10 = (bf16[104,768]{1,0:T(8,128)(2,1)S(1)}, bf16[104,768]{1,0:T(8,128)(2,1)S(1)}, u32[]{:S(2)}, u32[]{:S(2)}) collective-permute-start(bf16[104,768]{1,0:T(8,128)(2,1)S(1)} %get-tuple-element.322), channel_id=1, source_target_pairs={{0,8},{8,0},{16,24},{24,16},{1,9},{9,1},{17,25},{25,17},{2,10},{10... | collective-permute-start | bytes 479240 | tf_op jit(solution)/shard_map/ppermute | solution.py:486
  40.5 12.7 %collective-permute-start.11 = (bf16[104,768]{1,0:T(8,128)(2,1)S(1)}, bf16[104,768]{1,0:T(8,128)(2,1)S(1)}, u32[]{:S(2)}, u32[]{:S(2)}) collective-permute-start(bf16[104,768]{1,0:T(8,128)(2,1)S(1)} %get-tuple-element.323), channel_id=1, source_target_pairs={{0,16},{8,24},{16,0},{24,8},{1,17},{9,25},{17,1},{25,9},{2,18},{10... | collective-permute-start | bytes 479240 | tf_op jit(solution)/shard_map/ppermute | solution.py:486
  42.0 14.1 %collective-permute-start.12 = (bf16[104,768]{1,0:T(8,128)(2,1)S(1)}, bf16[104,768]{1,0:T(8,128)(2,1)S(1)}, u32[]{:S(2)}, u32[]{:S(2)}) collective-permute-start(bf16[104,768]{1,0:T(8,128)(2,1)S(1)} %get-tuple-element.324), channel_id=1, source_target_pairs={{0,24},{8,16},{16,8},{24,0},{1,25},{9,17},{17,9},{25,1},{2,26},{10... | collective-permute-start | bytes 479240 | tf_op jit(solution)/shard_map/ppermute | solution.py:486
  46.4 11.1 %collective-permute-start.13 = (bf16[104,768]{1,0:T(8,128)(2,1)S(1)}, bf16[104,768]{1,0:T(8,128)(2,1)S(1)}, u32[]{:S(2)}, u32[]{:S(2)}) collective-permute-start(bf16[104,768]{1,0:T(8,128)(2,1)S(1)} %get-tuple-element.330), channel_id=1, source_target_pairs={{0,3},{1,0},{2,1},{3,2},{8,11},{9,8},{10,9},{11,10},{16,19},{17,16... | collective-permute-start | bytes 479240 | tf_op jit(solution)/shard_map/ppermute | solution.py:491
  50.1 7.9 %collective-permute-start.14 = (bf16[104,768]{1,0:T(8,128)(2,1)S(1)}, bf16[104,768]{1,0:T(8,128)(2,1)S(1)}, u32[]{:S(2)}, u32[]{:S(2)}) collective-permute-start(bf16[104,768]{1,0:T(8,128)(2,1)S(1)} %get-tuple-element.331), channel_id=1, source_target_pairs={{0,11},{1,8},{2,9},{3,10},{8,3},{9,0},{10,1},{11,2},{16,27},{17,24... | collective-permute-start | bytes 479240 | tf_op jit(solution)/shard_map/ppermute | solution.py:491
  50.1 10.8 %collective-permute-start.15 = (bf16[104,768]{1,0:T(8,128)(2,1)S(1)}, bf16[104,768]{1,0:T(8,128)(2,1)S(1)}, u32[]{:S(2)}, u32[]{:S(2)}) collective-permute-start(bf16[104,768]{1,0:T(8,128)(2,1)S(1)} %get-tuple-element.332), channel_id=1, source_target_pairs={{0,19},{1,16},{2,17},{3,18},{8,27},{9,24},{10,25},{11,26},{16,3},{... | collective-permute-start | bytes 479240 | tf_op jit(solution)/shard_map/ppermute | solution.py:491
  53.2 9.5 %collective-permute-start.16 = (bf16[104,768]{1,0:T(8,128)(2,1)S(1)}, bf16[104,768]{1,0:T(8,128)(2,1)S(1)}, u32[]{:S(2)}, u32[]{:S(2)}) collective-permute-start(bf16[104,768]{1,0:T(8,128)(2,1)S(1)} %get-tuple-element.333), channel_id=1, source_target_pairs={{0,27},{1,24},{2,25},{3,26},{8,19},{9,16},{10,17},{11,18},{16,11},... | collective-permute-start | bytes 479240 | tf_op jit(solution)/shard_map/ppermute | solution.py:491
  56.1 7.9 %collective-permute-start.17 = (bf16[528,768]{1,0:T(8,128)(2,1)S(1)}, bf16[528,768]{1,0:T(8,128)(2,1)S(1)}, u32[]{:S(2)}, u32[]{:S(2)}) collective-permute-start(bf16[528,768]{1,0:T(8,128)(2,1)S(1)} %get-tuple-element.310.refs_0_), channel_id=1, source_target_pairs={{0,4},{4,0},{1,5},{5,1},{2,6},{6,2},{3,7},{7,3},{8,12},{12,8},{9,1... | collective-permute-start | bytes 2433032 | tf_op jit(solution)/shard_map/ppermute | solution.py:507
  57.5 6.6 %collective-permute-start.19 = (bf16[528,768]{1,0:T(8,128)(2,1)S(1)}, bf16[528,768]{1,0:T(8,128)(2,1)S(1)}, u32[]{:S(2)}, u32[]{:S(2)}) collective-permute-start(bf16[528,768]{1,0:T(8,128)(2,1)S(1)} %get-tuple-element.325.refs_2_), channel_id=1, source_target_pairs={{0,4},{4,0},{1,5},{5,1},{2,6},{6,2},{3,7},{7,3},{8,12},{12,8},{9,1... | collective-permute-start | bytes 2433032 | tf_op jit(solution)/shard_map/ppermute | solution.py:507
  58.1 6.0 %collective-permute-start.18 = (bf16[528,768]{1,0:T(8,128)(2,1)S(1)}, bf16[528,768]{1,0:T(8,128)(2,1)S(1)}, u32[]{:S(2)}, u32[]{:S(2)}) collective-permute-start(bf16[528,768]{1,0:T(8,128)(2,1)S(1)} %get-tuple-element.319.refs_1_), channel_id=1, source_target_pairs={{0,4},{4,0},{1,5},{5,1},{2,6},{6,2},{3,7},{7,3},{8,12},{12,8},{9,1... | collective-permute-start | bytes 2433032 | tf_op jit(solution)/shard_map/ppermute | solution.py:507
  64.0 2.4 %collective-permute-start.20 = (bf16[528,768]{1,0:T(8,128)(2,1)S(1)}, bf16[528,768]{1,0:T(8,128)(2,1)S(1)}, u32[]{:S(2)}, u32[]{:S(2)}) collective-permute-start(bf16[528,768]{1,0:T(8,128)(2,1)S(1)} %get-tuple-element.334.refs_3_), channel_id=1, source_target_pairs={{0,4},{4,0},{1,5},{5,1},{2,6},{6,2},{3,7},{7,3},{8,12},{12,8},{9,1... | collective-permute-start | bytes 2433032 | tf_op jit(solution)/shard_map/ppermute | solution.py:507
  66.4 15.9 %copy-start.3 = (s32[1024]{0:T(1024)S(1)}, s32[1024]{0:T(1024)}, u32[]{:S(2)}) copy-start(s32[1024]{0:T(1024)} %param.9) | copy-start | bytes 12292
  66.4 17.5 %copy-start = (f32[1024,768]{1,0:T(8,128)S(1)}, f32[1024,768]{1,0:T(8,128)}, u32[]{:S(2)}) copy-start(f32[1024,768]{1,0:T(8,128)} %emb_ref.1) | copy-start | bytes 9437188
  71.3 10.9 %all-to-all-start.3 = ((f32[16,1,128]{2,1,0:T(1,128)}), f32[16,1,128]{2,1,0:T(1,128)S(1)}, u32[]{:S(2)}, u32[]{:S(2)}) async-start(f32[16,1,128]{2,1,0:T(1,128)} %bitcast.14), calls=%async_computation.3 | async-start | bytes 16384 | tf_op jit(solution)/shard_map/all_to_all | solution.py:549
